TPU v7x, 128 devices: a whole 4x4x4 slice. The times are simulated.
128 devices in a mesh: row: 8 (over x, z_hi), col: 16 (over z_lo, y, core).
Axes of the slice: x: 4, y: 4, z: 4 (z_hi: 2, z_lo: 2; z = z_hi * 2 + z_lo), core: 2. Of those that a mesh axis runs over, the one named last changes fastest.
Arguments:
- fine_qkv: bfloat16 [3, 128, 256, 384], P(None, 'row', 'col'), may hold values from -256 to 256
- coarse_qkv: bfloat16 [3, 128, 64, 1536], P(None, 'col', None, 'row'), may hold values from -256 to 256
- grad_coarse: bfloat16 [128, 64, 1536], P('col', None, 'row'), may hold values from -256 to 256
- merge_weight: bfloat16 [1536, 1536], replicated, may hold values from -0.15625 to 0.15625
- qkv_weight: bfloat16 [3, 1536, 1536], P(None, None, 'row'), may hold values from -0.15625 to 0.15625
Outputs:
- grad_query_fine: bfloat16 [128, 256, 384], P('row', 'col')
- grad_key_fine: bfloat16 [128, 256, 384], P('row', 'col')
- grad_value_fine: bfloat16 [128, 256, 384], P('row', 'col')
All inputs are finite; a program needn't handle non-finite values.
Results may differ from a plain program's by a relative error of at most 0.025.
Values may be sent and summed in bfloat16 or wider, within the bound.
No kernel may reach another device: no remote copies, remote signals or barrier semaphores. Data moves between devices by JAX's collectives and lax.ppermute only.
A program may use at most 320 MiB of HBM per device.

v0:
```python
import jax
import jax.numpy as jnp
from jax import lax
from jax.experimental import pallas as pl
from jax.experimental.pallas import tpu as pltpu
from jax.sharding import Mesh
from jax.sharding import PartitionSpec as P

HD = 64
RADIUS = 7
SCALE = 0.125
SIDE = 32
RIM = 8
HIDDEN = -1e30
ROW = ("x", "zh")
COL = ("zl", "y", "c")
F32 = jnp.float32
BF16 = jnp.bfloat16
VMEM = 60 << 20


def nt(left, right):
    return lax.dot_general(left, right, (((1,), (1,)), ((), ())), preferred_element_type=F32)


def nn(left, right):
    return lax.dot_general(left, right, (((1,), (0,)), ((), ())), preferred_element_type=F32)


def half(pair, which):
    lane = lax.broadcasted_iota(jnp.int32, pair.shape, 1)
    return jnp.where((lane < HD) == (which == 0), pair, jnp.zeros_like(pair))


def cost(flops, bytes_accessed, exps):
    return pl.CostEstimate(flops=flops, bytes_accessed=bytes_accessed, transcendentals=exps)


def prepare(coarse_qkv, grad_coarse):
    _, tokens, group = coarse_qkv.shape
    heads = group // HD

    def body(qkv_ref, up_ref, kv_out, qu_out):
        for head in range(heads):
            lanes = slice(head * HD, head * HD + HD)
            kv_out[head] = jnp.concatenate([qkv_ref[1, :, lanes], qkv_ref[2, :, lanes]], axis=1)
            qu_out[head] = jnp.concatenate([qkv_ref[0, :, lanes], up_ref[:, lanes]], axis=1)

    return whole_call(
        body,
        [jax.ShapeDtypeStruct((heads, tokens, 2 * HD), BF16)] * 2,
        "prepare",
        1 << 20,
        [],
        coarse_qkv,
        grad_coarse,
    )


def own_block(step, tokens):
    count = lax.axis_size("y")
    owner = (lax.axis_index("y") + count - step) % count
    return pl.ds(pl.multiple_of(owner * tokens, tokens), tokens)


def coarse_stats(key_values, query_ups, key_tile):
    heads, tokens, _ = key_values[0].shape
    blocks = len(query_ups)
    per_block = tokens // key_tile

    def body(*refs):
        kv_refs, qu_refs = refs[:blocks], refs[blocks : 2 * blocks]
        out_ref, held = refs[2 * blocks :]
        for at in range(blocks):

            @pl.when(pl.program_id(1) == at)
            def _():
                held[...] = qu_refs[at][0]

        query = half(held[...], 0) * BF16(SCALE)
        upstream = half(held[...], 1)
        peak = jnp.full((1, tokens), -jnp.inf, F32)
        total = jnp.zeros((1, tokens), F32)
        weighted = jnp.zeros((1, tokens), F32)
        for i in range(blocks * per_block):
            start = (i % per_block) * key_tile
            tile = kv_refs[i // per_block][0, start : start + key_tile, :]
            score = nt(tile, query)
            product = nt(tile, upstream)
            new_peak = jnp.maximum(peak, jnp.max(score, axis=0, keepdims=True))
            decay = jnp.exp(peak - new_peak)
            share = jnp.exp(score - new_peak)
            total = total * decay + jnp.sum(share, axis=0, keepdims=True)
            weighted = weighted * decay + jnp.sum(share * product, axis=0, keepdims=True)
            peak = new_peak
        found = jnp.concatenate([peak + jnp.log(total), weighted / total], axis=0)
        out_ref[0, :, own_block(pl.program_id(1), tokens)] = found

    pairs = heads * (blocks * tokens) ** 2
    return pl.pallas_call(
        body,
        grid=(heads, blocks),
        in_specs=[pl.BlockSpec((1, tokens, 128), lambda h, q: (h, 0, 0))] * (2 * blocks),
        out_specs=pl.BlockSpec((1, 2, blocks * tokens), lambda h, q: (h, 0, 0)),
        out_shape=jax.ShapeDtypeStruct((heads, 2, blocks * tokens), F32),
        scratch_shapes=[pltpu.VMEM((tokens, 128), BF16)],
        name="coarse_stats",
        cost_estimate=cost(4 * pairs * 256, 2 << 20, pairs),
        compiler_params=pltpu.CompilerParams(vmem_limit_bytes=VMEM),
    )(*key_values, *query_ups)


def coarse_grads(key_values, query_ups, stats):
    heads, tokens, _ = key_values[0].shape
    blocks = len(query_ups)
    parts = stats.shape[0]

    def body(*refs):
        kv_refs, qu_refs = refs[:blocks], refs[blocks : 2 * blocks]
        stats_ref, kept_ref, sent_ref = refs[2 * blocks : 2 * blocks + 3]
        q_outs = refs[-blocks - 2 : -2]
        acc, held = refs[-2:]
        for at in range(blocks):

            @pl.when(pl.program_id(1) == at)
            def _():
                held[...] = qu_refs[at][0]

        @pl.when(pl.program_id(1) == 0)
        def _():
            acc[...] = jnp.zeros_like(acc)

        query = half(held[...], 0) * BF16(SCALE)
        upstream = half(held[...], 1)
        found = [stats_ref[i, 0, :, own_block(pl.program_id(1), tokens)] for i in range(parts)]
        peak = found[0][:1]
        for part in found[1:]:
            peak = jnp.maximum(peak, part[:1])
        shares = [jnp.exp(part[:1] - peak) for part in found]
        total = sum(shares)
        log_total = peak + jnp.log(total)
        delta = sum(share * part[1:] for share, part in zip(shares, found)) / total
        found = jnp.zeros((HD, tokens), F32)
        for i in range(blocks):
            tile = kv_refs[i][0]
            share = jnp.exp(nt(tile, query) - log_total)
            grads = (share * (nt(tile, upstream) - delta)).astype(BF16)
            acc[i] += nn(grads, query) + nn(share.astype(BF16), upstream)
            found += nn(tile[:, :HD].T, grads)
        found = (found * SCALE).astype(BF16)
        for at in range(blocks):

            @pl.when(pl.program_id(1) == at)
            def _():
                q_outs[at][...] = found

        @pl.when(pl.program_id(1) == blocks - 1)
        def _():
            for i in range(blocks // 2):
                kept_ref[0, i] = acc[2 * i].astype(BF16)
                sent_ref[0, i] = acc[2 * i + 1].astype(BF16)

    pairs = heads * (blocks * tokens) ** 2
    out_shape = [jax.ShapeDtypeStruct((heads, blocks // 2, tokens, 128), BF16)] * 2
    out_shape += [jax.ShapeDtypeStruct((heads * HD, tokens), BF16)] * blocks
    return pl.pallas_call(
        body,
        grid=(heads, blocks),
        in_specs=[pl.BlockSpec((1, tokens, 128), lambda h, q: (h, 0, 0))] * (2 * blocks)
        + [pl.BlockSpec((parts, 1, 2, blocks * tokens), lambda h, q: (0, h, 0, 0))],
        out_specs=[pl.BlockSpec((1, blocks // 2, tokens, 128), lambda h, q: (h, 0, 0, 0))] * 2
        + [pl.BlockSpec((HD, tokens), lambda h, q: (h, 0))] * blocks,
        out_shape=out_shape,
        scratch_shapes=[
            pltpu.VMEM((blocks, tokens, 128), F32),
            pltpu.VMEM((tokens, 128), BF16),
        ],
        name="coarse_grads",
        cost_estimate=cost(10 * pairs * 256, 4 << 20, pairs),
        compiler_params=pltpu.CompilerParams(vmem_limit_bytes=VMEM),
    )(*key_values, *query_ups, stats)


def whole_call(body, out_shape, name, flops, scratch, *operands):
    return pl.pallas_call(
        body,
        out_shape=out_shape,
        scratch_shapes=scratch,
        name=name,
        cost_estimate=cost(flops, 6 << 20, 1 << 20),
        compiler_params=pltpu.CompilerParams(vmem_limit_bytes=VMEM),
    )(*operands)


def pairs_of(width):
    return [(pair, slice(pair * 128, pair * 128 + 128)) for pair in range(width // 128)]


def window_bias(own, rows, columns, part, transposed):
    count = SIDE * SIDE // 2
    shape = (own, count) if transposed else (count, own)
    ext = lax.broadcasted_iota(jnp.int32, shape, 1 if transposed else 0)
    inner = lax.broadcasted_iota(jnp.int32, shape, 0 if transposed else 1)
    if part == 0:
        ext_row, ext_column = ext >> 4, (ext & 15) + RIM
    else:
        ext_row = (ext & 255) >> 3
        ext_column = (ext & 7) + jnp.where(ext >= 256, SIDE - RIM, 0)
    row_gap = ext_row - (inner >> 4) - RIM
    column_gap = ext_column - (inner & 15) - RIM
    row = ext_row + (lax.axis_index(ROW) * rows - RIM)
    column = ext_column + (lax.axis_index(COL) * columns - RIM)
    seen = (jnp.abs(row_gap) <= RADIUS) & (jnp.abs(column_gap) <= RADIUS)
    seen &= (row >= 0) & (row < lax.axis_size(ROW) * rows)
    seen &= (column >= 0) & (column < lax.axis_size(COL) * columns)
    return jnp.where(seen, 0.0, HIDDEN).astype(F32)


def fill_bias(bias_ref, own, rows, columns):
    count = SIDE * SIDE // 2
    for part in range(2):
        bias_ref[part * count : (part + 1) * count, :] = window_bias(
            own, rows, columns, part, False
        )


def stacked(refs, which, lanes):
    return jnp.concatenate([ref[which, :, lanes] for ref in refs], axis=0)


def fine_grads(own_qkv, ext_kv, own_up, rows, columns):
    _, own, width = own_qkv.shape
    sizes = [ref.shape[1] for ref in ext_kv]
    places = [sum(sizes[:i]) for i in range(len(sizes))]

    def body(q_ref, mid_ref, low_ref, high_ref, up_ref, q_out, mid_out, low_out, high_out, bias_ref):
        fill_bias(bias_ref, own, rows, columns)
        ext = (mid_ref, low_ref, high_ref)
        outs = (mid_out, low_out, high_out)
        for pair, lanes in pairs_of(width):
            key = stacked(ext, 0, lanes)
            key_t = key.T
            value = stacked(ext, 1, lanes)
            parts = []
            key_sum = jnp.zeros((SIDE * SIDE, 128), F32)
            value_sum = jnp.zeros((SIDE * SIDE, 128), F32)
            for side in range(2):
                query = half(q_ref[0, :, lanes], side) * BF16(SCALE)
                up = half(up_ref[:, lanes], side)
                score = nt(key, query) + bias_ref[...]
                product = nt(value, up)
                share = jnp.exp(score - jnp.max(score, axis=0, keepdims=True))
                total = jnp.sum(share, axis=0, keepdims=True)
                delta = jnp.sum(share * product, axis=0, keepdims=True) / total
                share = share * (1.0 / total)
                grads = (share * (product - delta)).astype(BF16)
                key_sum += nn(grads, query)
                value_sum += nn(share.astype(BF16), up)
                parts.append(nn(key_t[side * HD : side * HD + HD], grads))
            q_out[:, lanes] = (jnp.concatenate(parts, axis=0).T * SCALE).astype(BF16)
            for out, place, size in zip(outs, places, sizes):
                right = slice(width + pair * 128, width + pair * 128 + 128)
                out[:, lanes] = key_sum[place : place + size].astype(out.dtype)
                out[:, right] = value_sum[place : place + size].astype(out.dtype)

    return whole_call(
        body,
        [jax.ShapeDtypeStruct((own, width), BF16)]
        + [
            jax.ShapeDtypeStruct((size, 2 * width), BF16 if i else F32)
            for i, size in enumerate(sizes)
        ],
        "fine_grads",
        2 << 30,
        [pltpu.VMEM((SIDE * SIDE, own), F32)],
        own_qkv,
        *ext_kv,
        own_up,
    )


def add_columns(mid, from_left, from_right, columns):
    cells, wide = mid.shape
    tall = cells // columns
    edge = RIM * columns

    def body(mid_ref, left_ref, right_ref, top_out, own_out, bottom_out):
        left = left_ref[...].astype(F32).reshape(tall, RIM, wide)
        right = right_ref[...].astype(F32).reshape(tall, RIM, wide)
        both = jnp.concatenate([left, right], axis=1).reshape(cells, wide)
        total = mid_ref[...] + both
        top_out[...] = total[:edge].astype(BF16)
        own_out[...] = total[edge : cells - edge]
        bottom_out[...] = total[cells - edge :].astype(BF16)

    return whole_call(
        body,
        [
            jax.ShapeDtypeStruct((edge, wide), BF16),
            jax.ShapeDtypeStruct((cells - 2 * edge, wide), F32),
            jax.ShapeDtypeStruct((edge, wide), BF16),
        ],
        "add_columns",
        1 << 20,
        [],
        mid,
        from_left,
        from_right,
    )


def add_rows(own, from_above, from_below):
    cells, wide = own.shape
    width = wide // 2

    def body(own_ref, above_ref, below_ref, k_out, v_out):
        arrived = jnp.concatenate([above_ref[...], below_ref[...]], axis=0)
        total = own_ref[...] + arrived.astype(F32)
        k_out[...] = total[:, :width].astype(BF16)
        v_out[...] = total[:, width:].astype(BF16)

    return whole_call(
        body,
        [jax.ShapeDtypeStruct((cells, width), BF16)] * 2,
        "add_rows",
        1 << 20,
        [],
        own,
        from_above,
        from_below,
    )


def project(query_pieces, kept, from_core, arrived, joint, columns, count):
    group, tokens = query_pieces[0].shape
    heads = kept.shape[0]
    rows = tokens // columns
    each = rows // count
    size = each * columns
    wide = joint.shape[2]

    def body(*refs):
        pieces = refs[: len(query_pieces)]
        kept_ref, core_ref, arrived_ref, joint_ref, out, held, weight = refs[len(query_pieces) :]
        for head in range(heads):
            total = kept_ref[head, 0].astype(F32) + core_ref[head, 0].astype(F32)
            held[:, head * 128 : head * 128 + 128] = total + arrived_ref[head].astype(F32)
            for part in range(2):
                at = head * 128 + part * HD
                weight[at : at + HD, :] = joint_ref[1 + part, head * HD : head * HD + HD, :]
        weight[2 * group :, :] = joint_ref[0]
        total = pieces[0][...].astype(F32)
        for piece in pieces[1:]:
            total += piece[...].astype(F32)
        held[:, 2 * group :] = total.T
        for at in range(count):
            taken = [
                held[c * rows + at * each : c * rows + (at + 1) * each, :] for c in range(columns)
            ]
            chosen = jnp.concatenate(taken, axis=0).astype(BF16)
            out[at] = nn(chosen, weight[...]).astype(BF16)

    return whole_call(
        body,
        jax.ShapeDtypeStruct((count, size, wide), BF16),
        "project",
        2 << 30,
        [pltpu.VMEM((tokens, 3 * group), F32), pltpu.VMEM((3 * group, wide), BF16)],
        *query_pieces,
        kept,
        from_core,
        arrived,
        joint,
    )


def spread(pieces, columns):
    count, tokens, wide = pieces.shape
    width = wide // 4

    def body(in_ref, out):
        total = in_ref[0].astype(F32)
        for at in range(1, count):
            total += in_ref[at].astype(F32)
        total = total.astype(BF16)
        cells = 2 * tokens
        fine = lax.broadcasted_iota(jnp.int32, (cells, tokens), 0)
        token = lax.broadcasted_iota(jnp.int32, (cells, tokens), 1)
        cell = (token & 7) * 2 * columns + (token >> 3) * 2
        for a in range(2):
            grid = jnp.zeros((cells, width), F32)
            for b in range(2):
                place = jnp.where(fine == cell + b, 1.0, 0.0).astype(BF16)
                lanes = slice((2 * a + b) * width, (2 * a + b + 1) * width)
                grid += nn(place, total[:, lanes])
            grid = grid.astype(BF16)
            for row in range(tokens // columns):
                at = (2 * row + a) * 2 * columns
                out[at : at + 2 * columns, :] = grid[row * 2 * columns : (row + 1) * 2 * columns]

    return whole_call(
        body,
        jax.ShapeDtypeStruct((4 * tokens, width), BF16),
        "spread",
        1 << 28,
        [],
        pieces,
    )


def shifted(array, axis, step):
    count = lax.axis_size(axis)
    return lax.ppermute(array, axis, [(i, (i + step) % count) for i in range(count)])


def swapped(array, axis):
    return lax.ppermute(array, axis, [(0, 1), (1, 0)])


def onward(low, high, axis):
    count = lax.axis_size(axis)
    forward = [(i, i + 1) for i in range(count - 1)]
    backward = [(i + 1, i) for i in range(count - 1)]
    return lax.ppermute(low, axis, forward), lax.ppermute(high, axis, backward)


def edges(block, axis, at):
    size = block.shape[at]
    return onward(
        lax.slice_in_dim(block, size - RIM, None, axis=at),
        lax.slice_in_dim(block, 0, RIM, axis=at),
        axis,
    )


def with_rows(block, dim):
    low, high = edges(block, ROW, dim)
    return jnp.concatenate([low, block, high], axis=dim)


def with_columns(block, dim):
    low, high = edges(block, COL, dim + 1)
    shape = block.shape[:dim] + (-1, block.shape[-1])
    return block.reshape(shape), low.reshape(shape), high.reshape(shape)


def shards(fine_qkv, coarse_qkv, grad_coarse, merge_weight, qkv_weight):
    rows, columns, width = fine_qkv.shape[1:]
    own = rows * columns
    coarse_columns, coarse_rows, group = grad_coarse.shape
    tokens = coarse_columns * coarse_rows

    key_value, query_up = prepare(
        coarse_qkv.reshape(3, tokens, group), grad_coarse.reshape(tokens, group)
    )
    across = swapped(key_value, "zl")
    beside = swapped(key_value, "c")
    queries = [query_up] + [shifted(query_up, "y", step) for step in (1, 3, 2)]
    queries = [queries[i] for i in (0, 1, 3, 2)]
    corner = swapped(across, "c")
    keys = [key_value, beside, across, corner]

    own_qkv = fine_qkv.reshape(3, own, width)
    tall = with_rows(fine_qkv[1:], 1)
    queries, tall = lax.optimization_barrier((queries, tall))
    ext_kv = with_columns(tall, 1)

    part = coarse_stats(keys, queries, 256)
    stats = lax.all_gather(part, "y", axis=0)
    kept, sent, *query_grads = coarse_grads(keys, queries, stats)

    sent, merge_weight = lax.optimization_barrier((sent, merge_weight))
    from_core = swapped(sent, "c")
    query_pieces = [query_grads[0]]
    for step in (1, 2, 3):
        query_pieces.append(shifted(query_grads[step], "y", -step))
    passed = (kept[:, 1].astype(F32) + from_core[:, 1].astype(F32)).astype(BF16)
    arrived = swapped(passed, "zl")
    joint = lax.dot_general(
        qkv_weight, merge_weight, (((1,), (1,)), ((), ())), preferred_element_type=F32
    ).astype(BF16)
    count = lax.axis_size(ROW)
    projected = project(
        query_pieces, kept, from_core, arrived, joint, coarse_columns, count
    )
    pieces = lax.all_to_all(projected, ROW, 0, 0)
    own_up = spread(pieces, coarse_columns)

    grad_query, mid, low, high = fine_grads(own_qkv, ext_kv, own_up, rows, columns)
    from_left, from_right = onward(high, low, COL)
    top, middle, bottom = add_columns(mid, from_left, from_right, columns)
    from_above, from_below = onward(bottom, top, ROW)
    grad_key, grad_value = add_rows(middle, from_above, from_below)
    shape = (rows, columns, width)
    return grad_query.reshape(shape), grad_key.reshape(shape), grad_value.reshape(shape)


def solution(mesh):
    split = Mesh(mesh.devices.reshape(4, 2, 2, 4, 2), ROW + COL)
    return jax.shard_map(
        shards,
        mesh=split,
        in_specs=(
            P(None, ROW, COL, None),
            P(None, COL, None, ROW),
            P(COL, None, ROW),
            P(),
            P(None, None, ROW),
        ),
        out_specs=(P(ROW, COL, None), P(ROW, COL, None), P(ROW, COL, None)),
        check_vma=False,
    )
```

profile of v0, /device:TPU:96, one launch (start us, length us, event | category | flops | bytes accessed | tf_op | source)
XLA Modules:
  0.0 209.7 jit_solution(2064881699965341772)
XLA Ops:
  0.6 0.0 copy-start
  0.6 0.0 copy-start.2
  0.7 0.0 slice-start
  0.7 2.5 %prepare.1 = (bf16[3,512,128]{2,1,0:T(8,128)(2,1)}, bf16[3,512,128]{2,1,0:T(8,128)(2,1)}) custom-call(bf16[3,512,192]{2,1,0:T(8,128)(2,1)} %bitcast.25, bf16[512,192]{1,0:T(8,128)(2,1)} %bitcast.28), custom_call_target="tpu_custom_call" | custom-call | flops 1048576 | bytes 6291456 | tf_op jit(solution)/shard_map/prepare/pallas_call | solution.py:185
  3.1 0.4 collective-permute-start.8
  3.6 3.1 %collective-permute-start.3 = (bf16[2,8,16,384]{3,2,1,0:T(8,128)(2,1)S(1)}, bf16[2,8,16,384]{3,2,1,0:T(8,128)(2,1)S(1)}, u32[]{:S(2)}, u32[]{:S(2)}) collective-permute-start(bf16[2,8,16,384]{3,2,1,0:T(8,128)(2,1)S(1)} %get-tuple-element.53), channel_id=1, source_target_pairs={{0,16},{16,32},{32,48},{48,64},{64,80},{80,96},{96,112},{1,17},{17... | collective-permute-start | bytes 589832 | tf_op jit(solution)/shard_map/ppermute | solution.py:424
  6.7 4.3 %collective-permute-start.4 = (bf16[2,8,16,384]{3,2,1,0:T(8,128)(2,1)S(1)}, bf16[2,8,16,384]{3,2,1,0:T(8,128)(2,1)S(1)}, u32[]{:S(2)}, u32[]{:S(2)}) collective-permute-start(bf16[2,8,16,384]{3,2,1,0:T(8,128)(2,1)S(1)} %get-tuple-element.54), channel_id=1, source_target_pairs={{16,0},{32,16},{48,32},{64,48},{80,64},{96,80},{112,96},{17,1},{33... | collective-permute-start | bytes 589832 | tf_op jit(solution)/shard_map/ppermute | solution.py:424
  11.0 1.6 collective-permute-start
  12.6 2.9 %collective-permute-start.1 = (bf16[3,512,128]{2,1,0:T(8,128)(2,1)}, bf16[3,512,128]{2,1,0:T(8,128)(2,1)}, u32[]{:S(2)}, u32[]{:S(2)}) collective-permute-start(bf16[3,512,128]{2,1,0:T(8,128)(2,1)} %get-tuple-element.30.refs_4_), channel_id=1, source_target_pairs={{0,4},{2,6},{4,0},{6,2},{1,5},{3,7},{5,1},{7,3},{8,12},{10,14},{12... | collective-permute-start | bytes 1179656 | tf_op jit(solution)/shard_map/ppermute | solution.py:413
  15.5 5.9 %collective-permute-done.3 = bf16[2,8,16,384]{3,2,1,0:T(8,128)(2,1)S(1)} collective-permute-done((bf16[2,8,16,384]{3,2,1,0:T(8,128)(2,1)S(1)}, bf16[2,8,16,384]{3,2,1,0:T(8,128)(2,1)S(1)}, u32[]{:S(2)}, u32[]{:S(2)}) %collective-permute-start.3) | collective-permute-done | bytes 196640 | tf_op jit(solution)/shard_map/ppermute | solution.py:424
  21.4 3.0 %collective-permute-start.2 = (bf16[3,512,128]{2,1,0:T(8,128)(2,1)}, bf16[3,512,128]{2,1,0:T(8,128)(2,1)}, u32[]{:S(2)}, u32[]{:S(2)}) collective-permute-start(bf16[3,512,128]{2,1,0:T(8,128)(2,1)} %get-tuple-element.30.refs_4_), channel_id=1, source_target_pairs={{0,6},{2,0},{4,2},{6,4},{1,7},{3,1},{5,3},{7,5},{8,14},{10,8},{12,... | collective-permute-start | bytes 1179656 | tf_op jit(solution)/shard_map/ppermute | solution.py:413
  24.4 0.0 collective-permute-done.4
  24.5 0.0 collective-permute-start.7
  24.5 0.0 collective-permute-done.8.refs_2_
  24.5 0.5 collective-permute-start.9
  25.0 0.1 pad_maximum_fusion
  25.1 0.0 collective-permute-done.refs_5_
  25.1 7.1 %collective-permute-done.1.refs_6_ = bf16[3,512,128]{2,1,0:T(8,128)(2,1)} collective-permute-done((bf16[3,512,128]{2,1,0:T(8,128)(2,1)}, bf16[3,512,128]{2,1,0:T(8,128)(2,1)}, u32[]{:S(2)}, u32[]{:S(2)}) %collective-permute-start.1) | collective-permute-done | bytes 393248 | tf_op jit(solution)/shard_map/ppermute | solution.py:413
  32.2 0.3 collective-permute-done.2.refs_7_
  32.6 0.0 collective-permute-done.7.refs_1_
  32.6 0.0 collective-permute-done.9.refs_3_
  32.6 23.3 %coarse_stats.1 = f32[3,2,2048]{2,1,0:T(2,128)} custom-call(bf16[3,512,128]{2,1,0:T(8,128)(2,1)} %get-tuple-element.29.refs_0_, bf16[3,512,128]{2,1,0:T(8,128)(2,1)} %collective-permute-done.7.refs_1_, bf16[3,512,128]{2,1,0:T(8,128)(2,1)} %copy-done.6, bf16[3,512,128]{2,1,0:T(8,128)(2,1)} %collective-permute-done.9.refs_3_, ...), custom_call_target="tpu_custom_call" | custom-call | flops 12884901888 | bytes 2097152 | tf_op jit(solution)/shard_map/coarse_stats/pallas_call | solution.py:100
  55.9 15.0 %all-gather = f32[12,2,2048]{2,1,0:T(2,128)} all-gather(f32[3,2,2048]{2,1,0:T(2,128)} %coarse_stats.1), channel_id=2, replica_groups=mesh['x'=4,'zh'=2,'zl'=2,'y'=4,'c'=2] {'y'}, dimensions={0}, use_global_device_ids=true | all-gather | bytes 245760 | tf_op jit(solution)/shard_map/all_gather | solution.py:469
  70.9 36.8 %coarse_grads.1 = (bf16[3,2,512,128]{3,2,1,0:T(8,128)(2,1)}, bf16[3,2,512,128]{3,2,1,0:T(8,128)(2,1)}, bf16[192,512]{1,0:T(8,128)(2,1)}, bf16[192,512]{1,0:T(8,1...) custom-call(bf16[3,512,128]{2,1,0:T(8,128)(2,1)} %get-tuple-element.29.refs_0_, ...), custom_call_target="tpu_custom_call" | custom-call | flops 32212254720 | bytes 4194304 | tf_op jit(solution)/shard_map/coarse_grads/pallas_call | solution.py:166
  107.8 1.2 copy.11
  108.9 0.1 collective-permute-start.13
  109.0 2.0 collective-permute-start.10
  111.0 0.9 collective-permute-start.11
  111.9 0.1 collective-permute-start.12
  112.0 4.9 %fusion.3 = f32[1536,576]{0,1:S(1)} fusion(bf16[1536,1536]{1,0:T(8,128)(2,1)} %param.8, bf16[1536,576]{0,1:T(8,128)(2,1)S(1)} %bitcast.20), kind=kOutput, calls=%fused_computation.6 | convolution fusion | flops 2717908992 | bytes 10027008
  116.9 0.0 collective-permute-done.13
  116.9 0.1 fusion
  117.0 1.4 collective-permute-start.14
  118.4 1.4 convert_bitcast_fusion.refs_7_
  119.9 0.9 copy.13.refs_5_
  120.8 0.0 collective-permute-done.10.refs_1_
  120.8 0.0 copy-start.11
  120.8 3.1 %collective-permute-done.12.refs_3_ = bf16[192,512]{1,0:T(8,128)(2,1)S(1)} collective-permute-done((bf16[192,512]{1,0:T(8,128)(2,1)}, bf16[192,512]{1,0:T(8,128)(2,1)S(1)}, u32[]{:S(2)}, u32[]{:S(2)}) %collective-permute-start.12) | collective-permute-done | bytes 196640 | tf_op jit(solution)/shard_map/ppermute | solution.py:413
  123.9 4.2 %collective-permute-done.14.refs_6_ = bf16[3,512,128]{2,1,0:T(8,128)(2,1)S(1)} collective-permute-done((bf16[3,512,128]{2,1,0:T(8,128)(2,1)S(1)}, bf16[3,512,128]{2,1,0:T(8,128)(2,1)S(1)}, u32[]{:S(2)}, u32[]{:S(2)}) %collective-permute-start.14) | collective-permute-done | bytes 393248 | tf_op jit(solution)/shard_map/ppermute | solution.py:417
  128.1 0.7 copy-done.7
  128.9 6.4 %project.1 = bf16[8,64,1536]{2,1,0:T(8,128)(2,1)} custom-call(bf16[192,512]{1,0:T(8,128)(2,1)} %get-tuple-element.34.refs_0_, bf16[192,512]{1,0:T(8,128)(2,1)} %copy-done.10, bf16[192,512]{1,0:T(8,128)(2,1)} %copy-done.11, bf16[192,512]{1,0:T(8,128)(2,1)} %copy-done.12, bf16[3,2,512,128]{3,2,1,0:T(8,128)(2,1)} %get-tuple-element.38.refs_4_, ...), custom_call_target="tpu_custom_call" | custom-call | flops 2147483648 | bytes 6291456 | tf_op jit(solution)/shard_map/project/pallas_call | solution.py:185
  135.3 7.5 %all-to-all-start = ((bf16[8,64,1536]{2,1,0:T(8,128)(2,1)}), bf16[8,64,1536]{2,1,0:T(8,128)(2,1)}, u32[]{:S(2)}, u32[]{:S(2)}) async-start(bf16[8,64,1536]{2,1,0:T(8,128)(2,1)} %project.1), calls=%async_computation | async-start | bytes 3145728 | tf_op jit(solution)/shard_map/all_to_all | solution.py:486
  142.8 0.1 fusion.1
  142.9 1.9 collective-permute-start.5
  144.8 5.8 %collective-permute-start.6 = (bf16[2,32,8,384]{3,2,1,0:T(8,128)(2,1)S(1)}, bf16[2,32,8,384]{3,2,1,0:T(8,128)(2,1)S(1)}, u32[]{:S(2)}, u32[]{:S(2)}) collective-permute-start(bf16[2,32,8,384]{3,2,1,0:T(8,128)(2,1)S(1)} %get-tuple-element.51), channel_id=1, source_target_pairs={{1,0},{2,1},{3,2},{4,3},{5,4},{6,5},{7,6},{8,7},{9,8},{10,9},{11,1... | collective-permute-start | bytes 1179656 | tf_op jit(solution)/shard_map/ppermute | solution.py:424
  150.6 11.4 %all-to-all-done.in_ref = bf16[8,64,1536]{2,1,0:T(8,128)(2,1)} async-done(((bf16[8,64,1536]{2,1,0:T(8,128)(2,1)}), bf16[8,64,1536]{2,1,0:T(8,128)(2,1)}, u32[]{:S(2)}, u32[]{:S(2)}) %all-to-all-start) | async-done | bytes 1572896 | tf_op jit(solution)/shard_map/all_to_all | solution.py:486
  161.9 2.5 %spread.1.up_ref = bf16[256,384]{1,0:T(8,128)(2,1)} custom-call(bf16[8,64,1536]{2,1,0:T(8,128)(2,1)} %all-to-all-done.in_ref), custom_call_target="tpu_custom_call" | custom-call | flops 268435456 | bytes 6291456 | tf_op jit(solution)/shard_map/spread/pallas_call | solution.py:185
  164.4 0.0 collective-permute-done.5
  164.4 0.0 collective-permute-done.6
  164.4 0.8 copy-done.8
  165.2 0.1 copy-done.9
  165.3 9.6 %fine_grads.1 = (bf16[256,384]{1,0:T(8,128)(2,1)}, f32[512,768]{1,0:T(8,128)}, bf16[256,768]{1,0:T(8,128)(2,1)}, bf16[256,768]{1,0:T(8,128)(2,1)}) custom-call(bf16[3,256,384]{2,1,0:T(8,128)(2,1)} %bitcast.23, bf16[2,512,384]{2,1,0:T(8,128)(2,1)} %bitcast.22, bf16[2,256,384]{2,1,0:T(8,128)(2,1)} %bitcast.26, bf16[2,256,384]{2,1,0:T(8,128)(2,1)} %bitcast.27, ...), custom_call_target="tpu_custom_call" | custom-call | flops 2147483648 | bytes 6291456 | tf_op jit(solution)/shard_map/fine_grads/pallas_call | solution.py:185
  174.9 1.9 collective-permute-start.15
  176.8 5.8 %collective-permute-start.16 = (bf16[256,768]{1,0:T(8,128)(2,1)}, bf16[256,768]{1,0:T(8,128)(2,1)S(1)}, u32[]{:S(2)}, u32[]{:S(2)}) collective-permute-start(bf16[256,768]{1,0:T(8,128)(2,1)} %get-tuple-element.45), channel_id=1, source_target_pairs={{1,0},{2,1},{3,2},{4,3},{5,4},{6,5},{7,6},{8,7},{9,8},{10,9},{11,1... | collective-permute-start | bytes 1179656 | tf_op jit(solution)/shard_map/ppermute | solution.py:424
  182.6 3.7 %collective-permute-done.15.left_ref = bf16[256,768]{1,0:T(8,128)(2,1)S(1)} collective-permute-done((bf16[256,768]{1,0:T(8,128)(2,1)}, bf16[256,768]{1,0:T(8,128)(2,1)S(1)}, u32[]{:S(2)}, u32[]{:S(2)}) %collective-permute-start.15) | collective-permute-done | bytes 393248 | tf_op jit(solution)/shard_map/ppermute | solution.py:424
  186.3 1.9 collective-permute-done.16.right_ref
  188.2 0.8 copy-done.4
  188.9 2.7 %add_columns.1 = (bf16[128,768]{1,0:T(8,128)(2,1)}, f32[256,768]{1,0:T(8,128)}, bf16[128,768]{1,0:T(8,128)(2,1)}) custom-call(f32[512,768]{1,0:T(8,128)} %get-tuple-element.43.mid_ref, bf16[256,768]{1,0:T(8,128)(2,1)} %copy-done.3, bf16[256,768]{1,0:T(8,128)(2,1)} %copy-done.4), custom_call_target="tpu_custom_call" | custom-call | flops 1048576 | bytes 6291456 | tf_op jit(solution)/shard_map/add_columns/pallas_call | solution.py:185
  191.6 4.0 %collective-permute-start.17 = (bf16[128,768]{1,0:T(8,128)(2,1)}, bf16[128,768]{1,0:T(8,128)(2,1)S(1)}, u32[]{:S(2)}, u32[]{:S(2)}) collective-permute-start(bf16[128,768]{1,0:T(8,128)(2,1)} %get-tuple-element.47), channel_id=1, source_target_pairs={{0,16},{16,32},{32,48},{48,64},{64,80},{80,96},{96,112},{1,17},{17... | collective-permute-start | bytes 589832 | tf_op jit(solution)/shard_map/ppermute | solution.py:424
  195.6 3.3 %collective-permute-start.18 = (bf16[128,768]{1,0:T(8,128)(2,1)}, bf16[128,768]{1,0:T(8,128)(2,1)S(1)}, u32[]{:S(2)}, u32[]{:S(2)}) collective-permute-start(bf16[128,768]{1,0:T(8,128)(2,1)} %get-tuple-element.48), channel_id=1, source_target_pairs={{16,0},{32,16},{48,32},{64,48},{80,64},{96,80},{112,96},{17,1},{33... | collective-permute-start | bytes 589832 | tf_op jit(solution)/shard_map/ppermute | solution.py:424
  198.9 3.4 %collective-permute-done.17.above_ref = bf16[128,768]{1,0:T(8,128)(2,1)S(1)} collective-permute-done((bf16[128,768]{1,0:T(8,128)(2,1)}, bf16[128,768]{1,0:T(8,128)(2,1)S(1)}, u32[]{:S(2)}, u32[]{:S(2)}) %collective-permute-start.17) | collective-permute-done | bytes 196640 | tf_op jit(solution)/shard_map/ppermute | solution.py:424
  202.3 4.6 %collective-permute-done.18.below_ref = bf16[128,768]{1,0:T(8,128)(2,1)S(1)} collective-permute-done((bf16[128,768]{1,0:T(8,128)(2,1)}, bf16[128,768]{1,0:T(8,128)(2,1)S(1)}, u32[]{:S(2)}, u32[]{:S(2)}) %collective-permute-start.18) | collective-permute-done | bytes 196640 | tf_op jit(solution)/shard_map/ppermute | solution.py:424
  207.0 0.7 copy-done.14
  207.7 2.0 add_rows.1
  (25 shorter events, 0.1 us)
Async XLA Ops:
  0.6 111.4 %copy-start = (bf16[3,1536,192]{1,2,0:T(8,128)(2,1)S(1)}, bf16[3,1536,192]{1,2,0:T(8,128)(2,1)}, u32[]{:S(2)}) copy-start(bf16[3,1536,192]{1,2,0:T(8,128)(2,1)} %param.9) | copy-start | bytes 5308420
  0.6 2.9 %copy-start.2 = (bf16[3,16,16,384]{3,2,1,0:T(8,128)(2,1)S(1)}, bf16[3,16,16,384]{3,2,1,0:T(8,128)(2,1)}, u32[]{:S(2)}) copy-start(bf16[3,16,16,384]{3,2,1,0:T(8,128)(2,1)} %param.5) | copy-start | bytes 1769476
  0.7 24.3 %slice-start = ((bf16[3,16,16,384]{3,2,1,0:T(8,128)(2,1)}), bf16[2,16,16,384]{3,2,1,0:T(8,128)(2,1)S(1)}, s32[]{:S(2)}) async-start(bf16[3,16,16,384]{3,2,1,0:T(8,128)(2,1)} %param.5), calls=%async_computation.1 | async-start | bytes 786432 | tf_op jit(solution)/shard_map/slice | solution.py:464
  3.1 21.3 %collective-permute-start.8 = (bf16[3,512,128]{2,1,0:T(8,128)(2,1)}, bf16[3,512,128]{2,1,0:T(8,128)(2,1)S(1)}, u32[]{:S(2)}, u32[]{:S(2)}) collective-permute-start(bf16[3,512,128]{2,1,0:T(8,128)(2,1)} %get-tuple-element.29.refs_0_), channel_id=1, source_target_pairs={{0,8},{8,0},{1,9},{9,1},{2,10},{10,2},{3,11},{11,3},{4,12},{12,4},... | collective-permute-start | bytes 1179656 | tf_op jit(solution)/shard_map/ppermute | solution.py:417
  3.6 17.9 %collective-permute-start.3 = (bf16[2,8,16,384]{3,2,1,0:T(8,128)(2,1)S(1)}, bf16[2,8,16,384]{3,2,1,0:T(8,128)(2,1)S(1)}, u32[]{:S(2)}, u32[]{:S(2)}) collective-permute-start(bf16[2,8,16,384]{3,2,1,0:T(8,128)(2,1)S(1)} %get-tuple-element.53), channel_id=1, source_target_pairs={{0,16},{16,32},{32,48},{48,64},{64,80},{80,96},{96,112},{1,17},{17... | collective-permute-start | bytes 589832 | tf_op jit(solution)/shard_map/ppermute | solution.py:424
  6.7 17.8 %collective-permute-start.4 = (bf16[2,8,16,384]{3,2,1,0:T(8,128)(2,1)S(1)}, bf16[2,8,16,384]{3,2,1,0:T(8,128)(2,1)S(1)}, u32[]{:S(2)}, u32[]{:S(2)}) collective-permute-start(bf16[2,8,16,384]{3,2,1,0:T(8,128)(2,1)S(1)} %get-tuple-element.54), channel_id=1, source_target_pairs={{16,0},{32,16},{48,32},{64,48},{80,64},{96,80},{112,96},{17,1},{33... | collective-permute-start | bytes 589832 | tf_op jit(solution)/shard_map/ppermute | solution.py:424
  11.0 14.1 %collective-permute-start = (bf16[3,512,128]{2,1,0:T(8,128)(2,1)}, bf16[3,512,128]{2,1,0:T(8,128)(2,1)}, u32[]{:S(2)}, u32[]{:S(2)}) collective-permute-start(bf16[3,512,128]{2,1,0:T(8,128)(2,1)} %get-tuple-element.30.refs_4_), channel_id=1, source_target_pairs={{0,2},{2,4},{4,6},{6,0},{1,3},{3,5},{5,7},{7,1},{8,10},{10,12},{12... | collective-permute-start | bytes 1179656 | tf_op jit(solution)/shard_map/ppermute | solution.py:413
  12.6 19.6 %collective-permute-start.1 = (bf16[3,512,128]{2,1,0:T(8,128)(2,1)}, bf16[3,512,128]{2,1,0:T(8,128)(2,1)}, u32[]{:S(2)}, u32[]{:S(2)}) collective-permute-start(bf16[3,512,128]{2,1,0:T(8,128)(2,1)} %get-tuple-element.30.refs_4_), channel_id=1, source_target_pairs={{0,4},{2,6},{4,0},{6,2},{1,5},{3,7},{5,1},{7,3},{8,12},{10,14},{12... | collective-permute-start | bytes 1179656 | tf_op jit(solution)/shard_map/ppermute | solution.py:413
  21.4 11.1 %collective-permute-start.2 = (bf16[3,512,128]{2,1,0:T(8,128)(2,1)}, bf16[3,512,128]{2,1,0:T(8,128)(2,1)}, u32[]{:S(2)}, u32[]{:S(2)}) collective-permute-start(bf16[3,512,128]{2,1,0:T(8,128)(2,1)} %get-tuple-element.30.refs_4_), channel_id=1, source_target_pairs={{0,6},{2,0},{4,2},{6,4},{1,7},{3,1},{5,3},{7,5},{8,14},{10,8},{12,... | collective-permute-start | bytes 1179656 | tf_op jit(solution)/shard_map/ppermute | solution.py:413
  24.5 8.1 %collective-permute-start.7 = (bf16[3,512,128]{2,1,0:T(8,128)(2,1)}, bf16[3,512,128]{2,1,0:T(8,128)(2,1)}, u32[]{:S(2)}, u32[]{:S(2)}) collective-permute-start(bf16[3,512,128]{2,1,0:T(8,128)(2,1)} %get-tuple-element.29.refs_0_), channel_id=1, source_target_pairs={{0,1},{1,0},{2,3},{3,2},{4,5},{5,4},{6,7},{7,6},{8,9},{9,8},{10,11... | collective-permute-start | bytes 1179656 | tf_op jit(solution)/shard_map/ppermute | solution.py:417
  24.5 8.1 %copy-start.6 = (bf16[3,512,128]{2,1,0:T(8,128)(2,1)}, bf16[3,512,128]{2,1,0:T(8,128)(2,1)S(1)}, u32[]{:S(2)}) copy-start(bf16[3,512,128]{2,1,0:T(8,128)(2,1)S(1)} %collective-permute-done.8.refs_2_) | copy-start | bytes 1179652
  24.5 8.1 %collective-permute-start.9 = (bf16[3,512,128]{2,1,0:T(8,128)(2,1)S(1)}, bf16[3,512,128]{2,1,0:T(8,128)(2,1)}, u32[]{:S(2)}, u32[]{:S(2)}) collective-permute-start(bf16[3,512,128]{2,1,0:T(8,128)(2,1)S(1)} %collective-permute-done.8.refs_2_), channel_id=1, source_target_pairs={{0,1},{1,0},{2,3},{3,2},{4,5},{5,4},{6,7},{7,6},{8,9},{9,8},{10,11... | collective-permute-start | bytes 1179656 | tf_op jit(solution)/shard_map/ppermute | solution.py:417
  25.1 117.7 %copy-start.1 = (bf16[2,32,16,384]{3,2,1,0:T(8,128)(2,1)}, bf16[2,32,16,384]{3,2,1,0:T(8,128)(2,1)S(1)}, u32[]{:S(2)}) copy-start(bf16[2,32,16,384]{3,2,1,0:T(8,128)(2,1)S(1)} %pad_maximum_fusion) | copy-start | bytes 2359300
  108.9 7.9 %collective-permute-start.13 = (bf16[3,2,512,128]{3,2,0,1:T(8,128)(2,1)S(1)}, bf16[3,2,512,128]{3,2,0,1:T(8,128)(2,1)S(1)}, u32[]{:S(2)}, u32[]{:S(2)}) collective-permute-start(bf16[3,2,512,128]{3,2,0,1:T(8,128)(2,1)S(1)} %copy.11), channel_id=1, source_target_pairs={{0,1},{1,0},{2,3},{3,2},{4,5},{5,4},{6,7},{7,6},{8,9},{9,8},{10,11... | collective-permute-start | bytes 2359304 | tf_op jit(solution)/shard_map/ppermute | solution.py:417
  109.0 11.8 %collective-permute-start.10 = (bf16[192,512]{1,0:T(8,128)(2,1)}, bf16[192,512]{1,0:T(8,128)(2,1)S(1)}, u32[]{:S(2)}, u32[]{:S(2)}) collective-permute-start(bf16[192,512]{1,0:T(8,128)(2,1)} %get-tuple-element.35), channel_id=1, source_target_pairs={{0,6},{2,0},{4,2},{6,4},{1,7},{3,1},{5,3},{7,5},{8,14},{10,8},{12,... | collective-permute-start | bytes 589832 | tf_op jit(solution)/shard_map/ppermute | solution.py:413
  111.0 9.8 %collective-permute-start.11 = (bf16[192,512]{1,0:T(8,128)(2,1)}, bf16[192,512]{1,0:T(8,128)(2,1)S(1)}, u32[]{:S(2)}, u32[]{:S(2)}) collective-permute-start(bf16[192,512]{1,0:T(8,128)(2,1)} %get-tuple-element.36), channel_id=1, source_target_pairs={{0,4},{2,6},{4,0},{6,2},{1,5},{3,7},{5,1},{7,3},{8,12},{10,14},{12... | collective-permute-start | bytes 589832 | tf_op jit(solution)/shard_map/ppermute | solution.py:413
  111.9 12.0 %collective-permute-start.12 = (bf16[192,512]{1,0:T(8,128)(2,1)}, bf16[192,512]{1,0:T(8,128)(2,1)S(1)}, u32[]{:S(2)}, u32[]{:S(2)}) collective-permute-start(bf16[192,512]{1,0:T(8,128)(2,1)} %get-tuple-element.37), channel_id=1, source_target_pairs={{0,2},{2,4},{4,6},{6,0},{1,3},{3,5},{5,7},{7,1},{8,10},{10,12},{12... | collective-permute-start | bytes 589832 | tf_op jit(solution)/shard_map/ppermute | solution.py:413
  112.0 4.9 %copy-start.5 = (bf16[3,2,512,128]{3,2,1,0:T(8,128)(2,1)S(1)}, bf16[3,2,512,128]{3,2,1,0:T(8,128)(2,1)}, u32[]{:S(2)}) copy-start(bf16[3,2,512,128]{3,2,1,0:T(8,128)(2,1)} %get-tuple-element.38.refs_4_) | copy-start | bytes 2359300
  117.0 11.1 %collective-permute-start.14 = (bf16[3,512,128]{2,1,0:T(8,128)(2,1)S(1)}, bf16[3,512,128]{2,1,0:T(8,128)(2,1)S(1)}, u32[]{:S(2)}, u32[]{:S(2)}) collective-permute-start(bf16[3,512,128]{2,1,0:T(8,128)(2,1)S(1)} %fusion), channel_id=1, source_target_pairs={{0,8},{8,0},{1,9},{9,1},{2,10},{10,2},{3,11},{11,3},{4,12},{12,4},... | collective-permute-start | bytes 1179656 | tf_op jit(solution)/shard_map/ppermute | solution.py:417
  120.8 7.3 %copy-start.10 = (bf16[192,512]{1,0:T(8,128)(2,1)}, bf16[192,512]{1,0:T(8,128)(2,1)S(1)}, u32[]{:S(2)}) copy-start(bf16[192,512]{1,0:T(8,128)(2,1)S(1)} %collective-permute-done.10.refs_1_) | copy-start | bytes 589828
  120.8 7.3 %copy-start.11 = (bf16[192,512]{1,0:T(8,128)(2,1)}, bf16[192,512]{1,0:T(8,128)(2,1)S(1)}, u32[]{:S(2)}) copy-start(bf16[192,512]{1,0:T(8,128)(2,1)S(1)} %collective-permute-done.11.refs_2_) | copy-start | bytes 589828
  123.9 4.2 %copy-start.12 = (bf16[192,512]{1,0:T(8,128)(2,1)}, bf16[192,512]{1,0:T(8,128)(2,1)S(1)}, u32[]{:S(2)}) copy-start(bf16[192,512]{1,0:T(8,128)(2,1)S(1)} %collective-permute-done.12.refs_3_) | copy-start | bytes 589828
  128.1 0.7 copy-start.7
  135.3 26.6 %all-to-all-start = ((bf16[8,64,1536]{2,1,0:T(8,128)(2,1)}), bf16[8,64,1536]{2,1,0:T(8,128)(2,1)}, u32[]{:S(2)}, u32[]{:S(2)}) async-start(bf16[8,64,1536]{2,1,0:T(8,128)(2,1)} %project.1), calls=%async_computation | async-start | bytes 3145728 | tf_op jit(solution)/shard_map/all_to_all | solution.py:486
  142.9 21.5 %collective-permute-start.5 = (bf16[2,32,8,384]{3,2,1,0:T(8,128)(2,1)S(1)}, bf16[2,32,8,384]{3,2,1,0:T(8,128)(2,1)S(1)}, u32[]{:S(2)}, u32[]{:S(2)}) collective-permute-start(bf16[2,32,8,384]{3,2,1,0:T(8,128)(2,1)S(1)} %get-tuple-element.52), channel_id=1, source_target_pairs={{0,1},{1,2},{2,3},{3,4},{4,5},{5,6},{6,7},{7,8},{8,9},{9,10},{10,1... | collective-permute-start | bytes 1179656 | tf_op jit(solution)/shard_map/ppermute | solution.py:424
  144.8 19.6 %collective-permute-start.6 = (bf16[2,32,8,384]{3,2,1,0:T(8,128)(2,1)S(1)}, bf16[2,32,8,384]{3,2,1,0:T(8,128)(2,1)S(1)}, u32[]{:S(2)}, u32[]{:S(2)}) collective-permute-start(bf16[2,32,8,384]{3,2,1,0:T(8,128)(2,1)S(1)} %get-tuple-element.51), channel_id=1, source_target_pairs={{1,0},{2,1},{3,2},{4,3},{5,4},{6,5},{7,6},{8,7},{9,8},{10,9},{11,1... | collective-permute-start | bytes 1179656 | tf_op jit(solution)/shard_map/ppermute | solution.py:424
  164.4 0.8 copy-start.8
  164.4 0.9 copy-start.9
  174.9 11.4 %collective-permute-start.15 = (bf16[256,768]{1,0:T(8,128)(2,1)}, bf16[256,768]{1,0:T(8,128)(2,1)S(1)}, u32[]{:S(2)}, u32[]{:S(2)}) collective-permute-start(bf16[256,768]{1,0:T(8,128)(2,1)} %get-tuple-element.44), channel_id=1, source_target_pairs={{0,1},{1,2},{2,3},{3,4},{4,5},{5,6},{6,7},{7,8},{8,9},{9,10},{10,1... | collective-permute-start | bytes 1179656 | tf_op jit(solution)/shard_map/ppermute | solution.py:424
  176.8 11.3 %collective-permute-start.16 = (bf16[256,768]{1,0:T(8,128)(2,1)}, bf16[256,768]{1,0:T(8,128)(2,1)S(1)}, u32[]{:S(2)}, u32[]{:S(2)}) collective-permute-start(bf16[256,768]{1,0:T(8,128)(2,1)} %get-tuple-element.45), channel_id=1, source_target_pairs={{1,0},{2,1},{3,2},{4,3},{5,4},{6,5},{7,6},{8,7},{9,8},{10,9},{11,1... | collective-permute-start | bytes 1179656 | tf_op jit(solution)/shard_map/ppermute | solution.py:424
  186.3 1.9 copy-start.3
  188.1 0.8 copy-start.4
  191.6 10.8 %collective-permute-start.17 = (bf16[128,768]{1,0:T(8,128)(2,1)}, bf16[128,768]{1,0:T(8,128)(2,1)S(1)}, u32[]{:S(2)}, u32[]{:S(2)}) collective-permute-start(bf16[128,768]{1,0:T(8,128)(2,1)} %get-tuple-element.47), channel_id=1, source_target_pairs={{0,16},{16,32},{32,48},{48,64},{64,80},{80,96},{96,112},{1,17},{17... | collective-permute-start | bytes 589832 | tf_op jit(solution)/shard_map/ppermute | solution.py:424
  195.6 11.4 %collective-permute-start.18 = (bf16[128,768]{1,0:T(8,128)(2,1)}, bf16[128,768]{1,0:T(8,128)(2,1)S(1)}, u32[]{:S(2)}, u32[]{:S(2)}) collective-permute-start(bf16[128,768]{1,0:T(8,128)(2,1)} %get-tuple-element.48), channel_id=1, source_target_pairs={{16,0},{32,16},{48,32},{64,48},{80,64},{96,80},{112,96},{17,1},{33... | collective-permute-start | bytes 589832 | tf_op jit(solution)/shard_map/ppermute | solution.py:424
  202.3 4.6 %copy-start.13 = (bf16[128,768]{1,0:T(8,128)(2,1)}, bf16[128,768]{1,0:T(8,128)(2,1)S(1)}, u32[]{:S(2)}) copy-start(bf16[128,768]{1,0:T(8,128)(2,1)S(1)} %collective-permute-done.17.above_ref) | copy-start | bytes 589828
  207.0 0.7 copy-start.14
where the time goes:
time: 212 us; the launch traced here: 210 us
  Pallas kernels  85.8 us (40%)
  starting transfers between devices  50.4 us (24%)
  waiting for transfers between devices  45.7 us (22%)
  blocking collectives  15 us (7%)
  local copies, waits for them, and re-layouts  5.37 us (3%)
  matrix products  4.89 us (2%)
    pallas_call x1, Pallas kernels, coarse_grads(): pl.pallas_call(body, grid=(heads, blocks), in_specs=[pl.BlockSpec((1, tok...  36.8 us
    pallas_call x6, Pallas kernels, whole_call(): pl.pallas_call(body, out_shape=out_shape, scratch_shapes=scratch, name=na...  25.6 us
    pallas_call x1, Pallas kernels, coarse_stats(): pl.pallas_call(body, grid=(heads, blocks), in_specs=[pl.BlockSpec((1, tok...  23.3 us
    ppermute x4, starting transfers between devices, onward(): lax.ppermute(high, axis, backward)  19.1 us
    all_gather x1, blocking collectives, shards(): stats = lax.all_gather(part, 'y', axis=0)  15 us
    ppermute x4, waiting for transfers between devices, onward(): lax.ppermute(low, axis, forward)  13.1 us
    all_to_all x1, waiting for transfers between devices, shards(): pieces = lax.all_to_all(projected, ROW, 0, 0)  11.4 us
    ppermute x4, starting transfers between devices, onward(): lax.ppermute(low, axis, forward)  10.9 us
  transfers between devices with their start and end apart: 20, of which 10 were waited for; matrix products, arithmetic and copies ran while one was open for 4% of the time, Pallas kernels for 1%

commit v1 on v0

--- a/solution.py
+++ b/solution.py
@@ -228,15 +228,34 @@
     return jnp.concatenate([ref[which, :, lanes] for ref in refs], axis=0)
 
 
+def window_pieces(columns, rows):
+    edge = RIM * columns
+    corner = RIM * RIM
+    middle = rows * columns
+    side = rows * RIM
+    base = 2 * edge + middle
+    wing = 2 * corner + side
+    return [
+        ((0, 0), edge, middle),
+        ((-1, 0), 0, edge),
+        ((1, 0), edge + middle, edge),
+        ((0, -1), base + corner, side),
+        ((0, 1), base + wing + corner, side),
+        ((-1, -1), base, corner),
+        ((1, -1), base + corner + side, corner),
+        ((-1, 1), base + wing, corner),
+        ((1, 1), base + wing + corner + side, corner),
+    ]
+
+
 def fine_grads(own_qkv, ext_kv, own_up, rows, columns):
     _, own, width = own_qkv.shape
-    sizes = [ref.shape[1] for ref in ext_kv]
-    places = [sum(sizes[:i]) for i in range(len(sizes))]
-
-    def body(q_ref, mid_ref, low_ref, high_ref, up_ref, q_out, mid_out, low_out, high_out, bias_ref):
+    pieces = window_pieces(columns, rows)
+
+    def body(q_ref, mid_ref, low_ref, high_ref, up_ref, q_out, *rest):
+        outs, bias_ref = rest[:-1], rest[-1]
         fill_bias(bias_ref, own, rows, columns)
         ext = (mid_ref, low_ref, high_ref)
-        outs = (mid_out, low_out, high_out)
         for pair, lanes in pairs_of(width):
             key = stacked(ext, 0, lanes)
             key_t = key.T
@@ -258,8 +277,8 @@
                 value_sum += nn(share.astype(BF16), up)
                 parts.append(nn(key_t[side * HD : side * HD + HD], grads))
             q_out[:, lanes] = (jnp.concatenate(parts, axis=0).T * SCALE).astype(BF16)
-            for out, place, size in zip(outs, places, sizes):
-                right = slice(width + pair * 128, width + pair * 128 + 128)
+            right = slice(width + pair * 128, width + pair * 128 + 128)
+            for out, (_, place, size) in zip(outs, pieces):
                 out[:, lanes] = key_sum[place : place + size].astype(out.dtype)
                 out[:, right] = value_sum[place : place + size].astype(out.dtype)
 
@@ -268,7 +287,7 @@
         [jax.ShapeDtypeStruct((own, width), BF16)]
         + [
             jax.ShapeDtypeStruct((size, 2 * width), BF16 if i else F32)
-            for i, size in enumerate(sizes)
+            for i, (_, _, size) in enumerate(pieces)
         ],
         "fine_grads",
         2 << 30,
@@ -279,55 +298,36 @@
     )
 
 
-def add_columns(mid, from_left, from_right, columns):
-    cells, wide = mid.shape
-    tall = cells // columns
-    edge = RIM * columns
-
-    def body(mid_ref, left_ref, right_ref, top_out, own_out, bottom_out):
-        left = left_ref[...].astype(F32).reshape(tall, RIM, wide)
-        right = right_ref[...].astype(F32).reshape(tall, RIM, wide)
-        both = jnp.concatenate([left, right], axis=1).reshape(cells, wide)
-        total = mid_ref[...] + both
-        top_out[...] = total[:edge].astype(BF16)
-        own_out[...] = total[edge : cells - edge]
-        bottom_out[...] = total[cells - edge :].astype(BF16)
-
-    return whole_call(
-        body,
-        [
-            jax.ShapeDtypeStruct((edge, wide), BF16),
-            jax.ShapeDtypeStruct((cells - 2 * edge, wide), F32),
-            jax.ShapeDtypeStruct((edge, wide), BF16),
-        ],
-        "add_columns",
-        1 << 20,
-        [],
-        mid,
-        from_left,
-        from_right,
-    )
-
-
-def add_rows(own, from_above, from_below):
+def add_arrived(own, arrived, rows, columns):
     cells, wide = own.shape
     width = wide // 2
 
-    def body(own_ref, above_ref, below_ref, k_out, v_out):
-        arrived = jnp.concatenate([above_ref[...], below_ref[...]], axis=0)
-        total = own_ref[...] + arrived.astype(F32)
+    def body(own_ref, *rest):
+        above, below, left, right, up_left, down_left, up_right, down_right = [
+            ref[...].astype(F32) for ref in rest[:-2]
+        ]
+        k_out, v_out = rest[-2:]
+        total = own_ref[...] + jnp.concatenate([above, below], axis=0)
+
+        def halves(first, second, tall):
+            first = first.reshape(tall, RIM, wide)
+            return jnp.concatenate([first, second.reshape(tall, RIM, wide)], axis=1)
+
+        total += halves(left, right, rows).reshape(cells, wide)
+        upper = halves(up_left, up_right, RIM)
+        lower = halves(down_left, down_right, RIM)
+        total += jnp.concatenate([upper, lower], axis=0).reshape(cells, wide)
         k_out[...] = total[:, :width].astype(BF16)
         v_out[...] = total[:, width:].astype(BF16)
 
     return whole_call(
         body,
         [jax.ShapeDtypeStruct((cells, width), BF16)] * 2,
-        "add_rows",
+        "add_arrived",
         1 << 20,
         [],
         own,
-        from_above,
-        from_below,
+        *arrived,
     )
 
 
@@ -338,40 +338,50 @@
     each = rows // count
     size = each * columns
     wide = joint.shape[2]
+    operands = (*query_pieces, kept, from_core, arrived, joint)
 
     def body(*refs):
         pieces = refs[: len(query_pieces)]
         kept_ref, core_ref, arrived_ref, joint_ref, out, held, weight = refs[len(query_pieces) :]
-        for head in range(heads):
-            total = kept_ref[head, 0].astype(F32) + core_ref[head, 0].astype(F32)
-            held[:, head * 128 : head * 128 + 128] = total + arrived_ref[head].astype(F32)
-            for part in range(2):
-                at = head * 128 + part * HD
-                weight[at : at + HD, :] = joint_ref[1 + part, head * HD : head * HD + HD, :]
-        weight[2 * group :, :] = joint_ref[0]
-        total = pieces[0][...].astype(F32)
-        for piece in pieces[1:]:
-            total += piece[...].astype(F32)
-        held[:, 2 * group :] = total.T
-        for at in range(count):
-            taken = [
-                held[c * rows + at * each : c * rows + (at + 1) * each, :] for c in range(columns)
-            ]
-            chosen = jnp.concatenate(taken, axis=0).astype(BF16)
-            out[at] = nn(chosen, weight[...]).astype(BF16)
-
-    return whole_call(
-        body,
-        jax.ShapeDtypeStruct((count, size, wide), BF16),
-        "project",
-        2 << 30,
-        [pltpu.VMEM((tokens, 3 * group), F32), pltpu.VMEM((3 * group, wide), BF16)],
-        *query_pieces,
-        kept,
-        from_core,
-        arrived,
-        joint,
-    )
+
+        @pl.when(pl.program_id(0) == 0)
+        def _():
+            for head in range(heads):
+                total = kept_ref[head, 0].astype(F32) + core_ref[head, 0].astype(F32)
+                held[:, head * 128 : head * 128 + 128] = total + arrived_ref[head].astype(F32)
+                for part in range(2):
+                    at = head * 128 + part * HD
+                    weight[at : at + HD, :] = joint_ref[1 + part, head * HD : head * HD + HD, :]
+            weight[2 * group :, :] = joint_ref[0]
+            total = pieces[0][...].astype(F32)
+            for piece in pieces[1:]:
+                total += piece[...].astype(F32)
+            held[:, 2 * group :] = total.T
+
+        taken = []
+        for c in range(columns):
+            start = pl.multiple_of(c * rows + pl.program_id(0) * each, each)
+            taken.append(held[pl.ds(start, each), :])
+        chosen = jnp.concatenate(taken, axis=0).astype(BF16)
+        out[0] = nn(chosen, weight[...]).astype(BF16)
+
+    return pl.pallas_call(
+        body,
+        grid=(count,),
+        in_specs=[
+            pl.BlockSpec(array.shape, lambda d, rank=array.ndim: (0,) * rank)
+            for array in operands
+        ],
+        out_specs=pl.BlockSpec((1, size, wide), lambda d: (d, 0, 0)),
+        out_shape=jax.ShapeDtypeStruct((count, size, wide), BF16),
+        scratch_shapes=[
+            pltpu.VMEM((tokens, 3 * group), F32),
+            pltpu.VMEM((3 * group, wide), BF16),
+        ],
+        name="project",
+        cost_estimate=cost(2 << 30, 6 << 20, 0),
+        compiler_params=pltpu.CompilerParams(vmem_limit_bytes=VMEM),
+    )(*operands)
 
 
 def spread(pieces, columns):
@@ -424,6 +434,17 @@
     return lax.ppermute(low, axis, forward), lax.ppermute(high, axis, backward)
 
 
+def toward(piece, down, across):
+    tall, wide = lax.axis_size(ROW), lax.axis_size(COL)
+    pairs = []
+    for row in range(tall):
+        for column in range(wide):
+            if 0 <= row + down < tall and 0 <= column + across < wide:
+                here = row * wide + column
+                pairs.append((here, here + down * wide + across))
+    return lax.ppermute(piece, ROW + COL, pairs)
+
+
 def edges(block, axis, at):
     size = block.shape[at]
     return onward(
@@ -455,42 +476,43 @@
     )
     across = swapped(key_value, "zl")
     beside = swapped(key_value, "c")
-    queries = [query_up] + [shifted(query_up, "y", step) for step in (1, 3, 2)]
-    queries = [queries[i] for i in (0, 1, 3, 2)]
+    queries = [query_up] + [shifted(query_up, "y", step) for step in (1, 2, 3)]
     corner = swapped(across, "c")
     keys = [key_value, beside, across, corner]
-
-    own_qkv = fine_qkv.reshape(3, own, width)
-    tall = with_rows(fine_qkv[1:], 1)
-    queries, tall = lax.optimization_barrier((queries, tall))
-    ext_kv = with_columns(tall, 1)
 
     part = coarse_stats(keys, queries, 256)
     stats = lax.all_gather(part, "y", axis=0)
     kept, sent, *query_grads = coarse_grads(keys, queries, stats)
 
-    sent, merge_weight = lax.optimization_barrier((sent, merge_weight))
     from_core = swapped(sent, "c")
     query_pieces = [query_grads[0]]
     for step in (1, 2, 3):
         query_pieces.append(shifted(query_grads[step], "y", -step))
     passed = (kept[:, 1].astype(F32) + from_core[:, 1].astype(F32)).astype(BF16)
     arrived = swapped(passed, "zl")
+    merge_weight, fine_qkv, _ = lax.optimization_barrier(
+        (merge_weight, fine_qkv, passed[0, :1, :1])
+    )
     joint = lax.dot_general(
         qkv_weight, merge_weight, (((1,), (1,)), ((), ())), preferred_element_type=F32
     ).astype(BF16)
+    own_qkv = fine_qkv.reshape(3, own, width)
+    tall = with_rows(fine_qkv[1:], 1)
     count = lax.axis_size(ROW)
     projected = project(
         query_pieces, kept, from_core, arrived, joint, coarse_columns, count
     )
+    projected, tall = lax.optimization_barrier((projected, tall))
+    ext_kv = with_columns(tall, 1)
     pieces = lax.all_to_all(projected, ROW, 0, 0)
     own_up = spread(pieces, coarse_columns)
 
-    grad_query, mid, low, high = fine_grads(own_qkv, ext_kv, own_up, rows, columns)
-    from_left, from_right = onward(high, low, COL)
-    top, middle, bottom = add_columns(mid, from_left, from_right, columns)
-    from_above, from_below = onward(bottom, top, ROW)
-    grad_key, grad_value = add_rows(middle, from_above, from_below)
+    grad_query, middle, *rims = fine_grads(own_qkv, ext_kv, own_up, rows, columns)
+    places = window_pieces(columns, rows)[1:]
+    arrived = [toward(rim, *place[0]) for rim, place in zip(rims, places)]
+    order = [(1, 0), (-1, 0), (0, 1), (0, -1), (1, 1), (-1, 1), (1, -1), (-1, -1)]
+    found = {place[0]: piece for place, piece in zip(places, arrived)}
+    grad_key, grad_value = add_arrived(middle, [found[at] for at in order], rows, columns)
     shape = (rows, columns, width)
     return grad_query.reshape(shape), grad_key.reshape(shape), grad_value.reshape(shape)
 

time: 212 us -> 222 us (1.047)
  starting transfers between devices: 50.4 us -> 63.2 us
    ppermute x0 -> x8, starting transfers between devices: none -> 29 us  [toward(): return lax.ppermute(piece, ROW + COL, pairs)]
    ppermute x4 -> x2, waiting for transfers between devices: 13.1 us -> 0.01 us  [onward(): lax.ppermute(low, axis, forward)]
    ppermute x4 -> x2, starting transfers between devices: 19.1 us -> 8.1 us  [onward(): lax.ppermute(high, axis, backward)]
    pallas_call x6 -> x4, Pallas kernels: 25.6 us -> 16.7 us  [whole_call(): pl.pallas_call(body, out_shape=out_shape, scratch_shapes=scratch, name=na...]
    ppermute x6, waiting for transfers between devices: 10.6 us -> 18.6 us  [shifted(): lax.ppermute(array, axis, [(i, (i + step) % count) for i in range(count)])]
    pallas_call x0 -> x1, Pallas kernels: none -> 7.81 us  [project(): pl.pallas_call(body, grid=(count,), in_specs=[pl.BlockSpec(array.shape, l...]
    ppermute x0 -> x8, waiting for transfers between devices: none -> 6.82 us  [toward(): return lax.ppermute(piece, ROW + COL, pairs)]
    ppermute x4 -> x2, waiting for transfers between devices: 6.5 us -> 0.01 us  [onward(): lax.ppermute(high, axis, backward)]
  transfers between devices with their start and end apart: 20 -> 24, of which waited for: 10 -> 8; matrix products, arithmetic and copies ran while one was open for 4% -> 4% of each run, Pallas kernels for 1% -> 1%
where the time goes in v1:
time: 222 us; the launch traced here: 221 us
  Pallas kernels  84.7 us (38%)
  starting transfers between devices  63.2 us (28%)
  waiting for transfers between devices  44.7 us (20%)
  blocking collectives  13.2 us (6%)
  local copies, waits for them, and re-layouts  7.13 us (3%)
  matrix products  4.92 us (2%)
    pallas_call x1, Pallas kernels, coarse_grads(): pl.pallas_call(body, grid=(heads, blocks), in_specs=[pl.BlockSpec((1, tok...  36.8 us
    ppermute x8, starting transfers between devices, toward(): return lax.ppermute(piece, ROW + COL, pairs)  29 us
    pallas_call x1, Pallas kernels, coarse_stats(): pl.pallas_call(body, grid=(heads, blocks), in_specs=[pl.BlockSpec((1, tok...  23.3 us
    ppermute x6, waiting for transfers between devices, shifted(): lax.ppermute(array, axis, [(i, (i + step) % count) for i in range(count)])  18.6 us
    pallas_call x4, Pallas kernels, whole_call(): pl.pallas_call(body, out_shape=out_shape, scratch_shapes=scratch, name=na...  16.7 us
    all_to_all x1, waiting for transfers between devices, shards(): pieces = lax.all_to_all(projected, ROW, 0, 0)  14.4 us
    all_gather x1, blocking collectives, shards(): stats = lax.all_gather(part, 'y', axis=0)  13.2 us
    ppermute x6, starting transfers between devices, shifted(): lax.ppermute(array, axis, [(i, (i + step) % count) for i in range(count)])  8.78 us
  transfers between devices with their start and end apart: 24, of which 8 were waited for; matrix products, arithmetic and copies ran while one was open for 4% of the time, Pallas kernels for 1%

profile of v1, /device:TPU:96, one launch (start us, length us, event | category | flops | bytes accessed | tf_op | source)
XLA Modules:
  0.0 220.7 jit_solution(6740678266482106108)
XLA Ops:
  0.6 0.0 copy-start
  0.6 2.4 %prepare.1 = (bf16[3,512,128]{2,1,0:T(8,128)(2,1)}, bf16[3,512,128]{2,1,0:T(8,128)(2,1)}) custom-call(bf16[3,512,192]{2,1,0:T(8,128)(2,1)} %bitcast.25, bf16[512,192]{1,0:T(8,128)(2,1)} %bitcast.28), custom_call_target="tpu_custom_call" | custom-call | flops 1048576 | bytes 6291456 | tf_op jit(solution)/shard_map/prepare/pallas_call | solution.py:185
  3.1 0.4 collective-permute-start.1
  3.5 0.0 collective-permute-start
  3.5 1.6 collective-permute-start.3
  5.1 2.9 %collective-permute-start.4 = (bf16[3,512,128]{2,1,0:T(8,128)(2,1)}, bf16[3,512,128]{2,1,0:T(8,128)(2,1)S(1)}, u32[]{:S(2)}, u32[]{:S(2)}) collective-permute-start(bf16[3,512,128]{2,1,0:T(8,128)(2,1)} %get-tuple-element.29.refs_4_), channel_id=1, source_target_pairs={{0,4},{2,6},{4,0},{6,2},{1,5},{3,7},{5,1},{7,3},{8,12},{10,14},{12... | collective-permute-start | bytes 1179656 | tf_op jit(solution)/shard_map/ppermute | solution.py:423
  8.0 1.3 collective-permute-start.5
  9.3 4.8 %collective-permute-done.1.refs_2_ = bf16[3,512,128]{2,1,0:T(8,128)(2,1)S(1)} collective-permute-done((bf16[3,512,128]{2,1,0:T(8,128)(2,1)}, bf16[3,512,128]{2,1,0:T(8,128)(2,1)S(1)}, u32[]{:S(2)}, u32[]{:S(2)}) %collective-permute-start.1) | collective-permute-done | bytes 393248 | tf_op jit(solution)/shard_map/ppermute | solution.py:427
  14.1 0.0 collective-permute-start.2
  14.1 0.0 collective-permute-done.refs_1_
  14.2 2.3 %collective-permute-done.3.refs_5_ = bf16[3,512,128]{2,1,0:T(8,128)(2,1)S(1)} collective-permute-done((bf16[3,512,128]{2,1,0:T(8,128)(2,1)}, bf16[3,512,128]{2,1,0:T(8,128)(2,1)S(1)}, u32[]{:S(2)}, u32[]{:S(2)}) %collective-permute-start.3) | collective-permute-done | bytes 393248 | tf_op jit(solution)/shard_map/ppermute | solution.py:423
  16.5 9.6 %collective-permute-done.4.refs_6_ = bf16[3,512,128]{2,1,0:T(8,128)(2,1)S(1)} collective-permute-done((bf16[3,512,128]{2,1,0:T(8,128)(2,1)}, bf16[3,512,128]{2,1,0:T(8,128)(2,1)S(1)}, u32[]{:S(2)}, u32[]{:S(2)}) %collective-permute-start.4) | collective-permute-done | bytes 393248 | tf_op jit(solution)/shard_map/ppermute | solution.py:423
  26.1 0.7 copy-done.7
  26.8 0.1 copy-done.8
  27.0 0.7 copy-done.10
  27.7 23.3 %coarse_stats.1 = f32[3,2,2048]{2,1,0:T(2,128)} custom-call(bf16[3,512,128]{2,1,0:T(8,128)(2,1)} %get-tuple-element.28.refs_0_, bf16[3,512,128]{2,1,0:T(8,128)(2,1)} %copy-done.5, bf16[3,512,128]{2,1,0:T(8,128)(2,1)} %copy-done.4, bf16[3,512,128]{2,1,0:T(8,128)(2,1)} %copy-done.10, bf16[3,512,128]{2,1,0:T(8,128)(2,1)} %get-tuple-element.29.refs_4_, ...), custom_call_target="tpu_custom_call" | custom-call | flops 12884901888 | bytes 2097152 | tf_op jit(solution)/shard_map/coarse_stats/pallas_call | solution.py:100
  51.0 13.2 %all-gather = f32[12,2,2048]{2,1,0:T(2,128)} all-gather(f32[3,2,2048]{2,1,0:T(2,128)} %coarse_stats.1), channel_id=2, replica_groups=mesh['x'=4,'zh'=2,'zl'=2,'y'=4,'c'=2] {'y'}, dimensions={0}, use_global_device_ids=true | all-gather | bytes 245760 | tf_op jit(solution)/shard_map/all_gather | solution.py:484
  64.3 36.8 %coarse_grads.1 = (bf16[3,2,512,128]{3,2,1,0:T(8,128)(2,1)}, bf16[3,2,512,128]{3,2,1,0:T(8,128)(2,1)}, bf16[192,512]{1,0:T(8,128)(2,1)}, bf16[192,512]{1,0:T(8,1...) custom-call(bf16[3,512,128]{2,1,0:T(8,128)(2,1)} %get-tuple-element.28.refs_0_, ...), custom_call_target="tpu_custom_call" | custom-call | flops 32212254720 | bytes 4194304 | tf_op jit(solution)/shard_map/coarse_grads/pallas_call | solution.py:166
  101.1 0.0 copy-start.2
  101.1 1.2 copy.11
  102.4 0.1 collective-permute-start.9
  102.5 2.2 collective-permute-start.12
  104.7 6.1 %collective-permute-start.11 = (bf16[2,8,16,384]{3,2,1,0:T(8,128)(2,1)S(1)}, bf16[2,8,16,384]{3,2,1,0:T(8,128)(2,1)S(1)}, u32[]{:S(2)}, u32[]{:S(2)}) collective-permute-start(bf16[2,8,16,384]{3,2,1,0:T(8,128)(2,1)S(1)} %get-tuple-element.53), channel_id=1, source_target_pairs={{0,16},{16,32},{32,48},{48,64},{64,80},{80,96},{96,112},{1,17},{17... | collective-permute-start | bytes 589832 | tf_op jit(solution)/shard_map/ppermute | solution.py:434
  110.8 0.0 copy-start.15
  110.8 0.0 copy-start.14
  110.8 4.9 %fusion.3 = f32[1536,576]{0,1:S(1)} fusion(bf16[1536,1536]{1,0:T(8,128)(2,1)} %param.8, bf16[1536,576]{0,1:T(8,128)(2,1)S(1)} %bitcast.20), kind=kOutput, calls=%fused_computation.6 | convolution fusion | flops 2717908992 | bytes 10027008
  115.8 1.9 collective-permute-start.6
  117.7 0.9 collective-permute-start.7
  118.5 0.2 collective-permute-start.8
  118.7 0.1 fusion
  118.9 1.7 collective-permute-start.10
  120.5 1.5 convert_bitcast_fusion.refs_7_
  122.0 0.1 pad_maximum_fusion
  122.1 1.0 copy.13.refs_5_
  123.1 3.0 %collective-permute-done.6.refs_1_ = bf16[192,512]{1,0:T(8,128)(2,1)S(1)} collective-permute-done((bf16[192,512]{1,0:T(8,128)(2,1)S(1)}, bf16[192,512]{1,0:T(8,128)(2,1)S(1)}, u32[]{:S(2)}, u32[]{:S(2)}) %collective-permute-start.6) | collective-permute-done | bytes 196640 | tf_op jit(solution)/shard_map/ppermute | solution.py:423
  126.2 0.8 collective-permute-done.7.refs_2_
  127.0 2.8 %collective-permute-done.8.refs_3_ = bf16[192,512]{1,0:T(8,128)(2,1)S(1)} collective-permute-done((bf16[192,512]{1,0:T(8,128)(2,1)S(1)}, bf16[192,512]{1,0:T(8,128)(2,1)S(1)}, u32[]{:S(2)}, u32[]{:S(2)}) %collective-permute-start.8) | collective-permute-done | bytes 196640 | tf_op jit(solution)/shard_map/ppermute | solution.py:423
  129.9 0.7 copy-done.21
  130.5 0.8 copy-done.9
  131.3 7.8 %project.1 = bf16[8,64,1536]{2,1,0:T(8,128)(2,1)} custom-call(bf16[192,512]{1,0:T(8,128)(2,1)} %get-tuple-element.30.refs_0_, bf16[192,512]{1,0:T(8,128)(2,1)} %copy-done.18, bf16[192,512]{1,0:T(8,128)(2,1)} %copy-done.19, bf16[192,512]{1,0:T(8,128)(2,1)} %copy-done.21, bf16[3,2,512,128]{3,2,1,0:T(8,128)(2,1)} %get-tuple-element.34.refs_4_, ...), custom_call_target="tpu_custom_call" | custom-call | flops 2147483648 | bytes 6291456 | tf_op jit(solution)/shard_map/project/pallas_call | solution.py:368
  139.1 7.2 %all-to-all-start = ((bf16[8,64,1536]{2,1,0:T(8,128)(2,1)}), bf16[8,64,1536]{2,1,0:T(8,128)(2,1)}, u32[]{:S(2)}, u32[]{:S(2)}) async-start(bf16[8,64,1536]{2,1,0:T(8,128)(2,1)} %project.1), calls=%async_computation | async-start | bytes 3145728 | tf_op jit(solution)/shard_map/all_to_all | solution.py:507
  146.3 0.1 fusion.1
  146.4 1.9 collective-permute-start.13
  148.3 5.9 %collective-permute-start.14 = (bf16[2,32,8,384]{3,2,1,0:T(8,128)(2,1)S(1)}, bf16[2,32,8,384]{3,2,1,0:T(8,128)(2,1)S(1)}, u32[]{:S(2)}, u32[]{:S(2)}) collective-permute-start(bf16[2,32,8,384]{3,2,1,0:T(8,128)(2,1)S(1)} %get-tuple-element.51), channel_id=1, source_target_pairs={{1,0},{2,1},{3,2},{4,3},{5,4},{6,5},{7,6},{8,7},{9,8},{10,9},{11,1... | collective-permute-start | bytes 1179656 | tf_op jit(solution)/shard_map/ppermute | solution.py:434
  154.3 14.4 %all-to-all-done.in_ref = bf16[8,64,1536]{2,1,0:T(8,128)(2,1)} async-done(((bf16[8,64,1536]{2,1,0:T(8,128)(2,1)}), bf16[8,64,1536]{2,1,0:T(8,128)(2,1)}, u32[]{:S(2)}, u32[]{:S(2)}) %all-to-all-start) | async-done | bytes 1572896 | tf_op jit(solution)/shard_map/all_to_all | solution.py:507
  168.7 2.5 %spread.1.up_ref = bf16[256,384]{1,0:T(8,128)(2,1)} custom-call(bf16[8,64,1536]{2,1,0:T(8,128)(2,1)} %all-to-all-done.in_ref), custom_call_target="tpu_custom_call" | custom-call | flops 268435456 | bytes 6291456 | tf_op jit(solution)/shard_map/spread/pallas_call | solution.py:185
  171.1 0.7 copy-done.11
  171.9 0.1 copy-done.12
  172.0 9.4 %fine_grads.1 = (bf16[256,384]{1,0:T(8,128)(2,1)}, f32[256,768]{1,0:T(8,128)}, bf16[128,768]{1,0:T(8,128)(2,1)}, bf16[128,768]{1,0:T(8,128)(2,1)}, bf16[128,768]...) custom-call(bf16[3,256,384]{2,1,0:T(8,128)(2,1)} %bitcast.23, ...), custom_call_target="tpu_custom_call" | custom-call | flops 2147483648 | bytes 6291456 | tf_op jit(solution)/shard_map/fine_grads/pallas_call | solution.py:185
  181.4 1.9 collective-permute-start.19
  183.4 1.9 collective-permute-start.20
  185.3 4.8 %collective-permute-start.15 = (bf16[128,768]{1,0:T(8,128)(2,1)}, bf16[128,768]{1,0:T(8,128)(2,1)S(1)}, u32[]{:S(2)}, u32[]{:S(2)}) collective-permute-start(bf16[128,768]{1,0:T(8,128)(2,1)} %get-tuple-element.41), channel_id=1, source_target_pairs={{0,16},{1,17},{2,18},{3,19},{4,20},{5,21},{6,22},{7,23},{8,24},{9,... | collective-permute-start | bytes 589832 | tf_op jit(solution)/shard_map/ppermute | solution.py:445
  190.1 2.5 %collective-permute-start.16 = (bf16[128,768]{1,0:T(8,128)(2,1)}, bf16[128,768]{1,0:T(8,128)(2,1)S(1)}, u32[]{:S(2)}, u32[]{:S(2)}) collective-permute-start(bf16[128,768]{1,0:T(8,128)(2,1)} %get-tuple-element.42), channel_id=1, source_target_pairs={{16,0},{17,1},{18,2},{19,3},{20,4},{21,5},{22,6},{23,7},{24,8},{25... | collective-permute-start | bytes 589832 | tf_op jit(solution)/shard_map/ppermute | solution.py:445
  192.7 8.2 %collective-permute-start.21 = (bf16[64,768]{1,0:T(8,128)(2,1)}, bf16[64,768]{1,0:T(8,128)(2,1)S(1)}, u32[]{:S(2)}, u32[]{:S(2)}) collective-permute-start(bf16[64,768]{1,0:T(8,128)(2,1)} %get-tuple-element.47), channel_id=1, source_target_pairs={{1,16},{2,17},{3,18},{4,19},{5,20},{6,21},{7,22},{8,23},{9,24},{10... | collective-permute-start | bytes 294920 | tf_op jit(solution)/shard_map/ppermute | solution.py:445
  200.9 1.9 collective-permute-start.17
  202.8 5.8 %collective-permute-start.18 = (bf16[128,768]{1,0:T(8,128)(2,1)}, bf16[128,768]{1,0:T(8,128)(2,1)S(1)}, u32[]{:S(2)}, u32[]{:S(2)}) collective-permute-start(bf16[128,768]{1,0:T(8,128)(2,1)} %get-tuple-element.44), channel_id=1, source_target_pairs={{1,0},{2,1},{3,2},{4,3},{5,4},{6,5},{7,6},{8,7},{9,8},{10,9},{11,1... | collective-permute-start | bytes 589832 | tf_op jit(solution)/shard_map/ppermute | solution.py:445
  208.6 1.9 collective-permute-start.22
  210.5 6.8 %collective-permute-done.22.rest_7_ = bf16[64,768]{1,0:T(8,128)(2,1)S(1)} collective-permute-done((bf16[64,768]{1,0:T(8,128)(2,1)}, bf16[64,768]{1,0:T(8,128)(2,1)S(1)}, u32[]{:S(2)}, u32[]{:S(2)}) %collective-permute-start.22) | collective-permute-done | bytes 98336 | tf_op jit(solution)/shard_map/ppermute | solution.py:445
  217.4 0.5 copy-done.26
  218.0 0.1 copy-done.16
  218.0 0.1 copy-done.17
  218.1 0.1 copy-done.20
  218.2 0.0 copy-done.22
  218.2 2.4 %add_arrived.1 = (bf16[256,384]{1,0:T(8,128)(2,1)}, bf16[256,384]{1,0:T(8,128)(2,1)}) custom-call(f32[256,768]{1,0:T(8,128)} %get-tuple-element.40.own_ref, bf16[128,768]{1,0:T(8,128)(2,1)} %copy-done.16, bf16[128,768]{1,0:T(8,128)(2,1)} %copy-done.17, bf16[128,768]{1,0:T(8,128)(2,1)} %copy-done.20, bf16[128,768]{1,0:T(8,128)(2,1)} %copy-done.22, ...), custom_call_target="tpu_custom_call" | custom-call | flops 1048576 | bytes 6291456 | tf_op jit(solution)/shard_map/add_arrived/pallas_call | solution.py:185
  (56 shorter events, 0.2 us)
Async XLA Ops:
  0.6 110.1 %copy-start = (bf16[3,1536,192]{1,2,0:T(8,128)(2,1)S(1)}, bf16[3,1536,192]{1,2,0:T(8,128)(2,1)}, u32[]{:S(2)}) copy-start(bf16[3,1536,192]{1,2,0:T(8,128)(2,1)} %param.9) | copy-start | bytes 5308420
  3.1 11.1 %collective-permute-start.1 = (bf16[3,512,128]{2,1,0:T(8,128)(2,1)}, bf16[3,512,128]{2,1,0:T(8,128)(2,1)S(1)}, u32[]{:S(2)}, u32[]{:S(2)}) collective-permute-start(bf16[3,512,128]{2,1,0:T(8,128)(2,1)} %get-tuple-element.28.refs_0_), channel_id=1, source_target_pairs={{0,8},{8,0},{1,9},{9,1},{2,10},{10,2},{3,11},{11,3},{4,12},{12,4},... | collective-permute-start | bytes 1179656 | tf_op jit(solution)/shard_map/ppermute | solution.py:427
  3.5 10.7 %collective-permute-start = (bf16[3,512,128]{2,1,0:T(8,128)(2,1)}, bf16[3,512,128]{2,1,0:T(8,128)(2,1)S(1)}, u32[]{:S(2)}, u32[]{:S(2)}) collective-permute-start(bf16[3,512,128]{2,1,0:T(8,128)(2,1)} %get-tuple-element.28.refs_0_), channel_id=1, source_target_pairs={{0,1},{1,0},{2,3},{3,2},{4,5},{5,4},{6,7},{7,6},{8,9},{9,8},{10,11... | collective-permute-start | bytes 1179656 | tf_op jit(solution)/shard_map/ppermute | solution.py:427
  3.5 13.0 %collective-permute-start.3 = (bf16[3,512,128]{2,1,0:T(8,128)(2,1)}, bf16[3,512,128]{2,1,0:T(8,128)(2,1)S(1)}, u32[]{:S(2)}, u32[]{:S(2)}) collective-permute-start(bf16[3,512,128]{2,1,0:T(8,128)(2,1)} %get-tuple-element.29.refs_4_), channel_id=1, source_target_pairs={{0,2},{2,4},{4,6},{6,0},{1,3},{3,5},{5,7},{7,1},{8,10},{10,12},{12... | collective-permute-start | bytes 1179656 | tf_op jit(solution)/shard_map/ppermute | solution.py:423
  5.1 21.0 %collective-permute-start.4 = (bf16[3,512,128]{2,1,0:T(8,128)(2,1)}, bf16[3,512,128]{2,1,0:T(8,128)(2,1)S(1)}, u32[]{:S(2)}, u32[]{:S(2)}) collective-permute-start(bf16[3,512,128]{2,1,0:T(8,128)(2,1)} %get-tuple-element.29.refs_4_), channel_id=1, source_target_pairs={{0,4},{2,6},{4,0},{6,2},{1,5},{3,7},{5,1},{7,3},{8,12},{10,14},{12... | collective-permute-start | bytes 1179656 | tf_op jit(solution)/shard_map/ppermute | solution.py:423
  8.0 18.1 %collective-permute-start.5 = (bf16[3,512,128]{2,1,0:T(8,128)(2,1)}, bf16[3,512,128]{2,1,0:T(8,128)(2,1)S(1)}, u32[]{:S(2)}, u32[]{:S(2)}) collective-permute-start(bf16[3,512,128]{2,1,0:T(8,128)(2,1)} %get-tuple-element.29.refs_4_), channel_id=1, source_target_pairs={{0,6},{2,0},{4,2},{6,4},{1,7},{3,1},{5,3},{7,5},{8,14},{10,8},{12,... | collective-permute-start | bytes 1179656 | tf_op jit(solution)/shard_map/ppermute | solution.py:423
  14.1 12.0 %copy-start.4 = (bf16[3,512,128]{2,1,0:T(8,128)(2,1)}, bf16[3,512,128]{2,1,0:T(8,128)(2,1)S(1)}, u32[]{:S(2)}) copy-start(bf16[3,512,128]{2,1,0:T(8,128)(2,1)S(1)} %collective-permute-done.1.refs_2_) | copy-start | bytes 1179652
  14.1 12.0 %collective-permute-start.2 = (bf16[3,512,128]{2,1,0:T(8,128)(2,1)S(1)}, bf16[3,512,128]{2,1,0:T(8,128)(2,1)S(1)}, u32[]{:S(2)}, u32[]{:S(2)}) collective-permute-start(bf16[3,512,128]{2,1,0:T(8,128)(2,1)S(1)} %collective-permute-done.1.refs_2_), channel_id=1, source_target_pairs={{0,1},{1,0},{2,3},{3,2},{4,5},{5,4},{6,7},{7,6},{8,9},{9,8},{10,11... | collective-permute-start | bytes 1179656 | tf_op jit(solution)/shard_map/ppermute | solution.py:427
  14.1 12.0 %copy-start.5 = (bf16[3,512,128]{2,1,0:T(8,128)(2,1)}, bf16[3,512,128]{2,1,0:T(8,128)(2,1)S(1)}, u32[]{:S(2)}) copy-start(bf16[3,512,128]{2,1,0:T(8,128)(2,1)S(1)} %collective-permute-done.refs_1_) | copy-start | bytes 1179652
  16.5 9.6 %copy-start.6 = (bf16[3,512,128]{2,1,0:T(8,128)(2,1)}, bf16[3,512,128]{2,1,0:T(8,128)(2,1)S(1)}, u32[]{:S(2)}) copy-start(bf16[3,512,128]{2,1,0:T(8,128)(2,1)S(1)} %collective-permute-done.3.refs_5_) | copy-start | bytes 1179652
  26.1 0.7 copy-start.7
  26.1 0.9 copy-start.8
  27.0 0.7 copy-start.10
  101.1 1.4 copy-start.2
  102.4 16.2 %collective-permute-start.9 = (bf16[3,2,512,128]{3,2,0,1:T(8,128)(2,1)S(1)}, bf16[3,2,512,128]{3,2,0,1:T(8,128)(2,1)S(1)}, u32[]{:S(2)}, u32[]{:S(2)}) collective-permute-start(bf16[3,2,512,128]{3,2,0,1:T(8,128)(2,1)S(1)} %copy.11), channel_id=1, source_target_pairs={{0,1},{1,0},{2,3},{3,2},{4,5},{5,4},{6,7},{7,6},{8,9},{9,8},{10,11... | collective-permute-start | bytes 2359304 | tf_op jit(solution)/shard_map/ppermute | solution.py:427
  102.5 16.3 %collective-permute-start.12 = (bf16[2,8,16,384]{3,2,1,0:T(8,128)(2,1)S(1)}, bf16[2,8,16,384]{3,2,1,0:T(8,128)(2,1)S(1)}, u32[]{:S(2)}, u32[]{:S(2)}) collective-permute-start(bf16[2,8,16,384]{3,2,1,0:T(8,128)(2,1)S(1)} %get-tuple-element.54), channel_id=1, source_target_pairs={{16,0},{32,16},{48,32},{64,48},{80,64},{96,80},{112,96},{17,1},{33... | collective-permute-start | bytes 589832 | tf_op jit(solution)/shard_map/ppermute | solution.py:434
  104.7 17.3 %collective-permute-start.11 = (bf16[2,8,16,384]{3,2,1,0:T(8,128)(2,1)S(1)}, bf16[2,8,16,384]{3,2,1,0:T(8,128)(2,1)S(1)}, u32[]{:S(2)}, u32[]{:S(2)}) collective-permute-start(bf16[2,8,16,384]{3,2,1,0:T(8,128)(2,1)S(1)} %get-tuple-element.53), channel_id=1, source_target_pairs={{0,16},{16,32},{32,48},{48,64},{64,80},{80,96},{96,112},{1,17},{17... | collective-permute-start | bytes 589832 | tf_op jit(solution)/shard_map/ppermute | solution.py:434
  110.8 5.0 %copy-start.15 = (bf16[192,512]{1,0:T(8,128)(2,1)S(1)}, bf16[192,512]{1,0:T(8,128)(2,1)}, u32[]{:S(2)}) copy-start(bf16[192,512]{1,0:T(8,128)(2,1)} %get-tuple-element.31) | copy-start | bytes 589828
  110.8 6.9 %copy-start.14 = (bf16[192,512]{1,0:T(8,128)(2,1)S(1)}, bf16[192,512]{1,0:T(8,128)(2,1)}, u32[]{:S(2)}) copy-start(bf16[192,512]{1,0:T(8,128)(2,1)} %get-tuple-element.32) | copy-start | bytes 589828
  110.8 7.7 %copy-start.13 = (bf16[192,512]{1,0:T(8,128)(2,1)S(1)}, bf16[192,512]{1,0:T(8,128)(2,1)}, u32[]{:S(2)}) copy-start(bf16[192,512]{1,0:T(8,128)(2,1)} %get-tuple-element.33) | copy-start | bytes 589828
  110.8 7.9 %copy-start.3 = (bf16[3,2,512,128]{3,2,1,0:T(8,128)(2,1)S(1)}, bf16[3,2,512,128]{3,2,1,0:T(8,128)(2,1)}, u32[]{:S(2)}) copy-start(bf16[3,2,512,128]{3,2,1,0:T(8,128)(2,1)} %get-tuple-element.34.refs_4_) | copy-start | bytes 2359300
  115.8 10.4 %collective-permute-start.6 = (bf16[192,512]{1,0:T(8,128)(2,1)S(1)}, bf16[192,512]{1,0:T(8,128)(2,1)S(1)}, u32[]{:S(2)}, u32[]{:S(2)}) collective-permute-start(bf16[192,512]{1,0:T(8,128)(2,1)S(1)} %copy-done.15), channel_id=1, source_target_pairs={{0,6},{2,0},{4,2},{6,4},{1,7},{3,1},{5,3},{7,5},{8,14},{10,8},{12,... | collective-permute-start | bytes 589832 | tf_op jit(solution)/shard_map/ppermute | solution.py:423
  117.7 9.4 %collective-permute-start.7 = (bf16[192,512]{1,0:T(8,128)(2,1)S(1)}, bf16[192,512]{1,0:T(8,128)(2,1)S(1)}, u32[]{:S(2)}, u32[]{:S(2)}) collective-permute-start(bf16[192,512]{1,0:T(8,128)(2,1)S(1)} %copy-done.14), channel_id=1, source_target_pairs={{0,4},{2,6},{4,0},{6,2},{1,5},{3,7},{5,1},{7,3},{8,12},{10,14},{12... | collective-permute-start | bytes 589832 | tf_op jit(solution)/shard_map/ppermute | solution.py:423
  118.5 11.3 %collective-permute-start.8 = (bf16[192,512]{1,0:T(8,128)(2,1)S(1)}, bf16[192,512]{1,0:T(8,128)(2,1)S(1)}, u32[]{:S(2)}, u32[]{:S(2)}) collective-permute-start(bf16[192,512]{1,0:T(8,128)(2,1)S(1)} %copy-done.13), channel_id=1, source_target_pairs={{0,2},{2,4},{4,6},{6,0},{1,3},{3,5},{5,7},{7,1},{8,10},{10,12},{12... | collective-permute-start | bytes 589832 | tf_op jit(solution)/shard_map/ppermute | solution.py:423
  118.9 11.0 %collective-permute-start.10 = (bf16[3,512,128]{2,1,0:T(8,128)(2,1)S(1)}, bf16[3,512,128]{2,1,0:T(8,128)(2,1)S(1)}, u32[]{:S(2)}, u32[]{:S(2)}) collective-permute-start(bf16[3,512,128]{2,1,0:T(8,128)(2,1)S(1)} %fusion), channel_id=1, source_target_pairs={{0,8},{8,0},{1,9},{9,1},{2,10},{10,2},{3,11},{11,3},{4,12},{12,4},... | collective-permute-start | bytes 1179656 | tf_op jit(solution)/shard_map/ppermute | solution.py:427
  120.5 1.5 slice-start
  122.1 24.2 %copy-start.1 = (bf16[2,32,16,384]{3,2,1,0:T(8,128)(2,1)}, bf16[2,32,16,384]{3,2,1,0:T(8,128)(2,1)S(1)}, u32[]{:S(2)}) copy-start(bf16[2,32,16,384]{3,2,1,0:T(8,128)(2,1)S(1)} %pad_maximum_fusion) | copy-start | bytes 2359300
  126.2 3.7 %copy-start.18 = (bf16[192,512]{1,0:T(8,128)(2,1)}, bf16[192,512]{1,0:T(8,128)(2,1)S(1)}, u32[]{:S(2)}) copy-start(bf16[192,512]{1,0:T(8,128)(2,1)S(1)} %collective-permute-done.6.refs_1_) | copy-start | bytes 589828
  127.0 2.8 %copy-start.19 = (bf16[192,512]{1,0:T(8,128)(2,1)}, bf16[192,512]{1,0:T(8,128)(2,1)S(1)}, u32[]{:S(2)}) copy-start(bf16[192,512]{1,0:T(8,128)(2,1)S(1)} %collective-permute-done.7.refs_2_) | copy-start | bytes 589828
  129.8 0.7 copy-start.21
  130.5 0.8 copy-start.9
  139.1 29.6 %all-to-all-start = ((bf16[8,64,1536]{2,1,0:T(8,128)(2,1)}), bf16[8,64,1536]{2,1,0:T(8,128)(2,1)}, u32[]{:S(2)}, u32[]{:S(2)}) async-start(bf16[8,64,1536]{2,1,0:T(8,128)(2,1)} %project.1), calls=%async_computation | async-start | bytes 3145728 | tf_op jit(solution)/shard_map/all_to_all | solution.py:507
  146.4 24.7 %collective-permute-start.13 = (bf16[2,32,8,384]{3,2,1,0:T(8,128)(2,1)S(1)}, bf16[2,32,8,384]{3,2,1,0:T(8,128)(2,1)S(1)}, u32[]{:S(2)}, u32[]{:S(2)}) collective-permute-start(bf16[2,32,8,384]{3,2,1,0:T(8,128)(2,1)S(1)} %get-tuple-element.52), channel_id=1, source_target_pairs={{0,1},{1,2},{2,3},{3,4},{4,5},{5,6},{6,7},{7,8},{8,9},{9,10},{10,1... | collective-permute-start | bytes 1179656 | tf_op jit(solution)/shard_map/ppermute | solution.py:434
  148.3 22.8 %collective-permute-start.14 = (bf16[2,32,8,384]{3,2,1,0:T(8,128)(2,1)S(1)}, bf16[2,32,8,384]{3,2,1,0:T(8,128)(2,1)S(1)}, u32[]{:S(2)}, u32[]{:S(2)}) collective-permute-start(bf16[2,32,8,384]{3,2,1,0:T(8,128)(2,1)S(1)} %get-tuple-element.51), channel_id=1, source_target_pairs={{1,0},{2,1},{3,2},{4,3},{5,4},{6,5},{7,6},{8,7},{9,8},{10,9},{11,1... | collective-permute-start | bytes 1179656 | tf_op jit(solution)/shard_map/ppermute | solution.py:434
  171.1 0.7 copy-start.11
  171.1 0.9 copy-start.12
  181.4 19.4 %collective-permute-start.19 = (bf16[64,768]{1,0:T(8,128)(2,1)}, bf16[64,768]{1,0:T(8,128)(2,1)S(1)}, u32[]{:S(2)}, u32[]{:S(2)}) collective-permute-start(bf16[64,768]{1,0:T(8,128)(2,1)} %get-tuple-element.45), channel_id=1, source_target_pairs={{0,17},{1,18},{2,19},{3,20},{4,21},{5,22},{6,23},{7,24},{8,25},{9,... | collective-permute-start | bytes 294920 | tf_op jit(solution)/shard_map/ppermute | solution.py:445
  183.4 19.4 %collective-permute-start.20 = (bf16[64,768]{1,0:T(8,128)(2,1)}, bf16[64,768]{1,0:T(8,128)(2,1)S(1)}, u32[]{:S(2)}, u32[]{:S(2)}) collective-permute-start(bf16[64,768]{1,0:T(8,128)(2,1)} %get-tuple-element.46), channel_id=1, source_target_pairs={{16,1},{17,2},{18,3},{19,4},{20,5},{21,6},{22,7},{23,8},{24,9},{25... | collective-permute-start | bytes 294920 | tf_op jit(solution)/shard_map/ppermute | solution.py:445
  185.3 32.0 %collective-permute-start.15 = (bf16[128,768]{1,0:T(8,128)(2,1)}, bf16[128,768]{1,0:T(8,128)(2,1)S(1)}, u32[]{:S(2)}, u32[]{:S(2)}) collective-permute-start(bf16[128,768]{1,0:T(8,128)(2,1)} %get-tuple-element.41), channel_id=1, source_target_pairs={{0,16},{1,17},{2,18},{3,19},{4,20},{5,21},{6,22},{7,23},{8,24},{9,... | collective-permute-start | bytes 589832 | tf_op jit(solution)/shard_map/ppermute | solution.py:445
  190.1 27.2 %collective-permute-start.16 = (bf16[128,768]{1,0:T(8,128)(2,1)}, bf16[128,768]{1,0:T(8,128)(2,1)S(1)}, u32[]{:S(2)}, u32[]{:S(2)}) collective-permute-start(bf16[128,768]{1,0:T(8,128)(2,1)} %get-tuple-element.42), channel_id=1, source_target_pairs={{16,0},{17,1},{18,2},{19,3},{20,4},{21,5},{22,6},{23,7},{24,8},{25... | collective-permute-start | bytes 589832 | tf_op jit(solution)/shard_map/ppermute | solution.py:445
  192.7 15.9 %collective-permute-start.21 = (bf16[64,768]{1,0:T(8,128)(2,1)}, bf16[64,768]{1,0:T(8,128)(2,1)S(1)}, u32[]{:S(2)}, u32[]{:S(2)}) collective-permute-start(bf16[64,768]{1,0:T(8,128)(2,1)} %get-tuple-element.47), channel_id=1, source_target_pairs={{1,16},{2,17},{3,18},{4,19},{5,20},{6,21},{7,22},{8,23},{9,24},{10... | collective-permute-start | bytes 294920 | tf_op jit(solution)/shard_map/ppermute | solution.py:445
  200.9 16.5 %copy-start.23 = (bf16[64,768]{1,0:T(8,128)(2,1)}, bf16[64,768]{1,0:T(8,128)(2,1)S(1)}, u32[]{:S(2)}) copy-start(bf16[64,768]{1,0:T(8,128)(2,1)S(1)} %collective-permute-done.19.rest_4_) | copy-start | bytes 294916
  200.9 16.5 %collective-permute-start.17 = (bf16[128,768]{1,0:T(8,128)(2,1)}, bf16[128,768]{1,0:T(8,128)(2,1)S(1)}, u32[]{:S(2)}, u32[]{:S(2)}) collective-permute-start(bf16[128,768]{1,0:T(8,128)(2,1)} %get-tuple-element.43), channel_id=1, source_target_pairs={{0,1},{1,2},{2,3},{3,4},{4,5},{5,6},{6,7},{7,8},{8,9},{9,10},{10,1... | collective-permute-start | bytes 589832 | tf_op jit(solution)/shard_map/ppermute | solution.py:445
  202.8 14.6 %copy-start.24 = (bf16[64,768]{1,0:T(8,128)(2,1)}, bf16[64,768]{1,0:T(8,128)(2,1)S(1)}, u32[]{:S(2)}) copy-start(bf16[64,768]{1,0:T(8,128)(2,1)S(1)} %collective-permute-done.20.rest_5_) | copy-start | bytes 294916
  202.8 14.6 %collective-permute-start.18 = (bf16[128,768]{1,0:T(8,128)(2,1)}, bf16[128,768]{1,0:T(8,128)(2,1)S(1)}, u32[]{:S(2)}, u32[]{:S(2)}) collective-permute-start(bf16[128,768]{1,0:T(8,128)(2,1)} %get-tuple-element.44), channel_id=1, source_target_pairs={{1,0},{2,1},{3,2},{4,3},{5,4},{6,5},{7,6},{8,7},{9,8},{10,9},{11,1... | collective-permute-start | bytes 589832 | tf_op jit(solution)/shard_map/ppermute | solution.py:445
  208.6 8.8 %copy-start.25 = (bf16[64,768]{1,0:T(8,128)(2,1)}, bf16[64,768]{1,0:T(8,128)(2,1)S(1)}, u32[]{:S(2)}) copy-start(bf16[64,768]{1,0:T(8,128)(2,1)S(1)} %collective-permute-done.21.rest_6_) | copy-start | bytes 294916
  208.6 8.7 %collective-permute-start.22 = (bf16[64,768]{1,0:T(8,128)(2,1)}, bf16[64,768]{1,0:T(8,128)(2,1)S(1)}, u32[]{:S(2)}, u32[]{:S(2)}) collective-permute-start(bf16[64,768]{1,0:T(8,128)(2,1)} %get-tuple-element.48), channel_id=1, source_target_pairs={{17,0},{18,1},{19,2},{20,3},{21,4},{22,5},{23,6},{24,7},{25,8},{26... | collective-permute-start | bytes 294920 | tf_op jit(solution)/shard_map/ppermute | solution.py:445
  217.3 0.6 copy-start.26
  217.3 0.7 copy-start.16
  217.4 0.8 copy-start.17
  217.4 0.8 copy-start.20
  217.4 0.8 copy-start.22

commit v2 on v1

--- a/solution.py
+++ b/solution.py
@@ -63,15 +63,21 @@
     return pl.ds(pl.multiple_of(owner * tokens, tokens), tokens)
 
 
-def coarse_stats(key_values, query_ups, key_tile):
+def coarse_stats(key_values, query_ups, steps, before, key_tile):
     heads, tokens, _ = key_values[0].shape
-    blocks = len(query_ups)
+    blocks, number = len(key_values), len(query_ups)
     per_block = tokens // key_tile
 
     def body(*refs):
-        kv_refs, qu_refs = refs[:blocks], refs[blocks : 2 * blocks]
-        out_ref, held = refs[2 * blocks :]
-        for at in range(blocks):
+        kv_refs, qu_refs = refs[:blocks], refs[blocks : blocks + number]
+        out_ref, held = refs[-2:]
+        if before:
+
+            @pl.when(pl.program_id(1) == 0)
+            def _():
+                out_ref[...] = refs[blocks + number][...]
+
+        for at in range(number):
 
             @pl.when(pl.program_id(1) == at)
             def _():
@@ -94,20 +100,25 @@
             weighted = weighted * decay + jnp.sum(share * product, axis=0, keepdims=True)
             peak = new_peak
         found = jnp.concatenate([peak + jnp.log(total), weighted / total], axis=0)
-        out_ref[0, :, own_block(pl.program_id(1), tokens)] = found
-
-    pairs = heads * (blocks * tokens) ** 2
+        for at, step in enumerate(steps):
+
+            @pl.when(pl.program_id(1) == at)
+            def _():
+                out_ref[0, :, own_block(step, tokens)] = found
+
+    pairs = heads * number * blocks * tokens**2
     return pl.pallas_call(
         body,
-        grid=(heads, blocks),
-        in_specs=[pl.BlockSpec((1, tokens, 128), lambda h, q: (h, 0, 0))] * (2 * blocks),
+        grid=(heads, number),
+        in_specs=[pl.BlockSpec((1, tokens, 128), lambda h, q: (h, 0, 0))] * (blocks + number)
+        + [pl.BlockSpec((1, 2, blocks * tokens), lambda h, q: (h, 0, 0))] * len(before),
         out_specs=pl.BlockSpec((1, 2, blocks * tokens), lambda h, q: (h, 0, 0)),
         out_shape=jax.ShapeDtypeStruct((heads, 2, blocks * tokens), F32),
         scratch_shapes=[pltpu.VMEM((tokens, 128), BF16)],
         name="coarse_stats",
         cost_estimate=cost(4 * pairs * 256, 2 << 20, pairs),
         compiler_params=pltpu.CompilerParams(vmem_limit_bytes=VMEM),
-    )(*key_values, *query_ups)
+    )(*key_values, *query_ups, *before)
 
 
 def coarse_grads(key_values, query_ups, stats):
@@ -228,32 +239,14 @@
     return jnp.concatenate([ref[which, :, lanes] for ref in refs], axis=0)
 
 
-def window_pieces(columns, rows):
-    edge = RIM * columns
-    corner = RIM * RIM
-    middle = rows * columns
-    side = rows * RIM
-    base = 2 * edge + middle
-    wing = 2 * corner + side
-    return [
-        ((0, 0), edge, middle),
-        ((-1, 0), 0, edge),
-        ((1, 0), edge + middle, edge),
-        ((0, -1), base + corner, side),
-        ((0, 1), base + wing + corner, side),
-        ((-1, -1), base, corner),
-        ((1, -1), base + corner + side, corner),
-        ((-1, 1), base + wing, corner),
-        ((1, 1), base + wing + corner + side, corner),
-    ]
-
-
 def fine_grads(own_qkv, ext_kv, own_up, rows, columns):
     _, own, width = own_qkv.shape
-    pieces = window_pieces(columns, rows)
-
-    def body(q_ref, mid_ref, low_ref, high_ref, up_ref, q_out, *rest):
-        outs, bias_ref = rest[:-1], rest[-1]
+    sizes = [ref.shape[1] for ref in ext_kv]
+    places = [sum(sizes[:i]) for i in range(len(sizes))]
+
+    def body(q_ref, mid_ref, low_ref, high_ref, up_ref, q_out, mid_out, *rest):
+        inner_out, outer_out, bias_ref = rest
+        first = lax.axis_index("c") == 0
         fill_bias(bias_ref, own, rows, columns)
         ext = (mid_ref, low_ref, high_ref)
         for pair, lanes in pairs_of(width):
@@ -278,16 +271,20 @@
                 parts.append(nn(key_t[side * HD : side * HD + HD], grads))
             q_out[:, lanes] = (jnp.concatenate(parts, axis=0).T * SCALE).astype(BF16)
             right = slice(width + pair * 128, width + pair * 128 + 128)
-            for out, (_, place, size) in zip(outs, pieces):
-                out[:, lanes] = key_sum[place : place + size].astype(out.dtype)
-                out[:, right] = value_sum[place : place + size].astype(out.dtype)
+            for at, total in ((lanes, key_sum), (right, value_sum)):
+                mid, low, high = [
+                    total[place : place + size] for place, size in zip(places, sizes)
+                ]
+                mid_out[:, at] = mid
+                inner_out[:, at] = jnp.where(first, high, low).astype(BF16)
+                outer_out[:, at] = jnp.where(first, low, high).astype(BF16)
 
     return whole_call(
         body,
         [jax.ShapeDtypeStruct((own, width), BF16)]
         + [
             jax.ShapeDtypeStruct((size, 2 * width), BF16 if i else F32)
-            for i, (_, _, size) in enumerate(pieces)
+            for i, size in enumerate(sizes)
         ],
         "fine_grads",
         2 << 30,
@@ -298,36 +295,59 @@
     )
 
 
-def add_arrived(own, arrived, rows, columns):
+def add_columns(mid, inner, outer, columns):
+    cells, wide = mid.shape
+    tall = cells // columns
+    edge = RIM * columns
+
+    def body(mid_ref, inner_ref, outer_ref, own_out, inner_out, outer_out):
+        first = lax.axis_index("c") == 0
+        inner = inner_ref[...].astype(F32).reshape(tall, RIM, wide)
+        outer = outer_ref[...].astype(F32).reshape(tall, RIM, wide)
+        left, right = jnp.where(first, outer, inner), jnp.where(first, inner, outer)
+        both = jnp.concatenate([left, right], axis=1).reshape(cells, wide)
+        total = mid_ref[...] + both
+        top, bottom = total[:edge], total[cells - edge :]
+        upper = lax.axis_index("zh") == 0
+        own_out[...] = total[edge : cells - edge]
+        inner_out[...] = jnp.where(upper, bottom, top).astype(BF16)
+        outer_out[...] = jnp.where(upper, top, bottom).astype(BF16)
+
+    return whole_call(
+        body,
+        [jax.ShapeDtypeStruct((cells - 2 * edge, wide), F32)]
+        + [jax.ShapeDtypeStruct((edge, wide), BF16)] * 2,
+        "add_columns",
+        1 << 20,
+        [],
+        mid,
+        inner,
+        outer,
+    )
+
+
+def add_rows(own, inner, outer):
     cells, wide = own.shape
     width = wide // 2
 
-    def body(own_ref, *rest):
-        above, below, left, right, up_left, down_left, up_right, down_right = [
-            ref[...].astype(F32) for ref in rest[:-2]
-        ]
-        k_out, v_out = rest[-2:]
+    def body(own_ref, inner_ref, outer_ref, k_out, v_out):
+        upper = lax.axis_index("zh") == 0
+        inner = inner_ref[...].astype(F32)
+        outer = outer_ref[...].astype(F32)
+        above, below = jnp.where(upper, outer, inner), jnp.where(upper, inner, outer)
         total = own_ref[...] + jnp.concatenate([above, below], axis=0)
-
-        def halves(first, second, tall):
-            first = first.reshape(tall, RIM, wide)
-            return jnp.concatenate([first, second.reshape(tall, RIM, wide)], axis=1)
-
-        total += halves(left, right, rows).reshape(cells, wide)
-        upper = halves(up_left, up_right, RIM)
-        lower = halves(down_left, down_right, RIM)
-        total += jnp.concatenate([upper, lower], axis=0).reshape(cells, wide)
         k_out[...] = total[:, :width].astype(BF16)
         v_out[...] = total[:, width:].astype(BF16)
 
     return whole_call(
         body,
         [jax.ShapeDtypeStruct((cells, width), BF16)] * 2,
-        "add_arrived",
+        "add_rows",
         1 << 20,
         [],
         own,
-        *arrived,
+        inner,
+        outer,
     )
 
 
@@ -434,15 +454,11 @@
     return lax.ppermute(low, axis, forward), lax.ppermute(high, axis, backward)
 
 
-def toward(piece, down, across):
-    tall, wide = lax.axis_size(ROW), lax.axis_size(COL)
-    pairs = []
-    for row in range(tall):
-        for column in range(wide):
-            if 0 <= row + down < tall and 0 <= column + across < wide:
-                here = row * wide + column
-                pairs.append((here, here + down * wide + across))
-    return lax.ppermute(piece, ROW + COL, pairs)
+def exchanged(inner, outer, axis):
+    count = lax.axis_size(axis)
+    beside = [(i, i ^ 1) for i in range(count)]
+    beyond = [(i, ((i + 1) ^ 1) - 1) for i in range(1, count - 1)]
+    return lax.ppermute(inner, axis, beside), lax.ppermute(outer, axis, beyond)
 
 
 def edges(block, axis, at):
@@ -477,10 +493,19 @@
     across = swapped(key_value, "zl")
     beside = swapped(key_value, "c")
     queries = [query_up] + [shifted(query_up, "y", step) for step in (1, 2, 3)]
+    across, merge_weight, fine_qkv = lax.optimization_barrier((across, merge_weight, fine_qkv))
     corner = swapped(across, "c")
+    joint = lax.dot_general(
+        qkv_weight, merge_weight, (((1,), (1,)), ((), ())), preferred_element_type=F32
+    ).astype(BF16)
+    own_qkv = fine_qkv.reshape(3, own, width)
+    tall = with_rows(fine_qkv[1:], 1)
+    corner, joint = lax.optimization_barrier((corner, joint))
     keys = [key_value, beside, across, corner]
 
-    part = coarse_stats(keys, queries, 256)
+    near = [0, 1, 3]
+    part = coarse_stats(keys, [queries[i] for i in near], near, (), 256)
+    part = coarse_stats(keys, [queries[2]], [2], (part,), 256)
     stats = lax.all_gather(part, "y", axis=0)
     kept, sent, *query_grads = coarse_grads(keys, queries, stats)
 
@@ -490,14 +515,6 @@
         query_pieces.append(shifted(query_grads[step], "y", -step))
     passed = (kept[:, 1].astype(F32) + from_core[:, 1].astype(F32)).astype(BF16)
     arrived = swapped(passed, "zl")
-    merge_weight, fine_qkv, _ = lax.optimization_barrier(
-        (merge_weight, fine_qkv, passed[0, :1, :1])
-    )
-    joint = lax.dot_general(
-        qkv_weight, merge_weight, (((1,), (1,)), ((), ())), preferred_element_type=F32
-    ).astype(BF16)
-    own_qkv = fine_qkv.reshape(3, own, width)
-    tall = with_rows(fine_qkv[1:], 1)
     count = lax.axis_size(ROW)
     projected = project(
         query_pieces, kept, from_core, arrived, joint, coarse_columns, count
@@ -507,12 +524,11 @@
     pieces = lax.all_to_all(projected, ROW, 0, 0)
     own_up = spread(pieces, coarse_columns)
 
-    grad_query, middle, *rims = fine_grads(own_qkv, ext_kv, own_up, rows, columns)
-    places = window_pieces(columns, rows)[1:]
-    arrived = [toward(rim, *place[0]) for rim, place in zip(rims, places)]
-    order = [(1, 0), (-1, 0), (0, 1), (0, -1), (1, 1), (-1, 1), (1, -1), (-1, -1)]
-    found = {place[0]: piece for place, piece in zip(places, arrived)}
-    grad_key, grad_value = add_arrived(middle, [found[at] for at in order], rows, columns)
+    grad_query, mid, inner, outer = fine_grads(own_qkv, ext_kv, own_up, rows, columns)
+    inner, outer = exchanged(inner, outer, COL)
+    middle, inner, outer = add_columns(mid, inner, outer, columns)
+    inner, outer = exchanged(inner, outer, ROW)
+    grad_key, grad_value = add_rows(middle, inner, outer)
     shape = (rows, columns, width)
     return grad_query.reshape(shape), grad_key.reshape(shape), grad_value.reshape(shape)
 

time: 222 us -> 210 us (0.946)
  starting transfers between devices: 63.2 us -> 43.7 us
  waiting for transfers between devices: 44.7 us -> 49.5 us
    ppermute x8 -> x4, starting transfers between devices: 29 us -> 7.9 us  [the longest x2 6.27 us: exchanged(): lax.ppermute(outer, axis, beyond)]
    ppermute x6, waiting for transfers between devices: 18.6 us -> 6.07 us  [shifted(): lax.ppermute(array, axis, [(i, (i + step) % count) for i in range(count)])]
    ppermute x8 -> x4, waiting for transfers between devices: 6.82 us -> 15.3 us  [the longest x2 10.8 us: exchanged(): lax.ppermute(outer, axis, beyond)]
    ppermute x2, waiting for transfers between devices: 0.01 us -> 8.48 us  [onward(): lax.ppermute(low, axis, forward)]
    pallas_call x4 -> x5, Pallas kernels: 16.7 us -> 19.3 us  [whole_call(): pl.pallas_call(body, out_shape=out_shape, scratch_shapes=scratch, name=na...]
    pallas_call x1 -> x2, Pallas kernels: 23.3 us -> 21.9 us  [coarse_stats(): pl.pallas_call(body, grid=(heads, number), in_specs=[pl.BlockSpec((1, tok...]
    unnamed x54 -> x46, local copies, waits for them, and re-layouts: 4.74 us -> 5.29 us
  transfers between devices with their start and end apart: 24 -> 20, of which waited for: 8 -> 8; matrix products, arithmetic and copies ran while one was open for 4% -> 4% of each run, Pallas kernels for 1% -> 8%
where the time goes in v2:
time: 210 us; the launch traced here: 208 us
  Pallas kernels  85.9 us (41%)
  waiting for transfers between devices  49.5 us (24%)
  starting transfers between devices  43.7 us (21%)
  blocking collectives  13.9 us (7%)
  local copies, waits for them, and re-layouts  7.75 us (4%)
  matrix products  4.97 us (2%)
    pallas_call x1, Pallas kernels, coarse_grads(): pl.pallas_call(body, grid=(heads, blocks), in_specs=[pl.BlockSpec((1, tok...  36.9 us
    pallas_call x2, Pallas kernels, coarse_stats(): pl.pallas_call(body, grid=(heads, number), in_specs=[pl.BlockSpec((1, tok...  21.9 us
    pallas_call x5, Pallas kernels, whole_call(): pl.pallas_call(body, out_shape=out_shape, scratch_shapes=scratch, name=na...  19.3 us
    all_to_all x1, waiting for transfers between devices, shards(): pieces = lax.all_to_all(projected, ROW, 0, 0)  14.7 us
    all_gather x1, blocking collectives, shards(): stats = lax.all_gather(part, 'y', axis=0)  13.9 us
    ppermute x2, waiting for transfers between devices, exchanged(): lax.ppermute(outer, axis, beyond)  10.8 us
    ppermute x6, starting transfers between devices, shifted(): lax.ppermute(array, axis, [(i, (i + step) % count) for i in range(count)])  8.78 us
    ppermute x2, starting transfers between devices, onward(): lax.ppermute(low, axis, forward)  8.58 us
  transfers between devices with their start and end apart: 20, of which 8 were waited for; matrix products, arithmetic and copies ran while one was open for 4% of the time, Pallas kernels for 8%

profile of v2, /device:TPU:96, one launch (start us, length us, event | category | flops | bytes accessed | tf_op | source)
XLA Modules:
  0.0 208.2 jit_solution(11423135294512806071)
XLA Ops:
  0.6 0.0 copy-start
  0.6 2.5 %prepare.1 = (bf16[3,512,128]{2,1,0:T(8,128)(2,1)}, bf16[3,512,128]{2,1,0:T(8,128)(2,1)}) custom-call(bf16[3,512,192]{2,1,0:T(8,128)(2,1)} %bitcast.25, bf16[512,192]{1,0:T(8,128)(2,1)} %bitcast.28), custom_call_target="tpu_custom_call" | custom-call | flops 1048576 | bytes 6291456 | tf_op jit(solution)/shard_map/prepare/pallas_call | solution.py:196
  3.1 0.4 collective-permute-start
  3.5 1.6 collective-permute-start.3
  5.1 2.9 %collective-permute-start.4 = (bf16[3,512,128]{2,1,0:T(8,128)(2,1)}, bf16[3,512,128]{2,1,0:T(8,128)(2,1)S(1)}, u32[]{:S(2)}, u32[]{:S(2)}) collective-permute-start(bf16[3,512,128]{2,1,0:T(8,128)(2,1)} %get-tuple-element.32.refs_4_), channel_id=1, source_target_pairs={{0,4},{2,6},{4,0},{6,2},{1,5},{3,7},{5,1},{7,3},{8,12},{10,14},{12... | collective-permute-start | bytes 1179656 | tf_op jit(solution)/shard_map/ppermute | solution.py:443
  8.0 1.3 collective-permute-start.5
  9.3 4.8 %collective-permute-done.refs_2_ = bf16[3,512,128]{2,1,0:T(8,128)(2,1)S(1)} collective-permute-done((bf16[3,512,128]{2,1,0:T(8,128)(2,1)}, bf16[3,512,128]{2,1,0:T(8,128)(2,1)S(1)}, u32[]{:S(2)}, u32[]{:S(2)}) %collective-permute-start) | collective-permute-done | bytes 393248 | tf_op jit(solution)/shard_map/ppermute | solution.py:447
  14.2 0.0 collective-permute-start.2
  14.2 5.0 %fusion.3 = f32[1536,576]{0,1:S(1)} fusion(bf16[1536,1536]{1,0:T(8,128)(2,1)} %param.8, bf16[1536,576]{0,1:T(8,128)(2,1)S(1)} %bitcast.20), kind=kOutput, calls=%fused_computation.6 | convolution fusion | flops 2717908992 | bytes 10027008
  19.2 1.5 convert_bitcast_fusion.refs_7_
  20.6 0.0 collective-permute-done.2.refs_3_
  20.7 0.0 collective-permute-done.3.refs_5_
  20.7 4.9 %collective-permute-done.5.refs_6_.refs_7_ = bf16[3,512,128]{2,1,0:T(8,128)(2,1)S(1)} collective-permute-done((bf16[3,512,128]{2,1,0:T(8,128)(2,1)}, bf16[3,512,128]{2,1,0:T(8,128)(2,1)S(1)}, u32[]{:S(2)}, u32[]{:S(2)}) %collective-permute-start.5) | collective-permute-done | bytes 393248 | tf_op jit(solution)/shard_map/ppermute | solution.py:443
  25.6 0.8 copy-done.11
  26.3 14.8 %coarse_stats.2.refs_5_ = f32[3,2,2048]{2,1,0:T(2,128)} custom-call(bf16[3,512,128]{2,1,0:T(8,128)(2,1)} %get-tuple-element.27.refs_0_, bf16[3,512,128]{2,1,0:T(8,128)(2,1)} %copy-done.7, bf16[3,512,128]{2,1,0:T(8,128)(2,1)} %copy-done.6, bf16[3,512,128]{2,1,0:T(8,128)(2,1)} %copy-done.12, bf16[3,512,128]{2,1,0:T(8,128)(2,1)} %get-tuple-element.32.refs_4_, ...), custom_call_target="tpu_custom_call" | custom-call | flops 9663676416 | bytes 2097152 | tf_op jit(solution)/shard_map/coarse_stats/pallas_call | solution.py:110
  41.2 0.8 copy-done.10
  41.9 7.1 %coarse_stats.3 = f32[3,2,2048]{2,1,0:T(2,128)} custom-call(bf16[3,512,128]{2,1,0:T(8,128)(2,1)} %get-tuple-element.27.refs_0_, bf16[3,512,128]{2,1,0:T(8,128)(2,1)} %copy-done.7, bf16[3,512,128]{2,1,0:T(8,128)(2,1)} %copy-done.6, bf16[3,512,128]{2,1,0:T(8,128)(2,1)} %copy-done.12, bf16[3,512,128]{2,1,0:T(8,128)(2,1)} %copy-done.10, ...), custom_call_target="tpu_custom_call" | custom-call | flops 3221225472 | bytes 2097152 | tf_op jit(solution)/shard_map/coarse_stats/pallas_call | solution.py:110
  49.0 13.9 %all-gather = f32[12,2,2048]{2,1,0:T(2,128)} all-gather(f32[3,2,2048]{2,1,0:T(2,128)} %coarse_stats.3), channel_id=2, replica_groups=mesh['x'=4,'zh'=2,'zl'=2,'y'=4,'c'=2] {'y'}, dimensions={0}, use_global_device_ids=true | all-gather | bytes 245760 | tf_op jit(solution)/shard_map/all_gather | solution.py:509
  62.8 36.9 %coarse_grads.1 = (bf16[3,2,512,128]{3,2,1,0:T(8,128)(2,1)}, bf16[3,2,512,128]{3,2,1,0:T(8,128)(2,1)}, bf16[192,512]{1,0:T(8,128)(2,1)}, bf16[192,512]{1,0:T(8,1...) custom-call(bf16[3,512,128]{2,1,0:T(8,128)(2,1)} %get-tuple-element.27.refs_0_, ...), custom_call_target="tpu_custom_call" | custom-call | flops 32212254720 | bytes 4194304 | tf_op jit(solution)/shard_map/coarse_grads/pallas_call | solution.py:177
  99.7 0.0 copy-start.2
  99.7 0.0 copy-start.17
  99.7 0.0 copy-start.16
  99.8 1.3 copy.11
  101.1 0.0 slice-start
  101.1 0.1 collective-permute-start.9
  101.2 2.2 %collective-permute-start.12 = (bf16[2,8,16,384]{3,2,1,0:T(8,128)(2,1)S(1)}, bf16[2,8,16,384]{3,2,1,0:T(8,128)(2,1)S(1)}, u32[]{:S(2)}, u32[]{:S(2)}) collective-permute-start(bf16[2,8,16,384]{3,2,1,0:T(8,128)(2,1)S(1)} %get-tuple-element.54), channel_id=1, source_target_pairs={{16,0},{32,16},{48,32},{64,48},{80,64},{96,80},{112,96},{17,1},{33... | collective-permute-start | bytes 589832 | tf_op jit(solution)/shard_map/ppermute | solution.py:454
  103.4 0.0 collective-permute-done.9
  103.5 0.1 fusion
  103.6 1.7 collective-permute-start.10
  105.3 6.7 %collective-permute-start.11 = (bf16[2,8,16,384]{3,2,1,0:T(8,128)(2,1)S(1)}, bf16[2,8,16,384]{3,2,1,0:T(8,128)(2,1)S(1)}, u32[]{:S(2)}, u32[]{:S(2)}) collective-permute-start(bf16[2,8,16,384]{3,2,1,0:T(8,128)(2,1)S(1)} %get-tuple-element.53), channel_id=1, source_target_pairs={{0,16},{16,32},{32,48},{48,64},{64,80},{80,96},{96,112},{1,17},{17... | collective-permute-start | bytes 589832 | tf_op jit(solution)/shard_map/ppermute | solution.py:454
  111.9 1.9 collective-permute-start.6
  113.8 0.9 collective-permute-start.7
  114.7 0.0 collective-permute-done.12
  114.7 0.2 collective-permute-start.8
  114.9 8.5 %collective-permute-done.11 = bf16[2,8,16,384]{3,2,1,0:T(8,128)(2,1)S(1)} collective-permute-done((bf16[2,8,16,384]{3,2,1,0:T(8,128)(2,1)S(1)}, bf16[2,8,16,384]{3,2,1,0:T(8,128)(2,1)S(1)}, u32[]{:S(2)}, u32[]{:S(2)}) %collective-permute-start.11) | collective-permute-done | bytes 196640 | tf_op jit(solution)/shard_map/ppermute | solution.py:454
  123.4 0.1 pad_maximum_fusion
  123.5 1.0 copy.13.refs_5_
  124.5 0.0 collective-permute-done.6.refs_1_
  124.5 0.0 collective-permute-done.7.refs_2_
  124.5 0.0 copy-start.19
  124.5 1.2 collective-permute-done.8.refs_3_
  125.7 0.0 collective-permute-done.10.refs_6_
  125.7 0.7 copy-done.20
  126.4 0.8 copy-done.8
  127.1 7.8 %project.1 = bf16[8,64,1536]{2,1,0:T(8,128)(2,1)} custom-call(bf16[192,512]{1,0:T(8,128)(2,1)} %get-tuple-element.33.refs_0_, bf16[192,512]{1,0:T(8,128)(2,1)} %copy-done.18, bf16[192,512]{1,0:T(8,128)(2,1)} %copy-done.19, bf16[192,512]{1,0:T(8,128)(2,1)} %copy-done.20, bf16[3,2,512,128]{3,2,1,0:T(8,128)(2,1)} %get-tuple-element.37.refs_4_, ...), custom_call_target="tpu_custom_call" | custom-call | flops 2147483648 | bytes 6291456 | tf_op jit(solution)/shard_map/project/pallas_call | solution.py:388
  135.0 8.3 %all-to-all-start = ((bf16[8,64,1536]{2,1,0:T(8,128)(2,1)}), bf16[8,64,1536]{2,1,0:T(8,128)(2,1)}, u32[]{:S(2)}, u32[]{:S(2)}) async-start(bf16[8,64,1536]{2,1,0:T(8,128)(2,1)} %project.1), calls=%async_computation | async-start | bytes 3145728 | tf_op jit(solution)/shard_map/all_to_all | solution.py:524
  143.3 0.1 fusion.1
  143.4 1.9 collective-permute-start.13
  145.3 5.8 %collective-permute-start.14 = (bf16[2,32,8,384]{3,2,1,0:T(8,128)(2,1)S(1)}, bf16[2,32,8,384]{3,2,1,0:T(8,128)(2,1)S(1)}, u32[]{:S(2)}, u32[]{:S(2)}) collective-permute-start(bf16[2,32,8,384]{3,2,1,0:T(8,128)(2,1)S(1)} %get-tuple-element.51), channel_id=1, source_target_pairs={{1,0},{2,1},{3,2},{4,3},{5,4},{6,5},{7,6},{8,7},{9,8},{10,9},{11,1... | collective-permute-start | bytes 1179656 | tf_op jit(solution)/shard_map/ppermute | solution.py:454
  151.1 14.7 %all-to-all-done.in_ref = bf16[8,64,1536]{2,1,0:T(8,128)(2,1)} async-done(((bf16[8,64,1536]{2,1,0:T(8,128)(2,1)}), bf16[8,64,1536]{2,1,0:T(8,128)(2,1)}, u32[]{:S(2)}, u32[]{:S(2)}) %all-to-all-start) | async-done | bytes 1572896 | tf_op jit(solution)/shard_map/all_to_all | solution.py:524
  165.8 2.5 %spread.1.up_ref = bf16[256,384]{1,0:T(8,128)(2,1)} custom-call(bf16[8,64,1536]{2,1,0:T(8,128)(2,1)} %all-to-all-done.in_ref), custom_call_target="tpu_custom_call" | custom-call | flops 268435456 | bytes 6291456 | tf_op jit(solution)/shard_map/spread/pallas_call | solution.py:196
  168.2 0.8 copy-done.13
  169.0 0.1 copy-done.14
  169.1 9.6 %fine_grads.1 = (bf16[256,384]{1,0:T(8,128)(2,1)}, f32[512,768]{1,0:T(8,128)}, bf16[256,768]{1,0:T(8,128)(2,1)}, bf16[256,768]{1,0:T(8,128)(2,1)}) custom-call(bf16[3,256,384]{2,1,0:T(8,128)(2,1)} %bitcast.23, bf16[2,512,384]{2,1,0:T(8,128)(2,1)} %bitcast.22, bf16[2,256,384]{2,1,0:T(8,128)(2,1)} %bitcast.26, bf16[2,256,384]{2,1,0:T(8,128)(2,1)} %bitcast.27, ...), custom_call_target="tpu_custom_call" | custom-call | flops 2147483648 | bytes 6291456 | tf_op jit(solution)/shard_map/fine_grads/pallas_call | solution.py:196
  178.7 3.0 %collective-permute-start.16 = (bf16[256,768]{1,0:T(8,128)(2,1)}, bf16[256,768]{1,0:T(8,128)(2,1)S(1)}, u32[]{:S(2)}, u32[]{:S(2)}) collective-permute-start(bf16[256,768]{1,0:T(8,128)(2,1)} %get-tuple-element.45), channel_id=1, source_target_pairs={{1,2},{2,1},{3,4},{4,3},{5,6},{6,5},{7,8},{8,7},{9,10},{10,9},{11,... | collective-permute-start | bytes 1179656 | tf_op jit(solution)/shard_map/ppermute | solution.py:461
  181.7 8.5 %collective-permute-done.16.outer_ref = bf16[256,768]{1,0:T(8,128)(2,1)S(1)} collective-permute-done((bf16[256,768]{1,0:T(8,128)(2,1)}, bf16[256,768]{1,0:T(8,128)(2,1)S(1)}, u32[]{:S(2)}, u32[]{:S(2)}) %collective-permute-start.16) | collective-permute-done | bytes 393248 | tf_op jit(solution)/shard_map/ppermute | solution.py:461
  190.2 0.7 copy-done.4
  190.9 2.7 %add_columns.1 = (f32[256,768]{1,0:T(8,128)}, bf16[128,768]{1,0:T(8,128)(2,1)}, bf16[128,768]{1,0:T(8,128)(2,1)}) custom-call(f32[512,768]{1,0:T(8,128)} %get-tuple-element.43.mid_ref, bf16[256,768]{1,0:T(8,128)(2,1)} %copy-done.3, bf16[256,768]{1,0:T(8,128)(2,1)} %copy-done.4), custom_call_target="tpu_custom_call" | custom-call | flops 1048576 | bytes 6291456 | tf_op jit(solution)/shard_map/add_columns/pallas_call | solution.py:196
  193.7 1.6 collective-permute-start.17
  195.3 3.3 %collective-permute-start.18 = (bf16[128,768]{1,0:T(8,128)(2,1)}, bf16[128,768]{1,0:T(8,128)(2,1)S(1)}, u32[]{:S(2)}, u32[]{:S(2)}) collective-permute-start(bf16[128,768]{1,0:T(8,128)(2,1)} %get-tuple-element.48), channel_id=1, source_target_pairs={{16,32},{32,16},{48,64},{64,48},{80,96},{96,80},{17,33},{33,17},{4... | collective-permute-start | bytes 589832 | tf_op jit(solution)/shard_map/ppermute | solution.py:461
  198.6 4.6 %collective-permute-done.17.inner_ref = bf16[128,768]{1,0:T(8,128)(2,1)S(1)} collective-permute-done((bf16[128,768]{1,0:T(8,128)(2,1)}, bf16[128,768]{1,0:T(8,128)(2,1)S(1)}, u32[]{:S(2)}, u32[]{:S(2)}) %collective-permute-start.17) | collective-permute-done | bytes 196640 | tf_op jit(solution)/shard_map/ppermute | solution.py:461
  203.1 2.3 %collective-permute-done.18.outer_ref = bf16[128,768]{1,0:T(8,128)(2,1)S(1)} collective-permute-done((bf16[128,768]{1,0:T(8,128)(2,1)}, bf16[128,768]{1,0:T(8,128)(2,1)S(1)}, u32[]{:S(2)}, u32[]{:S(2)}) %collective-permute-start.18) | collective-permute-done | bytes 196640 | tf_op jit(solution)/shard_map/ppermute | solution.py:461
  205.4 0.7 copy-done.22
  206.1 2.1 add_rows.1
  (42 shorter events, 0.1 us)
Async XLA Ops:
  0.6 13.5 %copy-start = (bf16[3,1536,192]{1,2,0:T(8,128)(2,1)S(1)}, bf16[3,1536,192]{1,2,0:T(8,128)(2,1)}, u32[]{:S(2)}) copy-start(bf16[3,1536,192]{1,2,0:T(8,128)(2,1)} %param.9) | copy-start | bytes 5308420
  3.1 11.1 %collective-permute-start = (bf16[3,512,128]{2,1,0:T(8,128)(2,1)}, bf16[3,512,128]{2,1,0:T(8,128)(2,1)S(1)}, u32[]{:S(2)}, u32[]{:S(2)}) collective-permute-start(bf16[3,512,128]{2,1,0:T(8,128)(2,1)} %get-tuple-element.27.refs_0_), channel_id=1, source_target_pairs={{0,8},{8,0},{1,9},{9,1},{2,10},{10,2},{3,11},{11,3},{4,12},{12,4},... | collective-permute-start | bytes 1179656 | tf_op jit(solution)/shard_map/ppermute | solution.py:447
  3.5 17.1 %collective-permute-start.1 = (bf16[3,512,128]{2,1,0:T(8,128)(2,1)}, bf16[3,512,128]{2,1,0:T(8,128)(2,1)S(1)}, u32[]{:S(2)}, u32[]{:S(2)}) collective-permute-start(bf16[3,512,128]{2,1,0:T(8,128)(2,1)} %get-tuple-element.27.refs_0_), channel_id=1, source_target_pairs={{0,1},{1,0},{2,3},{3,2},{4,5},{5,4},{6,7},{7,6},{8,9},{9,8},{10,11... | collective-permute-start | bytes 1179656 | tf_op jit(solution)/shard_map/ppermute | solution.py:447
  3.5 17.1 %collective-permute-start.3 = (bf16[3,512,128]{2,1,0:T(8,128)(2,1)}, bf16[3,512,128]{2,1,0:T(8,128)(2,1)S(1)}, u32[]{:S(2)}, u32[]{:S(2)}) collective-permute-start(bf16[3,512,128]{2,1,0:T(8,128)(2,1)} %get-tuple-element.32.refs_4_), channel_id=1, source_target_pairs={{0,2},{2,4},{4,6},{6,0},{1,3},{3,5},{5,7},{7,1},{8,10},{10,12},{12... | collective-permute-start | bytes 1179656 | tf_op jit(solution)/shard_map/ppermute | solution.py:443
  5.1 36.1 %collective-permute-start.4 = (bf16[3,512,128]{2,1,0:T(8,128)(2,1)}, bf16[3,512,128]{2,1,0:T(8,128)(2,1)S(1)}, u32[]{:S(2)}, u32[]{:S(2)}) collective-permute-start(bf16[3,512,128]{2,1,0:T(8,128)(2,1)} %get-tuple-element.32.refs_4_), channel_id=1, source_target_pairs={{0,4},{2,6},{4,0},{6,2},{1,5},{3,7},{5,1},{7,3},{8,12},{10,14},{12... | collective-permute-start | bytes 1179656 | tf_op jit(solution)/shard_map/ppermute | solution.py:443
  8.0 17.6 %collective-permute-start.5 = (bf16[3,512,128]{2,1,0:T(8,128)(2,1)}, bf16[3,512,128]{2,1,0:T(8,128)(2,1)S(1)}, u32[]{:S(2)}, u32[]{:S(2)}) collective-permute-start(bf16[3,512,128]{2,1,0:T(8,128)(2,1)} %get-tuple-element.32.refs_4_), channel_id=1, source_target_pairs={{0,6},{2,0},{4,2},{6,4},{1,7},{3,1},{5,3},{7,5},{8,14},{10,8},{12,... | collective-permute-start | bytes 1179656 | tf_op jit(solution)/shard_map/ppermute | solution.py:443
  14.2 5.0 %copy-start.6 = (bf16[3,512,128]{2,1,0:T(8,128)(2,1)}, bf16[3,512,128]{2,1,0:T(8,128)(2,1)S(1)}, u32[]{:S(2)}) copy-start(bf16[3,512,128]{2,1,0:T(8,128)(2,1)S(1)} %collective-permute-done.refs_2_) | copy-start | bytes 1179652
  14.2 6.5 %collective-permute-start.2 = (bf16[3,512,128]{2,1,0:T(8,128)(2,1)S(1)}, bf16[3,512,128]{2,1,0:T(8,128)(2,1)S(1)}, u32[]{:S(2)}, u32[]{:S(2)}) collective-permute-start(bf16[3,512,128]{2,1,0:T(8,128)(2,1)S(1)} %collective-permute-done.refs_2_), channel_id=1, source_target_pairs={{0,1},{1,0},{2,3},{3,2},{4,5},{5,4},{6,7},{7,6},{8,9},{9,8},{10,11... | collective-permute-start | bytes 1179656 | tf_op jit(solution)/shard_map/ppermute | solution.py:447
  20.6 4.9 %copy-start.12 = (bf16[3,512,128]{2,1,0:T(8,128)(2,1)}, bf16[3,512,128]{2,1,0:T(8,128)(2,1)S(1)}, u32[]{:S(2)}) copy-start(bf16[3,512,128]{2,1,0:T(8,128)(2,1)S(1)} %collective-permute-done.2.refs_3_) | copy-start | bytes 1179652
  20.6 4.9 %copy-start.7 = (bf16[3,512,128]{2,1,0:T(8,128)(2,1)}, bf16[3,512,128]{2,1,0:T(8,128)(2,1)S(1)}, u32[]{:S(2)}) copy-start(bf16[3,512,128]{2,1,0:T(8,128)(2,1)S(1)} %collective-permute-done.1.refs_1_) | copy-start | bytes 1179652
  20.7 4.9 %copy-start.9 = (bf16[3,512,128]{2,1,0:T(8,128)(2,1)}, bf16[3,512,128]{2,1,0:T(8,128)(2,1)S(1)}, u32[]{:S(2)}) copy-start(bf16[3,512,128]{2,1,0:T(8,128)(2,1)S(1)} %collective-permute-done.3.refs_5_) | copy-start | bytes 1179652
  25.6 0.8 copy-start.11
  41.2 0.8 copy-start.10
  99.7 1.5 copy-start.2
  99.7 3.7 %copy-start.5 = (bf16[3,2,512,128]{3,2,1,0:T(8,128)(2,1)S(1)}, bf16[3,2,512,128]{3,2,1,0:T(8,128)(2,1)}, u32[]{:S(2)}) copy-start(bf16[3,2,512,128]{3,2,1,0:T(8,128)(2,1)} %get-tuple-element.37.refs_4_) | copy-start | bytes 2359300
  99.7 12.2 %copy-start.17 = (bf16[192,512]{1,0:T(8,128)(2,1)S(1)}, bf16[192,512]{1,0:T(8,128)(2,1)}, u32[]{:S(2)}) copy-start(bf16[192,512]{1,0:T(8,128)(2,1)} %get-tuple-element.34) | copy-start | bytes 589828
  99.7 14.1 %copy-start.16 = (bf16[192,512]{1,0:T(8,128)(2,1)S(1)}, bf16[192,512]{1,0:T(8,128)(2,1)}, u32[]{:S(2)}) copy-start(bf16[192,512]{1,0:T(8,128)(2,1)} %get-tuple-element.35) | copy-start | bytes 589828
  99.7 14.9 %copy-start.15 = (bf16[192,512]{1,0:T(8,128)(2,1)S(1)}, bf16[192,512]{1,0:T(8,128)(2,1)}, u32[]{:S(2)}) copy-start(bf16[192,512]{1,0:T(8,128)(2,1)} %get-tuple-element.36) | copy-start | bytes 589828
  101.1 22.3 %slice-start = ((bf16[3,16,16,384]{3,2,1,0:T(8,128)(2,1)}), bf16[2,16,16,384]{3,2,1,0:T(8,128)(2,1)S(1)}, s32[]{:S(2)}) async-start(bf16[3,16,16,384]{3,2,1,0:T(8,128)(2,1)} %param.5), calls=%async_computation.1 | async-start | bytes 786432 | tf_op jit(solution)/shard_map/slice | solution.py:502
  101.1 2.4 %collective-permute-start.9 = (bf16[3,2,512,128]{3,2,0,1:T(8,128)(2,1)S(1)}, bf16[3,2,512,128]{3,2,0,1:T(8,128)(2,1)S(1)}, u32[]{:S(2)}, u32[]{:S(2)}) collective-permute-start(bf16[3,2,512,128]{3,2,0,1:T(8,128)(2,1)S(1)} %copy.11), channel_id=1, source_target_pairs={{0,1},{1,0},{2,3},{3,2},{4,5},{5,4},{6,7},{7,6},{8,9},{9,8},{10,11... | collective-permute-start | bytes 2359304 | tf_op jit(solution)/shard_map/ppermute | solution.py:447
  101.2 13.4 %collective-permute-start.12 = (bf16[2,8,16,384]{3,2,1,0:T(8,128)(2,1)S(1)}, bf16[2,8,16,384]{3,2,1,0:T(8,128)(2,1)S(1)}, u32[]{:S(2)}, u32[]{:S(2)}) collective-permute-start(bf16[2,8,16,384]{3,2,1,0:T(8,128)(2,1)S(1)} %get-tuple-element.54), channel_id=1, source_target_pairs={{16,0},{32,16},{48,32},{64,48},{80,64},{96,80},{112,96},{17,1},{33... | collective-permute-start | bytes 589832 | tf_op jit(solution)/shard_map/ppermute | solution.py:454
  103.6 22.1 %collective-permute-start.10 = (bf16[3,512,128]{2,1,0:T(8,128)(2,1)S(1)}, bf16[3,512,128]{2,1,0:T(8,128)(2,1)S(1)}, u32[]{:S(2)}, u32[]{:S(2)}) collective-permute-start(bf16[3,512,128]{2,1,0:T(8,128)(2,1)S(1)} %fusion), channel_id=1, source_target_pairs={{0,8},{8,0},{1,9},{9,1},{2,10},{10,2},{3,11},{11,3},{4,12},{12,4},... | collective-permute-start | bytes 1179656 | tf_op jit(solution)/shard_map/ppermute | solution.py:447
  105.3 18.1 %collective-permute-start.11 = (bf16[2,8,16,384]{3,2,1,0:T(8,128)(2,1)S(1)}, bf16[2,8,16,384]{3,2,1,0:T(8,128)(2,1)S(1)}, u32[]{:S(2)}, u32[]{:S(2)}) collective-permute-start(bf16[2,8,16,384]{3,2,1,0:T(8,128)(2,1)S(1)} %get-tuple-element.53), channel_id=1, source_target_pairs={{0,16},{16,32},{32,48},{48,64},{64,80},{80,96},{96,112},{1,17},{17... | collective-permute-start | bytes 589832 | tf_op jit(solution)/shard_map/ppermute | solution.py:454
  111.9 12.6 %collective-permute-start.6 = (bf16[192,512]{1,0:T(8,128)(2,1)S(1)}, bf16[192,512]{1,0:T(8,128)(2,1)S(1)}, u32[]{:S(2)}, u32[]{:S(2)}) collective-permute-start(bf16[192,512]{1,0:T(8,128)(2,1)S(1)} %copy-done.17), channel_id=1, source_target_pairs={{0,6},{2,0},{4,2},{6,4},{1,7},{3,1},{5,3},{7,5},{8,14},{10,8},{12,... | collective-permute-start | bytes 589832 | tf_op jit(solution)/shard_map/ppermute | solution.py:443
  113.8 10.7 %collective-permute-start.7 = (bf16[192,512]{1,0:T(8,128)(2,1)S(1)}, bf16[192,512]{1,0:T(8,128)(2,1)S(1)}, u32[]{:S(2)}, u32[]{:S(2)}) collective-permute-start(bf16[192,512]{1,0:T(8,128)(2,1)S(1)} %copy-done.16), channel_id=1, source_target_pairs={{0,4},{2,6},{4,0},{6,2},{1,5},{3,7},{5,1},{7,3},{8,12},{10,14},{12... | collective-permute-start | bytes 589832 | tf_op jit(solution)/shard_map/ppermute | solution.py:443
  114.7 11.0 %collective-permute-start.8 = (bf16[192,512]{1,0:T(8,128)(2,1)S(1)}, bf16[192,512]{1,0:T(8,128)(2,1)S(1)}, u32[]{:S(2)}, u32[]{:S(2)}) collective-permute-start(bf16[192,512]{1,0:T(8,128)(2,1)S(1)} %copy-done.15), channel_id=1, source_target_pairs={{0,2},{2,4},{4,6},{6,0},{1,3},{3,5},{5,7},{7,1},{8,10},{10,12},{12... | collective-permute-start | bytes 589832 | tf_op jit(solution)/shard_map/ppermute | solution.py:443
  123.5 19.8 %copy-start.1 = (bf16[2,32,16,384]{3,2,1,0:T(8,128)(2,1)}, bf16[2,32,16,384]{3,2,1,0:T(8,128)(2,1)S(1)}, u32[]{:S(2)}) copy-start(bf16[2,32,16,384]{3,2,1,0:T(8,128)(2,1)S(1)} %pad_maximum_fusion) | copy-start | bytes 2359300
  124.5 1.2 copy-start.18
  124.5 1.2 copy-start.19
  125.7 0.7 copy-start.20
  126.4 0.8 copy-start.8
  135.0 30.8 %all-to-all-start = ((bf16[8,64,1536]{2,1,0:T(8,128)(2,1)}), bf16[8,64,1536]{2,1,0:T(8,128)(2,1)}, u32[]{:S(2)}, u32[]{:S(2)}) async-start(bf16[8,64,1536]{2,1,0:T(8,128)(2,1)} %project.1), calls=%async_computation | async-start | bytes 3145728 | tf_op jit(solution)/shard_map/all_to_all | solution.py:524
  143.4 24.8 %collective-permute-start.13 = (bf16[2,32,8,384]{3,2,1,0:T(8,128)(2,1)S(1)}, bf16[2,32,8,384]{3,2,1,0:T(8,128)(2,1)S(1)}, u32[]{:S(2)}, u32[]{:S(2)}) collective-permute-start(bf16[2,32,8,384]{3,2,1,0:T(8,128)(2,1)S(1)} %get-tuple-element.52), channel_id=1, source_target_pairs={{0,1},{1,2},{2,3},{3,4},{4,5},{5,6},{6,7},{7,8},{8,9},{9,10},{10,1... | collective-permute-start | bytes 1179656 | tf_op jit(solution)/shard_map/ppermute | solution.py:454
  145.3 22.9 %collective-permute-start.14 = (bf16[2,32,8,384]{3,2,1,0:T(8,128)(2,1)S(1)}, bf16[2,32,8,384]{3,2,1,0:T(8,128)(2,1)S(1)}, u32[]{:S(2)}, u32[]{:S(2)}) collective-permute-start(bf16[2,32,8,384]{3,2,1,0:T(8,128)(2,1)S(1)} %get-tuple-element.51), channel_id=1, source_target_pairs={{1,0},{2,1},{3,2},{4,3},{5,4},{6,5},{7,6},{8,7},{9,8},{10,9},{11,1... | collective-permute-start | bytes 1179656 | tf_op jit(solution)/shard_map/ppermute | solution.py:454
  168.2 0.8 copy-start.13
  168.2 0.9 copy-start.14
  178.7 3.0 %collective-permute-start.15 = (bf16[256,768]{1,0:T(8,128)(2,1)}, bf16[256,768]{1,0:T(8,128)(2,1)S(1)}, u32[]{:S(2)}, u32[]{:S(2)}) collective-permute-start(bf16[256,768]{1,0:T(8,128)(2,1)} %get-tuple-element.44), channel_id=1, source_target_pairs={{0,1},{1,0},{2,3},{3,2},{4,5},{5,4},{6,7},{7,6},{8,9},{9,8},{10,11... | collective-permute-start | bytes 1179656 | tf_op jit(solution)/shard_map/ppermute | solution.py:461
  178.7 11.5 %collective-permute-start.16 = (bf16[256,768]{1,0:T(8,128)(2,1)}, bf16[256,768]{1,0:T(8,128)(2,1)S(1)}, u32[]{:S(2)}, u32[]{:S(2)}) collective-permute-start(bf16[256,768]{1,0:T(8,128)(2,1)} %get-tuple-element.45), channel_id=1, source_target_pairs={{1,2},{2,1},{3,4},{4,3},{5,6},{6,5},{7,8},{8,7},{9,10},{10,9},{11,... | collective-permute-start | bytes 1179656 | tf_op jit(solution)/shard_map/ppermute | solution.py:461
  181.7 8.5 %copy-start.3 = (bf16[256,768]{1,0:T(8,128)(2,1)}, bf16[256,768]{1,0:T(8,128)(2,1)S(1)}, u32[]{:S(2)}) copy-start(bf16[256,768]{1,0:T(8,128)(2,1)S(1)} %collective-permute-done.15.inner_ref) | copy-start | bytes 1179652
  190.2 0.7 copy-start.4
  193.7 9.5 %collective-permute-start.17 = (bf16[128,768]{1,0:T(8,128)(2,1)}, bf16[128,768]{1,0:T(8,128)(2,1)S(1)}, u32[]{:S(2)}, u32[]{:S(2)}) collective-permute-start(bf16[128,768]{1,0:T(8,128)(2,1)} %get-tuple-element.47), channel_id=1, source_target_pairs={{0,16},{16,0},{32,48},{48,32},{64,80},{80,64},{96,112},{112,96},{1... | collective-permute-start | bytes 589832 | tf_op jit(solution)/shard_map/ppermute | solution.py:461
  195.3 10.2 %collective-permute-start.18 = (bf16[128,768]{1,0:T(8,128)(2,1)}, bf16[128,768]{1,0:T(8,128)(2,1)S(1)}, u32[]{:S(2)}, u32[]{:S(2)}) collective-permute-start(bf16[128,768]{1,0:T(8,128)(2,1)} %get-tuple-element.48), channel_id=1, source_target_pairs={{16,32},{32,16},{48,64},{64,48},{80,96},{96,80},{17,33},{33,17},{4... | collective-permute-start | bytes 589832 | tf_op jit(solution)/shard_map/ppermute | solution.py:461
  203.1 2.3 %copy-start.21 = (bf16[128,768]{1,0:T(8,128)(2,1)}, bf16[128,768]{1,0:T(8,128)(2,1)S(1)}, u32[]{:S(2)}) copy-start(bf16[128,768]{1,0:T(8,128)(2,1)S(1)} %collective-permute-done.17.inner_ref) | copy-start | bytes 589828
  205.4 0.7 copy-start.22

commit v3 on v2

--- a/solution.py
+++ b/solution.py
@@ -58,8 +58,7 @@
 
 
 def own_block(step, tokens):
-    count = lax.axis_size("y")
-    owner = (lax.axis_index("y") + count - step) % count
+    owner = lax.axis_index("y") ^ step
     return pl.ds(pl.multiple_of(owner * tokens, tokens), tokens)
 
 
@@ -124,13 +123,15 @@
 def coarse_grads(key_values, query_ups, stats):
     heads, tokens, _ = key_values[0].shape
     blocks = len(query_ups)
-    parts = stats.shape[0]
+    parts = len(stats)
 
     def body(*refs):
         kv_refs, qu_refs = refs[:blocks], refs[blocks : 2 * blocks]
-        stats_ref, kept_ref, sent_ref = refs[2 * blocks : 2 * blocks + 3]
+        stats_refs = refs[2 * blocks : 2 * blocks + parts]
+        kept_ref, sent_ref = refs[2 * blocks + parts : 2 * blocks + parts + 2]
         q_outs = refs[-blocks - 2 : -2]
         acc, held = refs[-2:]
+        step = pl.program_id(1)
         for at in range(blocks):
 
             @pl.when(pl.program_id(1) == at)
@@ -143,7 +144,7 @@
 
         query = half(held[...], 0) * BF16(SCALE)
         upstream = half(held[...], 1)
-        found = [stats_ref[i, 0, :, own_block(pl.program_id(1), tokens)] for i in range(parts)]
+        found = [ref[0, :, own_block(step, tokens)] for ref in stats_refs]
         peak = found[0][:1]
         for part in found[1:]:
             peak = jnp.maximum(peak, part[:1])
@@ -168,18 +169,18 @@
         @pl.when(pl.program_id(1) == blocks - 1)
         def _():
             for i in range(blocks // 2):
-                kept_ref[0, i] = acc[2 * i].astype(BF16)
-                sent_ref[0, i] = acc[2 * i + 1].astype(BF16)
+                kept_ref[i, 0] = acc[2 * i].astype(BF16)
+                sent_ref[i, 0] = acc[2 * i + 1].astype(BF16)
 
     pairs = heads * (blocks * tokens) ** 2
-    out_shape = [jax.ShapeDtypeStruct((heads, blocks // 2, tokens, 128), BF16)] * 2
+    out_shape = [jax.ShapeDtypeStruct((blocks // 2, heads, tokens, 128), BF16)] * 2
     out_shape += [jax.ShapeDtypeStruct((heads * HD, tokens), BF16)] * blocks
     return pl.pallas_call(
         body,
         grid=(heads, blocks),
         in_specs=[pl.BlockSpec((1, tokens, 128), lambda h, q: (h, 0, 0))] * (2 * blocks)
-        + [pl.BlockSpec((parts, 1, 2, blocks * tokens), lambda h, q: (0, h, 0, 0))],
-        out_specs=[pl.BlockSpec((1, blocks // 2, tokens, 128), lambda h, q: (h, 0, 0, 0))] * 2
+        + [pl.BlockSpec((1, 2, blocks * tokens), lambda h, q: (h, 0, 0))] * parts,
+        out_specs=[pl.BlockSpec((blocks // 2, 1, tokens, 128), lambda h, q: (0, h, 0, 0))] * 2
         + [pl.BlockSpec((HD, tokens), lambda h, q: (h, 0))] * blocks,
         out_shape=out_shape,
         scratch_shapes=[
@@ -189,7 +190,7 @@
         name="coarse_grads",
         cost_estimate=cost(10 * pairs * 256, 4 << 20, pairs),
         compiler_params=pltpu.CompilerParams(vmem_limit_bytes=VMEM),
-    )(*key_values, *query_ups, stats)
+    )(*key_values, *query_ups, *stats)
 
 
 def whole_call(body, out_shape, name, flops, scratch, *operands):
@@ -353,65 +354,91 @@
 
 def project(query_pieces, kept, from_core, arrived, joint, columns, count):
     group, tokens = query_pieces[0].shape
-    heads = kept.shape[0]
+    heads = arrived.shape[0]
     rows = tokens // columns
     each = rows // count
     size = each * columns
-    wide = joint.shape[2]
+    wide = joint.shape[1]
+    first = count // 2
     operands = (*query_pieces, kept, from_core, arrived, joint)
-
-    def body(*refs):
+    params = pltpu.CompilerParams(vmem_limit_bytes=VMEM)
+
+    def whole(array):
+        return pl.BlockSpec(array.shape, lambda d: (0,) * array.ndim)
+
+    def pack(*refs):
         pieces = refs[: len(query_pieces)]
-        kept_ref, core_ref, arrived_ref, joint_ref, out, held, weight = refs[len(query_pieces) :]
+        kept_ref, core_ref, arrived_ref, joint_ref = refs[len(query_pieces) :][:4]
+        outs, packed, held = refs[len(operands) : -2], refs[-2], refs[-1]
 
         @pl.when(pl.program_id(0) == 0)
         def _():
             for head in range(heads):
-                total = kept_ref[head, 0].astype(F32) + core_ref[head, 0].astype(F32)
-                held[:, head * 128 : head * 128 + 128] = total + arrived_ref[head].astype(F32)
+                total = kept_ref[0, head].astype(F32) + core_ref[0, head].astype(F32)
+                total += arrived_ref[head].astype(F32)
                 for part in range(2):
-                    at = head * 128 + part * HD
-                    weight[at : at + HD, :] = joint_ref[1 + part, head * HD : head * HD + HD, :]
-            weight[2 * group :, :] = joint_ref[0]
+                    at = (1 + part) * group + head * HD
+                    held[:, at : at + HD] = total[:, part * HD : (part + 1) * HD]
             total = pieces[0][...].astype(F32)
             for piece in pieces[1:]:
                 total += piece[...].astype(F32)
-            held[:, 2 * group :] = total.T
-
-        taken = []
-        for c in range(columns):
-            start = pl.multiple_of(c * rows + pl.program_id(0) * each, each)
-            taken.append(held[pl.ds(start, each), :])
-        chosen = jnp.concatenate(taken, axis=0).astype(BF16)
-        out[0] = nn(chosen, weight[...]).astype(BF16)
-
-    return pl.pallas_call(
-        body,
-        grid=(count,),
-        in_specs=[
-            pl.BlockSpec(array.shape, lambda d, rank=array.ndim: (0,) * rank)
-            for array in operands
-        ],
-        out_specs=pl.BlockSpec((1, size, wide), lambda d: (d, 0, 0)),
-        out_shape=jax.ShapeDtypeStruct((count, size, wide), BF16),
-        scratch_shapes=[
-            pltpu.VMEM((tokens, 3 * group), F32),
-            pltpu.VMEM((3 * group, wide), BF16),
-        ],
+            held[:, :group] = total.T
+            for step in range(count):
+                target = lax.axis_index(ROW) ^ (count - 1 - step)
+                taken = []
+                for c in range(columns):
+                    start = pl.multiple_of(c * rows + target * each, each)
+                    taken.append(held[pl.ds(start, each), :])
+                packed[step] = jnp.concatenate(taken, axis=0).astype(BF16)
+
+        for step, out in enumerate(outs):
+
+            @pl.when(pl.program_id(0) == step)
+            def _():
+                out[...] = nn(packed[step], joint_ref[...]).astype(BF16)
+
+    def rest(packed, joint_ref, *outs):
+        for step, out in enumerate(outs):
+
+            @pl.when(pl.program_id(0) == step)
+            def _():
+                out[...] = nn(packed[first + step], joint_ref[...]).astype(BF16)
+
+    piece = jax.ShapeDtypeStruct((size, wide), BF16)
+    packed = jax.ShapeDtypeStruct((count, size, 3 * group), BF16)
+    early = pl.pallas_call(
+        pack,
+        grid=(first,),
+        in_specs=[whole(array) for array in operands],
+        out_specs=[whole(piece)] * first + [whole(packed)],
+        out_shape=[piece] * first + [packed],
+        scratch_shapes=[pltpu.VMEM((tokens, 3 * group), F32)],
         name="project",
-        cost_estimate=cost(2 << 30, 6 << 20, 0),
-        compiler_params=pltpu.CompilerParams(vmem_limit_bytes=VMEM),
+        cost_estimate=cost(1 << 30, 6 << 20, 0),
+        compiler_params=params,
     )(*operands)
+    late = pl.pallas_call(
+        rest,
+        grid=(count - first,),
+        in_specs=[whole(packed), whole(joint)],
+        out_specs=[whole(piece)] * (count - first),
+        out_shape=[piece] * (count - first),
+        name="project_rest",
+        cost_estimate=cost(1 << 30, 3 << 20, 0),
+        compiler_params=params,
+    )(early[-1], joint)
+    return [*early[:-1], *late]
 
 
 def spread(pieces, columns):
-    count, tokens, wide = pieces.shape
+    tokens, wide = pieces[0].shape
     width = wide // 4
 
-    def body(in_ref, out):
-        total = in_ref[0].astype(F32)
-        for at in range(1, count):
-            total += in_ref[at].astype(F32)
+    def body(*refs):
+        out = refs[-1]
+        total = refs[0][...].astype(F32)
+        for ref in refs[1:-1]:
+            total += ref[...].astype(F32)
         total = total.astype(BF16)
         cells = 2 * tokens
         fine = lax.broadcasted_iota(jnp.int32, (cells, tokens), 0)
@@ -434,49 +461,38 @@
         "spread",
         1 << 28,
         [],
-        pieces,
-    )
-
-
-def shifted(array, axis, step):
-    count = lax.axis_size(axis)
-    return lax.ppermute(array, axis, [(i, (i + step) % count) for i in range(count)])
-
-
-def swapped(array, axis):
-    return lax.ppermute(array, axis, [(0, 1), (1, 0)])
-
-
-def onward(low, high, axis):
-    count = lax.axis_size(axis)
-    forward = [(i, i + 1) for i in range(count - 1)]
-    backward = [(i + 1, i) for i in range(count - 1)]
-    return lax.ppermute(low, axis, forward), lax.ppermute(high, axis, backward)
+        *pieces,
+    )
+
+
+def swapped(array, axis, flip=1):
+    return lax.ppermute(array, axis, [(i, i ^ flip) for i in range(lax.axis_size(axis))])
 
 
 def exchanged(inner, outer, axis):
     count = lax.axis_size(axis)
-    beside = [(i, i ^ 1) for i in range(count)]
     beyond = [(i, ((i + 1) ^ 1) - 1) for i in range(1, count - 1)]
-    return lax.ppermute(inner, axis, beside), lax.ppermute(outer, axis, beyond)
-
-
-def edges(block, axis, at):
+    return swapped(inner, axis), lax.ppermute(outer, axis, beyond)
+
+
+def rims(block, axis, parity, at):
     size = block.shape[at]
-    return onward(
-        lax.slice_in_dim(block, size - RIM, None, axis=at),
-        lax.slice_in_dim(block, 0, RIM, axis=at),
-        axis,
-    )
+    low = lax.slice_in_dim(block, 0, RIM, axis=at)
+    high = lax.slice_in_dim(block, size - RIM, None, axis=at)
+    first = lax.axis_index(parity) == 0
+    inner, outer = exchanged(
+        jnp.where(first, high, low), jnp.where(first, low, high), axis
+    )
+    return jnp.where(first, outer, inner), jnp.where(first, inner, outer)
 
 
 def with_rows(block, dim):
-    low, high = edges(block, ROW, dim)
+    low, high = rims(block, ROW, "zh", dim)
     return jnp.concatenate([low, block, high], axis=dim)
 
 
 def with_columns(block, dim):
-    low, high = edges(block, COL, dim + 1)
+    low, high = rims(block, COL, "c", dim + 1)
     shape = block.shape[:dim] + (-1, block.shape[-1])
     return block.reshape(shape), low.reshape(shape), high.reshape(shape)
 
@@ -486,43 +502,46 @@
     own = rows * columns
     coarse_columns, coarse_rows, group = grad_coarse.shape
     tokens = coarse_columns * coarse_rows
+    wide = merge_weight.shape[0]
 
     key_value, query_up = prepare(
         coarse_qkv.reshape(3, tokens, group), grad_coarse.reshape(tokens, group)
     )
     across = swapped(key_value, "zl")
     beside = swapped(key_value, "c")
-    queries = [query_up] + [shifted(query_up, "y", step) for step in (1, 2, 3)]
+    queries = [query_up] + [swapped(query_up, "y", step) for step in (1, 2, 3)]
     across, merge_weight, fine_qkv = lax.optimization_barrier((across, merge_weight, fine_qkv))
     corner = swapped(across, "c")
     joint = lax.dot_general(
         qkv_weight, merge_weight, (((1,), (1,)), ((), ())), preferred_element_type=F32
-    ).astype(BF16)
+    ).astype(BF16).reshape(3 * group, wide)
     own_qkv = fine_qkv.reshape(3, own, width)
     tall = with_rows(fine_qkv[1:], 1)
-    corner, joint = lax.optimization_barrier((corner, joint))
+    corner, joint, tall = lax.optimization_barrier((corner, joint, tall))
     keys = [key_value, beside, across, corner]
 
     near = [0, 1, 3]
     part = coarse_stats(keys, [queries[i] for i in near], near, (), 256)
     part = coarse_stats(keys, [queries[2]], [2], (part,), 256)
-    stats = lax.all_gather(part, "y", axis=0)
+    stats = [part] + [swapped(part, "y", step) for step in (1, 2, 3)]
     kept, sent, *query_grads = coarse_grads(keys, queries, stats)
 
     from_core = swapped(sent, "c")
+    passed = (kept[1].astype(F32) + from_core[1].astype(F32)).astype(BF16)
+    arrived = swapped(passed, "zl")
     query_pieces = [query_grads[0]]
     for step in (1, 2, 3):
-        query_pieces.append(shifted(query_grads[step], "y", -step))
-    passed = (kept[:, 1].astype(F32) + from_core[:, 1].astype(F32)).astype(BF16)
-    arrived = swapped(passed, "zl")
+        query_pieces.append(swapped(query_grads[step], "y", step))
     count = lax.axis_size(ROW)
     projected = project(
         query_pieces, kept, from_core, arrived, joint, coarse_columns, count
     )
-    projected, tall = lax.optimization_barrier((projected, tall))
+    pieces = [
+        swapped(piece, ROW, count - 1 - step) for step, piece in enumerate(projected[:-1])
+    ]
+    kept_piece, tall = lax.optimization_barrier((projected[-1], tall))
     ext_kv = with_columns(tall, 1)
-    pieces = lax.all_to_all(projected, ROW, 0, 0)
-    own_up = spread(pieces, coarse_columns)
+    own_up = spread([kept_piece, *pieces], coarse_columns)
 
     grad_query, mid, inner, outer = fine_grads(own_qkv, ext_kv, own_up, rows, columns)
     inner, outer = exchanged(inner, outer, COL)

time: 210 us -> 212 us (level)
  blocking collectives: 13.9 us -> 0 us
  waiting for transfers between devices: 49.5 us -> 56.3 us
  other arithmetic: 1.68 us -> 5.97 us
  local copies, waits for them, and re-layouts: 7.75 us -> 3.97 us
  starting transfers between devices: 43.7 us -> 47.2 us
  Pallas kernels: 85.9 us -> 88.9 us
    ppermute x19 -> x29, waiting for transfers between devices: 34.8 us -> 56.3 us  [the longest x25 40.9 us: swapped(): lax.ppermute(array, axis, [(i, i ^ flip) for i in range(lax.axis_size(axi...]
    all_to_all x1 -> x0, waiting for transfers between devices: 14.7 us -> none  [shards(): pieces = lax.all_to_all(projected, ROW, 0, 0)]
    all_gather x1 -> x0, blocking collectives: 13.9 us -> none  [shards(): stats = lax.all_gather(part, 'y', axis=0)]
    ppermute x19 -> x29, starting transfers between devices: 35.4 us -> 47.2 us  [the longest x25 34.1 us: swapped(): lax.ppermute(array, axis, [(i, i ^ flip) for i in range(lax.axis_size(axi...]
    all_to_all x1 -> x0, starting transfers between devices: 8.31 us -> none  [shards(): pieces = lax.all_to_all(projected, ROW, 0, 0)]
    pallas_call x1 -> x2, Pallas kernels: 7.84 us -> 10.5 us  [the longest x1 6 us: project(): pl.pallas_call(pack, grid=(first,), in_specs=[whole(array) for array in o...]
    unnamed x46 -> x44, local copies, waits for them, and re-layouts: 5.29 us -> 3.96 us
  transfers between devices with their start and end apart: 20 -> 29, of which waited for: 8 -> 16; matrix products, arithmetic and copies ran while one was open for 4% -> 3% of each run, Pallas kernels for 8% -> 8%
where the time goes in v3:
time: 212 us; the launch traced here: 208 us
  Pallas kernels  88.9 us (42%)
  waiting for transfers between devices  56.3 us (27%)
  starting transfers between devices  47.2 us (22%)
  other arithmetic  5.97 us (3%)
  matrix products  4.83 us (2%)
  local copies, waits for them, and re-layouts  3.97 us (2%)
    ppermute x25, waiting for transfers between devices, swapped(): lax.ppermute(array, axis, [(i, i ^ flip) for i in range(lax.axis_size(axi...  40.9 us
    pallas_call x1, Pallas kernels, coarse_grads(): pl.pallas_call(body, grid=(heads, blocks), in_specs=[pl.BlockSpec((1, tok...  37.2 us
    ppermute x25, starting transfers between devices, swapped(): lax.ppermute(array, axis, [(i, i ^ flip) for i in range(lax.axis_size(axi...  34.1 us
    pallas_call x2, Pallas kernels, coarse_stats(): pl.pallas_call(body, grid=(heads, number), in_specs=[pl.BlockSpec((1, tok...  21.8 us
    pallas_call x5, Pallas kernels, whole_call(): pl.pallas_call(body, out_shape=out_shape, scratch_shapes=scratch, name=na...  19.4 us
    ppermute x4, waiting for transfers between devices, exchanged(): return (swapped(inner, axis), lax.ppermute(outer, axis, beyond))  15.5 us
    ppermute x4, starting transfers between devices, exchanged(): return (swapped(inner, axis), lax.ppermute(outer, axis, beyond))  13.1 us
    pallas_call x1, Pallas kernels, project(): pl.pallas_call(pack, grid=(first,), in_specs=[whole(array) for array in o...  6 us
  transfers between devices with their start and end apart: 29, of which 16 were waited for; matrix products, arithmetic and copies ran while one was open for 3% of the time, Pallas kernels for 8%

profile of v3, /device:TPU:96, one launch (start us, length us, event | category | flops | bytes accessed | tf_op | source)
XLA Modules:
  0.0 208.1 jit_solution(8424531907663613109)
XLA Ops:
  0.6 0.0 copy-start
  0.6 2.5 %prepare.1 = (bf16[3,512,128]{2,1,0:T(8,128)(2,1)}, bf16[3,512,128]{2,1,0:T(8,128)(2,1)}) custom-call(bf16[3,512,192]{2,1,0:T(8,128)(2,1)} %bitcast.28, bf16[512,192]{1,0:T(8,128)(2,1)} %bitcast.29), custom_call_target="tpu_custom_call" | custom-call | flops 1048576 | bytes 6291456 | tf_op jit(solution)/shard_map/prepare/pallas_call | solution.py:197
  3.1 0.4 collective-permute-start
  3.5 10.7 %collective-permute-done.refs_2_ = bf16[3,512,128]{2,1,0:T(8,128)(2,1)S(1)} collective-permute-done((bf16[3,512,128]{2,1,0:T(8,128)(2,1)}, bf16[3,512,128]{2,1,0:T(8,128)(2,1)S(1)}, u32[]{:S(2)}, u32[]{:S(2)}) %collective-permute-start) | collective-permute-done | bytes 393248 | tf_op jit(solution)/shard_map/ppermute | solution.py:469
  14.2 1.2 broadcast_select_fusion.5
  15.4 3.4 %collective-permute-start.3 = (bf16[2,8,16,384]{3,2,1,0:T(8,128)(2,1)S(1)}, bf16[2,8,16,384]{3,2,1,0:T(8,128)(2,1)S(1)}, u32[]{:S(2)}, u32[]{:S(2)}) collective-permute-start(bf16[2,8,16,384]{3,2,1,0:T(8,128)(2,1)S(1)} %get-tuple-element.75), channel_id=1, source_target_pairs={{16,32},{32,16},{48,64},{64,48},{80,96},{96,80},{17,33},{33,17},{4... | collective-permute-start | bytes 589832 | tf_op jit(solution)/shard_map/ppermute | solution.py:475
  18.8 0.1 collective-permute-start.1
  18.9 1.7 collective-permute-start.5
  20.5 2.2 %collective-permute-start.7 = (bf16[3,512,128]{2,1,0:T(8,128)(2,1)}, bf16[3,512,128]{2,1,0:T(8,128)(2,1)}, u32[]{:S(2)}, u32[]{:S(2)}) collective-permute-start(bf16[3,512,128]{2,1,0:T(8,128)(2,1)} %get-tuple-element.42.refs_4_), channel_id=1, source_target_pairs={{0,6},{2,4},{4,2},{6,0},{1,7},{3,5},{5,3},{7,1},{8,14},{10,12},{12... | collective-permute-start | bytes 1179656 | tf_op jit(solution)/shard_map/ppermute | solution.py:469
  22.7 2.7 %collective-permute-done.3 = bf16[2,8,16,384]{3,2,1,0:T(8,128)(2,1)S(1)} collective-permute-done((bf16[2,8,16,384]{3,2,1,0:T(8,128)(2,1)S(1)}, bf16[2,8,16,384]{3,2,1,0:T(8,128)(2,1)S(1)}, u32[]{:S(2)}, u32[]{:S(2)}) %collective-permute-start.3) | collective-permute-done | bytes 196640 | tf_op jit(solution)/shard_map/ppermute | solution.py:475
  25.5 4.8 %fusion.1 = f32[1536,576]{0,1:S(1)} fusion(bf16[1536,1536]{1,0:T(8,128)(2,1)} %param.8, bf16[1536,576]{0,1:T(8,128)(2,1)S(1)} %bitcast.22), kind=kOutput, calls=%fused_computation.11 | convolution fusion | flops 2717908992 | bytes 10027008
  30.3 1.5 convert_element_type.20
  31.8 3.3 %collective-permute-start.6 = (bf16[3,512,128]{2,1,0:T(8,128)(2,1)S(1)}, bf16[3,512,128]{2,1,0:T(8,128)(2,1)}, u32[]{:S(2)}, u32[]{:S(2)}) collective-permute-start(bf16[3,512,128]{2,1,0:T(8,128)(2,1)S(1)} %copy-done.6), channel_id=1, source_target_pairs={{0,4},{2,6},{4,0},{6,2},{1,5},{3,7},{5,1},{7,3},{8,12},{10,14},{12... | collective-permute-start | bytes 1179656 | tf_op jit(solution)/shard_map/ppermute | solution.py:469
  35.1 0.1 pad_maximum_fusion
  35.3 0.8 copy-done.9
  36.1 0.7 copy-done.8
  36.8 14.8 %coarse_stats.2.refs_5_ = f32[3,2,2048]{2,1,0:T(2,128)} custom-call(bf16[3,512,128]{2,1,0:T(8,128)(2,1)} %get-tuple-element.37.refs_0_, bf16[3,512,128]{2,1,0:T(8,128)(2,1)} %copy-done.8, bf16[3,512,128]{2,1,0:T(8,128)(2,1)} %copy-done.7, bf16[3,512,128]{2,1,0:T(8,128)(2,1)} %copy-done.9, bf16[3,512,128]{2,1,0:T(8,128)(2,1)} %get-tuple-element.42.refs_4_, ...), custom_call_target="tpu_custom_call" | custom-call | flops 9663676416 | bytes 2097152 | tf_op jit(solution)/shard_map/coarse_stats/pallas_call | solution.py:109
  51.6 7.1 %coarse_stats.3.refs_8_ = f32[3,2,2048]{2,1,0:T(2,128)} custom-call(bf16[3,512,128]{2,1,0:T(8,128)(2,1)} %get-tuple-element.37.refs_0_, bf16[3,512,128]{2,1,0:T(8,128)(2,1)} %copy-done.8, bf16[3,512,128]{2,1,0:T(8,128)(2,1)} %copy-done.7, bf16[3,512,128]{2,1,0:T(8,128)(2,1)} %copy-done.9, bf16[3,512,128]{2,1,0:T(8,128)(2,1)} %collective-permute-done.6.refs_4_.refs_6_, ...), custom_call_target="tpu_custom_call" | custom-call | flops 3221225472 | bytes 2097152 | tf_op jit(solution)/shard_map/coarse_stats/pallas_call | solution.py:109
  58.6 1.0 collective-permute-start.10
  59.6 3.7 %collective-permute-start.9 = (f32[3,2,2048]{2,1,0:T(2,128)}, f32[3,2,2048]{2,1,0:T(2,128)S(1)}, u32[]{:S(2)}, u32[]{:S(2)}) collective-permute-start(f32[3,2,2048]{2,1,0:T(2,128)} %coarse_stats.3.refs_8_), channel_id=1, source_target_pairs={{0,4},{2,6},{4,0},{6,2},{1,5},{3,7},{5,1},{7,3},{8,12},{10,14},{12... | collective-permute-start | bytes 147464 | tf_op jit(solution)/shard_map/ppermute | solution.py:469
  63.3 0.8 collective-permute-done.10.refs_11_
  64.1 0.2 collective-permute-done.8.refs_9_
  64.4 1.8 collective-permute-done.9.refs_10_
  66.2 0.6 copy-done.21
  66.8 37.2 %coarse_grads.1 = (bf16[2,3,512,128]{3,2,1,0:T(8,128)(2,1)}, bf16[2,3,512,128]{3,2,1,0:T(8,128)(2,1)}, bf16[192,512]{1,0:T(8,128)(2,1)}, bf16[192,512]{1,0:T(8,1...) custom-call(bf16[3,512,128]{2,1,0:T(8,128)(2,1)} %get-tuple-element.37.refs_0_, ...), custom_call_target="tpu_custom_call" | custom-call | flops 32212254720 | bytes 4194304 | tf_op jit(solution)/shard_map/coarse_grads/pallas_call | solution.py:178
  104.0 0.1 collective-permute-start.14
  104.1 2.5 %collective-permute-done.14.refs_5_ = bf16[2,3,512,128]{3,2,1,0:T(8,128)(2,1)S(1)} collective-permute-done((bf16[2,3,512,128]{3,2,1,0:T(8,128)(2,1)}, bf16[2,3,512,128]{3,2,1,0:T(8,128)(2,1)S(1)}, u32[]{:S(2)}, u32[]{:S(2)}) %collective-permute-start.14) | collective-permute-done | bytes 786464 | tf_op jit(solution)/shard_map/ppermute | solution.py:469
  106.6 2.1 %fusion = bf16[3,512,128]{2,1,0:T(8,128)(2,1)} fusion(bf16[2,3,512,128]{3,2,1,0:T(8,128)(2,1)S(1)} %collective-permute-done.14.refs_5_, bf16[2,3,512,128]{3,2,1,0:T(8,128)(2,1)} %get-tuple-element.47.refs_4_), kind=kLoop, calls=%fused_computation.2 | loop fusion | flops 786432 | bytes 1179648 | tf_op jit(solution)/shard_map/convert_element_type | solution.py:530
  108.7 0.4 collective-permute-start.15
  109.1 1.3 collective-permute-start.11
  110.4 1.7 collective-permute-start.12
  112.1 1.7 collective-permute-start.13
  113.8 3.3 %collective-permute-done.11.refs_1_ = bf16[192,512]{1,0:T(8,128)(2,1)S(1)} collective-permute-done((bf16[192,512]{1,0:T(8,128)(2,1)}, bf16[192,512]{1,0:T(8,128)(2,1)S(1)}, u32[]{:S(2)}, u32[]{:S(2)}) %collective-permute-start.11) | collective-permute-done | bytes 196640 | tf_op jit(solution)/shard_map/ppermute | solution.py:469
  117.1 4.5 %collective-permute-done.12.refs_2_ = bf16[192,512]{1,0:T(8,128)(2,1)} collective-permute-done((bf16[192,512]{1,0:T(8,128)(2,1)}, bf16[192,512]{1,0:T(8,128)(2,1)}, u32[]{:S(2)}, u32[]{:S(2)}) %collective-permute-start.12) | collective-permute-done | bytes 196640 | tf_op jit(solution)/shard_map/ppermute | solution.py:469
  121.6 2.6 %collective-permute-done.13.refs_3_ = bf16[192,512]{1,0:T(8,128)(2,1)} collective-permute-done((bf16[192,512]{1,0:T(8,128)(2,1)}, bf16[192,512]{1,0:T(8,128)(2,1)}, u32[]{:S(2)}, u32[]{:S(2)}) %collective-permute-start.13) | collective-permute-done | bytes 196640 | tf_op jit(solution)/shard_map/ppermute | solution.py:469
  124.2 6.0 %project.1 = (bf16[64,1536]{1,0:T(8,128)(2,1)}, bf16[64,1536]{1,0:T(8,128)(2,1)}, bf16[64,1536]{1,0:T(8,128)(2,1)}, bf16[64,1536]{1,0:T(8,128)(2,1)}, bf16[8,64,576]{2,1,0:T(8,128)(2,1)}) custom-call(bf16[192,512]{1,0:T(8,128)(2,1)} %get-tuple-element.43.refs_0_, bf16[192,512]{1,0:T(8,128)(2,1)} %copy-done.5, ...), custom_call_target="tpu_custom_call" | custom-call | flops 1073741824 | bytes 6291456 | tf_op jit(solution)/shard_map/project/pallas_call | solution.py:409
  130.2 4.5 %project_rest.1 = (bf16[64,1536]{1,0:T(8,128)(2,1)}, bf16[64,1536]{1,0:T(8,128)(2,1)}, bf16[64,1536]{1,0:T(8,128)(2,1)}, bf16[64,1536]{1,0:T(8,128)(2,1)}) custom-call(bf16[8,64,576]{2,1,0:T(8,128)(2,1)} %get-tuple-element.50.packed, bf16[576,1536]{1,0:T(8,128)(2,1)} %bitcast.24), custom_call_target="tpu_custom_call" | custom-call | flops 1073741824 | bytes 3145728 | tf_op jit(solution)/shard_map/project_rest/pallas_call | solution.py:420
  134.7 1.5 collective-permute-start.22
  136.2 0.0 collective-permute-start.23
  136.2 3.5 %collective-permute-start.24 = (bf16[64,1536]{1,0:T(8,128)(2,1)}, bf16[64,1536]{1,0:T(8,128)(2,1)S(1)}, u32[]{:S(2)}, u32[]{:S(2)}) collective-permute-start(bf16[64,1536]{1,0:T(8,128)(2,1)} %get-tuple-element.61), channel_id=1, source_target_pairs={{0,16},{16,0},{32,48},{48,32},{64,80},{80,64},{96,112},{112,96},{1... | collective-permute-start | bytes 589832 | tf_op jit(solution)/shard_map/ppermute | solution.py:469
  139.7 2.7 %collective-permute-start.18 = (bf16[64,1536]{1,0:T(8,128)(2,1)}, bf16[64,1536]{1,0:T(8,128)(2,1)S(1)}, u32[]{:S(2)}, u32[]{:S(2)}) collective-permute-start(bf16[64,1536]{1,0:T(8,128)(2,1)} %get-tuple-element.55), channel_id=1, source_target_pairs={{0,112},{16,96},{32,80},{48,64},{64,48},{80,32},{96,16},{112,0},{1... | collective-permute-start | bytes 589832 | tf_op jit(solution)/shard_map/ppermute | solution.py:469
  142.4 0.1 broadcast_select_fusion
  142.5 1.9 collective-permute-start.16
  144.4 1.2 collective-permute-done.22.refs_5_
  145.7 2.0 collective-permute-start.19
  147.7 3.9 %collective-permute-done.24.refs_7_ = bf16[64,1536]{1,0:T(8,128)(2,1)S(1)} collective-permute-done((bf16[64,1536]{1,0:T(8,128)(2,1)}, bf16[64,1536]{1,0:T(8,128)(2,1)S(1)}, u32[]{:S(2)}, u32[]{:S(2)}) %collective-permute-start.24) | collective-permute-done | bytes 196640 | tf_op jit(solution)/shard_map/ppermute | solution.py:469
  151.6 3.4 %collective-permute-start.20 = (bf16[64,1536]{1,0:T(8,128)(2,1)}, bf16[64,1536]{1,0:T(8,128)(2,1)S(1)}, u32[]{:S(2)}, u32[]{:S(2)}) collective-permute-start(bf16[64,1536]{1,0:T(8,128)(2,1)} %get-tuple-element.57), channel_id=1, source_target_pairs={{0,80},{16,64},{32,112},{48,96},{64,16},{80,0},{96,48},{112,32},{1... | collective-permute-start | bytes 589832 | tf_op jit(solution)/shard_map/ppermute | solution.py:469
  155.0 0.3 collective-permute-start.21
  155.3 8.1 %collective-permute-done.20.refs_3_ = bf16[64,1536]{1,0:T(8,128)(2,1)S(1)} collective-permute-done((bf16[64,1536]{1,0:T(8,128)(2,1)}, bf16[64,1536]{1,0:T(8,128)(2,1)S(1)}, u32[]{:S(2)}, u32[]{:S(2)}) %collective-permute-start.20) | collective-permute-done | bytes 196640 | tf_op jit(solution)/shard_map/ppermute | solution.py:469
  163.5 0.3 collective-permute-done.21.refs_4_
  163.8 0.4 copy-done.16
  164.1 2.5 %spread.1.up_ref = bf16[256,384]{1,0:T(8,128)(2,1)} custom-call(bf16[64,1536]{1,0:T(8,128)(2,1)} %get-tuple-element.54.refs_0_, bf16[64,1536]{1,0:T(8,128)(2,1)} %copy-done.14, bf16[64,1536]{1,0:T(8,128)(2,1)} %copy-done.15, bf16[64,1536]{1,0:T(8,128)(2,1)} %copy-done.16, bf16[64,1536]{1,0:T(8,128)(2,1)} %collective-permute-done.21.refs_4_, ...), custom_call_target="tpu_custom_call" | custom-call | flops 268435456 | bytes 6291456 | tf_op jit(solution)/shard_map/spread/pallas_call | solution.py:197
  166.6 1.0 select_bitcast_fusion
  167.6 9.6 %fine_grads.1 = (bf16[256,384]{1,0:T(8,128)(2,1)}, f32[512,768]{1,0:T(8,128)}, bf16[256,768]{1,0:T(8,128)(2,1)}, bf16[256,768]{1,0:T(8,128)(2,1)}) custom-call(bf16[3,256,384]{2,1,0:T(8,128)(2,1)} %bitcast.27, bf16[2,512,384]{2,1,0:T(8,128)(2,1)} %bitcast.26, bf16[2,256,384]{2,1,0:T(8,128)(2,1)} %get-tuple-element.72.low_ref, ...), custom_call_target="tpu_custom_call" | custom-call | flops 2147483648 | bytes 6291456 | tf_op jit(solution)/shard_map/fine_grads/pallas_call | solution.py:197
  177.2 4.6 %collective-permute-start.26 = (bf16[256,768]{1,0:T(8,128)(2,1)}, bf16[256,768]{1,0:T(8,128)(2,1)S(1)}, u32[]{:S(2)}, u32[]{:S(2)}) collective-permute-start(bf16[256,768]{1,0:T(8,128)(2,1)} %get-tuple-element.65), channel_id=1, source_target_pairs={{1,2},{2,1},{3,4},{4,3},{5,6},{6,5},{7,8},{8,7},{9,10},{10,9},{11,... | collective-permute-start | bytes 1179656 | tf_op jit(solution)/shard_map/ppermute | solution.py:475
  181.8 6.8 %collective-permute-done.26.outer_ref = bf16[256,768]{1,0:T(8,128)(2,1)S(1)} collective-permute-done((bf16[256,768]{1,0:T(8,128)(2,1)}, bf16[256,768]{1,0:T(8,128)(2,1)S(1)}, u32[]{:S(2)}, u32[]{:S(2)}) %collective-permute-start.26) | collective-permute-done | bytes 393248 | tf_op jit(solution)/shard_map/ppermute | solution.py:475
  188.6 0.7 copy-done.4
  189.4 2.7 %add_columns.1 = (f32[256,768]{1,0:T(8,128)}, bf16[128,768]{1,0:T(8,128)(2,1)}, bf16[128,768]{1,0:T(8,128)(2,1)}) custom-call(f32[512,768]{1,0:T(8,128)} %get-tuple-element.63.mid_ref, bf16[256,768]{1,0:T(8,128)(2,1)} %copy-done.3, bf16[256,768]{1,0:T(8,128)(2,1)} %copy-done.4), custom_call_target="tpu_custom_call" | custom-call | flops 1048576 | bytes 6291456 | tf_op jit(solution)/shard_map/add_columns/pallas_call | solution.py:197
  192.1 3.1 %collective-permute-start.27 = (bf16[128,768]{1,0:T(8,128)(2,1)}, bf16[128,768]{1,0:T(8,128)(2,1)S(1)}, u32[]{:S(2)}, u32[]{:S(2)}) collective-permute-start(bf16[128,768]{1,0:T(8,128)(2,1)} %get-tuple-element.67), channel_id=1, source_target_pairs={{0,16},{16,0},{32,48},{48,32},{64,80},{80,64},{96,112},{112,96},{1... | collective-permute-start | bytes 589832 | tf_op jit(solution)/shard_map/ppermute | solution.py:469
  195.2 3.3 %collective-permute-start.28 = (bf16[128,768]{1,0:T(8,128)(2,1)}, bf16[128,768]{1,0:T(8,128)(2,1)S(1)}, u32[]{:S(2)}, u32[]{:S(2)}) collective-permute-start(bf16[128,768]{1,0:T(8,128)(2,1)} %get-tuple-element.68), channel_id=1, source_target_pairs={{16,32},{32,16},{48,64},{64,48},{80,96},{96,80},{17,33},{33,17},{4... | collective-permute-start | bytes 589832 | tf_op jit(solution)/shard_map/ppermute | solution.py:475
  198.5 1.0 collective-permute-done.27.inner_ref
  199.5 5.9 %collective-permute-done.28.outer_ref = bf16[128,768]{1,0:T(8,128)(2,1)S(1)} collective-permute-done((bf16[128,768]{1,0:T(8,128)(2,1)}, bf16[128,768]{1,0:T(8,128)(2,1)S(1)}, u32[]{:S(2)}, u32[]{:S(2)}) %collective-permute-start.28) | collective-permute-done | bytes 196640 | tf_op jit(solution)/shard_map/ppermute | solution.py:475
  205.4 0.7 copy-done.18
  206.1 2.1 add_rows.1
  (58 shorter events, 0.2 us)
Async XLA Ops:
  0.6 24.8 %copy-start = (bf16[3,1536,192]{1,2,0:T(8,128)(2,1)S(1)}, bf16[3,1536,192]{1,2,0:T(8,128)(2,1)}, u32[]{:S(2)}) copy-start(bf16[3,1536,192]{1,2,0:T(8,128)(2,1)} %param.9) | copy-start | bytes 5308420
  3.1 11.1 %collective-permute-start = (bf16[3,512,128]{2,1,0:T(8,128)(2,1)}, bf16[3,512,128]{2,1,0:T(8,128)(2,1)S(1)}, u32[]{:S(2)}, u32[]{:S(2)}) collective-permute-start(bf16[3,512,128]{2,1,0:T(8,128)(2,1)} %get-tuple-element.37.refs_0_), channel_id=1, source_target_pairs={{0,8},{8,0},{1,9},{9,1},{2,10},{10,2},{3,11},{11,3},{4,12},{12,4},... | collective-permute-start | bytes 1179656 | tf_op jit(solution)/shard_map/ppermute | solution.py:469
  14.2 16.1 %copy-start.7 = (bf16[3,512,128]{2,1,0:T(8,128)(2,1)}, bf16[3,512,128]{2,1,0:T(8,128)(2,1)S(1)}, u32[]{:S(2)}) copy-start(bf16[3,512,128]{2,1,0:T(8,128)(2,1)S(1)} %collective-permute-done.refs_2_) | copy-start | bytes 1179652
  15.4 10.1 %collective-permute-start.3 = (bf16[2,8,16,384]{3,2,1,0:T(8,128)(2,1)S(1)}, bf16[2,8,16,384]{3,2,1,0:T(8,128)(2,1)S(1)}, u32[]{:S(2)}, u32[]{:S(2)}) collective-permute-start(bf16[2,8,16,384]{3,2,1,0:T(8,128)(2,1)S(1)} %get-tuple-element.75), channel_id=1, source_target_pairs={{16,32},{32,16},{48,64},{64,48},{80,96},{96,80},{17,33},{33,17},{4... | collective-permute-start | bytes 589832 | tf_op jit(solution)/shard_map/ppermute | solution.py:475
  18.8 16.5 %collective-permute-start.1 = (bf16[3,512,128]{2,1,0:T(8,128)(2,1)}, bf16[3,512,128]{2,1,0:T(8,128)(2,1)S(1)}, u32[]{:S(2)}, u32[]{:S(2)}) collective-permute-start(bf16[3,512,128]{2,1,0:T(8,128)(2,1)} %get-tuple-element.37.refs_0_), channel_id=1, source_target_pairs={{0,1},{1,0},{2,3},{3,2},{4,5},{5,4},{6,7},{7,6},{8,9},{9,8},{10,11... | collective-permute-start | bytes 1179656 | tf_op jit(solution)/shard_map/ppermute | solution.py:469
  18.9 17.2 %collective-permute-start.5 = (bf16[3,512,128]{2,1,0:T(8,128)(2,1)}, bf16[3,512,128]{2,1,0:T(8,128)(2,1)}, u32[]{:S(2)}, u32[]{:S(2)}) collective-permute-start(bf16[3,512,128]{2,1,0:T(8,128)(2,1)} %get-tuple-element.42.refs_4_), channel_id=1, source_target_pairs={{0,2},{2,0},{4,6},{6,4},{1,3},{3,1},{5,7},{7,5},{8,10},{10,8},{12,... | collective-permute-start | bytes 1179656 | tf_op jit(solution)/shard_map/ppermute | solution.py:469
  20.5 15.5 %collective-permute-start.7 = (bf16[3,512,128]{2,1,0:T(8,128)(2,1)}, bf16[3,512,128]{2,1,0:T(8,128)(2,1)}, u32[]{:S(2)}, u32[]{:S(2)}) collective-permute-start(bf16[3,512,128]{2,1,0:T(8,128)(2,1)} %get-tuple-element.42.refs_4_), channel_id=1, source_target_pairs={{0,6},{2,4},{4,2},{6,0},{1,7},{3,5},{5,3},{7,1},{8,14},{10,12},{12... | collective-permute-start | bytes 1179656 | tf_op jit(solution)/shard_map/ppermute | solution.py:469
  22.7 9.1 %collective-permute-start.4 = (bf16[2,8,16,384]{3,2,1,0:T(8,128)(2,1)S(1)}, bf16[2,8,16,384]{3,2,1,0:T(8,128)(2,1)S(1)}, u32[]{:S(2)}, u32[]{:S(2)}) collective-permute-start(bf16[2,8,16,384]{3,2,1,0:T(8,128)(2,1)S(1)} %get-tuple-element.76), channel_id=1, source_target_pairs={{0,16},{16,0},{32,48},{48,32},{64,80},{80,64},{96,112},{112,96},{1... | collective-permute-start | bytes 589832 | tf_op jit(solution)/shard_map/ppermute | solution.py:469
  25.5 9.8 %collective-permute-start.2 = (bf16[3,512,128]{2,1,0:T(8,128)(2,1)S(1)}, bf16[3,512,128]{2,1,0:T(8,128)(2,1)S(1)}, u32[]{:S(2)}, u32[]{:S(2)}) collective-permute-start(bf16[3,512,128]{2,1,0:T(8,128)(2,1)S(1)} %collective-permute-done.refs_2_), channel_id=1, source_target_pairs={{0,1},{1,0},{2,3},{3,2},{4,5},{5,4},{6,7},{7,6},{8,9},{9,8},{10,11... | collective-permute-start | bytes 1179656 | tf_op jit(solution)/shard_map/ppermute | solution.py:469
  30.3 1.5 copy-start.6
  30.3 4.8 %slice-start = ((bf16[3,16,16,384]{3,2,1,0:T(8,128)(2,1)}), bf16[2,16,16,384]{3,2,1,0:T(8,128)(2,1)S(1)}, s32[]{:S(2)}) async-start(bf16[3,16,16,384]{3,2,1,0:T(8,128)(2,1)} %param.5), calls=%async_computation | async-start | bytes 786432 | tf_op jit(solution)/shard_map/slice | solution.py:519
  31.8 19.8 %collective-permute-start.6 = (bf16[3,512,128]{2,1,0:T(8,128)(2,1)S(1)}, bf16[3,512,128]{2,1,0:T(8,128)(2,1)}, u32[]{:S(2)}, u32[]{:S(2)}) collective-permute-start(bf16[3,512,128]{2,1,0:T(8,128)(2,1)S(1)} %copy-done.6), channel_id=1, source_target_pairs={{0,4},{2,6},{4,0},{6,2},{1,5},{3,7},{5,1},{7,3},{8,12},{10,14},{12... | collective-permute-start | bytes 1179656 | tf_op jit(solution)/shard_map/ppermute | solution.py:469
  35.2 107.2 %copy-start.1 = (bf16[2,32,16,384]{3,2,1,0:T(8,128)(2,1)}, bf16[2,32,16,384]{3,2,1,0:T(8,128)(2,1)S(1)}, u32[]{:S(2)}) copy-start(bf16[2,32,16,384]{3,2,1,0:T(8,128)(2,1)S(1)} %pad_maximum_fusion) | copy-start | bytes 2359300
  35.3 0.8 copy-start.9
  36.1 0.7 copy-start.8
  58.6 5.5 %collective-permute-start.10 = (f32[3,2,2048]{2,1,0:T(2,128)}, f32[3,2,2048]{2,1,0:T(2,128)S(1)}, u32[]{:S(2)}, u32[]{:S(2)}) collective-permute-start(f32[3,2,2048]{2,1,0:T(2,128)} %coarse_stats.3.refs_8_), channel_id=1, source_target_pairs={{0,6},{2,4},{4,2},{6,0},{1,7},{3,5},{5,3},{7,1},{8,14},{10,12},{12... | collective-permute-start | bytes 147464 | tf_op jit(solution)/shard_map/ppermute | solution.py:469
  59.6 4.7 %collective-permute-start.8 = (f32[3,2,2048]{2,1,0:T(2,128)}, f32[3,2,2048]{2,1,0:T(2,128)S(1)}, u32[]{:S(2)}, u32[]{:S(2)}) collective-permute-start(f32[3,2,2048]{2,1,0:T(2,128)} %coarse_stats.3.refs_8_), channel_id=1, source_target_pairs={{0,2},{2,0},{4,6},{6,4},{1,3},{3,1},{5,7},{7,5},{8,10},{10,8},{12,... | collective-permute-start | bytes 147464 | tf_op jit(solution)/shard_map/ppermute | solution.py:469
  59.6 6.6 %collective-permute-start.9 = (f32[3,2,2048]{2,1,0:T(2,128)}, f32[3,2,2048]{2,1,0:T(2,128)S(1)}, u32[]{:S(2)}, u32[]{:S(2)}) collective-permute-start(f32[3,2,2048]{2,1,0:T(2,128)} %coarse_stats.3.refs_8_), channel_id=1, source_target_pairs={{0,4},{2,6},{4,0},{6,2},{1,5},{3,7},{5,1},{7,3},{8,12},{10,14},{12... | collective-permute-start | bytes 147464 | tf_op jit(solution)/shard_map/ppermute | solution.py:469
  64.1 2.0 copy-start.19
  64.4 1.8 copy-start.20
  66.2 0.6 copy-start.21
  104.0 2.6 %collective-permute-start.14 = (bf16[2,3,512,128]{3,2,1,0:T(8,128)(2,1)}, bf16[2,3,512,128]{3,2,1,0:T(8,128)(2,1)S(1)}, u32[]{:S(2)}, u32[]{:S(2)}) collective-permute-start(bf16[2,3,512,128]{3,2,1,0:T(8,128)(2,1)} %get-tuple-element.48), channel_id=1, source_target_pairs={{0,1},{1,0},{2,3},{3,2},{4,5},{5,4},{6,7},{7,6},{8,9},{9,8},{10,11... | collective-permute-start | bytes 2359304 | tf_op jit(solution)/shard_map/ppermute | solution.py:469
  106.6 17.6 %copy-start.2 = (bf16[2,3,512,128]{3,2,1,0:T(8,128)(2,1)}, bf16[2,3,512,128]{3,2,1,0:T(8,128)(2,1)S(1)}, u32[]{:S(2)}) copy-start(bf16[2,3,512,128]{3,2,1,0:T(8,128)(2,1)S(1)} %collective-permute-done.14.refs_5_) | copy-start | bytes 2359300
  108.7 15.5 %collective-permute-start.15 = (bf16[3,512,128]{2,1,0:T(8,128)(2,1)}, bf16[3,512,128]{2,1,0:T(8,128)(2,1)}, u32[]{:S(2)}, u32[]{:S(2)}) collective-permute-start(bf16[3,512,128]{2,1,0:T(8,128)(2,1)} %fusion), channel_id=1, source_target_pairs={{0,8},{8,0},{1,9},{9,1},{2,10},{10,2},{3,11},{11,3},{4,12},{12,4},... | collective-permute-start | bytes 1179656 | tf_op jit(solution)/shard_map/ppermute | solution.py:469
  109.1 8.0 %collective-permute-start.11 = (bf16[192,512]{1,0:T(8,128)(2,1)}, bf16[192,512]{1,0:T(8,128)(2,1)S(1)}, u32[]{:S(2)}, u32[]{:S(2)}) collective-permute-start(bf16[192,512]{1,0:T(8,128)(2,1)} %get-tuple-element.44), channel_id=1, source_target_pairs={{0,2},{2,0},{4,6},{6,4},{1,3},{3,1},{5,7},{7,5},{8,10},{10,8},{12,... | collective-permute-start | bytes 589832 | tf_op jit(solution)/shard_map/ppermute | solution.py:469
  110.4 11.2 %collective-permute-start.12 = (bf16[192,512]{1,0:T(8,128)(2,1)}, bf16[192,512]{1,0:T(8,128)(2,1)}, u32[]{:S(2)}, u32[]{:S(2)}) collective-permute-start(bf16[192,512]{1,0:T(8,128)(2,1)} %get-tuple-element.45), channel_id=1, source_target_pairs={{0,4},{2,6},{4,0},{6,2},{1,5},{3,7},{5,1},{7,3},{8,12},{10,14},{12... | collective-permute-start | bytes 589832 | tf_op jit(solution)/shard_map/ppermute | solution.py:469
  112.1 12.0 %collective-permute-start.13 = (bf16[192,512]{1,0:T(8,128)(2,1)}, bf16[192,512]{1,0:T(8,128)(2,1)}, u32[]{:S(2)}, u32[]{:S(2)}) collective-permute-start(bf16[192,512]{1,0:T(8,128)(2,1)} %get-tuple-element.46), channel_id=1, source_target_pairs={{0,6},{2,4},{4,2},{6,0},{1,7},{3,5},{5,3},{7,1},{8,14},{10,12},{12... | collective-permute-start | bytes 589832 | tf_op jit(solution)/shard_map/ppermute | solution.py:469
  117.1 7.1 %copy-start.5 = (bf16[192,512]{1,0:T(8,128)(2,1)}, bf16[192,512]{1,0:T(8,128)(2,1)S(1)}, u32[]{:S(2)}) copy-start(bf16[192,512]{1,0:T(8,128)(2,1)S(1)} %collective-permute-done.11.refs_1_) | copy-start | bytes 589828
  130.2 24.8 %copy-start.10 = (bf16[64,1536]{1,0:T(8,128)(2,1)S(1)}, bf16[64,1536]{1,0:T(8,128)(2,1)}, u32[]{:S(2)}) copy-start(bf16[64,1536]{1,0:T(8,128)(2,1)} %get-tuple-element.58) | copy-start | bytes 589828
  134.7 10.9 %collective-permute-start.22 = (bf16[64,1536]{1,0:T(8,128)(2,1)}, bf16[64,1536]{1,0:T(8,128)(2,1)S(1)}, u32[]{:S(2)}, u32[]{:S(2)}) collective-permute-start(bf16[64,1536]{1,0:T(8,128)(2,1)} %get-tuple-element.59), channel_id=1, source_target_pairs={{0,48},{16,32},{32,16},{48,0},{64,112},{80,96},{96,80},{112,64},{1... | collective-permute-start | bytes 589832 | tf_op jit(solution)/shard_map/ppermute | solution.py:469
  136.2 9.5 %collective-permute-start.23 = (bf16[64,1536]{1,0:T(8,128)(2,1)}, bf16[64,1536]{1,0:T(8,128)(2,1)S(1)}, u32[]{:S(2)}, u32[]{:S(2)}) collective-permute-start(bf16[64,1536]{1,0:T(8,128)(2,1)} %get-tuple-element.60), channel_id=1, source_target_pairs={{0,32},{16,48},{32,0},{48,16},{64,96},{80,112},{96,64},{112,80},{1... | collective-permute-start | bytes 589832 | tf_op jit(solution)/shard_map/ppermute | solution.py:469
  136.2 15.3 %collective-permute-start.24 = (bf16[64,1536]{1,0:T(8,128)(2,1)}, bf16[64,1536]{1,0:T(8,128)(2,1)S(1)}, u32[]{:S(2)}, u32[]{:S(2)}) collective-permute-start(bf16[64,1536]{1,0:T(8,128)(2,1)} %get-tuple-element.61), channel_id=1, source_target_pairs={{0,16},{16,0},{32,48},{48,32},{64,80},{80,64},{96,112},{112,96},{1... | collective-permute-start | bytes 589832 | tf_op jit(solution)/shard_map/ppermute | solution.py:469
  139.7 15.3 %collective-permute-start.18 = (bf16[64,1536]{1,0:T(8,128)(2,1)}, bf16[64,1536]{1,0:T(8,128)(2,1)S(1)}, u32[]{:S(2)}, u32[]{:S(2)}) collective-permute-start(bf16[64,1536]{1,0:T(8,128)(2,1)} %get-tuple-element.55), channel_id=1, source_target_pairs={{0,112},{16,96},{32,80},{48,64},{64,48},{80,32},{96,16},{112,0},{1... | collective-permute-start | bytes 589832 | tf_op jit(solution)/shard_map/ppermute | solution.py:469
  142.5 24.1 %collective-permute-start.16 = (bf16[2,32,8,384]{3,2,1,0:T(8,128)(2,1)S(1)}, bf16[2,32,8,384]{3,2,1,0:T(8,128)(2,1)S(1)}, u32[]{:S(2)}, u32[]{:S(2)}) collective-permute-start(bf16[2,32,8,384]{3,2,1,0:T(8,128)(2,1)S(1)} %get-tuple-element.74), channel_id=1, source_target_pairs={{1,2},{2,1},{3,4},{4,3},{5,6},{6,5},{7,8},{8,7},{9,10},{10,9},{11,... | collective-permute-start | bytes 1179656 | tf_op jit(solution)/shard_map/ppermute | solution.py:475
  145.6 9.7 %copy-start.11 = (bf16[64,1536]{1,0:T(8,128)(2,1)}, bf16[64,1536]{1,0:T(8,128)(2,1)S(1)}, u32[]{:S(2)}) copy-start(bf16[64,1536]{1,0:T(8,128)(2,1)S(1)} %collective-permute-done.22.refs_5_) | copy-start | bytes 589828
  145.6 21.0 %collective-permute-start.17 = (bf16[2,32,8,384]{3,2,1,0:T(8,128)(2,1)S(1)}, bf16[2,32,8,384]{3,2,1,0:T(8,128)(2,1)S(1)}, u32[]{:S(2)}, u32[]{:S(2)}) collective-permute-start(bf16[2,32,8,384]{3,2,1,0:T(8,128)(2,1)S(1)} %get-tuple-element.73), channel_id=1, source_target_pairs={{0,1},{1,0},{2,3},{3,2},{4,5},{5,4},{6,7},{7,6},{8,9},{9,8},{10,11... | collective-permute-start | bytes 1179656 | tf_op jit(solution)/shard_map/ppermute | solution.py:469
  145.7 9.7 %copy-start.12 = (bf16[64,1536]{1,0:T(8,128)(2,1)}, bf16[64,1536]{1,0:T(8,128)(2,1)S(1)}, u32[]{:S(2)}) copy-start(bf16[64,1536]{1,0:T(8,128)(2,1)S(1)} %collective-permute-done.23.refs_6_) | copy-start | bytes 589828
  145.7 9.6 %collective-permute-start.19 = (bf16[64,1536]{1,0:T(8,128)(2,1)}, bf16[64,1536]{1,0:T(8,128)(2,1)S(1)}, u32[]{:S(2)}, u32[]{:S(2)}) collective-permute-start(bf16[64,1536]{1,0:T(8,128)(2,1)} %get-tuple-element.56), channel_id=1, source_target_pairs={{0,96},{16,112},{32,64},{48,80},{64,32},{80,48},{96,0},{112,16},{1... | collective-permute-start | bytes 589832 | tf_op jit(solution)/shard_map/ppermute | solution.py:469
  151.5 11.9 %copy-start.13 = (bf16[64,1536]{1,0:T(8,128)(2,1)}, bf16[64,1536]{1,0:T(8,128)(2,1)S(1)}, u32[]{:S(2)}) copy-start(bf16[64,1536]{1,0:T(8,128)(2,1)S(1)} %collective-permute-done.24.refs_7_) | copy-start | bytes 589828
  151.6 11.9 %collective-permute-start.20 = (bf16[64,1536]{1,0:T(8,128)(2,1)}, bf16[64,1536]{1,0:T(8,128)(2,1)S(1)}, u32[]{:S(2)}, u32[]{:S(2)}) collective-permute-start(bf16[64,1536]{1,0:T(8,128)(2,1)} %get-tuple-element.57), channel_id=1, source_target_pairs={{0,80},{16,64},{32,112},{48,96},{64,16},{80,0},{96,48},{112,32},{1... | collective-permute-start | bytes 589832 | tf_op jit(solution)/shard_map/ppermute | solution.py:469
  155.0 8.5 %copy-start.14 = (bf16[64,1536]{1,0:T(8,128)(2,1)}, bf16[64,1536]{1,0:T(8,128)(2,1)S(1)}, u32[]{:S(2)}) copy-start(bf16[64,1536]{1,0:T(8,128)(2,1)S(1)} %collective-permute-done.18.refs_1_) | copy-start | bytes 589828
  155.0 8.8 %collective-permute-start.21 = (bf16[64,1536]{1,0:T(8,128)(2,1)S(1)}, bf16[64,1536]{1,0:T(8,128)(2,1)}, u32[]{:S(2)}, u32[]{:S(2)}) collective-permute-start(bf16[64,1536]{1,0:T(8,128)(2,1)S(1)} %copy-done.10), channel_id=1, source_target_pairs={{0,64},{16,80},{32,96},{48,112},{64,0},{80,16},{96,32},{112,48},{1... | collective-permute-start | bytes 589832 | tf_op jit(solution)/shard_map/ppermute | solution.py:469
  155.3 8.5 %copy-start.15 = (bf16[64,1536]{1,0:T(8,128)(2,1)}, bf16[64,1536]{1,0:T(8,128)(2,1)S(1)}, u32[]{:S(2)}) copy-start(bf16[64,1536]{1,0:T(8,128)(2,1)S(1)} %collective-permute-done.19.refs_2_) | copy-start | bytes 589828
  163.5 0.7 copy-start.16
  177.2 4.6 %collective-permute-start.25 = (bf16[256,768]{1,0:T(8,128)(2,1)}, bf16[256,768]{1,0:T(8,128)(2,1)S(1)}, u32[]{:S(2)}, u32[]{:S(2)}) collective-permute-start(bf16[256,768]{1,0:T(8,128)(2,1)} %get-tuple-element.64), channel_id=1, source_target_pairs={{0,1},{1,0},{2,3},{3,2},{4,5},{5,4},{6,7},{7,6},{8,9},{9,8},{10,11... | collective-permute-start | bytes 1179656 | tf_op jit(solution)/shard_map/ppermute | solution.py:469
  177.2 11.4 %collective-permute-start.26 = (bf16[256,768]{1,0:T(8,128)(2,1)}, bf16[256,768]{1,0:T(8,128)(2,1)S(1)}, u32[]{:S(2)}, u32[]{:S(2)}) collective-permute-start(bf16[256,768]{1,0:T(8,128)(2,1)} %get-tuple-element.65), channel_id=1, source_target_pairs={{1,2},{2,1},{3,4},{4,3},{5,6},{6,5},{7,8},{8,7},{9,10},{10,9},{11,... | collective-permute-start | bytes 1179656 | tf_op jit(solution)/shard_map/ppermute | solution.py:475
  181.8 6.8 %copy-start.3 = (bf16[256,768]{1,0:T(8,128)(2,1)}, bf16[256,768]{1,0:T(8,128)(2,1)S(1)}, u32[]{:S(2)}) copy-start(bf16[256,768]{1,0:T(8,128)(2,1)S(1)} %collective-permute-done.25.inner_ref) | copy-start | bytes 1179652
  188.6 0.7 copy-start.4
  192.1 7.4 %collective-permute-start.27 = (bf16[128,768]{1,0:T(8,128)(2,1)}, bf16[128,768]{1,0:T(8,128)(2,1)S(1)}, u32[]{:S(2)}, u32[]{:S(2)}) collective-permute-start(bf16[128,768]{1,0:T(8,128)(2,1)} %get-tuple-element.67), channel_id=1, source_target_pairs={{0,16},{16,0},{32,48},{48,32},{64,80},{80,64},{96,112},{112,96},{1... | collective-permute-start | bytes 589832 | tf_op jit(solution)/shard_map/ppermute | solution.py:469
  195.2 10.2 %collective-permute-start.28 = (bf16[128,768]{1,0:T(8,128)(2,1)}, bf16[128,768]{1,0:T(8,128)(2,1)S(1)}, u32[]{:S(2)}, u32[]{:S(2)}) collective-permute-start(bf16[128,768]{1,0:T(8,128)(2,1)} %get-tuple-element.68), channel_id=1, source_target_pairs={{16,32},{32,16},{48,64},{64,48},{80,96},{96,80},{17,33},{33,17},{4... | collective-permute-start | bytes 589832 | tf_op jit(solution)/shard_map/ppermute | solution.py:475
  199.5 5.9 %copy-start.17 = (bf16[128,768]{1,0:T(8,128)(2,1)}, bf16[128,768]{1,0:T(8,128)(2,1)S(1)}, u32[]{:S(2)}) copy-start(bf16[128,768]{1,0:T(8,128)(2,1)S(1)} %collective-permute-done.27.inner_ref) | copy-start | bytes 589828
  205.4 0.7 copy-start.18

commit v4 on v3

--- a/solution.py
+++ b/solution.py
@@ -359,17 +359,12 @@
     each = rows // count
     size = each * columns
     wide = joint.shape[1]
-    first = count // 2
-    operands = (*query_pieces, kept, from_core, arrived, joint)
-    params = pltpu.CompilerParams(vmem_limit_bytes=VMEM)
-
-    def whole(array):
-        return pl.BlockSpec(array.shape, lambda d: (0,) * array.ndim)
-
-    def pack(*refs):
-        pieces = refs[: len(query_pieces)]
-        kept_ref, core_ref, arrived_ref, joint_ref = refs[len(query_pieces) :][:4]
-        outs, packed, held = refs[len(operands) : -2], refs[-2], refs[-1]
+    chunk = 256
+    blocks = len(query_pieces)
+
+    def body(*refs):
+        pieces = refs[:blocks]
+        kept_ref, core_ref, arrived_ref, joint_ref, out, held, packed = refs[blocks:]
 
         @pl.when(pl.program_id(0) == 0)
         def _():
@@ -383,62 +378,46 @@
             for piece in pieces[1:]:
                 total += piece[...].astype(F32)
             held[:, :group] = total.T
-            for step in range(count):
-                target = lax.axis_index(ROW) ^ (count - 1 - step)
+            for target in range(count):
                 taken = []
                 for c in range(columns):
-                    start = pl.multiple_of(c * rows + target * each, each)
-                    taken.append(held[pl.ds(start, each), :])
-                packed[step] = jnp.concatenate(taken, axis=0).astype(BF16)
-
-        for step, out in enumerate(outs):
-
-            @pl.when(pl.program_id(0) == step)
-            def _():
-                out[...] = nn(packed[step], joint_ref[...]).astype(BF16)
-
-    def rest(packed, joint_ref, *outs):
-        for step, out in enumerate(outs):
-
-            @pl.when(pl.program_id(0) == step)
-            def _():
-                out[...] = nn(packed[first + step], joint_ref[...]).astype(BF16)
-
-    piece = jax.ShapeDtypeStruct((size, wide), BF16)
-    packed = jax.ShapeDtypeStruct((count, size, 3 * group), BF16)
-    early = pl.pallas_call(
-        pack,
-        grid=(first,),
-        in_specs=[whole(array) for array in operands],
-        out_specs=[whole(piece)] * first + [whole(packed)],
-        out_shape=[piece] * first + [packed],
-        scratch_shapes=[pltpu.VMEM((tokens, 3 * group), F32)],
+                    start = c * rows + target * each
+                    taken.append(held[start : start + each, :])
+                chosen = jnp.concatenate(taken, axis=0).astype(BF16)
+                packed[target * size : (target + 1) * size, :] = chosen
+
+        out[...] = nn(packed[...], joint_ref[...]).astype(BF16)
+
+    half_spec = pl.BlockSpec((1, heads, tokens, 128), lambda n: (0, 0, 0, 0))
+    return pl.pallas_call(
+        body,
+        grid=(wide // chunk,),
+        in_specs=[pl.BlockSpec((group, tokens), lambda n: (0, 0))] * blocks
+        + [half_spec] * 2
+        + [
+            pl.BlockSpec(arrived.shape, lambda n: (0, 0, 0)),
+            pl.BlockSpec((3 * group, chunk), lambda n: (0, n)),
+        ],
+        out_specs=pl.BlockSpec((tokens, chunk), lambda n: (0, n)),
+        out_shape=jax.ShapeDtypeStruct((tokens, wide), BF16),
+        scratch_shapes=[
+            pltpu.VMEM((tokens, 3 * group), F32),
+            pltpu.VMEM((tokens, 3 * group), BF16),
+        ],
         name="project",
-        cost_estimate=cost(1 << 30, 6 << 20, 0),
-        compiler_params=params,
-    )(*operands)
-    late = pl.pallas_call(
-        rest,
-        grid=(count - first,),
-        in_specs=[whole(packed), whole(joint)],
-        out_specs=[whole(piece)] * (count - first),
-        out_shape=[piece] * (count - first),
-        name="project_rest",
-        cost_estimate=cost(1 << 30, 3 << 20, 0),
-        compiler_params=params,
-    )(early[-1], joint)
-    return [*early[:-1], *late]
+        cost_estimate=cost(2 << 30, 6 << 20, 0),
+        compiler_params=pltpu.CompilerParams(vmem_limit_bytes=VMEM),
+    )(*query_pieces, kept, from_core, arrived, joint)
 
 
 def spread(pieces, columns):
-    tokens, wide = pieces[0].shape
+    count, tokens, wide = pieces.shape
     width = wide // 4
 
-    def body(*refs):
-        out = refs[-1]
-        total = refs[0][...].astype(F32)
-        for ref in refs[1:-1]:
-            total += ref[...].astype(F32)
+    def body(in_ref, out):
+        total = in_ref[0].astype(F32)
+        for at in range(1, count):
+            total += in_ref[at].astype(F32)
         total = total.astype(BF16)
         cells = 2 * tokens
         fine = lax.broadcasted_iota(jnp.int32, (cells, tokens), 0)
@@ -461,7 +440,7 @@
         "spread",
         1 << 28,
         [],
-        *pieces,
+        pieces,
     )
 
 
@@ -475,26 +454,17 @@
     return swapped(inner, axis), lax.ppermute(outer, axis, beyond)
 
 
-def rims(block, axis, parity, at):
+def sent_rims(block, axis, parity, at):
     size = block.shape[at]
     low = lax.slice_in_dim(block, 0, RIM, axis=at)
     high = lax.slice_in_dim(block, size - RIM, None, axis=at)
     first = lax.axis_index(parity) == 0
-    inner, outer = exchanged(
-        jnp.where(first, high, low), jnp.where(first, low, high), axis
-    )
+    return exchanged(jnp.where(first, high, low), jnp.where(first, low, high), axis)
+
+
+def placed_rims(inner, outer, parity):
+    first = lax.axis_index(parity) == 0
     return jnp.where(first, outer, inner), jnp.where(first, inner, outer)
-
-
-def with_rows(block, dim):
-    low, high = rims(block, ROW, "zh", dim)
-    return jnp.concatenate([low, block, high], axis=dim)
-
-
-def with_columns(block, dim):
-    low, high = rims(block, COL, "c", dim + 1)
-    shape = block.shape[:dim] + (-1, block.shape[-1])
-    return block.reshape(shape), low.reshape(shape), high.reshape(shape)
 
 
 def shards(fine_qkv, coarse_qkv, grad_coarse, merge_weight, qkv_weight):
@@ -508,22 +478,25 @@
         coarse_qkv.reshape(3, tokens, group), grad_coarse.reshape(tokens, group)
     )
     across = swapped(key_value, "zl")
+    near = [query_up, swapped(query_up, "y", 1), swapped(query_up, "y", 3)]
     beside = swapped(key_value, "c")
-    queries = [query_up] + [swapped(query_up, "y", step) for step in (1, 2, 3)]
-    across, merge_weight, fine_qkv = lax.optimization_barrier((across, merge_weight, fine_qkv))
-    corner = swapped(across, "c")
+    beside, merge_weight = lax.optimization_barrier((beside, merge_weight))
     joint = lax.dot_general(
         qkv_weight, merge_weight, (((1,), (1,)), ((), ())), preferred_element_type=F32
     ).astype(BF16).reshape(3 * group, wide)
+    corner = swapped(across, "c")
+    *near, joint = lax.optimization_barrier((*near, joint))
+    far = swapped(near[0], "y", 2)
+    keys = [key_value, beside, across, corner]
+    queries = [near[0], near[1], far, near[2]]
+
+    part = coarse_stats(keys, near, [0, 1, 3], (), 256)
+    part, fine_qkv = lax.optimization_barrier((part, fine_qkv))
     own_qkv = fine_qkv.reshape(3, own, width)
-    tall = with_rows(fine_qkv[1:], 1)
-    corner, joint, tall = lax.optimization_barrier((corner, joint, tall))
-    keys = [key_value, beside, across, corner]
-
-    near = [0, 1, 3]
-    part = coarse_stats(keys, [queries[i] for i in near], near, (), 256)
-    part = coarse_stats(keys, [queries[2]], [2], (part,), 256)
-    stats = [part] + [swapped(part, "y", step) for step in (1, 2, 3)]
+    edges = sent_rims(fine_qkv[1:], ROW, "zh", 1)
+    part = coarse_stats(keys, [far], [2], (part,), 256)
+    part, *edges = lax.optimization_barrier((part, *edges))
+    stats = [part] + [swapped(part, "y", step) for step in (1, 3, 2)]
     kept, sent, *query_grads = coarse_grads(keys, queries, stats)
 
     from_core = swapped(sent, "c")
@@ -536,12 +509,13 @@
     projected = project(
         query_pieces, kept, from_core, arrived, joint, coarse_columns, count
     )
-    pieces = [
-        swapped(piece, ROW, count - 1 - step) for step, piece in enumerate(projected[:-1])
-    ]
-    kept_piece, tall = lax.optimization_barrier((projected[-1], tall))
-    ext_kv = with_columns(tall, 1)
-    own_up = spread([kept_piece, *pieces], coarse_columns)
+    projected, *edges = lax.optimization_barrier((projected, *edges))
+    pieces = lax.all_to_all(projected.reshape(count, -1, wide), ROW, 0, 0)
+    low, high = placed_rims(*edges, "zh")
+    tall = jnp.concatenate([low, fine_qkv[1:], high], axis=1)
+    low, high = placed_rims(*sent_rims(tall, COL, "c", 2), "c")
+    ext_kv = [array.reshape(2, -1, width) for array in (tall, low, high)]
+    own_up = spread(pieces, coarse_columns)
 
     grad_query, mid, inner, outer = fine_grads(own_qkv, ext_kv, own_up, rows, columns)
     inner, outer = exchanged(inner, outer, COL)

time: 212 us -> 200 us (0.943)
  starting transfers between devices: 47.2 us -> 42.1 us
  Pallas kernels: 88.9 us -> 85 us
    ppermute x25 -> x18, waiting for transfers between devices: 40.9 us -> 26 us  [swapped(): lax.ppermute(array, axis, [(i, i ^ flip) for i in range(lax.axis_size(axi...]
    ppermute x25 -> x18, starting transfers between devices: 34.1 us -> 20.3 us  [swapped(): lax.ppermute(array, axis, [(i, i ^ flip) for i in range(lax.axis_size(axi...]
    ppermute x4, waiting for transfers between devices: 15.5 us -> 26.3 us  [exchanged(): return (swapped(inner, axis), lax.ppermute(outer, axis, beyond))]
    all_to_all x0 -> x1, starting transfers between devices: none -> 7.11 us  [shards(): pieces = lax.all_to_all(projected.reshape(count, -1, wide), ROW, 0, 0)]
    pallas_call x2 -> x1, Pallas kernels: 10.5 us -> 6.7 us  [project(): pl.pallas_call(body, grid=(wide // chunk,), in_specs=[pl.BlockSpec((group...]
    all_to_all x0 -> x1, waiting for transfers between devices: none -> 2.44 us  [shards(): pieces = lax.all_to_all(projected.reshape(count, -1, wide), ROW, 0, 0)]
    unnamed x44 -> x42, local copies, waits for them, and re-layouts: 3.96 us -> 5.76 us
  transfers between devices with their start and end apart: 29 -> 23, of which waited for: 16 -> 12; matrix products, arithmetic and copies ran while one was open for 3% -> 4% of each run, Pallas kernels for 8% -> 11%
where the time goes in v4:
time: 200 us; the launch traced here: 198 us
  Pallas kernels  85 us (42%)
  waiting for transfers between devices  54.8 us (27%)
  starting transfers between devices  42.1 us (21%)
  local copies, waits for them, and re-layouts  5.77 us (3%)
  matrix products  4.97 us (2%)
  other arithmetic  4.07 us (2%)
    pallas_call x1, Pallas kernels, coarse_grads(): pl.pallas_call(body, grid=(heads, blocks), in_specs=[pl.BlockSpec((1, tok...  37.2 us
    ppermute x4, waiting for transfers between devices, exchanged(): return (swapped(inner, axis), lax.ppermute(outer, axis, beyond))  26.3 us
    ppermute x18, waiting for transfers between devices, swapped(): lax.ppermute(array, axis, [(i, i ^ flip) for i in range(lax.axis_size(axi...  26 us
    pallas_call x2, Pallas kernels, coarse_stats(): pl.pallas_call(body, grid=(heads, number), in_specs=[pl.BlockSpec((1, tok...  21.8 us
    ppermute x18, starting transfers between devices, swapped(): lax.ppermute(array, axis, [(i, i ^ flip) for i in range(lax.axis_size(axi...  20.3 us
    pallas_call x5, Pallas kernels, whole_call(): pl.pallas_call(body, out_shape=out_shape, scratch_shapes=scratch, name=na...  19.3 us
    ppermute x4, starting transfers between devices, exchanged(): return (swapped(inner, axis), lax.ppermute(outer, axis, beyond))  14.7 us
    all_to_all x1, starting transfers between devices, shards(): pieces = lax.all_to_all(projected.reshape(count, -1, wide), ROW, 0, 0)  7.11 us
  transfers between devices with their start and end apart: 23, of which 12 were waited for; matrix products, arithmetic and copies ran while one was open for 4% of the time, Pallas kernels for 11%

profile of v4, /device:TPU:96, one launch (start us, length us, event | category | flops | bytes accessed | tf_op | source)
XLA Modules:
  0.0 197.6 jit_solution(15573131432764219976)
XLA Ops:
  0.6 0.0 copy-start
  0.6 2.5 %prepare.1 = (bf16[3,512,128]{2,1,0:T(8,128)(2,1)}, bf16[3,512,128]{2,1,0:T(8,128)(2,1)}) custom-call(bf16[3,512,192]{2,1,0:T(8,128)(2,1)} %bitcast.29, bf16[512,192]{1,0:T(8,128)(2,1)} %bitcast.30), custom_call_target="tpu_custom_call" | custom-call | flops 1048576 | bytes 6291456 | tf_op jit(solution)/shard_map/prepare/pallas_call | solution.py:197
  3.1 0.4 collective-permute-start.1
  3.5 1.6 collective-permute-start.3
  5.1 2.2 %collective-permute-start.4 = (bf16[3,512,128]{2,1,0:T(8,128)(2,1)}, bf16[3,512,128]{2,1,0:T(8,128)(2,1)}, u32[]{:S(2)}, u32[]{:S(2)}) collective-permute-start(bf16[3,512,128]{2,1,0:T(8,128)(2,1)} %get-tuple-element.38.refs_4_), channel_id=1, source_target_pairs={{0,6},{2,4},{4,2},{6,0},{1,7},{3,5},{5,3},{7,1},{8,14},{10,12},{12... | collective-permute-start | bytes 1179656 | tf_op jit(solution)/shard_map/ppermute | solution.py:448
  7.3 0.0 collective-permute-done.refs_1_
  7.3 7.6 %collective-permute-done.1.refs_2_ = bf16[3,512,128]{2,1,0:T(8,128)(2,1)S(1)} collective-permute-done((bf16[3,512,128]{2,1,0:T(8,128)(2,1)}, bf16[3,512,128]{2,1,0:T(8,128)(2,1)S(1)}, u32[]{:S(2)}, u32[]{:S(2)}) %collective-permute-start.1) | collective-permute-done | bytes 393248 | tf_op jit(solution)/shard_map/ppermute | solution.py:448
  14.9 5.0 %fusion.1 = f32[1536,576]{0,1:S(1)} fusion(bf16[1536,1536]{1,0:T(8,128)(2,1)} %param.8, bf16[1536,576]{0,1:T(8,128)(2,1)S(1)} %bitcast.23), kind=kOutput, calls=%fused_computation.11 | convolution fusion | flops 2717908992 | bytes 10027008
  19.9 1.5 convert_element_type.20
  21.3 0.0 collective-permute-done.3.refs_5_
  21.3 0.8 copy-done.9
  22.1 3.2 %collective-permute-start.5 = (bf16[3,512,128]{2,1,0:T(8,128)(2,1)S(1)}, bf16[3,512,128]{2,1,0:T(8,128)(2,1)S(1)}, u32[]{:S(2)}, u32[]{:S(2)}) collective-permute-start(bf16[3,512,128]{2,1,0:T(8,128)(2,1)S(1)} %copy-done.6), channel_id=1, source_target_pairs={{0,4},{2,6},{4,0},{6,2},{1,5},{3,7},{5,1},{7,3},{8,12},{10,14},{12... | collective-permute-start | bytes 1179656 | tf_op jit(solution)/shard_map/ppermute | solution.py:448
  25.3 0.0 collective-permute-done.2.refs_3_
  25.3 0.8 copy-done.10
  26.1 14.8 %coarse_stats.2.refs_5_ = f32[3,2,2048]{2,1,0:T(2,128)} custom-call(bf16[3,512,128]{2,1,0:T(8,128)(2,1)} %get-tuple-element.34.refs_0_, bf16[3,512,128]{2,1,0:T(8,128)(2,1)} %copy-done.7, bf16[3,512,128]{2,1,0:T(8,128)(2,1)} %copy-done.8, bf16[3,512,128]{2,1,0:T(8,128)(2,1)} %copy-done.10, bf16[3,512,128]{2,1,0:T(8,128)(2,1)} %get-tuple-element.38.refs_4_, ...), custom_call_target="tpu_custom_call" | custom-call | flops 9663676416 | bytes 2097152 | tf_op jit(solution)/shard_map/coarse_stats/pallas_call | solution.py:109
  40.9 0.6 collective-permute-start.6
  41.5 5.8 %collective-permute-start.7 = (bf16[2,8,16,384]{3,2,1,0:T(8,128)(2,1)S(1)}, bf16[2,8,16,384]{3,2,1,0:T(8,128)(2,1)S(1)}, u32[]{:S(2)}, u32[]{:S(2)}) collective-permute-start(bf16[2,8,16,384]{3,2,1,0:T(8,128)(2,1)S(1)} %get-tuple-element.69), channel_id=1, source_target_pairs={{16,32},{32,16},{48,64},{64,48},{80,96},{96,80},{17,33},{33,17},{4... | collective-permute-start | bytes 589832 | tf_op jit(solution)/shard_map/ppermute | solution.py:454
  47.3 0.0 collective-permute-done.5.refs_4_.refs_6_
  47.3 0.8 copy-done.11
  48.1 7.0 %coarse_stats.3.refs_8_ = f32[3,2,2048]{2,1,0:T(2,128)} custom-call(bf16[3,512,128]{2,1,0:T(8,128)(2,1)} %get-tuple-element.34.refs_0_, bf16[3,512,128]{2,1,0:T(8,128)(2,1)} %copy-done.7, bf16[3,512,128]{2,1,0:T(8,128)(2,1)} %copy-done.8, bf16[3,512,128]{2,1,0:T(8,128)(2,1)} %copy-done.10, bf16[3,512,128]{2,1,0:T(8,128)(2,1)} %copy-done.11, ...), custom_call_target="tpu_custom_call" | custom-call | flops 3221225472 | bytes 2097152 | tf_op jit(solution)/shard_map/coarse_stats/pallas_call | solution.py:109
  55.1 0.0 collective-permute-done.6
  55.1 0.0 collective-permute-done.7
  55.1 0.4 collective-permute-start.10
  55.5 1.6 collective-permute-start.8
  57.1 2.2 %collective-permute-start.9 = (f32[3,2,2048]{2,1,0:T(2,128)}, f32[3,2,2048]{2,1,0:T(2,128)S(1)}, u32[]{:S(2)}, u32[]{:S(2)}) collective-permute-start(f32[3,2,2048]{2,1,0:T(2,128)} %coarse_stats.3.refs_8_), channel_id=1, source_target_pairs={{0,6},{2,4},{4,2},{6,0},{1,7},{3,5},{5,3},{7,1},{8,14},{10,12},{12... | collective-permute-start | bytes 147464 | tf_op jit(solution)/shard_map/ppermute | solution.py:448
  59.3 1.9 collective-permute-done.10.refs_11_
  61.2 0.0 collective-permute-done.8.refs_9_
  61.2 1.5 collective-permute-done.9.refs_10_
  62.7 0.6 copy-done.20
  63.3 37.2 %coarse_grads.1 = (bf16[2,3,512,128]{3,2,1,0:T(8,128)(2,1)}, bf16[2,3,512,128]{3,2,1,0:T(8,128)(2,1)}, bf16[192,512]{1,0:T(8,128)(2,1)}, bf16[192,512]{1,0:T(8,1...) custom-call(bf16[3,512,128]{2,1,0:T(8,128)(2,1)} %get-tuple-element.34.refs_0_, ...), custom_call_target="tpu_custom_call" | custom-call | flops 32212254720 | bytes 4194304 | tf_op jit(solution)/shard_map/coarse_grads/pallas_call | solution.py:178
  100.5 0.1 collective-permute-start.14
  100.6 2.5 %collective-permute-done.14.refs_5_ = bf16[2,3,512,128]{3,2,1,0:T(8,128)(2,1)S(1)} collective-permute-done((bf16[2,3,512,128]{3,2,1,0:T(8,128)(2,1)}, bf16[2,3,512,128]{3,2,1,0:T(8,128)(2,1)S(1)}, u32[]{:S(2)}, u32[]{:S(2)}) %collective-permute-start.14) | collective-permute-done | bytes 786464 | tf_op jit(solution)/shard_map/ppermute | solution.py:448
  103.1 1.4 fusion
  104.4 0.5 collective-permute-start.15
  104.9 3.6 %collective-permute-start.12 = (bf16[192,512]{1,0:T(8,128)(2,1)}, bf16[192,512]{1,0:T(8,128)(2,1)S(1)}, u32[]{:S(2)}, u32[]{:S(2)}) collective-permute-start(bf16[192,512]{1,0:T(8,128)(2,1)} %get-tuple-element.46), channel_id=1, source_target_pairs={{0,4},{2,6},{4,0},{6,2},{1,5},{3,7},{5,1},{7,3},{8,12},{10,14},{12... | collective-permute-start | bytes 589832 | tf_op jit(solution)/shard_map/ppermute | solution.py:448
  108.5 1.1 collective-permute-start.13
  109.6 3.3 %collective-permute-done.11.refs_1_ = bf16[192,512]{1,0:T(8,128)(2,1)S(1)} collective-permute-done((bf16[192,512]{1,0:T(8,128)(2,1)}, bf16[192,512]{1,0:T(8,128)(2,1)S(1)}, u32[]{:S(2)}, u32[]{:S(2)}) %collective-permute-start.11) | collective-permute-done | bytes 196640 | tf_op jit(solution)/shard_map/ppermute | solution.py:448
  112.9 4.8 %collective-permute-done.12.refs_2_ = bf16[192,512]{1,0:T(8,128)(2,1)S(1)} collective-permute-done((bf16[192,512]{1,0:T(8,128)(2,1)}, bf16[192,512]{1,0:T(8,128)(2,1)S(1)}, u32[]{:S(2)}, u32[]{:S(2)}) %collective-permute-start.12) | collective-permute-done | bytes 196640 | tf_op jit(solution)/shard_map/ppermute | solution.py:448
  117.7 2.6 %collective-permute-done.13.refs_3_ = bf16[192,512]{1,0:T(8,128)(2,1)S(1)} collective-permute-done((bf16[192,512]{1,0:T(8,128)(2,1)}, bf16[192,512]{1,0:T(8,128)(2,1)S(1)}, u32[]{:S(2)}, u32[]{:S(2)}) %collective-permute-start.13) | collective-permute-done | bytes 196640 | tf_op jit(solution)/shard_map/ppermute | solution.py:448
  120.3 0.0 collective-permute-done.15.refs_6_
  120.3 0.7 copy-done.15
  120.9 0.7 copy-done.12
  121.7 6.7 %project.1 = bf16[512,1536]{1,0:T(8,128)(2,1)} custom-call(bf16[192,512]{1,0:T(8,128)(2,1)} %get-tuple-element.44.refs_0_, bf16[192,512]{1,0:T(8,128)(2,1)} %copy-done.13, bf16[192,512]{1,0:T(8,128)(2,1)} %copy-done.14, bf16[192,512]{1,0:T(8,128)(2,1)} %copy-done.15, bf16[2,3,512,128]{3,2,1,0:T(8,128)(2,1)} %get-tuple-element.48.refs_4_, ...), custom_call_target="tpu_custom_call" | custom-call | flops 2147483648 | bytes 6291456 | tf_op jit(solution)/shard_map/project/pallas_call | solution.py:392
  128.4 7.1 %all-to-all-start = ((bf16[8,64,1536]{2,1,0:T(8,128)(2,1)}), bf16[8,64,1536]{2,1,0:T(8,128)(2,1)}, u32[]{:S(2)}, u32[]{:S(2)}) async-start(bf16[8,64,1536]{2,1,0:T(8,128)(2,1)} %bitcast.27), calls=%async_computation | async-start | bytes 3145728 | tf_op jit(solution)/shard_map/all_to_all | solution.py:513
  135.5 0.1 pad_maximum_fusion
  135.7 0.1 broadcast_select_fusion
  135.8 2.1 %collective-permute-start.16 = (bf16[2,32,8,384]{3,2,1,0:T(8,128)(2,1)S(1)}, bf16[2,32,8,384]{3,2,1,0:T(8,128)(2,1)S(1)}, u32[]{:S(2)}, u32[]{:S(2)}) collective-permute-start(bf16[2,32,8,384]{3,2,1,0:T(8,128)(2,1)S(1)} %get-tuple-element.68), channel_id=1, source_target_pairs={{1,2},{2,1},{3,4},{4,3},{5,6},{6,5},{7,8},{8,7},{9,10},{10,9},{11,... | collective-permute-start | bytes 1179656 | tf_op jit(solution)/shard_map/ppermute | solution.py:454
  137.9 0.1 collective-permute-start.17
  138.0 13.6 %collective-permute-done.16 = bf16[2,32,8,384]{3,2,1,0:T(8,128)(2,1)S(1)} collective-permute-done((bf16[2,32,8,384]{3,2,1,0:T(8,128)(2,1)S(1)}, bf16[2,32,8,384]{3,2,1,0:T(8,128)(2,1)S(1)}, u32[]{:S(2)}, u32[]{:S(2)}) %collective-permute-start.16) | collective-permute-done | bytes 393248 | tf_op jit(solution)/shard_map/ppermute | solution.py:454
  151.5 0.0 collective-permute-done.17
  151.5 1.0 select_bitcast_fusion
  152.5 2.4 %all-to-all-done.in_ref = bf16[8,64,1536]{2,1,0:T(8,128)(2,1)} async-done(((bf16[8,64,1536]{2,1,0:T(8,128)(2,1)}), bf16[8,64,1536]{2,1,0:T(8,128)(2,1)}, u32[]{:S(2)}, u32[]{:S(2)}) %all-to-all-start) | async-done | bytes 1572896 | tf_op jit(solution)/shard_map/all_to_all | solution.py:513
  155.0 2.5 %spread.1.up_ref = bf16[256,384]{1,0:T(8,128)(2,1)} custom-call(bf16[8,64,1536]{2,1,0:T(8,128)(2,1)} %all-to-all-done.in_ref), custom_call_target="tpu_custom_call" | custom-call | flops 268435456 | bytes 6291456 | tf_op jit(solution)/shard_map/spread/pallas_call | solution.py:197
  157.4 9.6 %fine_grads.1 = (bf16[256,384]{1,0:T(8,128)(2,1)}, f32[512,768]{1,0:T(8,128)}, bf16[256,768]{1,0:T(8,128)(2,1)}, bf16[256,768]{1,0:T(8,128)(2,1)}) custom-call(bf16[3,256,384]{2,1,0:T(8,128)(2,1)} %bitcast.28, bf16[2,512,384]{2,1,0:T(8,128)(2,1)} %bitcast.25, bf16[2,256,384]{2,1,0:T(8,128)(2,1)} %get-tuple-element.66.low_ref, ...), custom_call_target="tpu_custom_call" | custom-call | flops 2147483648 | bytes 6291456 | tf_op jit(solution)/shard_map/fine_grads/pallas_call | solution.py:197
  167.0 4.2 %collective-permute-start.19 = (bf16[256,768]{1,0:T(8,128)(2,1)}, bf16[256,768]{1,0:T(8,128)(2,1)S(1)}, u32[]{:S(2)}, u32[]{:S(2)}) collective-permute-start(bf16[256,768]{1,0:T(8,128)(2,1)} %get-tuple-element.59), channel_id=1, source_target_pairs={{1,2},{2,1},{3,4},{4,3},{5,6},{6,5},{7,8},{8,7},{9,10},{10,9},{11,... | collective-permute-start | bytes 1179656 | tf_op jit(solution)/shard_map/ppermute | solution.py:454
  171.2 7.2 %collective-permute-done.19.outer_ref = bf16[256,768]{1,0:T(8,128)(2,1)S(1)} collective-permute-done((bf16[256,768]{1,0:T(8,128)(2,1)}, bf16[256,768]{1,0:T(8,128)(2,1)S(1)}, u32[]{:S(2)}, u32[]{:S(2)}) %collective-permute-start.19) | collective-permute-done | bytes 393248 | tf_op jit(solution)/shard_map/ppermute | solution.py:454
  178.4 0.7 copy-done.4
  179.2 2.7 %add_columns.1 = (f32[256,768]{1,0:T(8,128)}, bf16[128,768]{1,0:T(8,128)(2,1)}, bf16[128,768]{1,0:T(8,128)(2,1)}) custom-call(f32[512,768]{1,0:T(8,128)} %get-tuple-element.57.mid_ref, bf16[256,768]{1,0:T(8,128)(2,1)} %copy-done.3, bf16[256,768]{1,0:T(8,128)(2,1)} %copy-done.4), custom_call_target="tpu_custom_call" | custom-call | flops 1048576 | bytes 6291456 | tf_op jit(solution)/shard_map/add_columns/pallas_call | solution.py:197
  181.9 2.7 %collective-permute-start.20 = (bf16[128,768]{1,0:T(8,128)(2,1)}, bf16[128,768]{1,0:T(8,128)(2,1)S(1)}, u32[]{:S(2)}, u32[]{:S(2)}) collective-permute-start(bf16[128,768]{1,0:T(8,128)(2,1)} %get-tuple-element.61), channel_id=1, source_target_pairs={{0,16},{16,0},{32,48},{48,32},{64,80},{80,64},{96,112},{112,96},{1... | collective-permute-start | bytes 589832 | tf_op jit(solution)/shard_map/ppermute | solution.py:448
  184.6 2.7 %collective-permute-start.21 = (bf16[128,768]{1,0:T(8,128)(2,1)}, bf16[128,768]{1,0:T(8,128)(2,1)S(1)}, u32[]{:S(2)}, u32[]{:S(2)}) collective-permute-start(bf16[128,768]{1,0:T(8,128)(2,1)} %get-tuple-element.62), channel_id=1, source_target_pairs={{16,32},{32,16},{48,64},{64,48},{80,96},{96,80},{17,33},{33,17},{4... | collective-permute-start | bytes 589832 | tf_op jit(solution)/shard_map/ppermute | solution.py:454
  187.3 2.0 collective-permute-done.20.inner_ref
  189.3 5.5 %collective-permute-done.21.outer_ref = bf16[128,768]{1,0:T(8,128)(2,1)S(1)} collective-permute-done((bf16[128,768]{1,0:T(8,128)(2,1)}, bf16[128,768]{1,0:T(8,128)(2,1)S(1)}, u32[]{:S(2)}, u32[]{:S(2)}) %collective-permute-start.21) | collective-permute-done | bytes 196640 | tf_op jit(solution)/shard_map/ppermute | solution.py:454
  194.8 0.7 copy-done.17
  195.5 2.1 %add_rows.1 = (bf16[256,384]{1,0:T(8,128)(2,1)}, bf16[256,384]{1,0:T(8,128)(2,1)}) custom-call(f32[256,768]{1,0:T(8,128)} %get-tuple-element.60.own_ref, bf16[128,768]{1,0:T(8,128)(2,1)} %copy-done.16, bf16[128,768]{1,0:T(8,128)(2,1)} %copy-done.17), custom_call_target="tpu_custom_call" | custom-call | flops 1048576 | bytes 6291456 | tf_op jit(solution)/shard_map/add_rows/pallas_call | solution.py:197
  (43 shorter events, 0.2 us)
Async XLA Ops:
  0.6 14.2 %copy-start = (bf16[3,1536,192]{1,2,0:T(8,128)(2,1)S(1)}, bf16[3,1536,192]{1,2,0:T(8,128)(2,1)}, u32[]{:S(2)}) copy-start(bf16[3,1536,192]{1,2,0:T(8,128)(2,1)} %param.9) | copy-start | bytes 5308420
  3.1 4.2 %collective-permute-start = (bf16[3,512,128]{2,1,0:T(8,128)(2,1)}, bf16[3,512,128]{2,1,0:T(8,128)(2,1)S(1)}, u32[]{:S(2)}, u32[]{:S(2)}) collective-permute-start(bf16[3,512,128]{2,1,0:T(8,128)(2,1)} %get-tuple-element.34.refs_0_), channel_id=1, source_target_pairs={{0,1},{1,0},{2,3},{3,2},{4,5},{5,4},{6,7},{7,6},{8,9},{9,8},{10,11... | collective-permute-start | bytes 1179656 | tf_op jit(solution)/shard_map/ppermute | solution.py:448
  3.1 11.7 %collective-permute-start.1 = (bf16[3,512,128]{2,1,0:T(8,128)(2,1)}, bf16[3,512,128]{2,1,0:T(8,128)(2,1)S(1)}, u32[]{:S(2)}, u32[]{:S(2)}) collective-permute-start(bf16[3,512,128]{2,1,0:T(8,128)(2,1)} %get-tuple-element.34.refs_0_), channel_id=1, source_target_pairs={{0,8},{8,0},{1,9},{9,1},{2,10},{10,2},{3,11},{11,3},{4,12},{12,4},... | collective-permute-start | bytes 1179656 | tf_op jit(solution)/shard_map/ppermute | solution.py:448
  3.5 17.8 %collective-permute-start.3 = (bf16[3,512,128]{2,1,0:T(8,128)(2,1)}, bf16[3,512,128]{2,1,0:T(8,128)(2,1)S(1)}, u32[]{:S(2)}, u32[]{:S(2)}) collective-permute-start(bf16[3,512,128]{2,1,0:T(8,128)(2,1)} %get-tuple-element.38.refs_4_), channel_id=1, source_target_pairs={{0,2},{2,0},{4,6},{6,4},{1,3},{3,1},{5,7},{7,5},{8,10},{10,8},{12,... | collective-permute-start | bytes 1179656 | tf_op jit(solution)/shard_map/ppermute | solution.py:448
  5.1 16.2 %collective-permute-start.4 = (bf16[3,512,128]{2,1,0:T(8,128)(2,1)}, bf16[3,512,128]{2,1,0:T(8,128)(2,1)}, u32[]{:S(2)}, u32[]{:S(2)}) collective-permute-start(bf16[3,512,128]{2,1,0:T(8,128)(2,1)} %get-tuple-element.38.refs_4_), channel_id=1, source_target_pairs={{0,6},{2,4},{4,2},{6,0},{1,7},{3,5},{5,3},{7,1},{8,14},{10,12},{12... | collective-permute-start | bytes 1179656 | tf_op jit(solution)/shard_map/ppermute | solution.py:448
  7.3 12.6 %copy-start.7 = (bf16[3,512,128]{2,1,0:T(8,128)(2,1)}, bf16[3,512,128]{2,1,0:T(8,128)(2,1)S(1)}, u32[]{:S(2)}) copy-start(bf16[3,512,128]{2,1,0:T(8,128)(2,1)S(1)} %collective-permute-done.refs_1_) | copy-start | bytes 1179652
  14.8 5.0 %copy-start.8 = (bf16[3,512,128]{2,1,0:T(8,128)(2,1)}, bf16[3,512,128]{2,1,0:T(8,128)(2,1)S(1)}, u32[]{:S(2)}) copy-start(bf16[3,512,128]{2,1,0:T(8,128)(2,1)S(1)} %collective-permute-done.1.refs_2_) | copy-start | bytes 1179652
  14.8 10.4 %collective-permute-start.2 = (bf16[3,512,128]{2,1,0:T(8,128)(2,1)S(1)}, bf16[3,512,128]{2,1,0:T(8,128)(2,1)S(1)}, u32[]{:S(2)}, u32[]{:S(2)}) collective-permute-start(bf16[3,512,128]{2,1,0:T(8,128)(2,1)S(1)} %collective-permute-done.1.refs_2_), channel_id=1, source_target_pairs={{0,1},{1,0},{2,3},{3,2},{4,5},{5,4},{6,7},{7,6},{8,9},{9,8},{10,11... | collective-permute-start | bytes 1179656 | tf_op jit(solution)/shard_map/ppermute | solution.py:448
  19.9 2.2 %copy-start.6 = (bf16[3,512,128]{2,1,0:T(8,128)(2,1)S(1)}, bf16[3,512,128]{2,1,0:T(8,128)(2,1)}, u32[]{:S(2)}) copy-start(bf16[3,512,128]{2,1,0:T(8,128)(2,1)} %get-tuple-element.38.refs_4_) | copy-start | bytes 1179652
  21.3 0.8 copy-start.9
  22.1 18.8 %copy-start.2 = (bf16[3,16,16,384]{3,2,1,0:T(8,128)(2,1)S(1)}, bf16[3,16,16,384]{3,2,1,0:T(8,128)(2,1)}, u32[]{:S(2)}) copy-start(bf16[3,16,16,384]{3,2,1,0:T(8,128)(2,1)} %param.5) | copy-start | bytes 1769476
  22.1 25.2 %collective-permute-start.5 = (bf16[3,512,128]{2,1,0:T(8,128)(2,1)S(1)}, bf16[3,512,128]{2,1,0:T(8,128)(2,1)S(1)}, u32[]{:S(2)}, u32[]{:S(2)}) collective-permute-start(bf16[3,512,128]{2,1,0:T(8,128)(2,1)S(1)} %copy-done.6), channel_id=1, source_target_pairs={{0,4},{2,6},{4,0},{6,2},{1,5},{3,7},{5,1},{7,3},{8,12},{10,14},{12... | collective-permute-start | bytes 1179656 | tf_op jit(solution)/shard_map/ppermute | solution.py:448
  25.3 0.8 copy-start.10
  40.9 14.3 %collective-permute-start.6 = (bf16[2,8,16,384]{3,2,1,0:T(8,128)(2,1)S(1)}, bf16[2,8,16,384]{3,2,1,0:T(8,128)(2,1)S(1)}, u32[]{:S(2)}, u32[]{:S(2)}) collective-permute-start(bf16[2,8,16,384]{3,2,1,0:T(8,128)(2,1)S(1)} %get-tuple-element.70), channel_id=1, source_target_pairs={{0,16},{16,0},{32,48},{48,32},{64,80},{80,64},{96,112},{112,96},{1... | collective-permute-start | bytes 589832 | tf_op jit(solution)/shard_map/ppermute | solution.py:448
  41.5 13.6 %collective-permute-start.7 = (bf16[2,8,16,384]{3,2,1,0:T(8,128)(2,1)S(1)}, bf16[2,8,16,384]{3,2,1,0:T(8,128)(2,1)S(1)}, u32[]{:S(2)}, u32[]{:S(2)}) collective-permute-start(bf16[2,8,16,384]{3,2,1,0:T(8,128)(2,1)S(1)} %get-tuple-element.69), channel_id=1, source_target_pairs={{16,32},{32,16},{48,64},{64,48},{80,96},{96,80},{17,33},{33,17},{4... | collective-permute-start | bytes 589832 | tf_op jit(solution)/shard_map/ppermute | solution.py:454
  47.3 0.8 copy-start.11
  55.1 6.0 %collective-permute-start.10 = (f32[3,2,2048]{2,1,0:T(2,128)}, f32[3,2,2048]{2,1,0:T(2,128)S(1)}, u32[]{:S(2)}, u32[]{:S(2)}) collective-permute-start(f32[3,2,2048]{2,1,0:T(2,128)} %coarse_stats.3.refs_8_), channel_id=1, source_target_pairs={{0,4},{2,6},{4,0},{6,2},{1,5},{3,7},{5,1},{7,3},{8,12},{10,14},{12... | collective-permute-start | bytes 147464 | tf_op jit(solution)/shard_map/ppermute | solution.py:448
  55.5 5.6 %collective-permute-start.8 = (f32[3,2,2048]{2,1,0:T(2,128)}, f32[3,2,2048]{2,1,0:T(2,128)S(1)}, u32[]{:S(2)}, u32[]{:S(2)}) collective-permute-start(f32[3,2,2048]{2,1,0:T(2,128)} %coarse_stats.3.refs_8_), channel_id=1, source_target_pairs={{0,2},{2,0},{4,6},{6,4},{1,3},{3,1},{5,7},{7,5},{8,10},{10,8},{12,... | collective-permute-start | bytes 147464 | tf_op jit(solution)/shard_map/ppermute | solution.py:448
  57.1 5.5 %collective-permute-start.9 = (f32[3,2,2048]{2,1,0:T(2,128)}, f32[3,2,2048]{2,1,0:T(2,128)S(1)}, u32[]{:S(2)}, u32[]{:S(2)}) collective-permute-start(f32[3,2,2048]{2,1,0:T(2,128)} %coarse_stats.3.refs_8_), channel_id=1, source_target_pairs={{0,6},{2,4},{4,2},{6,0},{1,7},{3,5},{5,3},{7,1},{8,14},{10,12},{12... | collective-permute-start | bytes 147464 | tf_op jit(solution)/shard_map/ppermute | solution.py:448
  61.2 1.5 copy-start.18
  61.2 1.5 copy-start.19
  62.6 0.6 copy-start.20
  100.5 2.6 %collective-permute-start.14 = (bf16[2,3,512,128]{3,2,1,0:T(8,128)(2,1)}, bf16[2,3,512,128]{3,2,1,0:T(8,128)(2,1)S(1)}, u32[]{:S(2)}, u32[]{:S(2)}) collective-permute-start(bf16[2,3,512,128]{3,2,1,0:T(8,128)(2,1)} %get-tuple-element.49), channel_id=1, source_target_pairs={{0,1},{1,0},{2,3},{3,2},{4,5},{5,4},{6,7},{7,6},{8,9},{9,8},{10,11... | collective-permute-start | bytes 2359304 | tf_op jit(solution)/shard_map/ppermute | solution.py:448
  103.1 17.9 %copy-start.5 = (bf16[2,3,512,128]{3,2,1,0:T(8,128)(2,1)}, bf16[2,3,512,128]{3,2,1,0:T(8,128)(2,1)S(1)}, u32[]{:S(2)}) copy-start(bf16[2,3,512,128]{3,2,1,0:T(8,128)(2,1)S(1)} %collective-permute-done.14.refs_5_) | copy-start | bytes 2359300
  104.4 15.8 %collective-permute-start.15 = (bf16[3,512,128]{2,1,0:T(8,128)(2,1)S(1)}, bf16[3,512,128]{2,1,0:T(8,128)(2,1)S(1)}, u32[]{:S(2)}, u32[]{:S(2)}) collective-permute-start(bf16[3,512,128]{2,1,0:T(8,128)(2,1)S(1)} %fusion), channel_id=1, source_target_pairs={{0,8},{8,0},{1,9},{9,1},{2,10},{10,2},{3,11},{11,3},{4,12},{12,4},... | collective-permute-start | bytes 1179656 | tf_op jit(solution)/shard_map/ppermute | solution.py:448
  104.9 8.0 %collective-permute-start.11 = (bf16[192,512]{1,0:T(8,128)(2,1)}, bf16[192,512]{1,0:T(8,128)(2,1)S(1)}, u32[]{:S(2)}, u32[]{:S(2)}) collective-permute-start(bf16[192,512]{1,0:T(8,128)(2,1)} %get-tuple-element.45), channel_id=1, source_target_pairs={{0,2},{2,0},{4,6},{6,4},{1,3},{3,1},{5,7},{7,5},{8,10},{10,8},{12,... | collective-permute-start | bytes 589832 | tf_op jit(solution)/shard_map/ppermute | solution.py:448
  104.9 12.8 %collective-permute-start.12 = (bf16[192,512]{1,0:T(8,128)(2,1)}, bf16[192,512]{1,0:T(8,128)(2,1)S(1)}, u32[]{:S(2)}, u32[]{:S(2)}) collective-permute-start(bf16[192,512]{1,0:T(8,128)(2,1)} %get-tuple-element.46), channel_id=1, source_target_pairs={{0,4},{2,6},{4,0},{6,2},{1,5},{3,7},{5,1},{7,3},{8,12},{10,14},{12... | collective-permute-start | bytes 589832 | tf_op jit(solution)/shard_map/ppermute | solution.py:448
  108.5 11.7 %collective-permute-start.13 = (bf16[192,512]{1,0:T(8,128)(2,1)}, bf16[192,512]{1,0:T(8,128)(2,1)S(1)}, u32[]{:S(2)}, u32[]{:S(2)}) collective-permute-start(bf16[192,512]{1,0:T(8,128)(2,1)} %get-tuple-element.47), channel_id=1, source_target_pairs={{0,6},{2,4},{4,2},{6,0},{1,7},{3,5},{5,3},{7,1},{8,14},{10,12},{12... | collective-permute-start | bytes 589832 | tf_op jit(solution)/shard_map/ppermute | solution.py:448
  112.9 7.4 %copy-start.13 = (bf16[192,512]{1,0:T(8,128)(2,1)}, bf16[192,512]{1,0:T(8,128)(2,1)S(1)}, u32[]{:S(2)}) copy-start(bf16[192,512]{1,0:T(8,128)(2,1)S(1)} %collective-permute-done.11.refs_1_) | copy-start | bytes 589828
  117.7 2.6 %copy-start.14 = (bf16[192,512]{1,0:T(8,128)(2,1)}, bf16[192,512]{1,0:T(8,128)(2,1)S(1)}, u32[]{:S(2)}) copy-start(bf16[192,512]{1,0:T(8,128)(2,1)S(1)} %collective-permute-done.12.refs_2_) | copy-start | bytes 589828
  120.3 0.7 copy-start.15
  120.9 0.7 copy-start.12
  128.4 7.2 %slice-start = ((bf16[3,16,16,384]{3,2,1,0:T(8,128)(2,1)}), bf16[2,16,16,384]{3,2,1,0:T(8,128)(2,1)S(1)}, s32[]{:S(2)}) async-start(bf16[3,16,16,384]{3,2,1,0:T(8,128)(2,1)} %param.5), calls=%async_computation.1 | async-start | bytes 786432 | tf_op jit(solution)/shard_map/slice | solution.py:496
  128.4 26.6 %all-to-all-start = ((bf16[8,64,1536]{2,1,0:T(8,128)(2,1)}), bf16[8,64,1536]{2,1,0:T(8,128)(2,1)}, u32[]{:S(2)}, u32[]{:S(2)}) async-start(bf16[8,64,1536]{2,1,0:T(8,128)(2,1)} %bitcast.27), calls=%async_computation | async-start | bytes 3145728 | tf_op jit(solution)/shard_map/all_to_all | solution.py:513
  135.7 21.8 %copy-start.1 = (bf16[2,32,16,384]{3,2,1,0:T(8,128)(2,1)}, bf16[2,32,16,384]{3,2,1,0:T(8,128)(2,1)S(1)}, u32[]{:S(2)}) copy-start(bf16[2,32,16,384]{3,2,1,0:T(8,128)(2,1)S(1)} %pad_maximum_fusion) | copy-start | bytes 2359300
  135.8 15.8 %collective-permute-start.16 = (bf16[2,32,8,384]{3,2,1,0:T(8,128)(2,1)S(1)}, bf16[2,32,8,384]{3,2,1,0:T(8,128)(2,1)S(1)}, u32[]{:S(2)}, u32[]{:S(2)}) collective-permute-start(bf16[2,32,8,384]{3,2,1,0:T(8,128)(2,1)S(1)} %get-tuple-element.68), channel_id=1, source_target_pairs={{1,2},{2,1},{3,4},{4,3},{5,6},{6,5},{7,8},{8,7},{9,10},{10,9},{11,... | collective-permute-start | bytes 1179656 | tf_op jit(solution)/shard_map/ppermute | solution.py:454
  137.9 13.7 %collective-permute-start.17 = (bf16[2,32,8,384]{3,2,1,0:T(8,128)(2,1)S(1)}, bf16[2,32,8,384]{3,2,1,0:T(8,128)(2,1)S(1)}, u32[]{:S(2)}, u32[]{:S(2)}) collective-permute-start(bf16[2,32,8,384]{3,2,1,0:T(8,128)(2,1)S(1)} %get-tuple-element.67), channel_id=1, source_target_pairs={{0,1},{1,0},{2,3},{3,2},{4,5},{5,4},{6,7},{7,6},{8,9},{9,8},{10,11... | collective-permute-start | bytes 1179656 | tf_op jit(solution)/shard_map/ppermute | solution.py:448
  167.0 4.2 %collective-permute-start.18 = (bf16[256,768]{1,0:T(8,128)(2,1)}, bf16[256,768]{1,0:T(8,128)(2,1)S(1)}, u32[]{:S(2)}, u32[]{:S(2)}) collective-permute-start(bf16[256,768]{1,0:T(8,128)(2,1)} %get-tuple-element.58), channel_id=1, source_target_pairs={{0,1},{1,0},{2,3},{3,2},{4,5},{5,4},{6,7},{7,6},{8,9},{9,8},{10,11... | collective-permute-start | bytes 1179656 | tf_op jit(solution)/shard_map/ppermute | solution.py:448
  167.0 11.4 %collective-permute-start.19 = (bf16[256,768]{1,0:T(8,128)(2,1)}, bf16[256,768]{1,0:T(8,128)(2,1)S(1)}, u32[]{:S(2)}, u32[]{:S(2)}) collective-permute-start(bf16[256,768]{1,0:T(8,128)(2,1)} %get-tuple-element.59), channel_id=1, source_target_pairs={{1,2},{2,1},{3,4},{4,3},{5,6},{6,5},{7,8},{8,7},{9,10},{10,9},{11,... | collective-permute-start | bytes 1179656 | tf_op jit(solution)/shard_map/ppermute | solution.py:454
  171.2 7.2 %copy-start.3 = (bf16[256,768]{1,0:T(8,128)(2,1)}, bf16[256,768]{1,0:T(8,128)(2,1)S(1)}, u32[]{:S(2)}) copy-start(bf16[256,768]{1,0:T(8,128)(2,1)S(1)} %collective-permute-done.18.inner_ref) | copy-start | bytes 1179652
  178.4 0.7 copy-start.4
  181.9 7.4 %collective-permute-start.20 = (bf16[128,768]{1,0:T(8,128)(2,1)}, bf16[128,768]{1,0:T(8,128)(2,1)S(1)}, u32[]{:S(2)}, u32[]{:S(2)}) collective-permute-start(bf16[128,768]{1,0:T(8,128)(2,1)} %get-tuple-element.61), channel_id=1, source_target_pairs={{0,16},{16,0},{32,48},{48,32},{64,80},{80,64},{96,112},{112,96},{1... | collective-permute-start | bytes 589832 | tf_op jit(solution)/shard_map/ppermute | solution.py:448
  184.6 10.2 %collective-permute-start.21 = (bf16[128,768]{1,0:T(8,128)(2,1)}, bf16[128,768]{1,0:T(8,128)(2,1)S(1)}, u32[]{:S(2)}, u32[]{:S(2)}) collective-permute-start(bf16[128,768]{1,0:T(8,128)(2,1)} %get-tuple-element.62), channel_id=1, source_target_pairs={{16,32},{32,16},{48,64},{64,48},{80,96},{96,80},{17,33},{33,17},{4... | collective-permute-start | bytes 589832 | tf_op jit(solution)/shard_map/ppermute | solution.py:454
  189.3 5.5 %copy-start.16 = (bf16[128,768]{1,0:T(8,128)(2,1)}, bf16[128,768]{1,0:T(8,128)(2,1)S(1)}, u32[]{:S(2)}) copy-start(bf16[128,768]{1,0:T(8,128)(2,1)S(1)} %collective-permute-done.20.inner_ref) | copy-start | bytes 589828
  194.8 0.7 copy-start.17

commit v5 on v4

--- a/solution.py
+++ b/solution.py
@@ -240,19 +240,46 @@
     return jnp.concatenate([ref[which, :, lanes] for ref in refs], axis=0)
 
 
-def fine_grads(own_qkv, ext_kv, own_up, rows, columns):
+def fine_shares(own_qkv, ext_kv, rows, columns):
     _, own, width = own_qkv.shape
-    sizes = [ref.shape[1] for ref in ext_kv]
-    places = [sum(sizes[:i]) for i in range(len(sizes))]
-
-    def body(q_ref, mid_ref, low_ref, high_ref, up_ref, q_out, mid_out, *rest):
-        inner_out, outer_out, bias_ref = rest
-        first = lax.axis_index("c") == 0
+    heads = width // HD
+
+    def body(q_ref, mid_ref, low_ref, high_ref, out_ref, bias_ref):
         fill_bias(bias_ref, own, rows, columns)
         ext = (mid_ref, low_ref, high_ref)
         for pair, lanes in pairs_of(width):
             key = stacked(ext, 0, lanes)
-            key_t = key.T
+            for side in range(2):
+                query = half(q_ref[0, :, lanes], side) * BF16(SCALE)
+                score = nt(key, query) + bias_ref[...]
+                share = jnp.exp(score - jnp.max(score, axis=0, keepdims=True))
+                total = jnp.sum(share, axis=0, keepdims=True)
+                out_ref[2 * pair + side] = (share * (1.0 / total)).astype(BF16)
+
+    return whole_call(
+        body,
+        jax.ShapeDtypeStruct((heads, SIDE * SIDE, own), BF16),
+        "fine_shares",
+        1 << 30,
+        [pltpu.VMEM((SIDE * SIDE, own), F32)],
+        own_qkv,
+        *ext_kv,
+    )
+
+
+def fine_grads(own_qkv, ext_kv, own_up, shares, rows, columns):
+    _, own, width = own_qkv.shape
+    edge, side_size, corner = RIM * columns, RIM * rows, RIM * RIM
+    tall = side_size + 2 * corner
+    base = 2 * edge + own
+    sizes = [edge, edge, side_size, side_size, corner, corner, corner, corner]
+
+    def body(q_ref, mid_ref, low_ref, high_ref, up_ref, share_ref, q_out, own_out, *outs):
+        first = lax.axis_index("c") == 0
+        upper = lax.axis_index("zh") == 0
+        ext = (mid_ref, low_ref, high_ref)
+        for pair, lanes in pairs_of(width):
+            key_t = stacked(ext, 0, lanes).T
             value = stacked(ext, 1, lanes)
             parts = []
             key_sum = jnp.zeros((SIDE * SIDE, 128), F32)
@@ -260,95 +287,99 @@
             for side in range(2):
                 query = half(q_ref[0, :, lanes], side) * BF16(SCALE)
                 up = half(up_ref[:, lanes], side)
-                score = nt(key, query) + bias_ref[...]
+                rounded = share_ref[2 * pair + side]
+                share = rounded.astype(F32)
                 product = nt(value, up)
-                share = jnp.exp(score - jnp.max(score, axis=0, keepdims=True))
                 total = jnp.sum(share, axis=0, keepdims=True)
                 delta = jnp.sum(share * product, axis=0, keepdims=True) / total
-                share = share * (1.0 / total)
                 grads = (share * (product - delta)).astype(BF16)
                 key_sum += nn(grads, query)
-                value_sum += nn(share.astype(BF16), up)
+                value_sum += nn(rounded, up)
                 parts.append(nn(key_t[side * HD : side * HD + HD], grads))
             q_out[:, lanes] = (jnp.concatenate(parts, axis=0).T * SCALE).astype(BF16)
             right = slice(width + pair * 128, width + pair * 128 + 128)
             for at, total in ((lanes, key_sum), (right, value_sum)):
-                mid, low, high = [
-                    total[place : place + size] for place, size in zip(places, sizes)
-                ]
-                mid_out[:, at] = mid
-                inner_out[:, at] = jnp.where(first, high, low).astype(BF16)
-                outer_out[:, at] = jnp.where(first, low, high).astype(BF16)
+                top, bottom = total[:edge], total[edge + own : base]
+                low, high = total[base : base + tall], total[base + tall :]
+                own_out[:, at] = total[edge : edge + own]
+                wings = [jnp.where(first, high, low), jnp.where(first, low, high)]
+                found = [jnp.where(upper, bottom, top), jnp.where(upper, top, bottom)]
+                found += [wing[corner : corner + side_size] for wing in wings]
+                for wing in wings:
+                    above, below = wing[:corner], wing[corner + side_size :]
+                    found += [jnp.where(upper, below, above), jnp.where(upper, above, below)]
+                for out, piece in zip(outs, found):
+                    out[:, at] = piece.astype(BF16)
 
     return whole_call(
         body,
-        [jax.ShapeDtypeStruct((own, width), BF16)]
-        + [
-            jax.ShapeDtypeStruct((size, 2 * width), BF16 if i else F32)
-            for i, size in enumerate(sizes)
-        ],
+        [jax.ShapeDtypeStruct((own, width), BF16), jax.ShapeDtypeStruct((own, 2 * width), F32)]
+        + [jax.ShapeDtypeStruct((size, 2 * width), BF16) for size in sizes],
         "fine_grads",
         2 << 30,
-        [pltpu.VMEM((SIDE * SIDE, own), F32)],
+        [],
         own_qkv,
         *ext_kv,
         own_up,
-    )
-
-
-def add_columns(mid, inner, outer, columns):
-    cells, wide = mid.shape
-    tall = cells // columns
-    edge = RIM * columns
-
-    def body(mid_ref, inner_ref, outer_ref, own_out, inner_out, outer_out):
-        first = lax.axis_index("c") == 0
-        inner = inner_ref[...].astype(F32).reshape(tall, RIM, wide)
-        outer = outer_ref[...].astype(F32).reshape(tall, RIM, wide)
-        left, right = jnp.where(first, outer, inner), jnp.where(first, inner, outer)
-        both = jnp.concatenate([left, right], axis=1).reshape(cells, wide)
-        total = mid_ref[...] + both
-        top, bottom = total[:edge], total[cells - edge :]
-        upper = lax.axis_index("zh") == 0
-        own_out[...] = total[edge : cells - edge]
-        inner_out[...] = jnp.where(upper, bottom, top).astype(BF16)
-        outer_out[...] = jnp.where(upper, top, bottom).astype(BF16)
-
-    return whole_call(
-        body,
-        [jax.ShapeDtypeStruct((cells - 2 * edge, wide), F32)]
-        + [jax.ShapeDtypeStruct((edge, wide), BF16)] * 2,
-        "add_columns",
-        1 << 20,
-        [],
-        mid,
-        inner,
-        outer,
-    )
-
-
-def add_rows(own, inner, outer):
+        shares,
+    )
+
+
+def sent_around(pieces):
+    tall, wide = lax.axis_size(ROW), lax.axis_size(COL)
+
+    def partner(index, kind, count):
+        if kind == "same":
+            return index
+        other = index ^ 1 if kind == "inner" else ((index + 1) ^ 1) - 1
+        return other if 0 <= other < count else None
+
+    kinds = [("inner", "same"), ("outer", "same"), ("same", "inner"), ("same", "outer")]
+    kinds += [(down, across) for across in ("inner", "outer") for down in ("inner", "outer")]
+    arrived = []
+    for piece, (down, across) in zip(pieces, kinds):
+        pairs = []
+        for row in range(tall):
+            for column in range(wide):
+                there = partner(row, down, tall), partner(column, across, wide)
+                if None not in there:
+                    pairs.append((row * wide + column, there[0] * wide + there[1]))
+        arrived.append(lax.ppermute(piece, ROW + COL, pairs))
+    return arrived
+
+
+def add_arrived(own, arrived, rows, columns):
     cells, wide = own.shape
     width = wide // 2
 
-    def body(own_ref, inner_ref, outer_ref, k_out, v_out):
+    def body(own_ref, *rest):
+        first = lax.axis_index("c") == 0
         upper = lax.axis_index("zh") == 0
-        inner = inner_ref[...].astype(F32)
-        outer = outer_ref[...].astype(F32)
-        above, below = jnp.where(upper, outer, inner), jnp.where(upper, inner, outer)
-        total = own_ref[...] + jnp.concatenate([above, below], axis=0)
+        row_in, row_out, side_in, side_out, *corners = [
+            ref[...].astype(F32) for ref in rest[:-2]
+        ]
+        k_out, v_out = rest[-2:]
+
+        def placed(inner, outer):
+            above, below = jnp.where(upper, outer, inner), jnp.where(upper, inner, outer)
+            return jnp.concatenate([above, below], axis=0)
+
+        total = own_ref[...] + placed(row_in, row_out)
+        inner = (side_in + placed(*corners[:2])).reshape(rows, RIM, wide)
+        outer = (side_out + placed(*corners[2:])).reshape(rows, RIM, wide)
+        left, right = jnp.where(first, outer, inner), jnp.where(first, inner, outer)
+        total += jnp.concatenate([left, right], axis=1).reshape(cells, wide)
         k_out[...] = total[:, :width].astype(BF16)
         v_out[...] = total[:, width:].astype(BF16)
 
     return whole_call(
         body,
         [jax.ShapeDtypeStruct((cells, width), BF16)] * 2,
-        "add_rows",
+        "add_arrived",
         1 << 20,
         [],
         own,
-        inner,
-        outer,
+        *arrived,
     )
 
 
@@ -484,6 +515,7 @@
     joint = lax.dot_general(
         qkv_weight, merge_weight, (((1,), (1,)), ((), ())), preferred_element_type=F32
     ).astype(BF16).reshape(3 * group, wide)
+    across, joint = lax.optimization_barrier((across, joint))
     corner = swapped(across, "c")
     *near, joint = lax.optimization_barrier((*near, joint))
     far = swapped(near[0], "y", 2)
@@ -515,13 +547,12 @@
     tall = jnp.concatenate([low, fine_qkv[1:], high], axis=1)
     low, high = placed_rims(*sent_rims(tall, COL, "c", 2), "c")
     ext_kv = [array.reshape(2, -1, width) for array in (tall, low, high)]
+    shares = fine_shares(own_qkv, ext_kv, rows, columns)
+    pieces, shares = lax.optimization_barrier((pieces, shares))
     own_up = spread(pieces, coarse_columns)
 
-    grad_query, mid, inner, outer = fine_grads(own_qkv, ext_kv, own_up, rows, columns)
-    inner, outer = exchanged(inner, outer, COL)
-    middle, inner, outer = add_columns(mid, inner, outer, columns)
-    inner, outer = exchanged(inner, outer, ROW)
-    grad_key, grad_value = add_rows(middle, inner, outer)
+    grad_query, middle, *rims = fine_grads(own_qkv, ext_kv, own_up, shares, rows, columns)
+    grad_key, grad_value = add_arrived(middle, sent_around(rims), rows, columns)
     shape = (rows, columns, width)
     return grad_query.reshape(shape), grad_key.reshape(shape), grad_value.reshape(shape)
 

time: 200 us -> 203 us (1.015)
  starting transfers between devices: 42.1 us -> 52.2 us
  waiting for transfers between devices: 54.8 us -> 47.1 us
  Pallas kernels: 85 us -> 88.7 us
    ppermute x0 -> x8, starting transfers between devices: none -> 19.2 us  [sent_around(): arrived.append(lax.ppermute(piece, ROW + COL, pairs))]
    ppermute x4 -> x2, waiting for transfers between devices: 26.3 us -> 13.6 us  [exchanged(): return (swapped(inner, axis), lax.ppermute(outer, axis, beyond))]
    ppermute x0 -> x8, waiting for transfers between devices: none -> 12.2 us  [sent_around(): arrived.append(lax.ppermute(piece, ROW + COL, pairs))]
    ppermute x4 -> x2, starting transfers between devices: 14.7 us -> 8.79 us  [exchanged(): return (swapped(inner, axis), lax.ppermute(outer, axis, beyond))]
    ppermute x18 -> x16, waiting for transfers between devices: 26 us -> 21.2 us  [swapped(): lax.ppermute(array, axis, [(i, i ^ flip) for i in range(lax.axis_size(axi...]
    pallas_call x5, Pallas kernels: 19.3 us -> 22.9 us  [whole_call(): pl.pallas_call(body, out_shape=out_shape, scratch_shapes=scratch, name=na...]
    ppermute x18 -> x16, starting transfers between devices: 20.3 us -> 17.1 us  [swapped(): lax.ppermute(array, axis, [(i, i ^ flip) for i in range(lax.axis_size(axi...]
    all_to_all x1, waiting for transfers between devices: 2.44 us -> 0.01 us  [shards(): pieces = lax.all_to_all(projected.reshape(count, -1, wide), ROW, 0, 0)]
  transfers between devices with their start and end apart: 23 -> 27, of which waited for: 12 -> 13; matrix products, arithmetic and copies ran while one was open for 4% -> 4% of each run, Pallas kernels for 11% -> 14%
where the time goes in v5:
time: 203 us; the launch traced here: 202 us
  Pallas kernels  88.7 us (44%)
  starting transfers between devices  52.2 us (26%)
  waiting for transfers between devices  47.1 us (23%)
  matrix products  4.96 us (2%)
  other arithmetic  4.18 us (2%)
  local copies, waits for them, and re-layouts  3.8 us (2%)
    pallas_call x1, Pallas kernels, coarse_grads(): pl.pallas_call(body, grid=(heads, blocks), in_specs=[pl.BlockSpec((1, tok...  37.2 us
    pallas_call x5, Pallas kernels, whole_call(): pl.pallas_call(body, out_shape=out_shape, scratch_shapes=scratch, name=na...  22.9 us
    pallas_call x2, Pallas kernels, coarse_stats(): pl.pallas_call(body, grid=(heads, number), in_specs=[pl.BlockSpec((1, tok...  21.8 us
    ppermute x16, waiting for transfers between devices, swapped(): lax.ppermute(array, axis, [(i, i ^ flip) for i in range(lax.axis_size(axi...  21.2 us
    ppermute x8, starting transfers between devices, sent_around(): arrived.append(lax.ppermute(piece, ROW + COL, pairs))  19.2 us
    ppermute x16, starting transfers between devices, swapped(): lax.ppermute(array, axis, [(i, i ^ flip) for i in range(lax.axis_size(axi...  17.1 us
    ppermute x2, waiting for transfers between devices, exchanged(): return (swapped(inner, axis), lax.ppermute(outer, axis, beyond))  13.6 us
    ppermute x8, waiting for transfers between devices, sent_around(): arrived.append(lax.ppermute(piece, ROW + COL, pairs))  12.2 us
  transfers between devices with their start and end apart: 27, of which 13 were waited for; matrix products, arithmetic and copies ran while one was open for 4% of the time, Pallas kernels for 14%

profile of v5, /device:TPU:96, one launch (start us, length us, event | category | flops | bytes accessed | tf_op | source)
XLA Modules:
  0.0 201.9 jit_solution(12769133571266485637)
XLA Ops:
  0.6 0.0 copy-start
  0.6 2.4 %prepare.1 = (bf16[3,512,128]{2,1,0:T(8,128)(2,1)}, bf16[3,512,128]{2,1,0:T(8,128)(2,1)}) custom-call(bf16[3,512,192]{2,1,0:T(8,128)(2,1)} %bitcast.31, bf16[512,192]{1,0:T(8,128)(2,1)} %bitcast.32), custom_call_target="tpu_custom_call" | custom-call | flops 1048576 | bytes 6291456 | tf_op jit(solution)/shard_map/prepare/pallas_call | solution.py:197
  3.1 0.0 collective-permute-start
  3.1 0.4 collective-permute-start.1
  3.5 1.6 collective-permute-start.3
  5.1 2.2 %collective-permute-start.4 = (bf16[3,512,128]{2,1,0:T(8,128)(2,1)}, bf16[3,512,128]{2,1,0:T(8,128)(2,1)}, u32[]{:S(2)}, u32[]{:S(2)}) collective-permute-start(bf16[3,512,128]{2,1,0:T(8,128)(2,1)} %get-tuple-element.47.refs_4_), channel_id=1, source_target_pairs={{0,6},{2,4},{4,2},{6,0},{1,7},{3,5},{5,3},{7,1},{8,14},{10,12},{12... | collective-permute-start | bytes 1179656 | tf_op jit(solution)/shard_map/ppermute | solution.py:479
  7.3 5.0 %fusion.1 = f32[1536,576]{0,1:S(1)} fusion(bf16[1536,1536]{1,0:T(8,128)(2,1)} %param.8, bf16[1536,576]{0,1:T(8,128)(2,1)S(1)} %bitcast.23), kind=kOutput, calls=%fused_computation.11 | convolution fusion | flops 2717908992 | bytes 10027008
  12.2 1.5 convert_element_type.20
  13.7 1.1 collective-permute-done.1.refs_2_
  14.8 0.2 collective-permute-done.3.refs_5_
  15.1 2.5 %collective-permute-done.4.refs_6_.refs_7_ = bf16[3,512,128]{2,1,0:T(8,128)(2,1)} collective-permute-done((bf16[3,512,128]{2,1,0:T(8,128)(2,1)}, bf16[3,512,128]{2,1,0:T(8,128)(2,1)}, u32[]{:S(2)}, u32[]{:S(2)}) %collective-permute-start.4) | collective-permute-done | bytes 393248 | tf_op jit(solution)/shard_map/ppermute | solution.py:479
  17.6 1.7 collective-permute-start.5
  19.3 0.7 copy-done.7
  20.0 14.8 %coarse_stats.2.refs_5_ = f32[3,2,2048]{2,1,0:T(2,128)} custom-call(bf16[3,512,128]{2,1,0:T(8,128)(2,1)} %get-tuple-element.41.refs_0_, bf16[3,512,128]{2,1,0:T(8,128)(2,1)} %copy-done.5, bf16[3,512,128]{2,1,0:T(8,128)(2,1)} %copy-done.6, bf16[3,512,128]{2,1,0:T(8,128)(2,1)} %copy-done.7, bf16[3,512,128]{2,1,0:T(8,128)(2,1)} %get-tuple-element.47.refs_4_, ...), custom_call_target="tpu_custom_call" | custom-call | flops 9663676416 | bytes 2097152 | tf_op jit(solution)/shard_map/coarse_stats/pallas_call | solution.py:109
  34.8 0.6 collective-permute-start.6
  35.4 5.9 %collective-permute-start.7 = (bf16[2,8,16,384]{3,2,1,0:T(8,128)(2,1)S(1)}, bf16[2,8,16,384]{3,2,1,0:T(8,128)(2,1)S(1)}, u32[]{:S(2)}, u32[]{:S(2)}) collective-permute-start(bf16[2,8,16,384]{3,2,1,0:T(8,128)(2,1)S(1)} %get-tuple-element.83), channel_id=1, source_target_pairs={{16,32},{32,16},{48,64},{64,48},{80,96},{96,80},{17,33},{33,17},{4... | collective-permute-start | bytes 589832 | tf_op jit(solution)/shard_map/ppermute | solution.py:485
  41.3 0.7 copy-done.8
  42.0 7.0 %coarse_stats.3.refs_8_ = f32[3,2,2048]{2,1,0:T(2,128)} custom-call(bf16[3,512,128]{2,1,0:T(8,128)(2,1)} %get-tuple-element.41.refs_0_, bf16[3,512,128]{2,1,0:T(8,128)(2,1)} %copy-done.5, bf16[3,512,128]{2,1,0:T(8,128)(2,1)} %copy-done.6, bf16[3,512,128]{2,1,0:T(8,128)(2,1)} %copy-done.7, bf16[3,512,128]{2,1,0:T(8,128)(2,1)} %copy-done.8, ...), custom_call_target="tpu_custom_call" | custom-call | flops 3221225472 | bytes 2097152 | tf_op jit(solution)/shard_map/coarse_stats/pallas_call | solution.py:109
  49.1 0.0 collective-permute-done.6
  49.1 1.4 collective-permute-start.8
  50.5 1.1 collective-permute-start.9
  51.6 1.7 collective-permute-start.10
  53.3 0.6 collective-permute-done.8.refs_9_
  53.9 2.1 %collective-permute-done.9.refs_10_ = f32[3,2,2048]{2,1,0:T(2,128)S(1)} collective-permute-done((f32[3,2,2048]{2,1,0:T(2,128)}, f32[3,2,2048]{2,1,0:T(2,128)S(1)}, u32[]{:S(2)}, u32[]{:S(2)}) %collective-permute-start.9) | collective-permute-done | bytes 49184 | tf_op jit(solution)/shard_map/ppermute | solution.py:479
  56.0 1.4 collective-permute-done.10.refs_11_
  57.4 0.6 copy-done.20
  58.0 37.2 %coarse_grads.1 = (bf16[2,3,512,128]{3,2,1,0:T(8,128)(2,1)}, bf16[2,3,512,128]{3,2,1,0:T(8,128)(2,1)}, bf16[192,512]{1,0:T(8,128)(2,1)}, bf16[192,512]{1,0:T(8,1...) custom-call(bf16[3,512,128]{2,1,0:T(8,128)(2,1)} %get-tuple-element.41.refs_0_, ...), custom_call_target="tpu_custom_call" | custom-call | flops 32212254720 | bytes 4194304 | tf_op jit(solution)/shard_map/coarse_grads/pallas_call | solution.py:178
  95.2 0.1 collective-permute-start.14
  95.3 2.5 %collective-permute-done.14.refs_5_ = bf16[2,3,512,128]{3,2,1,0:T(8,128)(2,1)S(1)} collective-permute-done((bf16[2,3,512,128]{3,2,1,0:T(8,128)(2,1)}, bf16[2,3,512,128]{3,2,1,0:T(8,128)(2,1)S(1)}, u32[]{:S(2)}, u32[]{:S(2)}) %collective-permute-start.14) | collective-permute-done | bytes 786464 | tf_op jit(solution)/shard_map/ppermute | solution.py:479
  97.8 1.4 fusion
  99.2 1.7 collective-permute-start.15
  100.9 3.6 %collective-permute-start.12 = (bf16[192,512]{1,0:T(8,128)(2,1)}, bf16[192,512]{1,0:T(8,128)(2,1)}, u32[]{:S(2)}, u32[]{:S(2)}) collective-permute-start(bf16[192,512]{1,0:T(8,128)(2,1)} %get-tuple-element.55), channel_id=1, source_target_pairs={{0,4},{2,6},{4,0},{6,2},{1,5},{3,7},{5,1},{7,3},{8,12},{10,14},{12... | collective-permute-start | bytes 589832 | tf_op jit(solution)/shard_map/ppermute | solution.py:479
  104.5 1.1 collective-permute-start.13
  105.6 3.4 %collective-permute-done.11.refs_1_ = bf16[192,512]{1,0:T(8,128)(2,1)} collective-permute-done((bf16[192,512]{1,0:T(8,128)(2,1)}, bf16[192,512]{1,0:T(8,128)(2,1)}, u32[]{:S(2)}, u32[]{:S(2)}) %collective-permute-start.11) | collective-permute-done | bytes 196640 | tf_op jit(solution)/shard_map/ppermute | solution.py:479
  109.0 4.8 %collective-permute-done.12.refs_2_ = bf16[192,512]{1,0:T(8,128)(2,1)} collective-permute-done((bf16[192,512]{1,0:T(8,128)(2,1)}, bf16[192,512]{1,0:T(8,128)(2,1)}, u32[]{:S(2)}, u32[]{:S(2)}) %collective-permute-start.12) | collective-permute-done | bytes 196640 | tf_op jit(solution)/shard_map/ppermute | solution.py:479
  113.8 2.6 %collective-permute-done.13.refs_3_ = bf16[192,512]{1,0:T(8,128)(2,1)} collective-permute-done((bf16[192,512]{1,0:T(8,128)(2,1)}, bf16[192,512]{1,0:T(8,128)(2,1)}, u32[]{:S(2)}, u32[]{:S(2)}) %collective-permute-start.13) | collective-permute-done | bytes 196640 | tf_op jit(solution)/shard_map/ppermute | solution.py:479
  116.4 0.8 copy-done.9
  117.1 6.8 %project.1 = bf16[512,1536]{1,0:T(8,128)(2,1)} custom-call(bf16[192,512]{1,0:T(8,128)(2,1)} %get-tuple-element.53.refs_0_, bf16[192,512]{1,0:T(8,128)(2,1)} %collective-permute-done.11.refs_1_, bf16[192,512]{1,0:T(8,128)(2,1)} %collective-permute-done.12.refs_2_, bf16[192,512]{1,0:T(8,128)(2,1)} %collective-permute-done.13.refs_3_, ...), custom_call_target="tpu_custom_call" | custom-call | flops 2147483648 | bytes 6291456 | tf_op jit(solution)/shard_map/project/pallas_call | solution.py:423
  123.9 7.1 %all-to-all-start = ((bf16[8,64,1536]{2,1,0:T(8,128)(2,1)}), bf16[8,64,1536]{2,1,0:T(8,128)(2,1)}, u32[]{:S(2)}, u32[]{:S(2)}) async-start(bf16[8,64,1536]{2,1,0:T(8,128)(2,1)} %bitcast.30), calls=%async_computation | async-start | bytes 3145728 | tf_op jit(solution)/shard_map/all_to_all | solution.py:545
  131.0 0.1 pad_maximum_fusion
  131.2 0.1 broadcast_select_fusion
  131.3 0.1 collective-permute-start.17
  131.3 2.9 %collective-permute-start.16 = (bf16[2,32,8,384]{3,2,1,0:T(8,128)(2,1)S(1)}, bf16[2,32,8,384]{3,2,1,0:T(8,128)(2,1)S(1)}, u32[]{:S(2)}, u32[]{:S(2)}) collective-permute-start(bf16[2,32,8,384]{3,2,1,0:T(8,128)(2,1)S(1)} %get-tuple-element.82), channel_id=1, source_target_pairs={{1,2},{2,1},{3,4},{4,3},{5,6},{6,5},{7,8},{8,7},{9,10},{10,9},{11,... | collective-permute-start | bytes 1179656 | tf_op jit(solution)/shard_map/ppermute | solution.py:485
  134.3 13.6 %collective-permute-done.16 = bf16[2,32,8,384]{3,2,1,0:T(8,128)(2,1)S(1)} collective-permute-done((bf16[2,32,8,384]{3,2,1,0:T(8,128)(2,1)S(1)}, bf16[2,32,8,384]{3,2,1,0:T(8,128)(2,1)S(1)}, u32[]{:S(2)}, u32[]{:S(2)}) %collective-permute-start.16) | collective-permute-done | bytes 393248 | tf_op jit(solution)/shard_map/ppermute | solution.py:485
  147.9 1.1 select_bitcast_fusion
  149.0 6.3 %fine_shares.1.share_ref = bf16[6,1024,256]{2,1,0:T(8,128)(2,1)} custom-call(bf16[3,256,384]{2,1,0:T(8,128)(2,1)} %bitcast.27, bf16[2,512,384]{2,1,0:T(8,128)(2,1)} %bitcast.24, bf16[2,256,384]{2,1,0:T(8,128)(2,1)} %get-tuple-element.80.low_ref, bf16[2,256,384]{2,1,0:T(8,128)(2,1)} %get-tuple-element.79.high_ref), custom_call_target="tpu_custom_call" | custom-call | flops 1073741824 | bytes 6291456 | tf_op jit(solution)/shard_map/fine_shares/pallas_call | solution.py:197
  155.3 2.5 %spread.1.up_ref = bf16[256,384]{1,0:T(8,128)(2,1)} custom-call(bf16[8,64,1536]{2,1,0:T(8,128)(2,1)} %all-to-all-done.in_ref), custom_call_target="tpu_custom_call" | custom-call | flops 268435456 | bytes 6291456 | tf_op jit(solution)/shard_map/spread/pallas_call | solution.py:197
  157.7 9.1 %fine_grads.1 = (bf16[256,384]{1,0:T(8,128)(2,1)}, f32[256,768]{1,0:T(8,128)}, bf16[128,768]{1,0:T(8,128)(2,1)}, bf16[128,768]{1,0:T(8,128)(2,1)}, bf16[128,768]...) custom-call(bf16[3,256,384]{2,1,0:T(8,128)(2,1)} %bitcast.28, ...), custom_call_target="tpu_custom_call" | custom-call | flops 2147483648 | bytes 6291456 | tf_op jit(solution)/shard_map/fine_grads/pallas_call | solution.py:197
  166.9 0.1 collective-permute-start.22
  167.0 5.1 %collective-permute-start.23 = (bf16[64,768]{1,0:T(8,128)(2,1)}, bf16[64,768]{1,0:T(8,128)(2,1)S(1)}, u32[]{:S(2)}, u32[]{:S(2)}) collective-permute-start(bf16[64,768]{1,0:T(8,128)(2,1)} %get-tuple-element.74), channel_id=1, source_target_pairs={{16,33},{17,32},{18,35},{19,34},{20,37},{21,36},{22,39},{23,38},{2... | collective-permute-start | bytes 294920 | tf_op jit(solution)/shard_map/ppermute | solution.py:347
  172.1 0.1 collective-permute-start.18
  172.2 6.3 %collective-permute-start.19 = (bf16[128,768]{1,0:T(8,128)(2,1)}, bf16[128,768]{1,0:T(8,128)(2,1)S(1)}, u32[]{:S(2)}, u32[]{:S(2)}) collective-permute-start(bf16[128,768]{1,0:T(8,128)(2,1)} %get-tuple-element.70), channel_id=1, source_target_pairs={{16,32},{17,33},{18,34},{19,35},{20,36},{21,37},{22,38},{23,39},{2... | collective-permute-start | bytes 589832 | tf_op jit(solution)/shard_map/ppermute | solution.py:347
  178.6 1.9 collective-permute-start.24
  180.5 0.1 collective-permute-start.20
  180.6 2.0 %collective-permute-start.21 = (bf16[128,768]{1,0:T(8,128)(2,1)}, bf16[128,768]{1,0:T(8,128)(2,1)S(1)}, u32[]{:S(2)}, u32[]{:S(2)}) collective-permute-start(bf16[128,768]{1,0:T(8,128)(2,1)} %get-tuple-element.72), channel_id=1, source_target_pairs={{1,2},{2,1},{3,4},{4,3},{5,6},{6,5},{7,8},{8,7},{9,10},{10,9},{11,... | collective-permute-start | bytes 589832 | tf_op jit(solution)/shard_map/ppermute | solution.py:347
  182.7 5.4 %collective-permute-done.24.rest_6_ = bf16[64,768]{1,0:T(8,128)(2,1)S(1)} collective-permute-done((bf16[64,768]{1,0:T(8,128)(2,1)}, bf16[64,768]{1,0:T(8,128)(2,1)S(1)}, u32[]{:S(2)}, u32[]{:S(2)}) %collective-permute-start.24) | collective-permute-done | bytes 98336 | tf_op jit(solution)/shard_map/ppermute | solution.py:347
  188.0 3.5 %collective-permute-start.25 = (bf16[64,768]{1,0:T(8,128)(2,1)}, bf16[64,768]{1,0:T(8,128)(2,1)S(1)}, u32[]{:S(2)}, u32[]{:S(2)}) collective-permute-start(bf16[64,768]{1,0:T(8,128)(2,1)} %get-tuple-element.76), channel_id=1, source_target_pairs={{17,34},{18,33},{19,36},{20,35},{21,38},{22,37},{23,40},{24,39},{2... | collective-permute-start | bytes 294920 | tf_op jit(solution)/shard_map/ppermute | solution.py:347
  191.6 6.8 %collective-permute-done.25.rest_7_ = bf16[64,768]{1,0:T(8,128)(2,1)S(1)} collective-permute-done((bf16[64,768]{1,0:T(8,128)(2,1)}, bf16[64,768]{1,0:T(8,128)(2,1)S(1)}, u32[]{:S(2)}, u32[]{:S(2)}) %collective-permute-start.25) | collective-permute-done | bytes 98336 | tf_op jit(solution)/shard_map/ppermute | solution.py:347
  198.5 0.5 copy-done.17
  199.0 0.1 copy-done.10
  199.1 0.1 copy-done.11
  199.2 0.1 copy-done.12
  199.3 0.1 copy-done.13
  199.4 2.6 %add_arrived.1 = (bf16[256,384]{1,0:T(8,128)(2,1)}, bf16[256,384]{1,0:T(8,128)(2,1)}) custom-call(f32[256,768]{1,0:T(8,128)} %get-tuple-element.68.own_ref, bf16[128,768]{1,0:T(8,128)(2,1)} %copy-done.10, bf16[128,768]{1,0:T(8,128)(2,1)} %copy-done.11, bf16[128,768]{1,0:T(8,128)(2,1)} %copy-done.12, bf16[128,768]{1,0:T(8,128)(2,1)} %copy-done.13, ...), custom_call_target="tpu_custom_call" | custom-call | flops 1048576 | bytes 6291456 | tf_op jit(solution)/shard_map/add_arrived/pallas_call | solution.py:197
  (51 shorter events, 0.2 us)
Async XLA Ops:
  0.6 6.6 %copy-start = (bf16[3,1536,192]{1,2,0:T(8,128)(2,1)S(1)}, bf16[3,1536,192]{1,2,0:T(8,128)(2,1)}, u32[]{:S(2)}) copy-start(bf16[3,1536,192]{1,2,0:T(8,128)(2,1)} %param.9) | copy-start | bytes 5308420
  3.1 4.2 %collective-permute-start = (bf16[3,512,128]{2,1,0:T(8,128)(2,1)}, bf16[3,512,128]{2,1,0:T(8,128)(2,1)S(1)}, u32[]{:S(2)}, u32[]{:S(2)}) collective-permute-start(bf16[3,512,128]{2,1,0:T(8,128)(2,1)} %get-tuple-element.41.refs_0_), channel_id=1, source_target_pairs={{0,1},{1,0},{2,3},{3,2},{4,5},{5,4},{6,7},{7,6},{8,9},{9,8},{10,11... | collective-permute-start | bytes 1179656 | tf_op jit(solution)/shard_map/ppermute | solution.py:479
  3.1 11.7 %collective-permute-start.1 = (bf16[3,512,128]{2,1,0:T(8,128)(2,1)}, bf16[3,512,128]{2,1,0:T(8,128)(2,1)S(1)}, u32[]{:S(2)}, u32[]{:S(2)}) collective-permute-start(bf16[3,512,128]{2,1,0:T(8,128)(2,1)} %get-tuple-element.41.refs_0_), channel_id=1, source_target_pairs={{0,8},{8,0},{1,9},{9,1},{2,10},{10,2},{3,11},{11,3},{4,12},{12,4},... | collective-permute-start | bytes 1179656 | tf_op jit(solution)/shard_map/ppermute | solution.py:479
  3.5 11.6 %collective-permute-start.3 = (bf16[3,512,128]{2,1,0:T(8,128)(2,1)}, bf16[3,512,128]{2,1,0:T(8,128)(2,1)}, u32[]{:S(2)}, u32[]{:S(2)}) collective-permute-start(bf16[3,512,128]{2,1,0:T(8,128)(2,1)} %get-tuple-element.47.refs_4_), channel_id=1, source_target_pairs={{0,2},{2,0},{4,6},{6,4},{1,3},{3,1},{5,7},{7,5},{8,10},{10,8},{12,... | collective-permute-start | bytes 1179656 | tf_op jit(solution)/shard_map/ppermute | solution.py:479
  5.1 12.5 %collective-permute-start.4 = (bf16[3,512,128]{2,1,0:T(8,128)(2,1)}, bf16[3,512,128]{2,1,0:T(8,128)(2,1)}, u32[]{:S(2)}, u32[]{:S(2)}) collective-permute-start(bf16[3,512,128]{2,1,0:T(8,128)(2,1)} %get-tuple-element.47.refs_4_), channel_id=1, source_target_pairs={{0,6},{2,4},{4,2},{6,0},{1,7},{3,5},{5,3},{7,1},{8,14},{10,12},{12... | collective-permute-start | bytes 1179656 | tf_op jit(solution)/shard_map/ppermute | solution.py:479
  7.3 5.0 %copy-start.5 = (bf16[3,512,128]{2,1,0:T(8,128)(2,1)}, bf16[3,512,128]{2,1,0:T(8,128)(2,1)S(1)}, u32[]{:S(2)}) copy-start(bf16[3,512,128]{2,1,0:T(8,128)(2,1)S(1)} %collective-permute-done.refs_1_) | copy-start | bytes 1179652
  12.2 5.3 %copy-start.4 = (bf16[3,512,128]{2,1,0:T(8,128)(2,1)S(1)}, bf16[3,512,128]{2,1,0:T(8,128)(2,1)}, u32[]{:S(2)}) copy-start(bf16[3,512,128]{2,1,0:T(8,128)(2,1)} %get-tuple-element.47.refs_4_) | copy-start | bytes 1179652
  14.8 4.4 %copy-start.6 = (bf16[3,512,128]{2,1,0:T(8,128)(2,1)}, bf16[3,512,128]{2,1,0:T(8,128)(2,1)S(1)}, u32[]{:S(2)}) copy-start(bf16[3,512,128]{2,1,0:T(8,128)(2,1)S(1)} %collective-permute-done.1.refs_2_) | copy-start | bytes 1179652
  14.8 4.4 %collective-permute-start.2 = (bf16[3,512,128]{2,1,0:T(8,128)(2,1)S(1)}, bf16[3,512,128]{2,1,0:T(8,128)(2,1)S(1)}, u32[]{:S(2)}, u32[]{:S(2)}) collective-permute-start(bf16[3,512,128]{2,1,0:T(8,128)(2,1)S(1)} %collective-permute-done.1.refs_2_), channel_id=1, source_target_pairs={{0,1},{1,0},{2,3},{3,2},{4,5},{5,4},{6,7},{7,6},{8,9},{9,8},{10,11... | collective-permute-start | bytes 1179656 | tf_op jit(solution)/shard_map/ppermute | solution.py:479
  14.8 19.9 %copy-start.2 = (bf16[3,16,16,384]{3,2,1,0:T(8,128)(2,1)S(1)}, bf16[3,16,16,384]{3,2,1,0:T(8,128)(2,1)}, u32[]{:S(2)}) copy-start(bf16[3,16,16,384]{3,2,1,0:T(8,128)(2,1)} %param.5) | copy-start | bytes 1769476
  17.6 23.7 %collective-permute-start.5 = (bf16[3,512,128]{2,1,0:T(8,128)(2,1)S(1)}, bf16[3,512,128]{2,1,0:T(8,128)(2,1)S(1)}, u32[]{:S(2)}, u32[]{:S(2)}) collective-permute-start(bf16[3,512,128]{2,1,0:T(8,128)(2,1)S(1)} %copy-done.4), channel_id=1, source_target_pairs={{0,4},{2,6},{4,0},{6,2},{1,5},{3,7},{5,1},{7,3},{8,12},{10,14},{12... | collective-permute-start | bytes 1179656 | tf_op jit(solution)/shard_map/ppermute | solution.py:479
  19.3 0.7 copy-start.7
  34.8 14.3 %collective-permute-start.6 = (bf16[2,8,16,384]{3,2,1,0:T(8,128)(2,1)S(1)}, bf16[2,8,16,384]{3,2,1,0:T(8,128)(2,1)S(1)}, u32[]{:S(2)}, u32[]{:S(2)}) collective-permute-start(bf16[2,8,16,384]{3,2,1,0:T(8,128)(2,1)S(1)} %get-tuple-element.84), channel_id=1, source_target_pairs={{0,16},{16,0},{32,48},{48,32},{64,80},{80,64},{96,112},{112,96},{1... | collective-permute-start | bytes 589832 | tf_op jit(solution)/shard_map/ppermute | solution.py:479
  35.4 13.7 %collective-permute-start.7 = (bf16[2,8,16,384]{3,2,1,0:T(8,128)(2,1)S(1)}, bf16[2,8,16,384]{3,2,1,0:T(8,128)(2,1)S(1)}, u32[]{:S(2)}, u32[]{:S(2)}) collective-permute-start(bf16[2,8,16,384]{3,2,1,0:T(8,128)(2,1)S(1)} %get-tuple-element.83), channel_id=1, source_target_pairs={{16,32},{32,16},{48,64},{64,48},{80,96},{96,80},{17,33},{33,17},{4... | collective-permute-start | bytes 589832 | tf_op jit(solution)/shard_map/ppermute | solution.py:485
  41.3 0.8 copy-start.8
  49.1 4.8 %collective-permute-start.8 = (f32[3,2,2048]{2,1,0:T(2,128)}, f32[3,2,2048]{2,1,0:T(2,128)S(1)}, u32[]{:S(2)}, u32[]{:S(2)}) collective-permute-start(f32[3,2,2048]{2,1,0:T(2,128)} %coarse_stats.3.refs_8_), channel_id=1, source_target_pairs={{0,2},{2,0},{4,6},{6,4},{1,3},{3,1},{5,7},{7,5},{8,10},{10,8},{12,... | collective-permute-start | bytes 147464 | tf_op jit(solution)/shard_map/ppermute | solution.py:479
  50.5 5.5 %collective-permute-start.9 = (f32[3,2,2048]{2,1,0:T(2,128)}, f32[3,2,2048]{2,1,0:T(2,128)S(1)}, u32[]{:S(2)}, u32[]{:S(2)}) collective-permute-start(f32[3,2,2048]{2,1,0:T(2,128)} %coarse_stats.3.refs_8_), channel_id=1, source_target_pairs={{0,6},{2,4},{4,2},{6,0},{1,7},{3,5},{5,3},{7,1},{8,14},{10,12},{12... | collective-permute-start | bytes 147464 | tf_op jit(solution)/shard_map/ppermute | solution.py:479
  51.6 5.8 %collective-permute-start.10 = (f32[3,2,2048]{2,1,0:T(2,128)}, f32[3,2,2048]{2,1,0:T(2,128)S(1)}, u32[]{:S(2)}, u32[]{:S(2)}) collective-permute-start(f32[3,2,2048]{2,1,0:T(2,128)} %coarse_stats.3.refs_8_), channel_id=1, source_target_pairs={{0,4},{2,6},{4,0},{6,2},{1,5},{3,7},{5,1},{7,3},{8,12},{10,14},{12... | collective-permute-start | bytes 147464 | tf_op jit(solution)/shard_map/ppermute | solution.py:479
  53.9 3.5 %copy-start.18 = (f32[3,2,2048]{2,1,0:T(2,128)}, f32[3,2,2048]{2,1,0:T(2,128)S(1)}, u32[]{:S(2)}) copy-start(f32[3,2,2048]{2,1,0:T(2,128)S(1)} %collective-permute-done.8.refs_9_) | copy-start | bytes 147460
  56.0 1.4 copy-start.19
  57.4 0.6 copy-start.20
  95.2 2.6 %collective-permute-start.14 = (bf16[2,3,512,128]{3,2,1,0:T(8,128)(2,1)}, bf16[2,3,512,128]{3,2,1,0:T(8,128)(2,1)S(1)}, u32[]{:S(2)}, u32[]{:S(2)}) collective-permute-start(bf16[2,3,512,128]{3,2,1,0:T(8,128)(2,1)} %get-tuple-element.58), channel_id=1, source_target_pairs={{0,1},{1,0},{2,3},{3,2},{4,5},{5,4},{6,7},{7,6},{8,9},{9,8},{10,11... | collective-permute-start | bytes 2359304 | tf_op jit(solution)/shard_map/ppermute | solution.py:479
  97.8 3.1 %copy-start.3 = (bf16[2,3,512,128]{3,2,1,0:T(8,128)(2,1)}, bf16[2,3,512,128]{3,2,1,0:T(8,128)(2,1)S(1)}, u32[]{:S(2)}) copy-start(bf16[2,3,512,128]{3,2,1,0:T(8,128)(2,1)S(1)} %collective-permute-done.14.refs_5_) | copy-start | bytes 2359300
  99.2 17.2 %collective-permute-start.15 = (bf16[3,512,128]{2,1,0:T(8,128)(2,1)S(1)}, bf16[3,512,128]{2,1,0:T(8,128)(2,1)S(1)}, u32[]{:S(2)}, u32[]{:S(2)}) collective-permute-start(bf16[3,512,128]{2,1,0:T(8,128)(2,1)S(1)} %fusion), channel_id=1, source_target_pairs={{0,8},{8,0},{1,9},{9,1},{2,10},{10,2},{3,11},{11,3},{4,12},{12,4},... | collective-permute-start | bytes 1179656 | tf_op jit(solution)/shard_map/ppermute | solution.py:479
  100.9 8.1 %collective-permute-start.11 = (bf16[192,512]{1,0:T(8,128)(2,1)}, bf16[192,512]{1,0:T(8,128)(2,1)}, u32[]{:S(2)}, u32[]{:S(2)}) collective-permute-start(bf16[192,512]{1,0:T(8,128)(2,1)} %get-tuple-element.54), channel_id=1, source_target_pairs={{0,2},{2,0},{4,6},{6,4},{1,3},{3,1},{5,7},{7,5},{8,10},{10,8},{12,... | collective-permute-start | bytes 589832 | tf_op jit(solution)/shard_map/ppermute | solution.py:479
  100.9 12.9 %collective-permute-start.12 = (bf16[192,512]{1,0:T(8,128)(2,1)}, bf16[192,512]{1,0:T(8,128)(2,1)}, u32[]{:S(2)}, u32[]{:S(2)}) collective-permute-start(bf16[192,512]{1,0:T(8,128)(2,1)} %get-tuple-element.55), channel_id=1, source_target_pairs={{0,4},{2,6},{4,0},{6,2},{1,5},{3,7},{5,1},{7,3},{8,12},{10,14},{12... | collective-permute-start | bytes 589832 | tf_op jit(solution)/shard_map/ppermute | solution.py:479
  104.5 11.8 %collective-permute-start.13 = (bf16[192,512]{1,0:T(8,128)(2,1)}, bf16[192,512]{1,0:T(8,128)(2,1)}, u32[]{:S(2)}, u32[]{:S(2)}) collective-permute-start(bf16[192,512]{1,0:T(8,128)(2,1)} %get-tuple-element.56), channel_id=1, source_target_pairs={{0,6},{2,4},{4,2},{6,0},{1,7},{3,5},{5,3},{7,1},{8,14},{10,12},{12... | collective-permute-start | bytes 589832 | tf_op jit(solution)/shard_map/ppermute | solution.py:479
  116.4 0.8 copy-start.9
  123.9 7.2 %slice-start = ((bf16[3,16,16,384]{3,2,1,0:T(8,128)(2,1)}), bf16[2,16,16,384]{3,2,1,0:T(8,128)(2,1)S(1)}, s32[]{:S(2)}) async-start(bf16[3,16,16,384]{3,2,1,0:T(8,128)(2,1)} %param.5), calls=%async_computation.1 | async-start | bytes 786432 | tf_op jit(solution)/shard_map/slice | solution.py:528
  123.9 31.4 %all-to-all-start = ((bf16[8,64,1536]{2,1,0:T(8,128)(2,1)}), bf16[8,64,1536]{2,1,0:T(8,128)(2,1)}, u32[]{:S(2)}, u32[]{:S(2)}) async-start(bf16[8,64,1536]{2,1,0:T(8,128)(2,1)} %bitcast.30), calls=%async_computation | async-start | bytes 3145728 | tf_op jit(solution)/shard_map/all_to_all | solution.py:545
  131.2 17.8 %copy-start.1 = (bf16[2,32,16,384]{3,2,1,0:T(8,128)(2,1)}, bf16[2,32,16,384]{3,2,1,0:T(8,128)(2,1)S(1)}, u32[]{:S(2)}) copy-start(bf16[2,32,16,384]{3,2,1,0:T(8,128)(2,1)S(1)} %pad_maximum_fusion) | copy-start | bytes 2359300
  131.3 3.0 %collective-permute-start.17 = (bf16[2,32,8,384]{3,2,1,0:T(8,128)(2,1)S(1)}, bf16[2,32,8,384]{3,2,1,0:T(8,128)(2,1)S(1)}, u32[]{:S(2)}, u32[]{:S(2)}) collective-permute-start(bf16[2,32,8,384]{3,2,1,0:T(8,128)(2,1)S(1)} %get-tuple-element.81), channel_id=1, source_target_pairs={{0,1},{1,0},{2,3},{3,2},{4,5},{5,4},{6,7},{7,6},{8,9},{9,8},{10,11... | collective-permute-start | bytes 1179656 | tf_op jit(solution)/shard_map/ppermute | solution.py:479
  131.3 16.5 %collective-permute-start.16 = (bf16[2,32,8,384]{3,2,1,0:T(8,128)(2,1)S(1)}, bf16[2,32,8,384]{3,2,1,0:T(8,128)(2,1)S(1)}, u32[]{:S(2)}, u32[]{:S(2)}) collective-permute-start(bf16[2,32,8,384]{3,2,1,0:T(8,128)(2,1)S(1)} %get-tuple-element.82), channel_id=1, source_target_pairs={{1,2},{2,1},{3,4},{4,3},{5,6},{6,5},{7,8},{8,7},{9,10},{10,9},{11,... | collective-permute-start | bytes 1179656 | tf_op jit(solution)/shard_map/ppermute | solution.py:485
  166.9 13.6 %collective-permute-start.22 = (bf16[64,768]{1,0:T(8,128)(2,1)}, bf16[64,768]{1,0:T(8,128)(2,1)S(1)}, u32[]{:S(2)}, u32[]{:S(2)}) collective-permute-start(bf16[64,768]{1,0:T(8,128)(2,1)} %get-tuple-element.73), channel_id=1, source_target_pairs={{0,17},{1,16},{2,19},{3,18},{4,21},{5,20},{6,23},{7,22},{8,25},{9,... | collective-permute-start | bytes 294920 | tf_op jit(solution)/shard_map/ppermute | solution.py:347
  167.0 13.6 %collective-permute-start.23 = (bf16[64,768]{1,0:T(8,128)(2,1)}, bf16[64,768]{1,0:T(8,128)(2,1)S(1)}, u32[]{:S(2)}, u32[]{:S(2)}) collective-permute-start(bf16[64,768]{1,0:T(8,128)(2,1)} %get-tuple-element.74), channel_id=1, source_target_pairs={{16,33},{17,32},{18,35},{19,34},{20,37},{21,36},{22,39},{23,38},{2... | collective-permute-start | bytes 294920 | tf_op jit(solution)/shard_map/ppermute | solution.py:347
  172.1 26.3 %collective-permute-start.18 = (bf16[128,768]{1,0:T(8,128)(2,1)}, bf16[128,768]{1,0:T(8,128)(2,1)S(1)}, u32[]{:S(2)}, u32[]{:S(2)}) collective-permute-start(bf16[128,768]{1,0:T(8,128)(2,1)} %get-tuple-element.69), channel_id=1, source_target_pairs={{0,16},{1,17},{2,18},{3,19},{4,20},{5,21},{6,22},{7,23},{8,24},{9,... | collective-permute-start | bytes 589832 | tf_op jit(solution)/shard_map/ppermute | solution.py:347
  172.2 26.2 %collective-permute-start.19 = (bf16[128,768]{1,0:T(8,128)(2,1)}, bf16[128,768]{1,0:T(8,128)(2,1)S(1)}, u32[]{:S(2)}, u32[]{:S(2)}) collective-permute-start(bf16[128,768]{1,0:T(8,128)(2,1)} %get-tuple-element.70), channel_id=1, source_target_pairs={{16,32},{17,33},{18,34},{19,35},{20,36},{21,37},{22,38},{23,39},{2... | collective-permute-start | bytes 589832 | tf_op jit(solution)/shard_map/ppermute | solution.py:347
  178.6 9.5 %collective-permute-start.24 = (bf16[64,768]{1,0:T(8,128)(2,1)}, bf16[64,768]{1,0:T(8,128)(2,1)S(1)}, u32[]{:S(2)}, u32[]{:S(2)}) collective-permute-start(bf16[64,768]{1,0:T(8,128)(2,1)} %get-tuple-element.75), channel_id=1, source_target_pairs={{1,18},{2,17},{3,20},{4,19},{5,22},{6,21},{7,24},{8,23},{9,26},{10... | collective-permute-start | bytes 294920 | tf_op jit(solution)/shard_map/ppermute | solution.py:347
  180.5 18.0 %copy-start.14 = (bf16[64,768]{1,0:T(8,128)(2,1)}, bf16[64,768]{1,0:T(8,128)(2,1)S(1)}, u32[]{:S(2)}) copy-start(bf16[64,768]{1,0:T(8,128)(2,1)S(1)} %collective-permute-done.22.rest_4_) | copy-start | bytes 294916
  180.5 17.9 %collective-permute-start.20 = (bf16[128,768]{1,0:T(8,128)(2,1)}, bf16[128,768]{1,0:T(8,128)(2,1)S(1)}, u32[]{:S(2)}, u32[]{:S(2)}) collective-permute-start(bf16[128,768]{1,0:T(8,128)(2,1)} %get-tuple-element.71), channel_id=1, source_target_pairs={{0,1},{1,0},{2,3},{3,2},{4,5},{5,4},{6,7},{7,6},{8,9},{9,8},{10,11... | collective-permute-start | bytes 589832 | tf_op jit(solution)/shard_map/ppermute | solution.py:347
  180.6 17.8 %copy-start.15 = (bf16[64,768]{1,0:T(8,128)(2,1)}, bf16[64,768]{1,0:T(8,128)(2,1)S(1)}, u32[]{:S(2)}) copy-start(bf16[64,768]{1,0:T(8,128)(2,1)S(1)} %collective-permute-done.23.rest_5_) | copy-start | bytes 294916
  180.6 17.8 %collective-permute-start.21 = (bf16[128,768]{1,0:T(8,128)(2,1)}, bf16[128,768]{1,0:T(8,128)(2,1)S(1)}, u32[]{:S(2)}, u32[]{:S(2)}) collective-permute-start(bf16[128,768]{1,0:T(8,128)(2,1)} %get-tuple-element.72), channel_id=1, source_target_pairs={{1,2},{2,1},{3,4},{4,3},{5,6},{6,5},{7,8},{8,7},{9,10},{10,9},{11,... | collective-permute-start | bytes 589832 | tf_op jit(solution)/shard_map/ppermute | solution.py:347
  188.0 10.4 %copy-start.16 = (bf16[64,768]{1,0:T(8,128)(2,1)}, bf16[64,768]{1,0:T(8,128)(2,1)S(1)}, u32[]{:S(2)}) copy-start(bf16[64,768]{1,0:T(8,128)(2,1)S(1)} %collective-permute-done.24.rest_6_) | copy-start | bytes 294916
  188.0 10.4 %collective-permute-start.25 = (bf16[64,768]{1,0:T(8,128)(2,1)}, bf16[64,768]{1,0:T(8,128)(2,1)S(1)}, u32[]{:S(2)}, u32[]{:S(2)}) collective-permute-start(bf16[64,768]{1,0:T(8,128)(2,1)} %get-tuple-element.76), channel_id=1, source_target_pairs={{17,34},{18,33},{19,36},{20,35},{21,38},{22,37},{23,40},{24,39},{2... | collective-permute-start | bytes 294920 | tf_op jit(solution)/shard_map/ppermute | solution.py:347
  198.4 0.6 copy-start.17
  198.4 0.7 copy-start.10
  198.4 0.8 copy-start.11
  198.4 0.8 copy-start.12
  198.5 0.9 copy-start.13

commit v6 on v4

--- a/solution.py
+++ b/solution.py
@@ -240,59 +240,104 @@
     return jnp.concatenate([ref[which, :, lanes] for ref in refs], axis=0)
 
 
-def fine_grads(own_qkv, ext_kv, own_up, rows, columns):
+def fine_shares(own_qkv, ext_kv, rows, columns):
     _, own, width = own_qkv.shape
-    sizes = [ref.shape[1] for ref in ext_kv]
-    places = [sum(sizes[:i]) for i in range(len(sizes))]
-
-    def body(q_ref, mid_ref, low_ref, high_ref, up_ref, q_out, mid_out, *rest):
-        inner_out, outer_out, bias_ref = rest
-        first = lax.axis_index("c") == 0
+    heads = width // HD
+
+    def body(q_ref, mid_ref, low_ref, high_ref, out_ref, bias_ref):
         fill_bias(bias_ref, own, rows, columns)
         ext = (mid_ref, low_ref, high_ref)
         for pair, lanes in pairs_of(width):
             key = stacked(ext, 0, lanes)
-            key_t = key.T
-            value = stacked(ext, 1, lanes)
-            parts = []
-            key_sum = jnp.zeros((SIDE * SIDE, 128), F32)
-            value_sum = jnp.zeros((SIDE * SIDE, 128), F32)
             for side in range(2):
                 query = half(q_ref[0, :, lanes], side) * BF16(SCALE)
-                up = half(up_ref[:, lanes], side)
                 score = nt(key, query) + bias_ref[...]
-                product = nt(value, up)
                 share = jnp.exp(score - jnp.max(score, axis=0, keepdims=True))
                 total = jnp.sum(share, axis=0, keepdims=True)
-                delta = jnp.sum(share * product, axis=0, keepdims=True) / total
-                share = share * (1.0 / total)
-                grads = (share * (product - delta)).astype(BF16)
-                key_sum += nn(grads, query)
-                value_sum += nn(share.astype(BF16), up)
-                parts.append(nn(key_t[side * HD : side * HD + HD], grads))
-            q_out[:, lanes] = (jnp.concatenate(parts, axis=0).T * SCALE).astype(BF16)
-            right = slice(width + pair * 128, width + pair * 128 + 128)
-            for at, total in ((lanes, key_sum), (right, value_sum)):
-                mid, low, high = [
-                    total[place : place + size] for place, size in zip(places, sizes)
-                ]
-                mid_out[:, at] = mid
-                inner_out[:, at] = jnp.where(first, high, low).astype(BF16)
-                outer_out[:, at] = jnp.where(first, low, high).astype(BF16)
+                out_ref[2 * pair + side] = (share * (1.0 / total)).astype(BF16)
 
     return whole_call(
         body,
-        [jax.ShapeDtypeStruct((own, width), BF16)]
-        + [
-            jax.ShapeDtypeStruct((size, 2 * width), BF16 if i else F32)
-            for i, size in enumerate(sizes)
+        jax.ShapeDtypeStruct((heads, SIDE * SIDE, own), BF16),
+        "fine_shares",
+        1 << 30,
+        [pltpu.VMEM((SIDE * SIDE, own), F32)],
+        own_qkv,
+        *ext_kv,
+    )
+
+
+def pair_call(body, out_shape, name, flops, *operands):
+    width = 384
+    pairs = width // 128
+
+    def spec(array):
+        shape = tuple(array.shape)
+        rank = len(shape)
+        if shape[0] == 2 * pairs:
+            return pl.BlockSpec((2,) + shape[1:], lambda p: (p,) + (0,) * (rank - 1))
+        return pl.BlockSpec(
+            shape[:-1] + (shape[-1] // pairs,), lambda p: (0,) * (rank - 1) + (p,)
+        )
+
+    return pl.pallas_call(
+        body,
+        grid=(pairs,),
+        in_specs=[spec(array) for array in operands],
+        out_specs=[spec(shape) for shape in out_shape],
+        out_shape=out_shape,
+        name=name,
+        cost_estimate=cost(flops, 6 << 20, 0),
+        compiler_params=pltpu.CompilerParams(vmem_limit_bytes=VMEM),
+    )(*operands)
+
+
+def fine_grads(own_qkv, ext_kv, own_up, shares, rows, columns):
+    _, own, width = own_qkv.shape
+    mid_size, side_size = ext_kv[0].shape[1], ext_kv[1].shape[1]
+
+    def body(q_ref, mid_ref, low_ref, high_ref, up_ref, share_ref, q_out, mid_out, *outs):
+        first = lax.axis_index("c") == 0
+        ext = (mid_ref, low_ref, high_ref)
+        key_t = jnp.concatenate([ref[0] for ref in ext], axis=0).T
+        value = jnp.concatenate([ref[1] for ref in ext], axis=0)
+        parts = []
+        key_sum = jnp.zeros((SIDE * SIDE, 128), F32)
+        value_sum = jnp.zeros((SIDE * SIDE, 128), F32)
+        for side in range(2):
+            query = half(q_ref[0], side) * BF16(SCALE)
+            up = half(up_ref[...], side)
+            rounded = share_ref[side]
+            share = rounded.astype(F32)
+            product = nt(value, up)
+            total = jnp.sum(share, axis=0, keepdims=True)
+            delta = jnp.sum(share * product, axis=0, keepdims=True) / total
+            grads = (share * (product - delta)).astype(BF16)
+            key_sum += nn(grads, query)
+            value_sum += nn(rounded, up)
+            parts.append(nn(key_t[side * HD : side * HD + HD], grads))
+        q_out[...] = (jnp.concatenate(parts, axis=0).T * SCALE).astype(BF16)
+        for at, total in ((slice(0, 128), key_sum), (slice(128, 256), value_sum)):
+            mid_out[:, at] = total[:mid_size]
+            low = total[mid_size : mid_size + side_size].astype(BF16)
+            high = total[mid_size + side_size :].astype(BF16)
+            outs[0][:, at] = jnp.where(first, high, low)
+            outs[1][:, at] = jnp.where(first, low, high)
+
+    return pair_call(
+        body,
+        [
+            jax.ShapeDtypeStruct((own, width), BF16),
+            jax.ShapeDtypeStruct((mid_size, 2 * width), F32),
+            jax.ShapeDtypeStruct((side_size, 2 * width), BF16),
+            jax.ShapeDtypeStruct((side_size, 2 * width), BF16),
         ],
         "fine_grads",
         2 << 30,
-        [pltpu.VMEM((SIDE * SIDE, own), F32)],
         own_qkv,
         *ext_kv,
         own_up,
+        shares,
     )
 
 
@@ -303,10 +348,10 @@
 
     def body(mid_ref, inner_ref, outer_ref, own_out, inner_out, outer_out):
         first = lax.axis_index("c") == 0
-        inner = inner_ref[...].astype(F32).reshape(tall, RIM, wide)
-        outer = outer_ref[...].astype(F32).reshape(tall, RIM, wide)
+        inner = inner_ref[...].astype(F32).reshape(tall, RIM, -1)
+        outer = outer_ref[...].astype(F32).reshape(tall, RIM, -1)
         left, right = jnp.where(first, outer, inner), jnp.where(first, inner, outer)
-        both = jnp.concatenate([left, right], axis=1).reshape(cells, wide)
+        both = jnp.concatenate([left, right], axis=1).reshape(mid_ref.shape)
         total = mid_ref[...] + both
         top, bottom = total[:edge], total[cells - edge :]
         upper = lax.axis_index("zh") == 0
@@ -314,13 +359,12 @@
         inner_out[...] = jnp.where(upper, bottom, top).astype(BF16)
         outer_out[...] = jnp.where(upper, top, bottom).astype(BF16)
 
-    return whole_call(
+    return pair_call(
         body,
         [jax.ShapeDtypeStruct((cells - 2 * edge, wide), F32)]
         + [jax.ShapeDtypeStruct((edge, wide), BF16)] * 2,
         "add_columns",
         1 << 20,
-        [],
         mid,
         inner,
         outer,
@@ -329,7 +373,6 @@
 
 def add_rows(own, inner, outer):
     cells, wide = own.shape
-    width = wide // 2
 
     def body(own_ref, inner_ref, outer_ref, k_out, v_out):
         upper = lax.axis_index("zh") == 0
@@ -337,15 +380,14 @@
         outer = outer_ref[...].astype(F32)
         above, below = jnp.where(upper, outer, inner), jnp.where(upper, inner, outer)
         total = own_ref[...] + jnp.concatenate([above, below], axis=0)
-        k_out[...] = total[:, :width].astype(BF16)
-        v_out[...] = total[:, width:].astype(BF16)
-
-    return whole_call(
-        body,
-        [jax.ShapeDtypeStruct((cells, width), BF16)] * 2,
+        k_out[...] = total[:, :128].astype(BF16)
+        v_out[...] = total[:, 128:].astype(BF16)
+
+    return pair_call(
+        body,
+        [jax.ShapeDtypeStruct((cells, wide // 2), BF16)] * 2,
         "add_rows",
         1 << 20,
-        [],
         own,
         inner,
         outer,
@@ -484,16 +526,20 @@
     joint = lax.dot_general(
         qkv_weight, merge_weight, (((1,), (1,)), ((), ())), preferred_element_type=F32
     ).astype(BF16).reshape(3 * group, wide)
+    across, joint = lax.optimization_barrier((across, joint))
     corner = swapped(across, "c")
-    *near, joint = lax.optimization_barrier((*near, joint))
+    *near, joint, fine_qkv = lax.optimization_barrier((*near, joint, fine_qkv))
     far = swapped(near[0], "y", 2)
     keys = [key_value, beside, across, corner]
     queries = [near[0], near[1], far, near[2]]
-
-    part = coarse_stats(keys, near, [0, 1, 3], (), 256)
-    part, fine_qkv = lax.optimization_barrier((part, fine_qkv))
     own_qkv = fine_qkv.reshape(3, own, width)
     edges = sent_rims(fine_qkv[1:], ROW, "zh", 1)
+
+    part = coarse_stats(keys, near, [0, 1, 3], (), 256)
+    part, *edges = lax.optimization_barrier((part, *edges))
+    low, high = placed_rims(*edges, "zh")
+    tall = jnp.concatenate([low, fine_qkv[1:], high], axis=1)
+    edges = sent_rims(tall, COL, "c", 2)
     part = coarse_stats(keys, [far], [2], (part,), 256)
     part, *edges = lax.optimization_barrier((part, *edges))
     stats = [part] + [swapped(part, "y", step) for step in (1, 3, 2)]
@@ -506,18 +552,19 @@
     for step in (1, 2, 3):
         query_pieces.append(swapped(query_grads[step], "y", step))
     count = lax.axis_size(ROW)
+    low, high = placed_rims(*edges, "c")
+    ext_kv = [array.reshape(2, -1, width) for array in (tall, low, high)]
+    shares = fine_shares(own_qkv, ext_kv, rows, columns)
+    arrived, shares = lax.optimization_barrier((arrived, shares))
     projected = project(
         query_pieces, kept, from_core, arrived, joint, coarse_columns, count
     )
-    projected, *edges = lax.optimization_barrier((projected, *edges))
     pieces = lax.all_to_all(projected.reshape(count, -1, wide), ROW, 0, 0)
-    low, high = placed_rims(*edges, "zh")
-    tall = jnp.concatenate([low, fine_qkv[1:], high], axis=1)
-    low, high = placed_rims(*sent_rims(tall, COL, "c", 2), "c")
-    ext_kv = [array.reshape(2, -1, width) for array in (tall, low, high)]
     own_up = spread(pieces, coarse_columns)
 
-    grad_query, mid, inner, outer = fine_grads(own_qkv, ext_kv, own_up, rows, columns)
+    grad_query, mid, inner, outer = fine_grads(
+        own_qkv, ext_kv, own_up, shares, rows, columns
+    )
     inner, outer = exchanged(inner, outer, COL)
     middle, inner, outer = add_columns(mid, inner, outer, columns)
     inner, outer = exchanged(inner, outer, ROW)

time: 200 us -> 197 us (0.985)
  blocking collectives: 0 us -> 28.6 us
  waiting for transfers between devices: 54.8 us -> 28.6 us
  starting transfers between devices: 42.1 us -> 31 us
  Pallas kernels: 85 us -> 91.5 us
    all_to_all x0 -> x1, blocking collectives: none -> 28.6 us  [shards(): pieces = lax.all_to_all(projected.reshape(count, -1, wide), ROW, 0, 0)]
    pallas_call x0 -> x3, Pallas kernels: none -> 14.6 us  [pair_call(): pl.pallas_call(body, grid=(pairs,), in_specs=[spec(array) for array in op...]
    ppermute x4, waiting for transfers between devices: 26.3 us -> 12.5 us  [exchanged(): return (swapped(inner, axis), lax.ppermute(outer, axis, beyond))]
    ppermute x18, waiting for transfers between devices: 26 us -> 16.2 us  [swapped(): lax.ppermute(array, axis, [(i, i ^ flip) for i in range(lax.axis_size(axi...]
    pallas_call x5 -> x3, Pallas kernels: 19.3 us -> 11.2 us  [whole_call(): pl.pallas_call(body, out_shape=out_shape, scratch_shapes=scratch, name=na...]
    all_to_all x1 -> x0, starting transfers between devices: 7.11 us -> none  [shards(): pieces = lax.all_to_all(projected.reshape(count, -1, wide), ROW, 0, 0)]
    ppermute x18, starting transfers between devices: 20.3 us -> 16.3 us  [swapped(): lax.ppermute(array, axis, [(i, i ^ flip) for i in range(lax.axis_size(axi...]
    all_to_all x1 -> x0, waiting for transfers between devices: 2.44 us -> none  [shards(): pieces = lax.all_to_all(projected.reshape(count, -1, wide), ROW, 0, 0)]
  transfers between devices with their start and end apart: 23 -> 22, of which waited for: 12 -> 10; matrix products, arithmetic and copies ran while one was open for 4% -> 4% of each run, Pallas kernels for 11% -> 14%
where the time goes in v6:
time: 197 us; the launch traced here: 196 us
  Pallas kernels  91.5 us (46%)
  starting transfers between devices  31 us (16%)
  waiting for transfers between devices  28.6 us (15%)
  blocking collectives  28.6 us (15%)
  local copies, waits for them, and re-layouts  5.7 us (3%)
  matrix products  4.97 us (3%)
  other arithmetic  4.87 us (2%)
    pallas_call x1, Pallas kernels, coarse_grads(): pl.pallas_call(body, grid=(heads, blocks), in_specs=[pl.BlockSpec((1, tok...  37.2 us
    all_to_all x1, blocking collectives, shards(): pieces = lax.all_to_all(projected.reshape(count, -1, wide), ROW, 0, 0)  28.6 us
    pallas_call x2, Pallas kernels, coarse_stats(): pl.pallas_call(body, grid=(heads, number), in_specs=[pl.BlockSpec((1, tok...  21.8 us
    ppermute x18, starting transfers between devices, swapped(): lax.ppermute(array, axis, [(i, i ^ flip) for i in range(lax.axis_size(axi...  16.3 us
    ppermute x18, waiting for transfers between devices, swapped(): lax.ppermute(array, axis, [(i, i ^ flip) for i in range(lax.axis_size(axi...  16.2 us
    ppermute x4, starting transfers between devices, exchanged(): return (swapped(inner, axis), lax.ppermute(outer, axis, beyond))  14.7 us
    pallas_call x3, Pallas kernels, pair_call(): pl.pallas_call(body, grid=(pairs,), in_specs=[spec(array) for array in op...  14.6 us
    ppermute x4, waiting for transfers between devices, exchanged(): return (swapped(inner, axis), lax.ppermute(outer, axis, beyond))  12.5 us
  transfers between devices with their start and end apart: 22, of which 10 were waited for; matrix products, arithmetic and copies ran while one was open for 4% of the time, Pallas kernels for 14%

profile of v6, /device:TPU:96, one launch (start us, length us, event | category | flops | bytes accessed | tf_op | source)
XLA Modules:
  0.0 196.3 jit_solution(2932485160719728008)
XLA Ops:
  0.6 0.0 copy-start
  0.6 2.5 %prepare.1 = (bf16[3,512,128]{2,1,0:T(8,128)(2,1)}, bf16[3,512,128]{2,1,0:T(8,128)(2,1)}) custom-call(bf16[3,512,192]{2,1,0:T(8,128)(2,1)} %bitcast.31, bf16[512,192]{1,0:T(8,128)(2,1)} %bitcast.32), custom_call_target="tpu_custom_call" | custom-call | flops 1048576 | bytes 6291456 | tf_op jit(solution)/shard_map/prepare/pallas_call | solution.py:197
  3.1 3.0 %collective-permute-start.1 = (bf16[3,512,128]{2,1,0:T(8,128)(2,1)}, bf16[3,512,128]{2,1,0:T(8,128)(2,1)S(1)}, u32[]{:S(2)}, u32[]{:S(2)}) collective-permute-start(bf16[3,512,128]{2,1,0:T(8,128)(2,1)} %get-tuple-element.44.refs_4_), channel_id=1, source_target_pairs={{0,6},{2,4},{4,2},{6,0},{1,7},{3,5},{5,3},{7,1},{8,14},{10,12},{12... | collective-permute-start | bytes 1179656 | tf_op jit(solution)/shard_map/ppermute | solution.py:490
  6.1 0.1 collective-permute-start
  6.3 0.4 collective-permute-start.2
  6.7 0.0 collective-permute-done.3.refs_1_
  6.7 5.0 %fusion.1 = f32[1536,576]{0,1:S(1)} fusion(bf16[1536,1536]{1,0:T(8,128)(2,1)} %param.8, bf16[1536,576]{0,1:T(8,128)(2,1)S(1)} %bitcast.23), kind=kOutput, calls=%fused_computation.11 | convolution fusion | flops 2717908992 | bytes 10027008
  11.7 0.0 copy-start.2
  11.7 1.4 convert_element_type.20
  13.1 4.6 %collective-permute-done.2.refs_2_ = bf16[3,512,128]{2,1,0:T(8,128)(2,1)} collective-permute-done((bf16[3,512,128]{2,1,0:T(8,128)(2,1)}, bf16[3,512,128]{2,1,0:T(8,128)(2,1)}, u32[]{:S(2)}, u32[]{:S(2)}) %collective-permute-start.2) | collective-permute-done | bytes 393248 | tf_op jit(solution)/shard_map/ppermute | solution.py:490
  17.7 0.0 collective-permute-done.1.refs_6_.refs_7_
  17.7 0.0 collective-permute-done.refs_5_
  17.7 0.8 copy-done.9
  18.5 0.8 copy-done.10
  19.3 3.4 %collective-permute-start.6 = (bf16[2,8,16,384]{3,2,1,0:T(8,128)(2,1)S(1)}, bf16[2,8,16,384]{3,2,1,0:T(8,128)(2,1)S(1)}, u32[]{:S(2)}, u32[]{:S(2)}) collective-permute-start(bf16[2,8,16,384]{3,2,1,0:T(8,128)(2,1)S(1)} %get-tuple-element.75), channel_id=1, source_target_pairs={{16,32},{32,16},{48,64},{64,48},{80,96},{96,80},{17,33},{33,17},{4... | collective-permute-start | bytes 589832 | tf_op jit(solution)/shard_map/ppermute | solution.py:496
  22.7 0.0 slice-start
  22.7 0.1 collective-permute-start.5
  22.8 1.5 collective-permute-start.7
  24.4 0.0 collective-permute-done.4.refs_3_
  24.4 0.7 copy-done.11
  25.1 14.8 %coarse_stats.2.refs_5_ = f32[3,2,2048]{2,1,0:T(2,128)} custom-call(bf16[3,512,128]{2,1,0:T(8,128)(2,1)} %get-tuple-element.38.refs_0_, bf16[3,512,128]{2,1,0:T(8,128)(2,1)} %copy-done.8, bf16[3,512,128]{2,1,0:T(8,128)(2,1)} %collective-permute-done.2.refs_2_, bf16[3,512,128]{2,1,0:T(8,128)(2,1)} %copy-done.11, ...), custom_call_target="tpu_custom_call" | custom-call | flops 9663676416 | bytes 2097152 | tf_op jit(solution)/shard_map/coarse_stats/pallas_call | solution.py:109
  39.9 0.0 collective-permute-done.6
  40.0 0.1 pad_maximum_fusion
  40.1 0.9 broadcast_select_fusion
  41.0 3.5 %collective-permute-start.9 = (bf16[2,32,8,384]{3,2,1,0:T(8,128)(2,1)}, bf16[2,32,8,384]{3,2,1,0:T(8,128)(2,1)S(1)}, u32[]{:S(2)}, u32[]{:S(2)}) collective-permute-start(bf16[2,32,8,384]{3,2,1,0:T(8,128)(2,1)} %get-tuple-element.73), channel_id=1, source_target_pairs={{1,2},{2,1},{3,4},{4,3},{5,6},{6,5},{7,8},{8,7},{9,10},{10,9},{11,... | collective-permute-start | bytes 1179656 | tf_op jit(solution)/shard_map/ppermute | solution.py:496
  44.5 0.1 collective-permute-start.8
  44.6 7.1 %coarse_stats.3.refs_8_ = f32[3,2,2048]{2,1,0:T(2,128)} custom-call(bf16[3,512,128]{2,1,0:T(8,128)(2,1)} %get-tuple-element.38.refs_0_, bf16[3,512,128]{2,1,0:T(8,128)(2,1)} %copy-done.8, bf16[3,512,128]{2,1,0:T(8,128)(2,1)} %collective-permute-done.2.refs_2_, bf16[3,512,128]{2,1,0:T(8,128)(2,1)} %copy-done.11, ...), custom_call_target="tpu_custom_call" | custom-call | flops 3221225472 | bytes 2097152 | tf_op jit(solution)/shard_map/coarse_stats/pallas_call | solution.py:109
  51.7 0.7 collective-permute-done.9
  52.4 2.2 %collective-permute-start.12 = (f32[3,2,2048]{2,1,0:T(2,128)}, f32[3,2,2048]{2,1,0:T(2,128)S(1)}, u32[]{:S(2)}, u32[]{:S(2)}) collective-permute-start(f32[3,2,2048]{2,1,0:T(2,128)} %coarse_stats.3.refs_8_), channel_id=1, source_target_pairs={{0,4},{2,6},{4,0},{6,2},{1,5},{3,7},{5,1},{7,3},{8,12},{10,14},{12... | collective-permute-start | bytes 147464 | tf_op jit(solution)/shard_map/ppermute | solution.py:490
  54.6 0.3 collective-permute-start.11
  54.9 1.0 collective-permute-start.10
  55.9 2.3 %collective-permute-done.12.refs_11_ = f32[3,2,2048]{2,1,0:T(2,128)S(1)} collective-permute-done((f32[3,2,2048]{2,1,0:T(2,128)}, f32[3,2,2048]{2,1,0:T(2,128)S(1)}, u32[]{:S(2)}, u32[]{:S(2)}) %collective-permute-start.12) | collective-permute-done | bytes 49184 | tf_op jit(solution)/shard_map/ppermute | solution.py:490
  58.2 1.9 collective-permute-done.11.refs_10_
  60.2 0.6 copy-done.17
  60.8 0.6 copy-done.18
  61.4 37.2 %coarse_grads.1 = (bf16[2,3,512,128]{3,2,1,0:T(8,128)(2,1)}, bf16[2,3,512,128]{3,2,1,0:T(8,128)(2,1)}, bf16[192,512]{1,0:T(8,128)(2,1)}, bf16[192,512]{1,0:T(8,1...) custom-call(bf16[3,512,128]{2,1,0:T(8,128)(2,1)} %get-tuple-element.38.refs_0_, ...), custom_call_target="tpu_custom_call" | custom-call | flops 32212254720 | bytes 4194304 | tf_op jit(solution)/shard_map/coarse_grads/pallas_call | solution.py:178
  98.6 0.1 collective-permute-start.16
  98.7 2.5 %collective-permute-done.16.refs_5_ = bf16[2,3,512,128]{3,2,1,0:T(8,128)(2,1)S(1)} collective-permute-done((bf16[2,3,512,128]{3,2,1,0:T(8,128)(2,1)}, bf16[2,3,512,128]{3,2,1,0:T(8,128)(2,1)S(1)}, u32[]{:S(2)}, u32[]{:S(2)}) %collective-permute-start.16) | collective-permute-done | bytes 786464 | tf_op jit(solution)/shard_map/ppermute | solution.py:490
  101.2 1.4 fusion
  102.5 0.1 collective-permute-start.17
  102.6 0.3 collective-permute-start.13
  102.9 2.8 %collective-permute-start.14 = (bf16[192,512]{1,0:T(8,128)(2,1)}, bf16[192,512]{1,0:T(8,128)(2,1)S(1)}, u32[]{:S(2)}, u32[]{:S(2)}) collective-permute-start(bf16[192,512]{1,0:T(8,128)(2,1)} %get-tuple-element.55), channel_id=1, source_target_pairs={{0,4},{2,6},{4,0},{6,2},{1,5},{3,7},{5,1},{7,3},{8,12},{10,14},{12... | collective-permute-start | bytes 589832 | tf_op jit(solution)/shard_map/ppermute | solution.py:490
  105.7 1.8 collective-permute-start.15
  107.6 1.0 select_bitcast_fusion
  108.6 6.3 %fine_shares.1.share_ref = bf16[6,1024,256]{2,1,0:T(8,128)(2,1)} custom-call(bf16[3,256,384]{2,1,0:T(8,128)(2,1)} %bitcast.27, bf16[2,512,384]{2,1,0:T(8,128)(2,1)} %bitcast.24, bf16[2,256,384]{2,1,0:T(8,128)(2,1)} %get-tuple-element.72.low_ref, bf16[2,256,384]{2,1,0:T(8,128)(2,1)} %get-tuple-element.71.high_ref), custom_call_target="tpu_custom_call" | custom-call | flops 1073741824 | bytes 6291456 | tf_op jit(solution)/shard_map/fine_shares/pallas_call | solution.py:197
  114.9 0.0 copy-start.13
  114.9 0.3 collective-permute-done.14.refs_2_
  115.2 2.6 %collective-permute-done.15.refs_3_ = bf16[192,512]{1,0:T(8,128)(2,1)S(1)} collective-permute-done((bf16[192,512]{1,0:T(8,128)(2,1)}, bf16[192,512]{1,0:T(8,128)(2,1)S(1)}, u32[]{:S(2)}, u32[]{:S(2)}) %collective-permute-start.15) | collective-permute-done | bytes 196640 | tf_op jit(solution)/shard_map/ppermute | solution.py:490
  117.8 0.7 copy-done.15
  118.4 6.7 %project.1 = bf16[512,1536]{1,0:T(8,128)(2,1)} custom-call(bf16[192,512]{1,0:T(8,128)(2,1)} %get-tuple-element.53.refs_0_, bf16[192,512]{1,0:T(8,128)(2,1)} %copy-done.13, bf16[192,512]{1,0:T(8,128)(2,1)} %copy-done.14, bf16[192,512]{1,0:T(8,128)(2,1)} %copy-done.15, bf16[2,3,512,128]{3,2,1,0:T(8,128)(2,1)} %get-tuple-element.57.refs_4_, ...), custom_call_target="tpu_custom_call" | custom-call | flops 2147483648 | bytes 6291456 | tf_op jit(solution)/shard_map/project/pallas_call | solution.py:434
  125.2 28.6 %all_to_all.5.in_ref = bf16[8,64,1536]{2,1,0:T(8,128)(2,1)} all-to-all(bf16[8,64,1536]{2,1,0:T(8,128)(2,1)} %bitcast.30), channel_id=1, replica_groups=mesh['x'=4,'zh'=2,'zl'=2,'y'=4,'c'=2] {'x','zh'}, dimensions={0} | all-to-all | bytes 3145728 | tf_op jit(solution)/shard_map/all_to_all | solution.py:562
  153.8 2.5 %spread.1.up_ref = bf16[256,384]{1,0:T(8,128)(2,1)} custom-call(bf16[8,64,1536]{2,1,0:T(8,128)(2,1)} %all_to_all.5.in_ref), custom_call_target="tpu_custom_call" | custom-call | flops 268435456 | bytes 6291456 | tf_op jit(solution)/shard_map/spread/pallas_call | solution.py:197
  156.3 8.3 %fine_grads.1 = (bf16[256,384]{1,0:T(8,128)(2,1)}, f32[512,768]{1,0:T(8,128)}, bf16[256,768]{1,0:T(8,128)(2,1)}, bf16[256,768]{1,0:T(8,128)(2,1)}) custom-call(bf16[3,256,384]{2,1,0:T(8,128)(2,1)} %bitcast.28, bf16[2,512,384]{2,1,0:T(8,128)(2,1)} %bitcast.25, bf16[2,256,384]{2,1,0:T(8,128)(2,1)} %get-tuple-element.72.low_ref, ...), custom_call_target="tpu_custom_call" | custom-call | flops 2147483648 | bytes 6291456 | tf_op jit(solution)/shard_map/fine_grads/pallas_call | solution.py:283
  164.5 0.1 collective-permute-start.18
  164.6 4.8 %collective-permute-start.19 = (bf16[256,768]{1,0:T(8,128)(2,1)}, bf16[256,768]{1,0:T(8,128)(2,1)S(1)}, u32[]{:S(2)}, u32[]{:S(2)}) collective-permute-start(bf16[256,768]{1,0:T(8,128)(2,1)} %get-tuple-element.65), channel_id=1, source_target_pairs={{1,2},{2,1},{3,4},{4,3},{5,6},{6,5},{7,8},{8,7},{9,10},{10,9},{11,... | collective-permute-start | bytes 1179656 | tf_op jit(solution)/shard_map/ppermute | solution.py:496
  169.4 6.6 %collective-permute-done.19.outer_ref = bf16[256,768]{1,0:T(8,128)(2,1)S(1)} collective-permute-done((bf16[256,768]{1,0:T(8,128)(2,1)}, bf16[256,768]{1,0:T(8,128)(2,1)S(1)}, u32[]{:S(2)}, u32[]{:S(2)}) %collective-permute-start.19) | collective-permute-done | bytes 393248 | tf_op jit(solution)/shard_map/ppermute | solution.py:496
  176.0 0.8 copy-done.4
  176.8 3.5 %add_columns.1 = (f32[256,768]{1,0:T(8,128)}, bf16[128,768]{1,0:T(8,128)(2,1)}, bf16[128,768]{1,0:T(8,128)(2,1)}) custom-call(f32[512,768]{1,0:T(8,128)} %get-tuple-element.63.mid_ref, bf16[256,768]{1,0:T(8,128)(2,1)} %copy-done.3, bf16[256,768]{1,0:T(8,128)(2,1)} %copy-done.4), custom_call_target="tpu_custom_call" | custom-call | flops 1048576 | bytes 6291456 | tf_op jit(solution)/shard_map/add_columns/pallas_call | solution.py:283
  180.3 2.3 %collective-permute-start.20 = (bf16[128,768]{1,0:T(8,128)(2,1)}, bf16[128,768]{1,0:T(8,128)(2,1)S(1)}, u32[]{:S(2)}, u32[]{:S(2)}) collective-permute-start(bf16[128,768]{1,0:T(8,128)(2,1)} %get-tuple-element.67), channel_id=1, source_target_pairs={{0,16},{16,0},{32,48},{48,32},{64,80},{80,64},{96,112},{112,96},{1... | collective-permute-start | bytes 589832 | tf_op jit(solution)/shard_map/ppermute | solution.py:490
  182.6 3.1 %collective-permute-start.21 = (bf16[128,768]{1,0:T(8,128)(2,1)}, bf16[128,768]{1,0:T(8,128)(2,1)S(1)}, u32[]{:S(2)}, u32[]{:S(2)}) collective-permute-start(bf16[128,768]{1,0:T(8,128)(2,1)} %get-tuple-element.68), channel_id=1, source_target_pairs={{16,32},{32,16},{48,64},{64,48},{80,96},{96,80},{17,33},{33,17},{4... | collective-permute-start | bytes 589832 | tf_op jit(solution)/shard_map/ppermute | solution.py:496
  185.7 2.0 collective-permute-done.20.inner_ref
  187.7 5.1 %collective-permute-done.21.outer_ref = bf16[128,768]{1,0:T(8,128)(2,1)S(1)} collective-permute-done((bf16[128,768]{1,0:T(8,128)(2,1)}, bf16[128,768]{1,0:T(8,128)(2,1)S(1)}, u32[]{:S(2)}, u32[]{:S(2)}) %collective-permute-start.21) | collective-permute-done | bytes 196640 | tf_op jit(solution)/shard_map/ppermute | solution.py:496
  192.8 0.7 copy-done.6
  193.5 2.8 %add_rows.1 = (bf16[256,384]{1,0:T(8,128)(2,1)}, bf16[256,384]{1,0:T(8,128)(2,1)}) custom-call(f32[256,768]{1,0:T(8,128)} %get-tuple-element.66.own_ref, bf16[128,768]{1,0:T(8,128)(2,1)} %copy-done.5, bf16[128,768]{1,0:T(8,128)(2,1)} %copy-done.6), custom_call_target="tpu_custom_call" | custom-call | flops 1048576 | bytes 6291456 | tf_op jit(solution)/shard_map/add_rows/pallas_call | solution.py:283
  (39 shorter events, 0.2 us)
Async XLA Ops:
  0.6 6.0 %copy-start = (bf16[3,1536,192]{1,2,0:T(8,128)(2,1)S(1)}, bf16[3,1536,192]{1,2,0:T(8,128)(2,1)}, u32[]{:S(2)}) copy-start(bf16[3,1536,192]{1,2,0:T(8,128)(2,1)} %param.9) | copy-start | bytes 5308420
  3.1 3.6 %collective-permute-start.3 = (bf16[3,512,128]{2,1,0:T(8,128)(2,1)}, bf16[3,512,128]{2,1,0:T(8,128)(2,1)S(1)}, u32[]{:S(2)}, u32[]{:S(2)}) collective-permute-start(bf16[3,512,128]{2,1,0:T(8,128)(2,1)} %get-tuple-element.38.refs_0_), channel_id=1, source_target_pairs={{0,1},{1,0},{2,3},{3,2},{4,5},{5,4},{6,7},{7,6},{8,9},{9,8},{10,11... | collective-permute-start | bytes 1179656 | tf_op jit(solution)/shard_map/ppermute | solution.py:490
  3.1 14.6 %collective-permute-start.1 = (bf16[3,512,128]{2,1,0:T(8,128)(2,1)}, bf16[3,512,128]{2,1,0:T(8,128)(2,1)S(1)}, u32[]{:S(2)}, u32[]{:S(2)}) collective-permute-start(bf16[3,512,128]{2,1,0:T(8,128)(2,1)} %get-tuple-element.44.refs_4_), channel_id=1, source_target_pairs={{0,6},{2,4},{4,2},{6,0},{1,7},{3,5},{5,3},{7,1},{8,14},{10,12},{12... | collective-permute-start | bytes 1179656 | tf_op jit(solution)/shard_map/ppermute | solution.py:490
  6.1 11.6 %collective-permute-start = (bf16[3,512,128]{2,1,0:T(8,128)(2,1)}, bf16[3,512,128]{2,1,0:T(8,128)(2,1)S(1)}, u32[]{:S(2)}, u32[]{:S(2)}) collective-permute-start(bf16[3,512,128]{2,1,0:T(8,128)(2,1)} %get-tuple-element.44.refs_4_), channel_id=1, source_target_pairs={{0,2},{2,0},{4,6},{6,4},{1,3},{3,1},{5,7},{7,5},{8,10},{10,8},{12,... | collective-permute-start | bytes 1179656 | tf_op jit(solution)/shard_map/ppermute | solution.py:490
  6.3 11.4 %collective-permute-start.2 = (bf16[3,512,128]{2,1,0:T(8,128)(2,1)}, bf16[3,512,128]{2,1,0:T(8,128)(2,1)}, u32[]{:S(2)}, u32[]{:S(2)}) collective-permute-start(bf16[3,512,128]{2,1,0:T(8,128)(2,1)} %get-tuple-element.38.refs_0_), channel_id=1, source_target_pairs={{0,8},{8,0},{1,9},{9,1},{2,10},{10,2},{3,11},{11,3},{4,12},{12,4},... | collective-permute-start | bytes 1179656 | tf_op jit(solution)/shard_map/ppermute | solution.py:490
  6.7 5.0 %copy-start.8 = (bf16[3,512,128]{2,1,0:T(8,128)(2,1)}, bf16[3,512,128]{2,1,0:T(8,128)(2,1)S(1)}, u32[]{:S(2)}) copy-start(bf16[3,512,128]{2,1,0:T(8,128)(2,1)S(1)} %collective-permute-done.3.refs_1_) | copy-start | bytes 1179652
  11.7 7.6 %copy-start.2 = (bf16[3,16,16,384]{3,2,1,0:T(8,128)(2,1)S(1)}, bf16[3,16,16,384]{3,2,1,0:T(8,128)(2,1)}, u32[]{:S(2)}) copy-start(bf16[3,16,16,384]{3,2,1,0:T(8,128)(2,1)} %param.5) | copy-start | bytes 1769476
  17.7 6.7 %collective-permute-start.4 = (bf16[3,512,128]{2,1,0:T(8,128)(2,1)}, bf16[3,512,128]{2,1,0:T(8,128)(2,1)S(1)}, u32[]{:S(2)}, u32[]{:S(2)}) collective-permute-start(bf16[3,512,128]{2,1,0:T(8,128)(2,1)} %collective-permute-done.2.refs_2_), channel_id=1, source_target_pairs={{0,1},{1,0},{2,3},{3,2},{4,5},{5,4},{6,7},{7,6},{8,9},{9,8},{10,11... | collective-permute-start | bytes 1179656 | tf_op jit(solution)/shard_map/ppermute | solution.py:490
  17.7 0.8 copy-start.9
  18.5 0.8 copy-start.10
  19.3 20.6 %collective-permute-start.6 = (bf16[2,8,16,384]{3,2,1,0:T(8,128)(2,1)S(1)}, bf16[2,8,16,384]{3,2,1,0:T(8,128)(2,1)S(1)}, u32[]{:S(2)}, u32[]{:S(2)}) collective-permute-start(bf16[2,8,16,384]{3,2,1,0:T(8,128)(2,1)S(1)} %get-tuple-element.75), channel_id=1, source_target_pairs={{16,32},{32,16},{48,64},{64,48},{80,96},{96,80},{17,33},{33,17},{4... | collective-permute-start | bytes 589832 | tf_op jit(solution)/shard_map/ppermute | solution.py:496
  22.7 17.2 %slice-start = ((bf16[3,16,16,384]{3,2,1,0:T(8,128)(2,1)}), bf16[2,16,16,384]{3,2,1,0:T(8,128)(2,1)S(1)}, s32[]{:S(2)}) async-start(bf16[3,16,16,384]{3,2,1,0:T(8,128)(2,1)} %param.5), calls=%async_computation.1 | async-start | bytes 786432 | tf_op jit(solution)/shard_map/slice | solution.py:536
  22.7 17.2 %collective-permute-start.5 = (bf16[2,8,16,384]{3,2,1,0:T(8,128)(2,1)S(1)}, bf16[2,8,16,384]{3,2,1,0:T(8,128)(2,1)S(1)}, u32[]{:S(2)}, u32[]{:S(2)}) collective-permute-start(bf16[2,8,16,384]{3,2,1,0:T(8,128)(2,1)S(1)} %get-tuple-element.76), channel_id=1, source_target_pairs={{0,16},{16,0},{32,48},{48,32},{64,80},{80,64},{96,112},{112,96},{1... | collective-permute-start | bytes 589832 | tf_op jit(solution)/shard_map/ppermute | solution.py:490
  22.8 21.8 %collective-permute-start.7 = (bf16[3,512,128]{2,1,0:T(8,128)(2,1)}, bf16[3,512,128]{2,1,0:T(8,128)(2,1)}, u32[]{:S(2)}, u32[]{:S(2)}) collective-permute-start(bf16[3,512,128]{2,1,0:T(8,128)(2,1)} %get-tuple-element.44.refs_4_), channel_id=1, source_target_pairs={{0,4},{2,6},{4,0},{6,2},{1,5},{3,7},{5,1},{7,3},{8,12},{10,14},{12... | collective-permute-start | bytes 1179656 | tf_op jit(solution)/shard_map/ppermute | solution.py:490
  24.4 0.8 copy-start.11
  40.1 11.6 %copy-start.1 = (bf16[2,32,16,384]{3,2,1,0:T(8,128)(2,1)}, bf16[2,32,16,384]{3,2,1,0:T(8,128)(2,1)S(1)}, u32[]{:S(2)}) copy-start(bf16[2,32,16,384]{3,2,1,0:T(8,128)(2,1)S(1)} %pad_maximum_fusion) | copy-start | bytes 2359300
  41.0 11.4 %collective-permute-start.9 = (bf16[2,32,8,384]{3,2,1,0:T(8,128)(2,1)}, bf16[2,32,8,384]{3,2,1,0:T(8,128)(2,1)S(1)}, u32[]{:S(2)}, u32[]{:S(2)}) collective-permute-start(bf16[2,32,8,384]{3,2,1,0:T(8,128)(2,1)} %get-tuple-element.73), channel_id=1, source_target_pairs={{1,2},{2,1},{3,4},{4,3},{5,6},{6,5},{7,8},{8,7},{9,10},{10,9},{11,... | collective-permute-start | bytes 1179656 | tf_op jit(solution)/shard_map/ppermute | solution.py:496
  44.5 7.9 %collective-permute-start.8 = (bf16[2,32,8,384]{3,2,1,0:T(8,128)(2,1)S(1)}, bf16[2,32,8,384]{3,2,1,0:T(8,128)(2,1)S(1)}, u32[]{:S(2)}, u32[]{:S(2)}) collective-permute-start(bf16[2,32,8,384]{3,2,1,0:T(8,128)(2,1)S(1)} %get-tuple-element.74), channel_id=1, source_target_pairs={{0,1},{1,0},{2,3},{3,2},{4,5},{5,4},{6,7},{7,6},{8,9},{9,8},{10,11... | collective-permute-start | bytes 1179656 | tf_op jit(solution)/shard_map/ppermute | solution.py:490
  52.4 5.8 %collective-permute-start.12 = (f32[3,2,2048]{2,1,0:T(2,128)}, f32[3,2,2048]{2,1,0:T(2,128)S(1)}, u32[]{:S(2)}, u32[]{:S(2)}) collective-permute-start(f32[3,2,2048]{2,1,0:T(2,128)} %coarse_stats.3.refs_8_), channel_id=1, source_target_pairs={{0,4},{2,6},{4,0},{6,2},{1,5},{3,7},{5,1},{7,3},{8,12},{10,14},{12... | collective-permute-start | bytes 147464 | tf_op jit(solution)/shard_map/ppermute | solution.py:490
  54.6 5.5 %collective-permute-start.11 = (f32[3,2,2048]{2,1,0:T(2,128)}, f32[3,2,2048]{2,1,0:T(2,128)S(1)}, u32[]{:S(2)}, u32[]{:S(2)}) collective-permute-start(f32[3,2,2048]{2,1,0:T(2,128)} %coarse_stats.3.refs_8_), channel_id=1, source_target_pairs={{0,6},{2,4},{4,2},{6,0},{1,7},{3,5},{5,3},{7,1},{8,14},{10,12},{12... | collective-permute-start | bytes 147464 | tf_op jit(solution)/shard_map/ppermute | solution.py:490
  54.9 5.2 %collective-permute-start.10 = (f32[3,2,2048]{2,1,0:T(2,128)}, f32[3,2,2048]{2,1,0:T(2,128)S(1)}, u32[]{:S(2)}, u32[]{:S(2)}) collective-permute-start(f32[3,2,2048]{2,1,0:T(2,128)} %coarse_stats.3.refs_8_), channel_id=1, source_target_pairs={{0,2},{2,0},{4,6},{6,4},{1,3},{3,1},{5,7},{7,5},{8,10},{10,8},{12,... | collective-permute-start | bytes 147464 | tf_op jit(solution)/shard_map/ppermute | solution.py:490
  58.2 2.0 copy-start.16
  60.1 0.6 copy-start.17
  60.8 0.6 copy-start.18
  98.6 2.6 %collective-permute-start.16 = (bf16[2,3,512,128]{3,2,1,0:T(8,128)(2,1)}, bf16[2,3,512,128]{3,2,1,0:T(8,128)(2,1)S(1)}, u32[]{:S(2)}, u32[]{:S(2)}) collective-permute-start(bf16[2,3,512,128]{3,2,1,0:T(8,128)(2,1)} %get-tuple-element.58), channel_id=1, source_target_pairs={{0,1},{1,0},{2,3},{3,2},{4,5},{5,4},{6,7},{7,6},{8,9},{9,8},{10,11... | collective-permute-start | bytes 2359304 | tf_op jit(solution)/shard_map/ppermute | solution.py:490
  101.2 1.5 copy-start.7
  102.5 12.3 %collective-permute-start.17 = (bf16[3,512,128]{2,1,0:T(8,128)(2,1)S(1)}, bf16[3,512,128]{2,1,0:T(8,128)(2,1)S(1)}, u32[]{:S(2)}, u32[]{:S(2)}) collective-permute-start(bf16[3,512,128]{2,1,0:T(8,128)(2,1)S(1)} %fusion), channel_id=1, source_target_pairs={{0,8},{8,0},{1,9},{9,1},{2,10},{10,2},{3,11},{11,3},{4,12},{12,4},... | collective-permute-start | bytes 1179656 | tf_op jit(solution)/shard_map/ppermute | solution.py:490
  102.6 12.2 %collective-permute-start.13 = (bf16[192,512]{1,0:T(8,128)(2,1)}, bf16[192,512]{1,0:T(8,128)(2,1)S(1)}, u32[]{:S(2)}, u32[]{:S(2)}) collective-permute-start(bf16[192,512]{1,0:T(8,128)(2,1)} %get-tuple-element.54), channel_id=1, source_target_pairs={{0,2},{2,0},{4,6},{6,4},{1,3},{3,1},{5,7},{7,5},{8,10},{10,8},{12,... | collective-permute-start | bytes 589832 | tf_op jit(solution)/shard_map/ppermute | solution.py:490
  102.9 12.3 %collective-permute-start.14 = (bf16[192,512]{1,0:T(8,128)(2,1)}, bf16[192,512]{1,0:T(8,128)(2,1)S(1)}, u32[]{:S(2)}, u32[]{:S(2)}) collective-permute-start(bf16[192,512]{1,0:T(8,128)(2,1)} %get-tuple-element.55), channel_id=1, source_target_pairs={{0,4},{2,6},{4,0},{6,2},{1,5},{3,7},{5,1},{7,3},{8,12},{10,14},{12... | collective-permute-start | bytes 589832 | tf_op jit(solution)/shard_map/ppermute | solution.py:490
  105.7 12.0 %collective-permute-start.15 = (bf16[192,512]{1,0:T(8,128)(2,1)}, bf16[192,512]{1,0:T(8,128)(2,1)S(1)}, u32[]{:S(2)}, u32[]{:S(2)}) collective-permute-start(bf16[192,512]{1,0:T(8,128)(2,1)} %get-tuple-element.56), channel_id=1, source_target_pairs={{0,6},{2,4},{4,2},{6,0},{1,7},{3,5},{5,3},{7,1},{8,14},{10,12},{12... | collective-permute-start | bytes 589832 | tf_op jit(solution)/shard_map/ppermute | solution.py:490
  114.9 2.9 %copy-start.12 = (bf16[3,512,128]{2,1,0:T(8,128)(2,1)}, bf16[3,512,128]{2,1,0:T(8,128)(2,1)S(1)}, u32[]{:S(2)}) copy-start(bf16[3,512,128]{2,1,0:T(8,128)(2,1)S(1)} %collective-permute-done.17.refs_6_) | copy-start | bytes 1179652
  114.9 2.9 %copy-start.13 = (bf16[192,512]{1,0:T(8,128)(2,1)}, bf16[192,512]{1,0:T(8,128)(2,1)S(1)}, u32[]{:S(2)}) copy-start(bf16[192,512]{1,0:T(8,128)(2,1)S(1)} %collective-permute-done.13.refs_1_) | copy-start | bytes 589828
  115.2 2.6 %copy-start.14 = (bf16[192,512]{1,0:T(8,128)(2,1)}, bf16[192,512]{1,0:T(8,128)(2,1)S(1)}, u32[]{:S(2)}) copy-start(bf16[192,512]{1,0:T(8,128)(2,1)S(1)} %collective-permute-done.14.refs_2_) | copy-start | bytes 589828
  117.8 0.7 copy-start.15
  164.5 4.9 %collective-permute-start.18 = (bf16[256,768]{1,0:T(8,128)(2,1)}, bf16[256,768]{1,0:T(8,128)(2,1)S(1)}, u32[]{:S(2)}, u32[]{:S(2)}) collective-permute-start(bf16[256,768]{1,0:T(8,128)(2,1)} %get-tuple-element.64), channel_id=1, source_target_pairs={{0,1},{1,0},{2,3},{3,2},{4,5},{5,4},{6,7},{7,6},{8,9},{9,8},{10,11... | collective-permute-start | bytes 1179656 | tf_op jit(solution)/shard_map/ppermute | solution.py:490
  164.6 11.4 %collective-permute-start.19 = (bf16[256,768]{1,0:T(8,128)(2,1)}, bf16[256,768]{1,0:T(8,128)(2,1)S(1)}, u32[]{:S(2)}, u32[]{:S(2)}) collective-permute-start(bf16[256,768]{1,0:T(8,128)(2,1)} %get-tuple-element.65), channel_id=1, source_target_pairs={{1,2},{2,1},{3,4},{4,3},{5,6},{6,5},{7,8},{8,7},{9,10},{10,9},{11,... | collective-permute-start | bytes 1179656 | tf_op jit(solution)/shard_map/ppermute | solution.py:496
  169.4 6.6 %copy-start.3 = (bf16[256,768]{1,0:T(8,128)(2,1)}, bf16[256,768]{1,0:T(8,128)(2,1)S(1)}, u32[]{:S(2)}) copy-start(bf16[256,768]{1,0:T(8,128)(2,1)S(1)} %collective-permute-done.18.inner_ref) | copy-start | bytes 1179652
  176.0 0.8 copy-start.4
  180.3 7.4 %collective-permute-start.20 = (bf16[128,768]{1,0:T(8,128)(2,1)}, bf16[128,768]{1,0:T(8,128)(2,1)S(1)}, u32[]{:S(2)}, u32[]{:S(2)}) collective-permute-start(bf16[128,768]{1,0:T(8,128)(2,1)} %get-tuple-element.67), channel_id=1, source_target_pairs={{0,16},{16,0},{32,48},{48,32},{64,80},{80,64},{96,112},{112,96},{1... | collective-permute-start | bytes 589832 | tf_op jit(solution)/shard_map/ppermute | solution.py:490
  182.6 10.2 %collective-permute-start.21 = (bf16[128,768]{1,0:T(8,128)(2,1)}, bf16[128,768]{1,0:T(8,128)(2,1)S(1)}, u32[]{:S(2)}, u32[]{:S(2)}) collective-permute-start(bf16[128,768]{1,0:T(8,128)(2,1)} %get-tuple-element.68), channel_id=1, source_target_pairs={{16,32},{32,16},{48,64},{64,48},{80,96},{96,80},{17,33},{33,17},{4... | collective-permute-start | bytes 589832 | tf_op jit(solution)/shard_map/ppermute | solution.py:496
  187.7 5.1 %copy-start.5 = (bf16[128,768]{1,0:T(8,128)(2,1)}, bf16[128,768]{1,0:T(8,128)(2,1)S(1)}, u32[]{:S(2)}) copy-start(bf16[128,768]{1,0:T(8,128)(2,1)S(1)} %collective-permute-done.20.inner_ref) | copy-start | bytes 589828
  192.8 0.7 copy-start.6

commit v7 on v6

--- a/solution.py
+++ b/solution.py
@@ -243,22 +243,31 @@
 def fine_shares(own_qkv, ext_kv, rows, columns):
     _, own, width = own_qkv.shape
     heads = width // HD
-
-    def body(q_ref, mid_ref, low_ref, high_ref, out_ref, bias_ref):
+    count = SIDE * SIDE // 2
+
+    def body(q_ref, mid_ref, low_ref, high_ref, mid_out, side_out, o_ref, bias_ref):
         fill_bias(bias_ref, own, rows, columns)
         ext = (mid_ref, low_ref, high_ref)
         for pair, lanes in pairs_of(width):
             key = stacked(ext, 0, lanes)
+            value_t = stacked(ext, 1, lanes).T
+            parts = []
             for side in range(2):
                 query = half(q_ref[0, :, lanes], side) * BF16(SCALE)
                 score = nt(key, query) + bias_ref[...]
                 share = jnp.exp(score - jnp.max(score, axis=0, keepdims=True))
                 total = jnp.sum(share, axis=0, keepdims=True)
-                out_ref[2 * pair + side] = (share * (1.0 / total)).astype(BF16)
+                rounded = (share * (1.0 / total)).astype(BF16)
+                mid_out[2 * pair + side] = rounded[:count]
+                side_out[2 * pair + side] = rounded[count:]
+                total = jnp.sum(rounded.astype(F32), axis=0, keepdims=True)
+                parts.append(nn(value_t[side * HD : side * HD + HD], rounded) / total)
+            o_ref[:, lanes] = jnp.concatenate(parts, axis=0).T
 
     return whole_call(
         body,
-        jax.ShapeDtypeStruct((heads, SIDE * SIDE, own), BF16),
+        [jax.ShapeDtypeStruct((heads, count, own), BF16)] * 2
+        + [jax.ShapeDtypeStruct((own, width), F32)],
         "fine_shares",
         1 << 30,
         [pltpu.VMEM((SIDE * SIDE, own), F32)],
@@ -292,105 +301,157 @@
     )(*operands)
 
 
-def fine_grads(own_qkv, ext_kv, own_up, shares, rows, columns):
+def head_sums(up, out):
+    head = lax.broadcasted_iota(jnp.int32, (8, up.shape[1]), 0)
+    lane = lax.broadcasted_iota(jnp.int32, (8, up.shape[1]), 1)
+    pick = jnp.where((lane >> 6) == head, 1.0, 0.0).astype(F32)
+    return lax.dot_general(
+        pick,
+        up * out,
+        (((1,), (1,)), ((), ())),
+        preferred_element_type=F32,
+        precision=lax.Precision.HIGHEST,
+    )
+
+
+def pair_grads(q_ref, ext, up_ref, o_ref, share_ref):
+    delta = head_sums(up_ref[...].astype(F32), o_ref[...])
+    key = jnp.concatenate([ref[0] for ref in ext], axis=0)
+    key_t = key.T
+    value = jnp.concatenate([ref[1] for ref in ext], axis=0)
+    parts = []
+    key_sum = jnp.zeros(key.shape, F32)
+    value_sum = jnp.zeros(key.shape, F32)
+    for side in range(2):
+        query = half(q_ref[0], side) * BF16(SCALE)
+        up = half(up_ref[...], side)
+        rounded = share_ref[side]
+        product = nt(value, up) - delta[side : side + 1]
+        grads = (rounded.astype(F32) * product).astype(BF16)
+        key_sum += nn(grads, query)
+        value_sum += nn(rounded, up)
+        parts.append(nn(key_t[side * HD : side * HD + HD], grads))
+    return jnp.concatenate(parts, axis=0).T, key_sum, value_sum
+
+
+def fine_sides(own_qkv, sides, own_up, out, shares):
     _, own, width = own_qkv.shape
-    mid_size, side_size = ext_kv[0].shape[1], ext_kv[1].shape[1]
-
-    def body(q_ref, mid_ref, low_ref, high_ref, up_ref, share_ref, q_out, mid_out, *outs):
+    size = sides[0].shape[1]
+
+    def body(q_ref, low_ref, high_ref, up_ref, o_ref, share_ref, q_out, inner_out, outer_out):
         first = lax.axis_index("c") == 0
-        ext = (mid_ref, low_ref, high_ref)
-        key_t = jnp.concatenate([ref[0] for ref in ext], axis=0).T
-        value = jnp.concatenate([ref[1] for ref in ext], axis=0)
-        parts = []
-        key_sum = jnp.zeros((SIDE * SIDE, 128), F32)
-        value_sum = jnp.zeros((SIDE * SIDE, 128), F32)
-        for side in range(2):
-            query = half(q_ref[0], side) * BF16(SCALE)
-            up = half(up_ref[...], side)
-            rounded = share_ref[side]
-            share = rounded.astype(F32)
-            product = nt(value, up)
-            total = jnp.sum(share, axis=0, keepdims=True)
-            delta = jnp.sum(share * product, axis=0, keepdims=True) / total
-            grads = (share * (product - delta)).astype(BF16)
-            key_sum += nn(grads, query)
-            value_sum += nn(rounded, up)
-            parts.append(nn(key_t[side * HD : side * HD + HD], grads))
-        q_out[...] = (jnp.concatenate(parts, axis=0).T * SCALE).astype(BF16)
-        for at, total in ((slice(0, 128), key_sum), (slice(128, 256), value_sum)):
-            mid_out[:, at] = total[:mid_size]
-            low = total[mid_size : mid_size + side_size].astype(BF16)
-            high = total[mid_size + side_size :].astype(BF16)
-            outs[0][:, at] = jnp.where(first, high, low)
-            outs[1][:, at] = jnp.where(first, low, high)
+        q_out[...], *sums = pair_grads(q_ref, (low_ref, high_ref), up_ref, o_ref, share_ref)
+        for at, total in zip((slice(0, 128), slice(128, 256)), sums):
+            low, high = total[:size].astype(BF16), total[size:].astype(BF16)
+            inner_out[:, at] = jnp.where(first, high, low)
+            outer_out[:, at] = jnp.where(first, low, high)
 
     return pair_call(
         body,
-        [
-            jax.ShapeDtypeStruct((own, width), BF16),
-            jax.ShapeDtypeStruct((mid_size, 2 * width), F32),
-            jax.ShapeDtypeStruct((side_size, 2 * width), BF16),
-            jax.ShapeDtypeStruct((side_size, 2 * width), BF16),
-        ],
-        "fine_grads",
-        2 << 30,
+        [jax.ShapeDtypeStruct((own, width), F32)]
+        + [jax.ShapeDtypeStruct((size, 2 * width), BF16)] * 2,
+        "fine_sides",
+        1 << 30,
         own_qkv,
-        *ext_kv,
+        *sides,
         own_up,
+        out,
         shares,
     )
 
 
-def add_columns(mid, inner, outer, columns):
-    cells, wide = mid.shape
-    tall = cells // columns
-    edge = RIM * columns
-
-    def body(mid_ref, inner_ref, outer_ref, own_out, inner_out, outer_out):
-        first = lax.axis_index("c") == 0
-        inner = inner_ref[...].astype(F32).reshape(tall, RIM, -1)
-        outer = outer_ref[...].astype(F32).reshape(tall, RIM, -1)
-        left, right = jnp.where(first, outer, inner), jnp.where(first, inner, outer)
-        both = jnp.concatenate([left, right], axis=1).reshape(mid_ref.shape)
-        total = mid_ref[...] + both
-        top, bottom = total[:edge], total[cells - edge :]
+def fine_middle(own_qkv, middle, own_up, out, shares, query_part):
+    _, own, width = own_qkv.shape
+    size = middle.shape[1]
+    edge = (size - own) // 2
+
+    def body(q_ref, mid_ref, up_ref, o_ref, share_ref, part_ref, q_out, top, inside, bottom):
+        found, *sums = pair_grads(q_ref, (mid_ref,), up_ref, o_ref, share_ref)
+        q_out[...] = ((found + part_ref[...]) * SCALE).astype(BF16)
+        for at, total in zip((slice(0, 128), slice(128, 256)), sums):
+            top[:, at] = total[:edge]
+            inside[:, at] = total[edge : edge + own]
+            bottom[:, at] = total[edge + own :]
+
+    return pair_call(
+        body,
+        [jax.ShapeDtypeStruct((own, width), BF16)]
+        + [jax.ShapeDtypeStruct((count, 2 * width), F32) for count in (edge, own, edge)],
+        "fine_middle",
+        1 << 30,
+        own_qkv,
+        middle,
+        own_up,
+        out,
+        shares,
+        query_part,
+    )
+
+
+def beside_each_other(inner, outer):
+    first = lax.axis_index("c") == 0
+    cells, wide = inner.shape
+    inner = inner.astype(F32).reshape(cells // RIM, RIM, wide)
+    outer = outer.astype(F32).reshape(cells // RIM, RIM, wide)
+    left, right = jnp.where(first, outer, inner), jnp.where(first, inner, outer)
+    return jnp.concatenate([left, right], axis=1).reshape(2 * cells, wide)
+
+
+def add_strips(top, bottom, inner, outer):
+    edge, wide = top.shape
+    corner = edge // 2
+
+    def body(top_ref, bottom_ref, inner_ref, outer_ref, inner_out, outer_out):
         upper = lax.axis_index("zh") == 0
-        own_out[...] = total[edge : cells - edge]
-        inner_out[...] = jnp.where(upper, bottom, top).astype(BF16)
-        outer_out[...] = jnp.where(upper, top, bottom).astype(BF16)
-
-    return pair_call(
-        body,
-        [jax.ShapeDtypeStruct((cells - 2 * edge, wide), F32)]
-        + [jax.ShapeDtypeStruct((edge, wide), BF16)] * 2,
-        "add_columns",
+        cells = inner_ref.shape[0]
+        above = top_ref[...] + beside_each_other(inner_ref[:corner], outer_ref[:corner])
+        below = bottom_ref[...] + beside_each_other(
+            inner_ref[cells - corner :], outer_ref[cells - corner :]
+        )
+        inner_out[...] = jnp.where(upper, below, above).astype(BF16)
+        outer_out[...] = jnp.where(upper, above, below).astype(BF16)
+
+    return whole_call(
+        body,
+        [jax.ShapeDtypeStruct((edge, wide), BF16)] * 2,
+        "add_strips",
         1 << 20,
-        mid,
+        [],
+        top,
+        bottom,
         inner,
         outer,
     )
 
 
-def add_rows(own, inner, outer):
+def add_all(own, side_inner, side_outer, row_inner, row_outer):
     cells, wide = own.shape
-
-    def body(own_ref, inner_ref, outer_ref, k_out, v_out):
+    width = wide // 2
+    half_cells = cells // 2
+
+    def body(own_ref, side_in, side_out, row_in, row_out, k_out, v_out):
         upper = lax.axis_index("zh") == 0
-        inner = inner_ref[...].astype(F32)
-        outer = outer_ref[...].astype(F32)
+        corner = (side_in.shape[0] - half_cells) // 2
+        middle = slice(corner, corner + half_cells)
+        inner, outer = row_in[...].astype(F32), row_out[...].astype(F32)
         above, below = jnp.where(upper, outer, inner), jnp.where(upper, inner, outer)
         total = own_ref[...] + jnp.concatenate([above, below], axis=0)
-        k_out[...] = total[:, :128].astype(BF16)
-        v_out[...] = total[:, 128:].astype(BF16)
-
-    return pair_call(
-        body,
-        [jax.ShapeDtypeStruct((cells, wide // 2), BF16)] * 2,
-        "add_rows",
+        total += beside_each_other(side_in[middle], side_out[middle])
+        for pair, lanes in pairs_of(width):
+            k_out[:, lanes] = total[:, pair * 256 : pair * 256 + 128].astype(BF16)
+            v_out[:, lanes] = total[:, pair * 256 + 128 : pair * 256 + 256].astype(BF16)
+
+    return whole_call(
+        body,
+        [jax.ShapeDtypeStruct((cells, width), BF16)] * 2,
+        "add_all",
         1 << 20,
+        [],
         own,
-        inner,
-        outer,
+        side_inner,
+        side_outer,
+        row_inner,
+        row_outer,
     )
 
 
@@ -520,20 +581,22 @@
         coarse_qkv.reshape(3, tokens, group), grad_coarse.reshape(tokens, group)
     )
     across = swapped(key_value, "zl")
+    beside = swapped(key_value, "c")
+    beside, query_up, merge_weight, fine_qkv = lax.optimization_barrier(
+        (beside, query_up, merge_weight, fine_qkv)
+    )
     near = [query_up, swapped(query_up, "y", 1), swapped(query_up, "y", 3)]
-    beside = swapped(key_value, "c")
-    beside, merge_weight = lax.optimization_barrier((beside, merge_weight))
+    own_qkv = fine_qkv.reshape(3, own, width)
+    edges = sent_rims(fine_qkv[1:], ROW, "zh", 1)
     joint = lax.dot_general(
         qkv_weight, merge_weight, (((1,), (1,)), ((), ())), preferred_element_type=F32
     ).astype(BF16).reshape(3 * group, wide)
-    across, joint = lax.optimization_barrier((across, joint))
+    across, joint, *edges = lax.optimization_barrier((across, joint, *edges))
     corner = swapped(across, "c")
-    *near, joint, fine_qkv = lax.optimization_barrier((*near, joint, fine_qkv))
+    *near, joint = lax.optimization_barrier((*near, joint))
     far = swapped(near[0], "y", 2)
     keys = [key_value, beside, across, corner]
     queries = [near[0], near[1], far, near[2]]
-    own_qkv = fine_qkv.reshape(3, own, width)
-    edges = sent_rims(fine_qkv[1:], ROW, "zh", 1)
 
     part = coarse_stats(keys, near, [0, 1, 3], (), 256)
     part, *edges = lax.optimization_barrier((part, *edges))
@@ -554,21 +617,22 @@
     count = lax.axis_size(ROW)
     low, high = placed_rims(*edges, "c")
     ext_kv = [array.reshape(2, -1, width) for array in (tall, low, high)]
-    shares = fine_shares(own_qkv, ext_kv, rows, columns)
-    arrived, shares = lax.optimization_barrier((arrived, shares))
+    mid_shares, side_shares, out = fine_shares(own_qkv, ext_kv, rows, columns)
+    arrived, out = lax.optimization_barrier((arrived, out))
     projected = project(
         query_pieces, kept, from_core, arrived, joint, coarse_columns, count
     )
     pieces = lax.all_to_all(projected.reshape(count, -1, wide), ROW, 0, 0)
     own_up = spread(pieces, coarse_columns)
 
-    grad_query, mid, inner, outer = fine_grads(
-        own_qkv, ext_kv, own_up, shares, rows, columns
-    )
-    inner, outer = exchanged(inner, outer, COL)
-    middle, inner, outer = add_columns(mid, inner, outer, columns)
-    inner, outer = exchanged(inner, outer, ROW)
-    grad_key, grad_value = add_rows(middle, inner, outer)
+    query_part, inner, outer = fine_sides(own_qkv, ext_kv[1:], own_up, out, side_shares)
+    side_inner, side_outer = exchanged(inner, outer, COL)
+    grad_query, top, middle, bottom = fine_middle(
+        own_qkv, ext_kv[0], own_up, out, mid_shares, query_part
+    )
+    strips = add_strips(top, bottom, side_inner, side_outer)
+    row_inner, row_outer = exchanged(*strips, ROW)
+    grad_key, grad_value = add_all(middle, side_inner, side_outer, row_inner, row_outer)
     shape = (rows, columns, width)
     return grad_query.reshape(shape), grad_key.reshape(shape), grad_value.reshape(shape)
 

time: 197 us -> 192 us (0.975)
  waiting for transfers between devices: 28.6 us -> 23.2 us
  Pallas kernels: 91.5 us -> 94.9 us
    pallas_call x3 -> x5, Pallas kernels: 11.2 us -> 18.2 us  [whole_call(): pl.pallas_call(body, out_shape=out_shape, scratch_shapes=scratch, name=na...]
    ppermute x4, waiting for transfers between devices: 12.5 us -> 8.79 us  [exchanged(): return (swapped(inner, axis), lax.ppermute(outer, axis, beyond))]
    pallas_call x3 -> x2, Pallas kernels: 14.6 us -> 11 us  [pair_call(): pl.pallas_call(body, grid=(pairs,), in_specs=[spec(array) for array in op...]
    unnamed x38 -> x34, local copies, waits for them, and re-layouts: 5.69 us -> 4.1 us
  transfers between devices with their start and end apart: 22 -> 22, of which waited for: 10 -> 11; matrix products, arithmetic and copies ran while one was open for 4% -> 4% of each run, Pallas kernels for 14% -> 19%
where the time goes in v7:
time: 192 us; the launch traced here: 191 us
  Pallas kernels  94.9 us (49%)
  starting transfers between devices  31 us (16%)
  blocking collectives  27.6 us (14%)
  waiting for transfers between devices  23.2 us (12%)
  other arithmetic  4.91 us (3%)
  matrix products  4.81 us (3%)
  local copies, waits for them, and re-layouts  4.1 us (2%)
    pallas_call x1, Pallas kernels, coarse_grads(): pl.pallas_call(body, grid=(heads, blocks), in_specs=[pl.BlockSpec((1, tok...  37.2 us
    all_to_all x1, blocking collectives, shards(): pieces = lax.all_to_all(projected.reshape(count, -1, wide), ROW, 0, 0)  27.6 us
    pallas_call x2, Pallas kernels, coarse_stats(): pl.pallas_call(body, grid=(heads, number), in_specs=[pl.BlockSpec((1, tok...  21.8 us
    pallas_call x5, Pallas kernels, whole_call(): pl.pallas_call(body, out_shape=out_shape, scratch_shapes=scratch, name=na...  18.2 us
    ppermute x18, starting transfers between devices, swapped(): lax.ppermute(array, axis, [(i, i ^ flip) for i in range(lax.axis_size(axi...  16.9 us
    ppermute x18, waiting for transfers between devices, swapped(): lax.ppermute(array, axis, [(i, i ^ flip) for i in range(lax.axis_size(axi...  14.4 us
    ppermute x4, starting transfers between devices, exchanged(): return (swapped(inner, axis), lax.ppermute(outer, axis, beyond))  14.1 us
    pallas_call x2, Pallas kernels, pair_call(): pl.pallas_call(body, grid=(pairs,), in_specs=[spec(array) for array in op...  11 us
  transfers between devices with their start and end apart: 22, of which 11 were waited for; matrix products, arithmetic and copies ran while one was open for 4% of the time, Pallas kernels for 19%

profile of v7, /device:TPU:96, one launch (start us, length us, event | category | flops | bytes accessed | tf_op | source)
XLA Modules:
  0.0 191.4 jit_solution(1155252686251708850)
XLA Ops:
  0.6 0.0 copy-start
  0.6 0.0 copy-start.2
  0.7 2.5 %prepare.1 = (bf16[3,512,128]{2,1,0:T(8,128)(2,1)}, bf16[3,512,128]{2,1,0:T(8,128)(2,1)}) custom-call(bf16[3,512,192]{2,1,0:T(8,128)(2,1)} %bitcast.32, bf16[512,192]{1,0:T(8,128)(2,1)} %bitcast.33), custom_call_target="tpu_custom_call" | custom-call | flops 1048576 | bytes 6291456 | tf_op jit(solution)/shard_map/prepare/pallas_call | solution.py:197
  3.1 0.0 collective-permute-start
  3.1 0.4 collective-permute-start.1
  3.5 1.5 collective-permute-done.refs_1_
  5.1 3.0 %collective-permute-start.6 = (bf16[3,512,128]{2,1,0:T(8,128)(2,1)}, bf16[3,512,128]{2,1,0:T(8,128)(2,1)}, u32[]{:S(2)}, u32[]{:S(2)}) collective-permute-start(bf16[3,512,128]{2,1,0:T(8,128)(2,1)} %get-tuple-element.53.refs_4_), channel_id=1, source_target_pairs={{0,6},{2,4},{4,2},{6,0},{1,7},{3,5},{5,3},{7,1},{8,14},{10,12},{12... | collective-permute-start | bytes 1179656 | tf_op jit(solution)/shard_map/ppermute | solution.py:551
  8.1 0.1 collective-permute-start.5
  8.3 3.4 %collective-permute-start.3 = (bf16[2,8,16,384]{3,2,1,0:T(8,128)(2,1)S(1)}, bf16[2,8,16,384]{3,2,1,0:T(8,128)(2,1)S(1)}, u32[]{:S(2)}, u32[]{:S(2)}) collective-permute-start(bf16[2,8,16,384]{3,2,1,0:T(8,128)(2,1)S(1)} %get-tuple-element.91), channel_id=1, source_target_pairs={{16,32},{32,16},{48,64},{64,48},{80,96},{96,80},{17,33},{33,17},{4... | collective-permute-start | bytes 589832 | tf_op jit(solution)/shard_map/ppermute | solution.py:557
  11.7 0.1 collective-permute-start.2
  11.8 4.8 %fusion.1 = f32[1536,576]{0,1:S(1)} fusion(bf16[1536,1536]{1,0:T(8,128)(2,1)} %param.8, bf16[1536,576]{0,1:T(8,128)(2,1)S(1)} %bitcast.23), kind=kOutput, calls=%fused_computation.11 | convolution fusion | flops 2717908992 | bytes 10027008
  16.6 1.5 convert_element_type.20
  18.1 1.1 collective-permute-done.3
  19.2 4.1 %collective-permute-done.2 = bf16[2,8,16,384]{3,2,1,0:T(8,128)(2,1)S(1)} collective-permute-done((bf16[2,8,16,384]{3,2,1,0:T(8,128)(2,1)S(1)}, bf16[2,8,16,384]{3,2,1,0:T(8,128)(2,1)S(1)}, u32[]{:S(2)}, u32[]{:S(2)}) %collective-permute-start.2) | collective-permute-done | bytes 196640 | tf_op jit(solution)/shard_map/ppermute | solution.py:551
  23.3 0.0 collective-permute-start.4
  23.3 2.1 %collective-permute-start.7 = (bf16[3,512,128]{2,1,0:T(8,128)(2,1)}, bf16[3,512,128]{2,1,0:T(8,128)(2,1)}, u32[]{:S(2)}, u32[]{:S(2)}) collective-permute-start(bf16[3,512,128]{2,1,0:T(8,128)(2,1)} %get-tuple-element.53.refs_4_), channel_id=1, source_target_pairs={{0,4},{2,6},{4,0},{6,2},{1,5},{3,7},{5,1},{7,3},{8,12},{10,14},{12... | collective-permute-start | bytes 1179656 | tf_op jit(solution)/shard_map/ppermute | solution.py:551
  25.4 0.7 copy-done.5
  26.2 14.8 %coarse_stats.2.refs_5_ = f32[3,2,2048]{2,1,0:T(2,128)} custom-call(bf16[3,512,128]{2,1,0:T(8,128)(2,1)} %get-tuple-element.45.refs_0_, bf16[3,512,128]{2,1,0:T(8,128)(2,1)} %copy-done.4, bf16[3,512,128]{2,1,0:T(8,128)(2,1)} %collective-permute-done.1.refs_2_, bf16[3,512,128]{2,1,0:T(8,128)(2,1)} %copy-done.5, ...), custom_call_target="tpu_custom_call" | custom-call | flops 9663676416 | bytes 2097152 | tf_op jit(solution)/shard_map/coarse_stats/pallas_call | solution.py:109
  41.0 0.1 pad_maximum_fusion
  41.1 0.9 broadcast_select_fusion
  42.0 3.9 %collective-permute-start.9 = (bf16[2,32,8,384]{3,2,1,0:T(8,128)(2,1)}, bf16[2,32,8,384]{3,2,1,0:T(8,128)(2,1)S(1)}, u32[]{:S(2)}, u32[]{:S(2)}) collective-permute-start(bf16[2,32,8,384]{3,2,1,0:T(8,128)(2,1)} %get-tuple-element.89), channel_id=1, source_target_pairs={{1,2},{2,1},{3,4},{4,3},{5,6},{6,5},{7,8},{8,7},{9,10},{10,9},{11,... | collective-permute-start | bytes 1179656 | tf_op jit(solution)/shard_map/ppermute | solution.py:557
  45.9 0.1 collective-permute-start.8
  46.0 7.1 %coarse_stats.3.refs_8_ = f32[3,2,2048]{2,1,0:T(2,128)} custom-call(bf16[3,512,128]{2,1,0:T(8,128)(2,1)} %get-tuple-element.45.refs_0_, bf16[3,512,128]{2,1,0:T(8,128)(2,1)} %copy-done.4, bf16[3,512,128]{2,1,0:T(8,128)(2,1)} %collective-permute-done.1.refs_2_, bf16[3,512,128]{2,1,0:T(8,128)(2,1)} %copy-done.5, ...), custom_call_target="tpu_custom_call" | custom-call | flops 3221225472 | bytes 2097152 | tf_op jit(solution)/shard_map/coarse_stats/pallas_call | solution.py:109
  53.1 0.4 collective-permute-done.9
  53.5 1.7 collective-permute-start.12
  55.2 0.6 collective-permute-start.11
  55.7 1.2 collective-permute-start.10
  56.9 2.3 %collective-permute-done.12.refs_11_ = f32[3,2,2048]{2,1,0:T(2,128)S(1)} collective-permute-done((f32[3,2,2048]{2,1,0:T(2,128)}, f32[3,2,2048]{2,1,0:T(2,128)S(1)}, u32[]{:S(2)}, u32[]{:S(2)}) %collective-permute-start.12) | collective-permute-done | bytes 49184 | tf_op jit(solution)/shard_map/ppermute | solution.py:551
  59.3 1.4 collective-permute-done.11.refs_10_
  60.7 0.6 copy-done.15
  61.3 0.6 copy-done.16
  61.9 37.2 %coarse_grads.1 = (bf16[2,3,512,128]{3,2,1,0:T(8,128)(2,1)}, bf16[2,3,512,128]{3,2,1,0:T(8,128)(2,1)}, bf16[192,512]{1,0:T(8,128)(2,1)}, bf16[192,512]{1,0:T(8,1...) custom-call(bf16[3,512,128]{2,1,0:T(8,128)(2,1)} %get-tuple-element.45.refs_0_, ...), custom_call_target="tpu_custom_call" | custom-call | flops 32212254720 | bytes 4194304 | tf_op jit(solution)/shard_map/coarse_grads/pallas_call | solution.py:178
  99.1 0.1 collective-permute-start.16
  99.2 2.5 %collective-permute-done.16.refs_5_ = bf16[2,3,512,128]{3,2,1,0:T(8,128)(2,1)S(1)} collective-permute-done((bf16[2,3,512,128]{3,2,1,0:T(8,128)(2,1)}, bf16[2,3,512,128]{3,2,1,0:T(8,128)(2,1)S(1)}, u32[]{:S(2)}, u32[]{:S(2)}) %collective-permute-start.16) | collective-permute-done | bytes 786464 | tf_op jit(solution)/shard_map/ppermute | solution.py:551
  101.7 1.4 fusion
  103.1 0.4 collective-permute-start.17
  103.5 0.1 collective-permute-start.13
  103.6 3.1 %collective-permute-start.14 = (bf16[192,512]{1,0:T(8,128)(2,1)}, bf16[192,512]{1,0:T(8,128)(2,1)S(1)}, u32[]{:S(2)}, u32[]{:S(2)}) collective-permute-start(bf16[192,512]{1,0:T(8,128)(2,1)} %get-tuple-element.64), channel_id=1, source_target_pairs={{0,4},{2,6},{4,0},{6,2},{1,5},{3,7},{5,1},{7,3},{8,12},{10,14},{12... | collective-permute-start | bytes 589832 | tf_op jit(solution)/shard_map/ppermute | solution.py:551
  106.7 1.5 collective-permute-start.15
  108.2 1.0 select_bitcast_fusion
  109.2 8.6 %fine_shares.1 = (bf16[6,512,256]{2,1,0:T(8,128)(2,1)}, bf16[6,512,256]{2,1,0:T(8,128)(2,1)}, f32[256,384]{1,0:T(8,128)}) custom-call(bf16[3,256,384]{2,1,0:T(8,128)(2,1)} %bitcast.29, bf16[2,512,384]{2,1,0:T(8,128)(2,1)} %bitcast.25, bf16[2,256,384]{2,1,0:T(8,128)(2,1)} %get-tuple-element.88.low_ref, bf16[2,256,384]{2,1,0:T(8,128)(2,1)} %get-tuple-element.87.high_ref), custom_call_target="tpu_custom_call" | custom-call | flops 1073741824 | bytes 6291456 | tf_op jit(solution)/shard_map/fine_shares/pallas_call | solution.py:197
  117.8 0.0 copy-start.9
  117.8 0.0 copy-start.10
  117.8 0.6 collective-permute-done.15.refs_3_
  118.4 0.1 copy-done.8
  118.5 0.1 copy-done.9
  118.6 0.1 copy-done.10
  118.7 0.4 copy-done.11
  119.1 6.7 %project.1 = bf16[512,1536]{1,0:T(8,128)(2,1)} custom-call(bf16[192,512]{1,0:T(8,128)(2,1)} %get-tuple-element.62.refs_0_, bf16[192,512]{1,0:T(8,128)(2,1)} %copy-done.9, bf16[192,512]{1,0:T(8,128)(2,1)} %copy-done.10, bf16[192,512]{1,0:T(8,128)(2,1)} %copy-done.11, bf16[2,3,512,128]{3,2,1,0:T(8,128)(2,1)} %get-tuple-element.66.refs_4_, ...), custom_call_target="tpu_custom_call" | custom-call | flops 2147483648 | bytes 6291456 | tf_op jit(solution)/shard_map/project/pallas_call | solution.py:495
  125.8 27.6 %all_to_all.5.in_ref = bf16[8,64,1536]{2,1,0:T(8,128)(2,1)} all-to-all(bf16[8,64,1536]{2,1,0:T(8,128)(2,1)} %bitcast.28), channel_id=1, replica_groups=mesh['x'=4,'zh'=2,'zl'=2,'y'=4,'c'=2] {'x','zh'}, dimensions={0} | all-to-all | bytes 3145728 | tf_op jit(solution)/shard_map/all_to_all | solution.py:625
  153.4 2.5 %spread.1.up_ref = bf16[256,384]{1,0:T(8,128)(2,1)} custom-call(bf16[8,64,1536]{2,1,0:T(8,128)(2,1)} %all_to_all.5.in_ref), custom_call_target="tpu_custom_call" | custom-call | flops 268435456 | bytes 6291456 | tf_op jit(solution)/shard_map/spread/pallas_call | solution.py:197
  155.9 5.5 %fine_sides.1 = (f32[256,384]{1,0:T(8,128)}, bf16[256,768]{1,0:T(8,128)(2,1)}, bf16[256,768]{1,0:T(8,128)(2,1)}) custom-call(bf16[3,256,384]{2,1,0:T(8,128)(2,1)} %bitcast.30, bf16[2,256,384]{2,1,0:T(8,128)(2,1)} %get-tuple-element.88.low_ref, bf16[2,256,384]{2,1,0:T(8,128)(2,1)} %get-tuple-element.87.high_ref, bf16[256,384]{1,0:T(8,128)(2,1)} %spread.1.up_ref, ...), custom_call_target="tpu_custom_call" | custom-call | flops 1073741824 | bytes 6291456 | tf_op jit(solution)/shard_map/fine_sides/pallas_call | solution.py:292
  161.4 0.1 collective-permute-start.18
  161.5 3.7 %collective-permute-start.19 = (bf16[256,768]{1,0:T(8,128)(2,1)}, bf16[256,768]{1,0:T(8,128)(2,1)S(1)}, u32[]{:S(2)}, u32[]{:S(2)}) collective-permute-start(bf16[256,768]{1,0:T(8,128)(2,1)} %get-tuple-element.80), channel_id=1, source_target_pairs={{1,2},{2,1},{3,4},{4,3},{5,6},{6,5},{7,8},{8,7},{9,10},{10,9},{11,... | collective-permute-start | bytes 1179656 | tf_op jit(solution)/shard_map/ppermute | solution.py:557
  165.2 5.5 %fine_middle.1 = (bf16[256,384]{1,0:T(8,128)(2,1)}, f32[128,768]{1,0:T(8,128)}, f32[256,768]{1,0:T(8,128)}, f32[128,768]{1,0:T(8,128)}) custom-call(bf16[3,256,384]{2,1,0:T(8,128)(2,1)} %bitcast.31, bf16[2,512,384]{2,1,0:T(8,128)(2,1)} %bitcast.26, bf16[256,384]{1,0:T(8,128)(2,1)} %spread.1.up_ref, f32[256,384]{1,0:T(8,128)} %get-tuple-element.73.o_ref, ...), custom_call_target="tpu_custom_call" | custom-call | flops 1073741824 | bytes 6291456 | tf_op jit(solution)/shard_map/fine_middle/pallas_call | solution.py:292
  170.7 2.2 %collective-permute-done.19.outer_ref.side_out = bf16[256,768]{1,0:T(8,128)(2,1)S(1)} collective-permute-done((bf16[256,768]{1,0:T(8,128)(2,1)}, bf16[256,768]{1,0:T(8,128)(2,1)S(1)}, u32[]{:S(2)}, u32[]{:S(2)}) %collective-permute-start.19) | collective-permute-done | bytes 393248 | tf_op jit(solution)/shard_map/ppermute | solution.py:557
  172.9 0.7 copy-done.7
  173.6 2.2 %add_strips.1 = (bf16[128,768]{1,0:T(8,128)(2,1)}, bf16[128,768]{1,0:T(8,128)(2,1)}) custom-call(f32[128,768]{1,0:T(8,128)} %get-tuple-element.81.top_ref, f32[128,768]{1,0:T(8,128)} %get-tuple-element.82.bottom_ref, bf16[256,768]{1,0:T(8,128)(2,1)} %copy-done.6, bf16[256,768]{1,0:T(8,128)(2,1)} %copy-done.7), custom_call_target="tpu_custom_call" | custom-call | flops 1048576 | bytes 6291456 | tf_op jit(solution)/shard_map/add_strips/pallas_call | solution.py:197
  175.9 2.3 %collective-permute-start.20 = (bf16[128,768]{1,0:T(8,128)(2,1)}, bf16[128,768]{1,0:T(8,128)(2,1)S(1)}, u32[]{:S(2)}, u32[]{:S(2)}) collective-permute-start(bf16[128,768]{1,0:T(8,128)(2,1)} %get-tuple-element.83), channel_id=1, source_target_pairs={{0,16},{16,0},{32,48},{48,32},{64,80},{80,64},{96,112},{112,96},{1... | collective-permute-start | bytes 589832 | tf_op jit(solution)/shard_map/ppermute | solution.py:551
  178.2 3.1 %collective-permute-start.21 = (bf16[128,768]{1,0:T(8,128)(2,1)}, bf16[128,768]{1,0:T(8,128)(2,1)S(1)}, u32[]{:S(2)}, u32[]{:S(2)}) collective-permute-start(bf16[128,768]{1,0:T(8,128)(2,1)} %get-tuple-element.84), channel_id=1, source_target_pairs={{16,32},{32,16},{48,64},{64,48},{80,96},{96,80},{17,33},{33,17},{4... | collective-permute-start | bytes 589832 | tf_op jit(solution)/shard_map/ppermute | solution.py:557
  181.3 2.0 %collective-permute-done.20.row_in = bf16[128,768]{1,0:T(8,128)(2,1)S(1)} collective-permute-done((bf16[128,768]{1,0:T(8,128)(2,1)}, bf16[128,768]{1,0:T(8,128)(2,1)S(1)}, u32[]{:S(2)}, u32[]{:S(2)}) %collective-permute-start.20) | collective-permute-done | bytes 196640 | tf_op jit(solution)/shard_map/ppermute | solution.py:551
  183.2 5.1 %collective-permute-done.21.row_out = bf16[128,768]{1,0:T(8,128)(2,1)S(1)} collective-permute-done((bf16[128,768]{1,0:T(8,128)(2,1)}, bf16[128,768]{1,0:T(8,128)(2,1)S(1)}, u32[]{:S(2)}, u32[]{:S(2)}) %collective-permute-start.21) | collective-permute-done | bytes 196640 | tf_op jit(solution)/shard_map/ppermute | solution.py:557
  188.3 0.7 copy-done.13
  189.0 2.4 %add_all.1 = (bf16[256,384]{1,0:T(8,128)(2,1)}, bf16[256,384]{1,0:T(8,128)(2,1)}) custom-call(f32[256,768]{1,0:T(8,128)} %get-tuple-element.78.own_ref, bf16[256,768]{1,0:T(8,128)(2,1)} %copy-done.6, bf16[256,768]{1,0:T(8,128)(2,1)} %copy-done.7, bf16[128,768]{1,0:T(8,128)(2,1)} %copy-done.12, bf16[128,768]{1,0:T(8,128)(2,1)} %copy-done.13), custom_call_target="tpu_custom_call" | custom-call | flops 1048576 | bytes 6291456 | tf_op jit(solution)/shard_map/add_all/pallas_call | solution.py:197
  (36 shorter events, 0.2 us)
Async XLA Ops:
  0.6 11.1 %copy-start = (bf16[3,1536,192]{1,2,0:T(8,128)(2,1)S(1)}, bf16[3,1536,192]{1,2,0:T(8,128)(2,1)}, u32[]{:S(2)}) copy-start(bf16[3,1536,192]{1,2,0:T(8,128)(2,1)} %param.9) | copy-start | bytes 5308420
  0.6 7.6 %copy-start.2 = (bf16[3,16,16,384]{3,2,1,0:T(8,128)(2,1)S(1)}, bf16[3,16,16,384]{3,2,1,0:T(8,128)(2,1)}, u32[]{:S(2)}) copy-start(bf16[3,16,16,384]{3,2,1,0:T(8,128)(2,1)} %param.5) | copy-start | bytes 1769476
  3.1 1.9 %collective-permute-start = (bf16[3,512,128]{2,1,0:T(8,128)(2,1)}, bf16[3,512,128]{2,1,0:T(8,128)(2,1)S(1)}, u32[]{:S(2)}, u32[]{:S(2)}) collective-permute-start(bf16[3,512,128]{2,1,0:T(8,128)(2,1)} %get-tuple-element.45.refs_0_), channel_id=1, source_target_pairs={{0,1},{1,0},{2,3},{3,2},{4,5},{5,4},{6,7},{7,6},{8,9},{9,8},{10,11... | collective-permute-start | bytes 1179656 | tf_op jit(solution)/shard_map/ppermute | solution.py:551
  3.1 14.9 %collective-permute-start.1 = (bf16[3,512,128]{2,1,0:T(8,128)(2,1)}, bf16[3,512,128]{2,1,0:T(8,128)(2,1)}, u32[]{:S(2)}, u32[]{:S(2)}) collective-permute-start(bf16[3,512,128]{2,1,0:T(8,128)(2,1)} %get-tuple-element.45.refs_0_), channel_id=1, source_target_pairs={{0,8},{8,0},{1,9},{9,1},{2,10},{10,2},{3,11},{11,3},{4,12},{12,4},... | collective-permute-start | bytes 1179656 | tf_op jit(solution)/shard_map/ppermute | solution.py:551
  5.1 11.5 %copy-start.4 = (bf16[3,512,128]{2,1,0:T(8,128)(2,1)}, bf16[3,512,128]{2,1,0:T(8,128)(2,1)S(1)}, u32[]{:S(2)}) copy-start(bf16[3,512,128]{2,1,0:T(8,128)(2,1)S(1)} %collective-permute-done.refs_1_) | copy-start | bytes 1179652
  5.1 18.3 %collective-permute-start.6 = (bf16[3,512,128]{2,1,0:T(8,128)(2,1)}, bf16[3,512,128]{2,1,0:T(8,128)(2,1)}, u32[]{:S(2)}, u32[]{:S(2)}) collective-permute-start(bf16[3,512,128]{2,1,0:T(8,128)(2,1)} %get-tuple-element.53.refs_4_), channel_id=1, source_target_pairs={{0,6},{2,4},{4,2},{6,0},{1,7},{3,5},{5,3},{7,1},{8,14},{10,12},{12... | collective-permute-start | bytes 1179656 | tf_op jit(solution)/shard_map/ppermute | solution.py:551
  8.1 15.3 %collective-permute-start.5 = (bf16[3,512,128]{2,1,0:T(8,128)(2,1)}, bf16[3,512,128]{2,1,0:T(8,128)(2,1)}, u32[]{:S(2)}, u32[]{:S(2)}) collective-permute-start(bf16[3,512,128]{2,1,0:T(8,128)(2,1)} %get-tuple-element.53.refs_4_), channel_id=1, source_target_pairs={{0,2},{2,0},{4,6},{6,4},{1,3},{3,1},{5,7},{7,5},{8,10},{10,8},{12,... | collective-permute-start | bytes 1179656 | tf_op jit(solution)/shard_map/ppermute | solution.py:551
  8.3 10.9 %collective-permute-start.3 = (bf16[2,8,16,384]{3,2,1,0:T(8,128)(2,1)S(1)}, bf16[2,8,16,384]{3,2,1,0:T(8,128)(2,1)S(1)}, u32[]{:S(2)}, u32[]{:S(2)}) collective-permute-start(bf16[2,8,16,384]{3,2,1,0:T(8,128)(2,1)S(1)} %get-tuple-element.91), channel_id=1, source_target_pairs={{16,32},{32,16},{48,64},{64,48},{80,96},{96,80},{17,33},{33,17},{4... | collective-permute-start | bytes 589832 | tf_op jit(solution)/shard_map/ppermute | solution.py:557
  11.7 11.6 %collective-permute-start.2 = (bf16[2,8,16,384]{3,2,1,0:T(8,128)(2,1)S(1)}, bf16[2,8,16,384]{3,2,1,0:T(8,128)(2,1)S(1)}, u32[]{:S(2)}, u32[]{:S(2)}) collective-permute-start(bf16[2,8,16,384]{3,2,1,0:T(8,128)(2,1)S(1)} %get-tuple-element.92), channel_id=1, source_target_pairs={{0,16},{16,0},{32,48},{48,32},{64,80},{80,64},{96,112},{112,96},{1... | collective-permute-start | bytes 589832 | tf_op jit(solution)/shard_map/ppermute | solution.py:551
  23.3 2.1 %collective-permute-start.4 = (bf16[3,512,128]{2,1,0:T(8,128)(2,1)}, bf16[3,512,128]{2,1,0:T(8,128)(2,1)S(1)}, u32[]{:S(2)}, u32[]{:S(2)}) collective-permute-start(bf16[3,512,128]{2,1,0:T(8,128)(2,1)} %collective-permute-done.1.refs_2_), channel_id=1, source_target_pairs={{0,1},{1,0},{2,3},{3,2},{4,5},{5,4},{6,7},{7,6},{8,9},{9,8},{10,11... | collective-permute-start | bytes 1179656 | tf_op jit(solution)/shard_map/ppermute | solution.py:551
  23.3 17.7 %slice-start = ((bf16[3,16,16,384]{3,2,1,0:T(8,128)(2,1)}), bf16[2,16,16,384]{3,2,1,0:T(8,128)(2,1)S(1)}, s32[]{:S(2)}) async-start(bf16[3,16,16,384]{3,2,1,0:T(8,128)(2,1)} %param.5), calls=%async_computation.1 | async-start | bytes 786432 | tf_op jit(solution)/shard_map/slice | solution.py:590
  23.3 22.7 %collective-permute-start.7 = (bf16[3,512,128]{2,1,0:T(8,128)(2,1)}, bf16[3,512,128]{2,1,0:T(8,128)(2,1)}, u32[]{:S(2)}, u32[]{:S(2)}) collective-permute-start(bf16[3,512,128]{2,1,0:T(8,128)(2,1)} %get-tuple-element.53.refs_4_), channel_id=1, source_target_pairs={{0,4},{2,6},{4,0},{6,2},{1,5},{3,7},{5,1},{7,3},{8,12},{10,14},{12... | collective-permute-start | bytes 1179656 | tf_op jit(solution)/shard_map/ppermute | solution.py:551
  25.4 0.7 copy-start.5
  41.1 12.0 %copy-start.1 = (bf16[2,32,16,384]{3,2,1,0:T(8,128)(2,1)}, bf16[2,32,16,384]{3,2,1,0:T(8,128)(2,1)S(1)}, u32[]{:S(2)}) copy-start(bf16[2,32,16,384]{3,2,1,0:T(8,128)(2,1)S(1)} %pad_maximum_fusion) | copy-start | bytes 2359300
  42.0 11.4 %collective-permute-start.9 = (bf16[2,32,8,384]{3,2,1,0:T(8,128)(2,1)}, bf16[2,32,8,384]{3,2,1,0:T(8,128)(2,1)S(1)}, u32[]{:S(2)}, u32[]{:S(2)}) collective-permute-start(bf16[2,32,8,384]{3,2,1,0:T(8,128)(2,1)} %get-tuple-element.89), channel_id=1, source_target_pairs={{1,2},{2,1},{3,4},{4,3},{5,6},{6,5},{7,8},{8,7},{9,10},{10,9},{11,... | collective-permute-start | bytes 1179656 | tf_op jit(solution)/shard_map/ppermute | solution.py:557
  45.9 7.5 %collective-permute-start.8 = (bf16[2,32,8,384]{3,2,1,0:T(8,128)(2,1)S(1)}, bf16[2,32,8,384]{3,2,1,0:T(8,128)(2,1)S(1)}, u32[]{:S(2)}, u32[]{:S(2)}) collective-permute-start(bf16[2,32,8,384]{3,2,1,0:T(8,128)(2,1)S(1)} %get-tuple-element.90), channel_id=1, source_target_pairs={{0,1},{1,0},{2,3},{3,2},{4,5},{5,4},{6,7},{7,6},{8,9},{9,8},{10,11... | collective-permute-start | bytes 1179656 | tf_op jit(solution)/shard_map/ppermute | solution.py:551
  53.5 5.8 %collective-permute-start.12 = (f32[3,2,2048]{2,1,0:T(2,128)}, f32[3,2,2048]{2,1,0:T(2,128)S(1)}, u32[]{:S(2)}, u32[]{:S(2)}) collective-permute-start(f32[3,2,2048]{2,1,0:T(2,128)} %coarse_stats.3.refs_8_), channel_id=1, source_target_pairs={{0,4},{2,6},{4,0},{6,2},{1,5},{3,7},{5,1},{7,3},{8,12},{10,14},{12... | collective-permute-start | bytes 147464 | tf_op jit(solution)/shard_map/ppermute | solution.py:551
  55.2 5.5 %collective-permute-start.11 = (f32[3,2,2048]{2,1,0:T(2,128)}, f32[3,2,2048]{2,1,0:T(2,128)S(1)}, u32[]{:S(2)}, u32[]{:S(2)}) collective-permute-start(f32[3,2,2048]{2,1,0:T(2,128)} %coarse_stats.3.refs_8_), channel_id=1, source_target_pairs={{0,6},{2,4},{4,2},{6,0},{1,7},{3,5},{5,3},{7,1},{8,14},{10,12},{12... | collective-permute-start | bytes 147464 | tf_op jit(solution)/shard_map/ppermute | solution.py:551
  55.7 5.0 %collective-permute-start.10 = (f32[3,2,2048]{2,1,0:T(2,128)}, f32[3,2,2048]{2,1,0:T(2,128)S(1)}, u32[]{:S(2)}, u32[]{:S(2)}) collective-permute-start(f32[3,2,2048]{2,1,0:T(2,128)} %coarse_stats.3.refs_8_), channel_id=1, source_target_pairs={{0,2},{2,0},{4,6},{6,4},{1,3},{3,1},{5,7},{7,5},{8,10},{10,8},{12,... | collective-permute-start | bytes 147464 | tf_op jit(solution)/shard_map/ppermute | solution.py:551
  59.3 1.4 copy-start.14
  60.7 0.6 copy-start.15
  61.3 0.6 copy-start.16
  99.1 2.6 %collective-permute-start.16 = (bf16[2,3,512,128]{3,2,1,0:T(8,128)(2,1)}, bf16[2,3,512,128]{3,2,1,0:T(8,128)(2,1)S(1)}, u32[]{:S(2)}, u32[]{:S(2)}) collective-permute-start(bf16[2,3,512,128]{3,2,1,0:T(8,128)(2,1)} %get-tuple-element.67), channel_id=1, source_target_pairs={{0,1},{1,0},{2,3},{3,2},{4,5},{5,4},{6,7},{7,6},{8,9},{9,8},{10,11... | collective-permute-start | bytes 2359304 | tf_op jit(solution)/shard_map/ppermute | solution.py:551
  101.7 1.8 copy-start.3
  103.1 14.7 %collective-permute-start.17 = (bf16[3,512,128]{2,1,0:T(8,128)(2,1)S(1)}, bf16[3,512,128]{2,1,0:T(8,128)(2,1)S(1)}, u32[]{:S(2)}, u32[]{:S(2)}) collective-permute-start(bf16[3,512,128]{2,1,0:T(8,128)(2,1)S(1)} %fusion), channel_id=1, source_target_pairs={{0,8},{8,0},{1,9},{9,1},{2,10},{10,2},{3,11},{11,3},{4,12},{12,4},... | collective-permute-start | bytes 1179656 | tf_op jit(solution)/shard_map/ppermute | solution.py:551
  103.5 14.3 %collective-permute-start.13 = (bf16[192,512]{1,0:T(8,128)(2,1)}, bf16[192,512]{1,0:T(8,128)(2,1)S(1)}, u32[]{:S(2)}, u32[]{:S(2)}) collective-permute-start(bf16[192,512]{1,0:T(8,128)(2,1)} %get-tuple-element.63), channel_id=1, source_target_pairs={{0,2},{2,0},{4,6},{6,4},{1,3},{3,1},{5,7},{7,5},{8,10},{10,8},{12,... | collective-permute-start | bytes 589832 | tf_op jit(solution)/shard_map/ppermute | solution.py:551
  103.6 14.2 %collective-permute-start.14 = (bf16[192,512]{1,0:T(8,128)(2,1)}, bf16[192,512]{1,0:T(8,128)(2,1)S(1)}, u32[]{:S(2)}, u32[]{:S(2)}) collective-permute-start(bf16[192,512]{1,0:T(8,128)(2,1)} %get-tuple-element.64), channel_id=1, source_target_pairs={{0,4},{2,6},{4,0},{6,2},{1,5},{3,7},{5,1},{7,3},{8,12},{10,14},{12... | collective-permute-start | bytes 589832 | tf_op jit(solution)/shard_map/ppermute | solution.py:551
  106.7 11.7 %collective-permute-start.15 = (bf16[192,512]{1,0:T(8,128)(2,1)}, bf16[192,512]{1,0:T(8,128)(2,1)S(1)}, u32[]{:S(2)}, u32[]{:S(2)}) collective-permute-start(bf16[192,512]{1,0:T(8,128)(2,1)} %get-tuple-element.65), channel_id=1, source_target_pairs={{0,6},{2,4},{4,2},{6,0},{1,7},{3,5},{5,3},{7,1},{8,14},{10,12},{12... | collective-permute-start | bytes 589832 | tf_op jit(solution)/shard_map/ppermute | solution.py:551
  117.8 0.8 copy-start.8
  117.8 0.8 copy-start.9
  117.8 0.8 copy-start.10
  118.4 0.7 copy-start.11
  161.4 9.3 %collective-permute-start.18 = (bf16[256,768]{1,0:T(8,128)(2,1)}, bf16[256,768]{1,0:T(8,128)(2,1)S(1)}, u32[]{:S(2)}, u32[]{:S(2)}) collective-permute-start(bf16[256,768]{1,0:T(8,128)(2,1)} %get-tuple-element.79), channel_id=1, source_target_pairs={{0,1},{1,0},{2,3},{3,2},{4,5},{5,4},{6,7},{7,6},{8,9},{9,8},{10,11... | collective-permute-start | bytes 1179656 | tf_op jit(solution)/shard_map/ppermute | solution.py:551
  161.5 11.4 %collective-permute-start.19 = (bf16[256,768]{1,0:T(8,128)(2,1)}, bf16[256,768]{1,0:T(8,128)(2,1)S(1)}, u32[]{:S(2)}, u32[]{:S(2)}) collective-permute-start(bf16[256,768]{1,0:T(8,128)(2,1)} %get-tuple-element.80), channel_id=1, source_target_pairs={{1,2},{2,1},{3,4},{4,3},{5,6},{6,5},{7,8},{8,7},{9,10},{10,9},{11,... | collective-permute-start | bytes 1179656 | tf_op jit(solution)/shard_map/ppermute | solution.py:557
  170.7 2.2 %copy-start.6 = (bf16[256,768]{1,0:T(8,128)(2,1)}, bf16[256,768]{1,0:T(8,128)(2,1)S(1)}, u32[]{:S(2)}) copy-start(bf16[256,768]{1,0:T(8,128)(2,1)S(1)} %collective-permute-done.18.inner_ref.side_in) | copy-start | bytes 1179652
  172.9 0.7 copy-start.7
  175.9 7.4 %collective-permute-start.20 = (bf16[128,768]{1,0:T(8,128)(2,1)}, bf16[128,768]{1,0:T(8,128)(2,1)S(1)}, u32[]{:S(2)}, u32[]{:S(2)}) collective-permute-start(bf16[128,768]{1,0:T(8,128)(2,1)} %get-tuple-element.83), channel_id=1, source_target_pairs={{0,16},{16,0},{32,48},{48,32},{64,80},{80,64},{96,112},{112,96},{1... | collective-permute-start | bytes 589832 | tf_op jit(solution)/shard_map/ppermute | solution.py:551
  178.2 10.2 %collective-permute-start.21 = (bf16[128,768]{1,0:T(8,128)(2,1)}, bf16[128,768]{1,0:T(8,128)(2,1)S(1)}, u32[]{:S(2)}, u32[]{:S(2)}) collective-permute-start(bf16[128,768]{1,0:T(8,128)(2,1)} %get-tuple-element.84), channel_id=1, source_target_pairs={{16,32},{32,16},{48,64},{64,48},{80,96},{96,80},{17,33},{33,17},{4... | collective-permute-start | bytes 589832 | tf_op jit(solution)/shard_map/ppermute | solution.py:557
  183.2 5.1 %copy-start.12 = (bf16[128,768]{1,0:T(8,128)(2,1)}, bf16[128,768]{1,0:T(8,128)(2,1)S(1)}, u32[]{:S(2)}) copy-start(bf16[128,768]{1,0:T(8,128)(2,1)S(1)} %collective-permute-done.20.row_in) | copy-start | bytes 589828
  188.3 0.7 copy-start.13

commit v8 on v7

--- a/solution.py
+++ b/solution.py
@@ -16,7 +16,7 @@
 COL = ("zl", "y", "c")
 F32 = jnp.float32
 BF16 = jnp.bfloat16
-VMEM = 60 << 20
+VMEM = 24 << 20
 
 
 def nt(left, right):
@@ -400,6 +400,7 @@
 def add_strips(top, bottom, inner, outer):
     edge, wide = top.shape
     corner = edge // 2
+    sent = edge // RIM * RADIUS
 
     def body(top_ref, bottom_ref, inner_ref, outer_ref, inner_out, outer_out):
         upper = lax.axis_index("zh") == 0
@@ -408,12 +409,13 @@
         below = bottom_ref[...] + beside_each_other(
             inner_ref[cells - corner :], outer_ref[cells - corner :]
         )
+        above, below = above[edge - sent :], below[:sent]
         inner_out[...] = jnp.where(upper, below, above).astype(BF16)
         outer_out[...] = jnp.where(upper, above, below).astype(BF16)
 
     return whole_call(
         body,
-        [jax.ShapeDtypeStruct((edge, wide), BF16)] * 2,
+        [jax.ShapeDtypeStruct((sent, wide), BF16)] * 2,
         "add_strips",
         1 << 20,
         [],
@@ -435,7 +437,8 @@
         middle = slice(corner, corner + half_cells)
         inner, outer = row_in[...].astype(F32), row_out[...].astype(F32)
         above, below = jnp.where(upper, outer, inner), jnp.where(upper, inner, outer)
-        total = own_ref[...] + jnp.concatenate([above, below], axis=0)
+        skipped = jnp.zeros((cells - 2 * above.shape[0], wide), F32)
+        total = own_ref[...] + jnp.concatenate([above, skipped, below], axis=0)
         total += beside_each_other(side_in[middle], side_out[middle])
         for pair, lanes in pairs_of(width):
             k_out[:, lanes] = total[:, pair * 256 : pair * 256 + 128].astype(BF16)
@@ -462,7 +465,7 @@
     each = rows // count
     size = each * columns
     wide = joint.shape[1]
-    chunk = 256
+    chunk = 512
     blocks = len(query_pieces)
 
     def body(*refs):

time: 192 us -> 173 us (0.901)
  Pallas kernels: 94.9 us -> 73.8 us
  waiting for transfers between devices: 23.2 us -> 29.3 us
  other arithmetic: 4.91 us -> 2.71 us
    pallas_call x5, Pallas kernels: 18.2 us -> 8.12 us  [whole_call(): pl.pallas_call(body, out_shape=out_shape, scratch_shapes=scratch, name=na...]
    pallas_call x1, Pallas kernels: 6.73 us -> 2.39 us  [project(): pl.pallas_call(body, grid=(wide // chunk,), in_specs=[pl.BlockSpec((group...]
    ppermute x4, waiting for transfers between devices: 8.79 us -> 12.3 us  [exchanged(): return (swapped(inner, axis), lax.ppermute(outer, axis, beyond))]
    pallas_call x2, Pallas kernels: 11 us -> 7.98 us  [pair_call(): pl.pallas_call(body, grid=(pairs,), in_specs=[spec(array) for array in op...]
    ppermute x18, waiting for transfers between devices: 14.4 us -> 17.1 us  [swapped(): lax.ppermute(array, axis, [(i, i ^ flip) for i in range(lax.axis_size(axi...]
    pallas_call x2, Pallas kernels: 21.8 us -> 19.3 us  [coarse_stats(): pl.pallas_call(body, grid=(heads, number), in_specs=[pl.BlockSpec((1, tok...]
    unnamed x34 -> x14, local copies, waits for them, and re-layouts: 4.1 us -> 3.22 us
  transfers between devices with their start and end apart: 22 -> 22, of which waited for: 11 -> 14; matrix products, arithmetic and copies ran while one was open for 4% -> 4% of each run, Pallas kernels for 19% -> 17%
where the time goes in v8:
time: 173 us
  Pallas kernels  73.8 us (43%)
  starting transfers between devices  30.9 us (18%)
  waiting for transfers between devices  29.3 us (17%)
  blocking collectives  27 us (16%)
  matrix products  4.82 us (3%)
  local copies, waits for them, and re-layouts  3.23 us (2%)
  other arithmetic  2.71 us (2%)
    pallas_call x1, Pallas kernels, coarse_grads(): pl.pallas_call(body, grid=(heads, blocks), in_specs=[pl.BlockSpec((1, tok...  36 us
    all_to_all x1, blocking collectives, shards(): pieces = lax.all_to_all(projected.reshape(count, -1, wide), ROW, 0, 0)  27 us
    pallas_call x2, Pallas kernels, coarse_stats(): pl.pallas_call(body, grid=(heads, number), in_specs=[pl.BlockSpec((1, tok...  19.3 us
    ppermute x18, waiting for transfers between devices, swapped(): lax.ppermute(array, axis, [(i, i ^ flip) for i in range(lax.axis_size(axi...  17.1 us
    ppermute x18, starting transfers between devices, swapped(): lax.ppermute(array, axis, [(i, i ^ flip) for i in range(lax.axis_size(axi...  16.4 us
    ppermute x4, starting transfers between devices, exchanged(): return (swapped(inner, axis), lax.ppermute(outer, axis, beyond))  14.5 us
    ppermute x4, waiting for transfers between devices, exchanged(): return (swapped(inner, axis), lax.ppermute(outer, axis, beyond))  12.3 us
    pallas_call x5, Pallas kernels, whole_call(): pl.pallas_call(body, out_shape=out_shape, scratch_shapes=scratch, name=na...  8.12 us
  transfers between devices with their start and end apart: 22, of which 14 were waited for; matrix products, arithmetic and copies ran while one was open for 4% of the time, Pallas kernels for 17%

profile of v8, /device:TPU:96, one launch (start us, length us, event | category | flops | bytes accessed | tf_op | source)
XLA Modules:
  0.0 172.6 jit_solution(8853673873296066317)
XLA Ops:
  0.6 0.0 copy-start
  0.7 1.3 copy-done.2
  1.9 0.9 copy-done.6
  2.9 1.1 prepare.1
  4.0 0.0 collective-permute-start
  4.0 0.4 collective-permute-start.1
  4.4 1.5 collective-permute-done.refs_1_
  5.9 3.0 %collective-permute-start.6 = (bf16[3,512,128]{2,1,0:T(8,128)(2,1)}, bf16[3,512,128]{2,1,0:T(8,128)(2,1)}, u32[]{:S(2)}, u32[]{:S(2)}) collective-permute-start(bf16[3,512,128]{2,1,0:T(8,128)(2,1)} %get-tuple-element.53.refs_4_), channel_id=1, source_target_pairs={{0,6},{2,4},{4,2},{6,0},{1,7},{3,5},{5,3},{7,1},{8,14},{10,12},{12... | collective-permute-start | bytes 1179656 | tf_op jit(solution)/shard_map/ppermute | solution.py:554
  8.9 0.1 collective-permute-start.5
  9.1 1.1 broadcast_select_fusion.4
  10.1 3.4 %collective-permute-start.3 = (bf16[2,8,16,384]{3,2,1,0:T(8,128)(2,1)S(1)}, bf16[2,8,16,384]{3,2,1,0:T(8,128)(2,1)}, u32[]{:S(2)}, u32[]{:S(2)}) collective-permute-start(bf16[2,8,16,384]{3,2,1,0:T(8,128)(2,1)S(1)} %get-tuple-element.91), channel_id=1, source_target_pairs={{16,32},{32,16},{48,64},{64,48},{80,96},{96,80},{17,33},{33,17},{4... | collective-permute-start | bytes 589832 | tf_op jit(solution)/shard_map/ppermute | solution.py:560
  13.5 0.1 collective-permute-start.2
  13.6 4.8 %fusion.1 = f32[1536,576]{0,1:S(1)} fusion(bf16[1536,1536]{1,0:T(8,128)(2,1)} %param.8, bf16[1536,576]{0,1:T(8,128)(2,1)S(1)} %bitcast.23), kind=kOutput, calls=%fused_computation.11 | convolution fusion | flops 2717908992 | bytes 10027008
  18.5 0.2 convert_element_type.20
  18.7 0.0 collective-permute-done.1.refs_2_
  18.7 2.5 %collective-permute-done.3 = bf16[2,8,16,384]{3,2,1,0:T(8,128)(2,1)} collective-permute-done((bf16[2,8,16,384]{3,2,1,0:T(8,128)(2,1)S(1)}, bf16[2,8,16,384]{3,2,1,0:T(8,128)(2,1)}, u32[]{:S(2)}, u32[]{:S(2)}) %collective-permute-start.3) | collective-permute-done | bytes 196640 | tf_op jit(solution)/shard_map/ppermute | solution.py:560
  21.2 4.1 %collective-permute-done.2 = bf16[2,8,16,384]{3,2,1,0:T(8,128)(2,1)} collective-permute-done((bf16[2,8,16,384]{3,2,1,0:T(8,128)(2,1)S(1)}, bf16[2,8,16,384]{3,2,1,0:T(8,128)(2,1)}, u32[]{:S(2)}, u32[]{:S(2)}) %collective-permute-start.2) | collective-permute-done | bytes 196640 | tf_op jit(solution)/shard_map/ppermute | solution.py:554
  25.3 0.0 collective-permute-start.4
  25.3 1.5 collective-permute-start.7
  26.9 0.5 collective-permute-done.4.refs_3_
  27.4 1.0 copy-done.4
  28.4 14.1 %coarse_stats.2.refs_5_ = f32[3,2,2048]{2,1,0:T(2,128)S(1)} custom-call(bf16[3,512,128]{2,1,0:T(8,128)(2,1)} %get-tuple-element.45.refs_0_, bf16[3,512,128]{2,1,0:T(8,128)(2,1)S(1)} %copy-done.4, bf16[3,512,128]{2,1,0:T(8,128)(2,1)} %collective-permute-done.1.refs_2_, bf16[3,512,128]{2,1,0:T(8,128)(2,1)} %collective-permute-done.4.refs_3_, ...), custom_call_target="tpu_custom_call" | custom-call | flops 9663676416 | bytes 2097152 | tf_op jit(solution)/shard_map/coarse_stats/pallas_call | solution.py:109
  42.4 1.1 broadcast_select_fusion.3
  43.5 0.1 pad_maximum_fusion
  43.6 0.1 broadcast_select_fusion
  43.7 3.6 %collective-permute-start.9 = (bf16[2,32,8,384]{3,2,1,0:T(8,128)(2,1)S(1)}, bf16[2,32,8,384]{3,2,1,0:T(8,128)(2,1)S(1)}, u32[]{:S(2)}, u32[]{:S(2)}) collective-permute-start(bf16[2,32,8,384]{3,2,1,0:T(8,128)(2,1)S(1)} %get-tuple-element.89), channel_id=1, source_target_pairs={{1,2},{2,1},{3,4},{4,3},{5,6},{6,5},{7,8},{8,7},{9,10},{10,9},{11,... | collective-permute-start | bytes 1179656 | tf_op jit(solution)/shard_map/ppermute | solution.py:560
  47.3 0.2 collective-permute-start.8
  47.6 5.2 %coarse_stats.3.refs_8_ = f32[3,2,2048]{2,1,0:T(2,128)S(1)} custom-call(bf16[3,512,128]{2,1,0:T(8,128)(2,1)} %get-tuple-element.45.refs_0_, bf16[3,512,128]{2,1,0:T(8,128)(2,1)S(1)} %copy-done.5, bf16[3,512,128]{2,1,0:T(8,128)(2,1)} %collective-permute-done.1.refs_2_, bf16[3,512,128]{2,1,0:T(8,128)(2,1)} %collective-permute-done.4.refs_3_, ...), custom_call_target="tpu_custom_call" | custom-call | flops 3221225472 | bytes 2097152 | tf_op jit(solution)/shard_map/coarse_stats/pallas_call | solution.py:109
  52.8 2.1 %collective-permute-done.9 = bf16[2,32,8,384]{3,2,1,0:T(8,128)(2,1)S(1)} collective-permute-done((bf16[2,32,8,384]{3,2,1,0:T(8,128)(2,1)S(1)}, bf16[2,32,8,384]{3,2,1,0:T(8,128)(2,1)S(1)}, u32[]{:S(2)}, u32[]{:S(2)}) %collective-permute-start.9) | collective-permute-done | bytes 393248 | tf_op jit(solution)/shard_map/ppermute | solution.py:560
  54.9 0.2 collective-permute-start.12
  55.1 2.1 %collective-permute-start.11 = (f32[3,2,2048]{2,1,0:T(2,128)S(1)}, f32[3,2,2048]{2,1,0:T(2,128)S(1)}, u32[]{:S(2)}, u32[]{:S(2)}) collective-permute-start(f32[3,2,2048]{2,1,0:T(2,128)S(1)} %coarse_stats.3.refs_8_), channel_id=1, source_target_pairs={{0,6},{2,4},{4,2},{6,0},{1,7},{3,5},{5,3},{7,1},{8,14},{10,12},{12... | collective-permute-start | bytes 147464 | tf_op jit(solution)/shard_map/ppermute | solution.py:554
  57.2 1.2 collective-permute-start.10
  58.4 2.5 %collective-permute-done.12.refs_11_ = f32[3,2,2048]{2,1,0:T(2,128)S(1)} collective-permute-done((f32[3,2,2048]{2,1,0:T(2,128)S(1)}, f32[3,2,2048]{2,1,0:T(2,128)S(1)}, u32[]{:S(2)}, u32[]{:S(2)}) %collective-permute-start.12) | collective-permute-done | bytes 49184 | tf_op jit(solution)/shard_map/ppermute | solution.py:554
  60.9 0.4 collective-permute-done.10.refs_9_
  61.3 36.0 %coarse_grads.1 = (bf16[2,3,512,128]{3,2,1,0:T(8,128)(2,1)S(1)}, bf16[2,3,512,128]{3,2,1,0:T(8,128)(2,1)S(1)}, bf16[192,512]{1,0:T(8,128)(2,1)S(1)}, bf16[192,51...) custom-call(bf16[3,512,128]{2,1,0:T(8,128)(2,1)} %get-tuple-element.45.refs_0_, ...), custom_call_target="tpu_custom_call" | custom-call | flops 32212254720 | bytes 4194304 | tf_op jit(solution)/shard_map/coarse_grads/pallas_call | solution.py:178
  97.3 0.0 copy-start.1
  97.3 0.1 collective-permute-start.16
  97.4 2.3 %collective-permute-done.16.refs_5_ = bf16[2,3,512,128]{3,2,1,0:T(8,128)(2,1)S(1)} collective-permute-done((bf16[2,3,512,128]{3,2,1,0:T(8,128)(2,1)S(1)}, bf16[2,3,512,128]{3,2,1,0:T(8,128)(2,1)S(1)}, u32[]{:S(2)}, u32[]{:S(2)}) %collective-permute-start.16) | collective-permute-done | bytes 786464 | tf_op jit(solution)/shard_map/ppermute | solution.py:554
  99.7 0.1 fusion
  99.8 0.1 collective-permute-start.17
  99.9 1.3 collective-permute-start.13
  101.2 1.9 %collective-permute-start.14 = (bf16[192,512]{1,0:T(8,128)(2,1)S(1)}, bf16[192,512]{1,0:T(8,128)(2,1)S(1)}, u32[]{:S(2)}, u32[]{:S(2)}) collective-permute-start(bf16[192,512]{1,0:T(8,128)(2,1)S(1)} %get-tuple-element.64), channel_id=1, source_target_pairs={{0,4},{2,6},{4,0},{6,2},{1,5},{3,7},{5,1},{7,3},{8,12},{10,14},{12... | collective-permute-start | bytes 589832 | tf_op jit(solution)/shard_map/ppermute | solution.py:554
  103.1 1.6 collective-permute-start.15
  104.7 0.1 select_bitcast_fusion
  104.8 5.6 %fine_shares.1 = (bf16[6,512,256]{2,1,0:T(8,128)(2,1)S(1)}, bf16[6,512,256]{2,1,0:T(8,128)(2,1)S(1)}, f32[256,384]{1,0:T(8,128)S(1)}) custom-call(bf16[3,256,384]{2,1,0:T(8,128)(2,1)S(1)} %bitcast.28, bf16[2,512,384]{2,1,0:T(8,128)(2,1)S(1)} %bitcast.24, bf16[2,256,384]{2,1,0:T(8,128)(2,1)S(1)} %get-tuple-element.88.low_ref, ...), custom_call_target="tpu_custom_call" | custom-call | flops 1073741824 | bytes 6291456 | tf_op jit(solution)/shard_map/fine_shares/pallas_call | solution.py:197
  110.4 0.7 collective-permute-done.17.refs_6_
  111.1 0.0 collective-permute-done.13.refs_1_
  111.1 1.0 collective-permute-done.14.refs_2_
  112.0 2.6 %collective-permute-done.15.refs_3_ = bf16[192,512]{1,0:T(8,128)(2,1)S(1)} collective-permute-done((bf16[192,512]{1,0:T(8,128)(2,1)S(1)}, bf16[192,512]{1,0:T(8,128)(2,1)S(1)}, u32[]{:S(2)}, u32[]{:S(2)}) %collective-permute-start.15) | collective-permute-done | bytes 196640 | tf_op jit(solution)/shard_map/ppermute | solution.py:554
  114.6 2.4 %project.1 = bf16[512,1536]{1,0:T(8,128)(2,1)S(1)} custom-call(bf16[192,512]{1,0:T(8,128)(2,1)S(1)} %get-tuple-element.62.refs_0_, bf16[192,512]{1,0:T(8,128)(2,1)S(1)} %collective-permute-done.13.refs_1_, bf16[192,512]{1,0:T(8,128)(2,1)S(1)} %collective-permute-done.14.refs_2_, bf16[192,512]{1,0:T(8,128)(2,1)S(1)} %collective-permute-done.15.refs_3_, ...), custom_call_target="tpu_custom_call" | custom-call | flops 2147483648 | bytes 6291456 | tf_op jit(solution)/shard_map/project/pallas_call | solution.py:498
  117.0 27.0 %all_to_all.5.in_ref = bf16[8,64,1536]{2,1,0:T(8,128)(2,1)S(1)} all-to-all(bf16[8,64,1536]{2,1,0:T(8,128)(2,1)S(1)} %bitcast.27), channel_id=1, replica_groups=mesh['x'=4,'zh'=2,'zl'=2,'y'=4,'c'=2] {'x','zh'}, dimensions={0} | all-to-all | bytes 3145728 | tf_op jit(solution)/shard_map/all_to_all | solution.py:628
  144.0 0.4 spread.1.up_ref
  144.3 3.7 %fine_sides.1 = (f32[256,384]{1,0:T(8,128)S(1)}, bf16[256,768]{1,0:T(8,128)(2,1)S(1)}, bf16[256,768]{1,0:T(8,128)(2,1)S(1)}) custom-call(bf16[3,256,384]{2,1,0:T(8,128)(2,1)S(1)} %bitcast.29, bf16[2,256,384]{2,1,0:T(8,128)(2,1)S(1)} %get-tuple-element.88.low_ref, bf16[2,256,384]{2,1,0:T(8,128)(2,1)S(1)} %get-tuple-element.87.high_ref, ...), custom_call_target="tpu_custom_call" | custom-call | flops 1073741824 | bytes 6291456 | tf_op jit(solution)/shard_map/fine_sides/pallas_call | solution.py:292
  148.0 0.1 collective-permute-start.18
  148.1 4.4 %collective-permute-start.19 = (bf16[256,768]{1,0:T(8,128)(2,1)S(1)}, bf16[256,768]{1,0:T(8,128)(2,1)S(1)}, u32[]{:S(2)}, u32[]{:S(2)}) collective-permute-start(bf16[256,768]{1,0:T(8,128)(2,1)S(1)} %get-tuple-element.80), channel_id=1, source_target_pairs={{1,2},{2,1},{3,4},{4,3},{5,6},{6,5},{7,8},{8,7},{9,10},{10,9},{11,... | collective-permute-start | bytes 1179656 | tf_op jit(solution)/shard_map/ppermute | solution.py:560
  152.5 4.3 %fine_middle.1 = (bf16[256,384]{1,0:T(8,128)(2,1)}, f32[128,768]{1,0:T(8,128)S(1)}, f32[256,768]{1,0:T(8,128)S(1)}, f32[128,768]{1,0:T(8,128)S(1)}) custom-call(bf16[3,256,384]{2,1,0:T(8,128)(2,1)S(1)} %bitcast.30, bf16[2,512,384]{2,1,0:T(8,128)(2,1)S(1)} %bitcast.25, bf16[256,384]{1,0:T(8,128)(2,1)S(1)} %spread.1.up_ref, ...), custom_call_target="tpu_custom_call" | custom-call | flops 1073741824 | bytes 6291456 | tf_op jit(solution)/shard_map/fine_middle/pallas_call | solution.py:292
  156.8 0.0 collective-permute-done.18.inner_ref.side_in
  156.8 2.6 %collective-permute-done.19.outer_ref.side_out = bf16[256,768]{1,0:T(8,128)(2,1)S(1)} collective-permute-done((bf16[256,768]{1,0:T(8,128)(2,1)S(1)}, bf16[256,768]{1,0:T(8,128)(2,1)S(1)}, u32[]{:S(2)}, u32[]{:S(2)}) %collective-permute-start.19) | collective-permute-done | bytes 393248 | tf_op jit(solution)/shard_map/ppermute | solution.py:560
  159.4 0.1 add_strips.1
  159.6 2.4 %collective-permute-start.20 = (bf16[112,768]{1,0:T(8,128)(2,1)S(1)}, bf16[112,768]{1,0:T(8,128)(2,1)S(1)}, u32[]{:S(2)}, u32[]{:S(2)}) collective-permute-start(bf16[112,768]{1,0:T(8,128)(2,1)S(1)} %get-tuple-element.83), channel_id=1, source_target_pairs={{0,16},{16,0},{32,48},{48,32},{64,80},{80,64},{96,112},{112,96},{1... | collective-permute-start | bytes 516104 | tf_op jit(solution)/shard_map/ppermute | solution.py:554
  162.0 3.1 %collective-permute-start.21 = (bf16[112,768]{1,0:T(8,128)(2,1)S(1)}, bf16[112,768]{1,0:T(8,128)(2,1)S(1)}, u32[]{:S(2)}, u32[]{:S(2)}) collective-permute-start(bf16[112,768]{1,0:T(8,128)(2,1)S(1)} %get-tuple-element.84), channel_id=1, source_target_pairs={{16,32},{32,16},{48,64},{64,48},{80,96},{96,80},{17,33},{33,17},{4... | collective-permute-start | bytes 516104 | tf_op jit(solution)/shard_map/ppermute | solution.py:560
  165.1 1.5 collective-permute-done.20.row_in
  166.6 5.1 %collective-permute-done.21.row_out = bf16[112,768]{1,0:T(8,128)(2,1)S(1)} collective-permute-done((bf16[112,768]{1,0:T(8,128)(2,1)S(1)}, bf16[112,768]{1,0:T(8,128)(2,1)S(1)}, u32[]{:S(2)}, u32[]{:S(2)}) %collective-permute-start.21) | collective-permute-done | bytes 172064 | tf_op jit(solution)/shard_map/ppermute | solution.py:560
  171.7 0.9 add_all.1
  (16 shorter events, 0.0 us)
Async XLA Ops:
  0.6 13.0 %copy-start = (bf16[3,1536,192]{1,2,0:T(8,128)(2,1)S(1)}, bf16[3,1536,192]{1,2,0:T(8,128)(2,1)}, u32[]{:S(2)}) copy-start(bf16[3,1536,192]{1,2,0:T(8,128)(2,1)} %param.9) | copy-start | bytes 5308420
  0.6 1.3 copy-start.2
  1.9 0.9 copy-start.6
  4.0 1.9 %collective-permute-start = (bf16[3,512,128]{2,1,0:T(8,128)(2,1)}, bf16[3,512,128]{2,1,0:T(8,128)(2,1)S(1)}, u32[]{:S(2)}, u32[]{:S(2)}) collective-permute-start(bf16[3,512,128]{2,1,0:T(8,128)(2,1)} %get-tuple-element.45.refs_0_), channel_id=1, source_target_pairs={{0,1},{1,0},{2,3},{3,2},{4,5},{5,4},{6,7},{7,6},{8,9},{9,8},{10,11... | collective-permute-start | bytes 1179656 | tf_op jit(solution)/shard_map/ppermute | solution.py:554
  4.0 14.7 %collective-permute-start.1 = (bf16[3,512,128]{2,1,0:T(8,128)(2,1)}, bf16[3,512,128]{2,1,0:T(8,128)(2,1)}, u32[]{:S(2)}, u32[]{:S(2)}) collective-permute-start(bf16[3,512,128]{2,1,0:T(8,128)(2,1)} %get-tuple-element.45.refs_0_), channel_id=1, source_target_pairs={{0,8},{8,0},{1,9},{9,1},{2,10},{10,2},{3,11},{11,3},{4,12},{12,4},... | collective-permute-start | bytes 1179656 | tf_op jit(solution)/shard_map/ppermute | solution.py:554
  5.9 12.6 %copy-start.3 = (bf16[3,512,128]{2,1,0:T(8,128)(2,1)}, bf16[3,512,128]{2,1,0:T(8,128)(2,1)S(1)}, u32[]{:S(2)}) copy-start(bf16[3,512,128]{2,1,0:T(8,128)(2,1)S(1)} %collective-permute-done.refs_1_) | copy-start | bytes 1179652
  5.9 19.4 %collective-permute-start.6 = (bf16[3,512,128]{2,1,0:T(8,128)(2,1)}, bf16[3,512,128]{2,1,0:T(8,128)(2,1)}, u32[]{:S(2)}, u32[]{:S(2)}) collective-permute-start(bf16[3,512,128]{2,1,0:T(8,128)(2,1)} %get-tuple-element.53.refs_4_), channel_id=1, source_target_pairs={{0,6},{2,4},{4,2},{6,0},{1,7},{3,5},{5,3},{7,1},{8,14},{10,12},{12... | collective-permute-start | bytes 1179656 | tf_op jit(solution)/shard_map/ppermute | solution.py:554
  8.9 16.4 %collective-permute-start.5 = (bf16[3,512,128]{2,1,0:T(8,128)(2,1)}, bf16[3,512,128]{2,1,0:T(8,128)(2,1)}, u32[]{:S(2)}, u32[]{:S(2)}) collective-permute-start(bf16[3,512,128]{2,1,0:T(8,128)(2,1)} %get-tuple-element.53.refs_4_), channel_id=1, source_target_pairs={{0,2},{2,0},{4,6},{6,4},{1,3},{3,1},{5,7},{7,5},{8,10},{10,8},{12,... | collective-permute-start | bytes 1179656 | tf_op jit(solution)/shard_map/ppermute | solution.py:554
  10.1 11.0 %collective-permute-start.3 = (bf16[2,8,16,384]{3,2,1,0:T(8,128)(2,1)S(1)}, bf16[2,8,16,384]{3,2,1,0:T(8,128)(2,1)}, u32[]{:S(2)}, u32[]{:S(2)}) collective-permute-start(bf16[2,8,16,384]{3,2,1,0:T(8,128)(2,1)S(1)} %get-tuple-element.91), channel_id=1, source_target_pairs={{16,32},{32,16},{48,64},{64,48},{80,96},{96,80},{17,33},{33,17},{4... | collective-permute-start | bytes 589832 | tf_op jit(solution)/shard_map/ppermute | solution.py:560
  13.5 11.7 %collective-permute-start.2 = (bf16[2,8,16,384]{3,2,1,0:T(8,128)(2,1)S(1)}, bf16[2,8,16,384]{3,2,1,0:T(8,128)(2,1)}, u32[]{:S(2)}, u32[]{:S(2)}) collective-permute-start(bf16[2,8,16,384]{3,2,1,0:T(8,128)(2,1)S(1)} %get-tuple-element.92), channel_id=1, source_target_pairs={{0,16},{16,0},{32,48},{48,32},{64,80},{80,64},{96,112},{112,96},{1... | collective-permute-start | bytes 589832 | tf_op jit(solution)/shard_map/ppermute | solution.py:554
  25.3 2.1 %collective-permute-start.4 = (bf16[3,512,128]{2,1,0:T(8,128)(2,1)}, bf16[3,512,128]{2,1,0:T(8,128)(2,1)}, u32[]{:S(2)}, u32[]{:S(2)}) collective-permute-start(bf16[3,512,128]{2,1,0:T(8,128)(2,1)} %collective-permute-done.1.refs_2_), channel_id=1, source_target_pairs={{0,1},{1,0},{2,3},{3,2},{4,5},{5,4},{6,7},{7,6},{8,9},{9,8},{10,11... | collective-permute-start | bytes 1179656 | tf_op jit(solution)/shard_map/ppermute | solution.py:554
  25.3 18.2 %slice-start = ((bf16[3,16,16,384]{3,2,1,0:T(8,128)(2,1)}), bf16[2,16,16,384]{3,2,1,0:T(8,128)(2,1)S(1)}, s32[]{:S(2)}) async-start(bf16[3,16,16,384]{3,2,1,0:T(8,128)(2,1)} %param.5), calls=%async_computation.1 | async-start | bytes 786432 | tf_op jit(solution)/shard_map/slice | solution.py:593
  25.3 22.2 %collective-permute-start.7 = (bf16[3,512,128]{2,1,0:T(8,128)(2,1)}, bf16[3,512,128]{2,1,0:T(8,128)(2,1)S(1)}, u32[]{:S(2)}, u32[]{:S(2)}) collective-permute-start(bf16[3,512,128]{2,1,0:T(8,128)(2,1)} %get-tuple-element.53.refs_4_), channel_id=1, source_target_pairs={{0,4},{2,6},{4,0},{6,2},{1,5},{3,7},{5,1},{7,3},{8,12},{10,14},{12... | collective-permute-start | bytes 1179656 | tf_op jit(solution)/shard_map/ppermute | solution.py:554
  27.4 1.0 copy-start.4
  43.5 4.1 %copy-start.5 = (bf16[3,512,128]{2,1,0:T(8,128)(2,1)S(1)}, bf16[3,512,128]{2,1,0:T(8,128)(2,1)}, u32[]{:S(2)}) copy-start(bf16[3,512,128]{2,1,0:T(8,128)(2,1)} %copy-done.3) | copy-start | bytes 1179652
  43.7 11.2 %collective-permute-start.9 = (bf16[2,32,8,384]{3,2,1,0:T(8,128)(2,1)S(1)}, bf16[2,32,8,384]{3,2,1,0:T(8,128)(2,1)S(1)}, u32[]{:S(2)}, u32[]{:S(2)}) collective-permute-start(bf16[2,32,8,384]{3,2,1,0:T(8,128)(2,1)S(1)} %get-tuple-element.89), channel_id=1, source_target_pairs={{1,2},{2,1},{3,4},{4,3},{5,6},{6,5},{7,8},{8,7},{9,10},{10,9},{11,... | collective-permute-start | bytes 1179656 | tf_op jit(solution)/shard_map/ppermute | solution.py:560
  47.3 7.6 %collective-permute-start.8 = (bf16[2,32,8,384]{3,2,1,0:T(8,128)(2,1)S(1)}, bf16[2,32,8,384]{3,2,1,0:T(8,128)(2,1)S(1)}, u32[]{:S(2)}, u32[]{:S(2)}) collective-permute-start(bf16[2,32,8,384]{3,2,1,0:T(8,128)(2,1)S(1)} %get-tuple-element.90), channel_id=1, source_target_pairs={{0,1},{1,0},{2,3},{3,2},{4,5},{5,4},{6,7},{7,6},{8,9},{9,8},{10,11... | collective-permute-start | bytes 1179656 | tf_op jit(solution)/shard_map/ppermute | solution.py:554
  54.9 6.0 %collective-permute-start.12 = (f32[3,2,2048]{2,1,0:T(2,128)S(1)}, f32[3,2,2048]{2,1,0:T(2,128)S(1)}, u32[]{:S(2)}, u32[]{:S(2)}) collective-permute-start(f32[3,2,2048]{2,1,0:T(2,128)S(1)} %coarse_stats.3.refs_8_), channel_id=1, source_target_pairs={{0,4},{2,6},{4,0},{6,2},{1,5},{3,7},{5,1},{7,3},{8,12},{10,14},{12... | collective-permute-start | bytes 147464 | tf_op jit(solution)/shard_map/ppermute | solution.py:554
  55.1 5.8 %collective-permute-start.11 = (f32[3,2,2048]{2,1,0:T(2,128)S(1)}, f32[3,2,2048]{2,1,0:T(2,128)S(1)}, u32[]{:S(2)}, u32[]{:S(2)}) collective-permute-start(f32[3,2,2048]{2,1,0:T(2,128)S(1)} %coarse_stats.3.refs_8_), channel_id=1, source_target_pairs={{0,6},{2,4},{4,2},{6,0},{1,7},{3,5},{5,3},{7,1},{8,14},{10,12},{12... | collective-permute-start | bytes 147464 | tf_op jit(solution)/shard_map/ppermute | solution.py:554
  57.2 4.1 %collective-permute-start.10 = (f32[3,2,2048]{2,1,0:T(2,128)S(1)}, f32[3,2,2048]{2,1,0:T(2,128)S(1)}, u32[]{:S(2)}, u32[]{:S(2)}) collective-permute-start(f32[3,2,2048]{2,1,0:T(2,128)S(1)} %coarse_stats.3.refs_8_), channel_id=1, source_target_pairs={{0,2},{2,0},{4,6},{6,4},{1,3},{3,1},{5,7},{7,5},{8,10},{10,8},{12,... | collective-permute-start | bytes 147464 | tf_op jit(solution)/shard_map/ppermute | solution.py:554
  97.3 7.4 %copy-start.1 = (bf16[3,16,16,384]{3,2,1,0:T(8,128)(2,1)S(1)}, bf16[3,16,16,384]{3,2,1,0:T(8,128)(2,1)}, u32[]{:S(2)}) copy-start(bf16[3,16,16,384]{3,2,1,0:T(8,128)(2,1)} %param.5) | copy-start | bytes 1769476
  97.3 2.4 %collective-permute-start.16 = (bf16[2,3,512,128]{3,2,1,0:T(8,128)(2,1)S(1)}, bf16[2,3,512,128]{3,2,1,0:T(8,128)(2,1)S(1)}, u32[]{:S(2)}, u32[]{:S(2)}) collective-permute-start(bf16[2,3,512,128]{3,2,1,0:T(8,128)(2,1)S(1)} %get-tuple-element.67), channel_id=1, source_target_pairs={{0,1},{1,0},{2,3},{3,2},{4,5},{5,4},{6,7},{7,6},{8,9},{9,8},{10,11... | collective-permute-start | bytes 2359304 | tf_op jit(solution)/shard_map/ppermute | solution.py:554
  99.8 11.2 %collective-permute-start.17 = (bf16[3,512,128]{2,1,0:T(8,128)(2,1)S(1)}, bf16[3,512,128]{2,1,0:T(8,128)(2,1)S(1)}, u32[]{:S(2)}, u32[]{:S(2)}) collective-permute-start(bf16[3,512,128]{2,1,0:T(8,128)(2,1)S(1)} %fusion), channel_id=1, source_target_pairs={{0,8},{8,0},{1,9},{9,1},{2,10},{10,2},{3,11},{11,3},{4,12},{12,4},... | collective-permute-start | bytes 1179656 | tf_op jit(solution)/shard_map/ppermute | solution.py:554
  99.9 11.1 %collective-permute-start.13 = (bf16[192,512]{1,0:T(8,128)(2,1)S(1)}, bf16[192,512]{1,0:T(8,128)(2,1)S(1)}, u32[]{:S(2)}, u32[]{:S(2)}) collective-permute-start(bf16[192,512]{1,0:T(8,128)(2,1)S(1)} %get-tuple-element.63), channel_id=1, source_target_pairs={{0,2},{2,0},{4,6},{6,4},{1,3},{3,1},{5,7},{7,5},{8,10},{10,8},{12,... | collective-permute-start | bytes 589832 | tf_op jit(solution)/shard_map/ppermute | solution.py:554
  101.2 10.9 %collective-permute-start.14 = (bf16[192,512]{1,0:T(8,128)(2,1)S(1)}, bf16[192,512]{1,0:T(8,128)(2,1)S(1)}, u32[]{:S(2)}, u32[]{:S(2)}) collective-permute-start(bf16[192,512]{1,0:T(8,128)(2,1)S(1)} %get-tuple-element.64), channel_id=1, source_target_pairs={{0,4},{2,6},{4,0},{6,2},{1,5},{3,7},{5,1},{7,3},{8,12},{10,14},{12... | collective-permute-start | bytes 589832 | tf_op jit(solution)/shard_map/ppermute | solution.py:554
  103.1 11.5 %collective-permute-start.15 = (bf16[192,512]{1,0:T(8,128)(2,1)S(1)}, bf16[192,512]{1,0:T(8,128)(2,1)S(1)}, u32[]{:S(2)}, u32[]{:S(2)}) collective-permute-start(bf16[192,512]{1,0:T(8,128)(2,1)S(1)} %get-tuple-element.65), channel_id=1, source_target_pairs={{0,6},{2,4},{4,2},{6,0},{1,7},{3,5},{5,3},{7,1},{8,14},{10,12},{12... | collective-permute-start | bytes 589832 | tf_op jit(solution)/shard_map/ppermute | solution.py:554
  148.0 8.8 %collective-permute-start.18 = (bf16[256,768]{1,0:T(8,128)(2,1)S(1)}, bf16[256,768]{1,0:T(8,128)(2,1)S(1)}, u32[]{:S(2)}, u32[]{:S(2)}) collective-permute-start(bf16[256,768]{1,0:T(8,128)(2,1)S(1)} %get-tuple-element.79), channel_id=1, source_target_pairs={{0,1},{1,0},{2,3},{3,2},{4,5},{5,4},{6,7},{7,6},{8,9},{9,8},{10,11... | collective-permute-start | bytes 1179656 | tf_op jit(solution)/shard_map/ppermute | solution.py:554
  148.1 11.3 %collective-permute-start.19 = (bf16[256,768]{1,0:T(8,128)(2,1)S(1)}, bf16[256,768]{1,0:T(8,128)(2,1)S(1)}, u32[]{:S(2)}, u32[]{:S(2)}) collective-permute-start(bf16[256,768]{1,0:T(8,128)(2,1)S(1)} %get-tuple-element.80), channel_id=1, source_target_pairs={{1,2},{2,1},{3,4},{4,3},{5,6},{6,5},{7,8},{8,7},{9,10},{10,9},{11,... | collective-permute-start | bytes 1179656 | tf_op jit(solution)/shard_map/ppermute | solution.py:560
  159.6 7.0 %collective-permute-start.20 = (bf16[112,768]{1,0:T(8,128)(2,1)S(1)}, bf16[112,768]{1,0:T(8,128)(2,1)S(1)}, u32[]{:S(2)}, u32[]{:S(2)}) collective-permute-start(bf16[112,768]{1,0:T(8,128)(2,1)S(1)} %get-tuple-element.83), channel_id=1, source_target_pairs={{0,16},{16,0},{32,48},{48,32},{64,80},{80,64},{96,112},{112,96},{1... | collective-permute-start | bytes 516104 | tf_op jit(solution)/shard_map/ppermute | solution.py:554
  162.0 9.7 %collective-permute-start.21 = (bf16[112,768]{1,0:T(8,128)(2,1)S(1)}, bf16[112,768]{1,0:T(8,128)(2,1)S(1)}, u32[]{:S(2)}, u32[]{:S(2)}) collective-permute-start(bf16[112,768]{1,0:T(8,128)(2,1)S(1)} %get-tuple-element.84), channel_id=1, source_target_pairs={{16,32},{32,16},{48,64},{64,48},{80,96},{96,80},{17,33},{33,17},{4... | collective-permute-start | bytes 516104 | tf_op jit(solution)/shard_map/ppermute | solution.py:560

commit v9 on v8

--- a/solution.py
+++ b/solution.py
@@ -134,9 +134,9 @@
         step = pl.program_id(1)
         for at in range(blocks):
 
-            @pl.when(pl.program_id(1) == at)
+            @pl.when(step == at // 2)
             def _():
-                held[...] = qu_refs[at][0]
+                held[at % 2 * tokens : (at % 2 + 1) * tokens] = qu_refs[at][0]
 
         @pl.when(pl.program_id(1) == 0)
         def _():
@@ -144,7 +144,12 @@
 
         query = half(held[...], 0) * BF16(SCALE)
         upstream = half(held[...], 1)
-        found = [ref[0, :, own_block(step, tokens)] for ref in stats_refs]
+        found = [
+            jnp.concatenate(
+                [ref[0, :, own_block(2 * step + i, tokens)] for i in range(2)], axis=1
+            )
+            for ref in stats_refs
+        ]
         peak = found[0][:1]
         for part in found[1:]:
             peak = jnp.maximum(peak, part[:1])
@@ -152,21 +157,22 @@
         total = sum(shares)
         log_total = peak + jnp.log(total)
         delta = sum(share * part[1:] for share, part in zip(shares, found)) / total
-        found = jnp.zeros((HD, tokens), F32)
+        found = jnp.zeros((HD, 2 * tokens), F32)
+        both = jnp.concatenate([query, upstream], axis=0)
         for i in range(blocks):
             tile = kv_refs[i][0]
             share = jnp.exp(nt(tile, query) - log_total)
             grads = (share * (nt(tile, upstream) - delta)).astype(BF16)
-            acc[i] += nn(grads, query) + nn(share.astype(BF16), upstream)
+            acc[i] += nn(jnp.concatenate([grads, share.astype(BF16)], axis=1), both)
             found += nn(tile[:, :HD].T, grads)
         found = (found * SCALE).astype(BF16)
         for at in range(blocks):
 
-            @pl.when(pl.program_id(1) == at)
+            @pl.when(step == at // 2)
             def _():
-                q_outs[at][...] = found
-
-        @pl.when(pl.program_id(1) == blocks - 1)
+                q_outs[at][...] = found[:, at % 2 * tokens : (at % 2 + 1) * tokens]
+
+        @pl.when(step == blocks // 2 - 1)
         def _():
             for i in range(blocks // 2):
                 kept_ref[i, 0] = acc[2 * i].astype(BF16)
@@ -177,7 +183,7 @@
     out_shape += [jax.ShapeDtypeStruct((heads * HD, tokens), BF16)] * blocks
     return pl.pallas_call(
         body,
-        grid=(heads, blocks),
+        grid=(heads, blocks // 2),
         in_specs=[pl.BlockSpec((1, tokens, 128), lambda h, q: (h, 0, 0))] * (2 * blocks)
         + [pl.BlockSpec((1, 2, blocks * tokens), lambda h, q: (h, 0, 0))] * parts,
         out_specs=[pl.BlockSpec((blocks // 2, 1, tokens, 128), lambda h, q: (0, h, 0, 0))] * 2
@@ -185,7 +191,7 @@
         out_shape=out_shape,
         scratch_shapes=[
             pltpu.VMEM((blocks, tokens, 128), F32),
-            pltpu.VMEM((tokens, 128), BF16),
+            pltpu.VMEM((2 * tokens, 128), BF16),
         ],
         name="coarse_grads",
         cost_estimate=cost(10 * pairs * 256, 4 << 20, pairs),

time: 173 us -> 171 us (0.988)
  Pallas kernels: 73.8 us -> 71.9 us
    pallas_call x1, Pallas kernels: 36 us -> 34.2 us  [coarse_grads(): pl.pallas_call(body, grid=(heads, blocks // 2), in_specs=[pl.BlockSpec((1...]
where the time goes in v9:
time: 171 us
  Pallas kernels  71.9 us (42%)
  starting transfers between devices  30.9 us (18%)
  waiting for transfers between devices  29.3 us (17%)
  blocking collectives  27 us (16%)
  matrix products  4.82 us (3%)
  local copies, waits for them, and re-layouts  3.23 us (2%)
  other arithmetic  2.71 us (2%)
    pallas_call x1, Pallas kernels, coarse_grads(): pl.pallas_call(body, grid=(heads, blocks // 2), in_specs=[pl.BlockSpec((1...  34.2 us
    all_to_all x1, blocking collectives, shards(): pieces = lax.all_to_all(projected.reshape(count, -1, wide), ROW, 0, 0)  27 us
    pallas_call x2, Pallas kernels, coarse_stats(): pl.pallas_call(body, grid=(heads, number), in_specs=[pl.BlockSpec((1, tok...  19.3 us
    ppermute x18, waiting for transfers between devices, swapped(): lax.ppermute(array, axis, [(i, i ^ flip) for i in range(lax.axis_size(axi...  17.1 us
    ppermute x18, starting transfers between devices, swapped(): lax.ppermute(array, axis, [(i, i ^ flip) for i in range(lax.axis_size(axi...  16.4 us
    ppermute x4, starting transfers between devices, exchanged(): return (swapped(inner, axis), lax.ppermute(outer, axis, beyond))  14.5 us
    ppermute x4, waiting for transfers between devices, exchanged(): return (swapped(inner, axis), lax.ppermute(outer, axis, beyond))  12.3 us
    pallas_call x5, Pallas kernels, whole_call(): pl.pallas_call(body, out_shape=out_shape, scratch_shapes=scratch, name=na...  8.12 us
  transfers between devices with their start and end apart: 22, of which 14 were waited for; matrix products, arithmetic and copies ran while one was open for 4% of the time, Pallas kernels for 17%

profile of v9, /device:TPU:96, one launch (start us, length us, event | category | flops | bytes accessed | tf_op | source)
XLA Modules:
  0.0 170.7 jit_solution(12222013993288015664)
XLA Ops:
  0.6 0.0 copy-start
  0.7 1.3 copy-done.2
  1.9 0.9 copy-done.6
  2.9 1.1 prepare.1
  4.0 0.0 collective-permute-start
  4.0 0.4 collective-permute-start.1
  4.4 1.5 collective-permute-done.refs_1_
  5.9 3.0 %collective-permute-start.6 = (bf16[3,512,128]{2,1,0:T(8,128)(2,1)}, bf16[3,512,128]{2,1,0:T(8,128)(2,1)}, u32[]{:S(2)}, u32[]{:S(2)}) collective-permute-start(bf16[3,512,128]{2,1,0:T(8,128)(2,1)} %get-tuple-element.53.refs_4_), channel_id=1, source_target_pairs={{0,6},{2,4},{4,2},{6,0},{1,7},{3,5},{5,3},{7,1},{8,14},{10,12},{12... | collective-permute-start | bytes 1179656 | tf_op jit(solution)/shard_map/ppermute | solution.py:560
  8.9 0.1 collective-permute-start.5
  9.1 1.1 broadcast_select_fusion.4
  10.1 3.4 %collective-permute-start.3 = (bf16[2,8,16,384]{3,2,1,0:T(8,128)(2,1)S(1)}, bf16[2,8,16,384]{3,2,1,0:T(8,128)(2,1)}, u32[]{:S(2)}, u32[]{:S(2)}) collective-permute-start(bf16[2,8,16,384]{3,2,1,0:T(8,128)(2,1)S(1)} %get-tuple-element.91), channel_id=1, source_target_pairs={{16,32},{32,16},{48,64},{64,48},{80,96},{96,80},{17,33},{33,17},{4... | collective-permute-start | bytes 589832 | tf_op jit(solution)/shard_map/ppermute | solution.py:566
  13.5 0.1 collective-permute-start.2
  13.6 4.8 %fusion.1 = f32[1536,576]{0,1:S(1)} fusion(bf16[1536,1536]{1,0:T(8,128)(2,1)} %param.8, bf16[1536,576]{0,1:T(8,128)(2,1)S(1)} %bitcast.23), kind=kOutput, calls=%fused_computation.11 | convolution fusion | flops 2717908992 | bytes 10027008
  18.5 0.2 convert_element_type.20
  18.7 0.0 collective-permute-done.1.refs_2_
  18.7 2.5 %collective-permute-done.3 = bf16[2,8,16,384]{3,2,1,0:T(8,128)(2,1)} collective-permute-done((bf16[2,8,16,384]{3,2,1,0:T(8,128)(2,1)S(1)}, bf16[2,8,16,384]{3,2,1,0:T(8,128)(2,1)}, u32[]{:S(2)}, u32[]{:S(2)}) %collective-permute-start.3) | collective-permute-done | bytes 196640 | tf_op jit(solution)/shard_map/ppermute | solution.py:566
  21.2 4.1 %collective-permute-done.2 = bf16[2,8,16,384]{3,2,1,0:T(8,128)(2,1)} collective-permute-done((bf16[2,8,16,384]{3,2,1,0:T(8,128)(2,1)S(1)}, bf16[2,8,16,384]{3,2,1,0:T(8,128)(2,1)}, u32[]{:S(2)}, u32[]{:S(2)}) %collective-permute-start.2) | collective-permute-done | bytes 196640 | tf_op jit(solution)/shard_map/ppermute | solution.py:560
  25.3 0.0 collective-permute-start.4
  25.3 0.0 collective-permute-done.6.refs_6_.refs_7_
  25.3 1.5 collective-permute-start.7
  26.9 0.5 collective-permute-done.4.refs_3_
  27.4 1.0 copy-done.4
  28.4 14.1 %coarse_stats.2.refs_5_ = f32[3,2,2048]{2,1,0:T(2,128)S(1)} custom-call(bf16[3,512,128]{2,1,0:T(8,128)(2,1)} %get-tuple-element.45.refs_0_, bf16[3,512,128]{2,1,0:T(8,128)(2,1)S(1)} %copy-done.4, bf16[3,512,128]{2,1,0:T(8,128)(2,1)} %collective-permute-done.1.refs_2_, bf16[3,512,128]{2,1,0:T(8,128)(2,1)} %collective-permute-done.4.refs_3_, ...), custom_call_target="tpu_custom_call" | custom-call | flops 9663676416 | bytes 2097152 | tf_op jit(solution)/shard_map/coarse_stats/pallas_call | solution.py:109
  42.4 1.1 broadcast_select_fusion.3
  43.5 0.1 pad_maximum_fusion
  43.6 0.1 broadcast_select_fusion
  43.7 3.6 %collective-permute-start.9 = (bf16[2,32,8,384]{3,2,1,0:T(8,128)(2,1)S(1)}, bf16[2,32,8,384]{3,2,1,0:T(8,128)(2,1)S(1)}, u32[]{:S(2)}, u32[]{:S(2)}) collective-permute-start(bf16[2,32,8,384]{3,2,1,0:T(8,128)(2,1)S(1)} %get-tuple-element.89), channel_id=1, source_target_pairs={{1,2},{2,1},{3,4},{4,3},{5,6},{6,5},{7,8},{8,7},{9,10},{10,9},{11,... | collective-permute-start | bytes 1179656 | tf_op jit(solution)/shard_map/ppermute | solution.py:566
  47.3 0.2 collective-permute-start.8
  47.6 5.2 %coarse_stats.3.refs_8_ = f32[3,2,2048]{2,1,0:T(2,128)S(1)} custom-call(bf16[3,512,128]{2,1,0:T(8,128)(2,1)} %get-tuple-element.45.refs_0_, bf16[3,512,128]{2,1,0:T(8,128)(2,1)S(1)} %copy-done.5, bf16[3,512,128]{2,1,0:T(8,128)(2,1)} %collective-permute-done.1.refs_2_, bf16[3,512,128]{2,1,0:T(8,128)(2,1)} %collective-permute-done.4.refs_3_, ...), custom_call_target="tpu_custom_call" | custom-call | flops 3221225472 | bytes 2097152 | tf_op jit(solution)/shard_map/coarse_stats/pallas_call | solution.py:109
  52.8 2.1 %collective-permute-done.9 = bf16[2,32,8,384]{3,2,1,0:T(8,128)(2,1)S(1)} collective-permute-done((bf16[2,32,8,384]{3,2,1,0:T(8,128)(2,1)S(1)}, bf16[2,32,8,384]{3,2,1,0:T(8,128)(2,1)S(1)}, u32[]{:S(2)}, u32[]{:S(2)}) %collective-permute-start.9) | collective-permute-done | bytes 393248 | tf_op jit(solution)/shard_map/ppermute | solution.py:566
  54.9 0.2 collective-permute-start.12
  55.1 2.1 %collective-permute-start.11 = (f32[3,2,2048]{2,1,0:T(2,128)S(1)}, f32[3,2,2048]{2,1,0:T(2,128)S(1)}, u32[]{:S(2)}, u32[]{:S(2)}) collective-permute-start(f32[3,2,2048]{2,1,0:T(2,128)S(1)} %coarse_stats.3.refs_8_), channel_id=1, source_target_pairs={{0,6},{2,4},{4,2},{6,0},{1,7},{3,5},{5,3},{7,1},{8,14},{10,12},{12... | collective-permute-start | bytes 147464 | tf_op jit(solution)/shard_map/ppermute | solution.py:560
  57.2 1.2 collective-permute-start.10
  58.4 2.5 %collective-permute-done.12.refs_11_ = f32[3,2,2048]{2,1,0:T(2,128)S(1)} collective-permute-done((f32[3,2,2048]{2,1,0:T(2,128)S(1)}, f32[3,2,2048]{2,1,0:T(2,128)S(1)}, u32[]{:S(2)}, u32[]{:S(2)}) %collective-permute-start.12) | collective-permute-done | bytes 49184 | tf_op jit(solution)/shard_map/ppermute | solution.py:560
  60.9 0.4 collective-permute-done.10.refs_9_
  61.3 34.2 %coarse_grads.1 = (bf16[2,3,512,128]{3,2,1,0:T(8,128)(2,1)S(1)}, bf16[2,3,512,128]{3,2,1,0:T(8,128)(2,1)S(1)}, bf16[192,512]{1,0:T(8,128)(2,1)S(1)}, bf16[192,51...) custom-call(bf16[3,512,128]{2,1,0:T(8,128)(2,1)} %get-tuple-element.45.refs_0_, ...), custom_call_target="tpu_custom_call" | custom-call | flops 32212254720 | bytes 4194304 | tf_op jit(solution)/shard_map/coarse_grads/pallas_call | solution.py:184
  95.5 0.0 copy-start.1
  95.5 0.1 collective-permute-start.16
  95.6 2.3 %collective-permute-done.16.refs_5_ = bf16[2,3,512,128]{3,2,1,0:T(8,128)(2,1)S(1)} collective-permute-done((bf16[2,3,512,128]{3,2,1,0:T(8,128)(2,1)S(1)}, bf16[2,3,512,128]{3,2,1,0:T(8,128)(2,1)S(1)}, u32[]{:S(2)}, u32[]{:S(2)}) %collective-permute-start.16) | collective-permute-done | bytes 786464 | tf_op jit(solution)/shard_map/ppermute | solution.py:560
  97.9 0.1 fusion
  98.0 0.1 collective-permute-start.17
  98.1 1.3 collective-permute-start.13
  99.3 1.9 %collective-permute-start.14 = (bf16[192,512]{1,0:T(8,128)(2,1)S(1)}, bf16[192,512]{1,0:T(8,128)(2,1)S(1)}, u32[]{:S(2)}, u32[]{:S(2)}) collective-permute-start(bf16[192,512]{1,0:T(8,128)(2,1)S(1)} %get-tuple-element.64), channel_id=1, source_target_pairs={{0,4},{2,6},{4,0},{6,2},{1,5},{3,7},{5,1},{7,3},{8,12},{10,14},{12... | collective-permute-start | bytes 589832 | tf_op jit(solution)/shard_map/ppermute | solution.py:560
  101.2 1.6 collective-permute-start.15
  102.8 0.1 select_bitcast_fusion
  102.9 5.6 %fine_shares.1 = (bf16[6,512,256]{2,1,0:T(8,128)(2,1)S(1)}, bf16[6,512,256]{2,1,0:T(8,128)(2,1)S(1)}, f32[256,384]{1,0:T(8,128)S(1)}) custom-call(bf16[3,256,384]{2,1,0:T(8,128)(2,1)S(1)} %bitcast.28, bf16[2,512,384]{2,1,0:T(8,128)(2,1)S(1)} %bitcast.24, bf16[2,256,384]{2,1,0:T(8,128)(2,1)S(1)} %get-tuple-element.88.low_ref, ...), custom_call_target="tpu_custom_call" | custom-call | flops 1073741824 | bytes 6291456 | tf_op jit(solution)/shard_map/fine_shares/pallas_call | solution.py:203
  108.5 0.7 collective-permute-done.17.refs_6_
  109.2 0.0 collective-permute-done.13.refs_1_
  109.2 1.0 collective-permute-done.14.refs_2_
  110.2 2.6 %collective-permute-done.15.refs_3_ = bf16[192,512]{1,0:T(8,128)(2,1)S(1)} collective-permute-done((bf16[192,512]{1,0:T(8,128)(2,1)S(1)}, bf16[192,512]{1,0:T(8,128)(2,1)S(1)}, u32[]{:S(2)}, u32[]{:S(2)}) %collective-permute-start.15) | collective-permute-done | bytes 196640 | tf_op jit(solution)/shard_map/ppermute | solution.py:560
  112.8 2.4 %project.1 = bf16[512,1536]{1,0:T(8,128)(2,1)S(1)} custom-call(bf16[192,512]{1,0:T(8,128)(2,1)S(1)} %get-tuple-element.62.refs_0_, bf16[192,512]{1,0:T(8,128)(2,1)S(1)} %collective-permute-done.13.refs_1_, bf16[192,512]{1,0:T(8,128)(2,1)S(1)} %collective-permute-done.14.refs_2_, bf16[192,512]{1,0:T(8,128)(2,1)S(1)} %collective-permute-done.15.refs_3_, ...), custom_call_target="tpu_custom_call" | custom-call | flops 2147483648 | bytes 6291456 | tf_op jit(solution)/shard_map/project/pallas_call | solution.py:504
  115.2 27.0 %all_to_all.5.in_ref = bf16[8,64,1536]{2,1,0:T(8,128)(2,1)S(1)} all-to-all(bf16[8,64,1536]{2,1,0:T(8,128)(2,1)S(1)} %bitcast.27), channel_id=1, replica_groups=mesh['x'=4,'zh'=2,'zl'=2,'y'=4,'c'=2] {'x','zh'}, dimensions={0} | all-to-all | bytes 3145728 | tf_op jit(solution)/shard_map/all_to_all | solution.py:634
  142.1 0.4 spread.1.up_ref
  142.5 3.7 %fine_sides.1 = (f32[256,384]{1,0:T(8,128)S(1)}, bf16[256,768]{1,0:T(8,128)(2,1)S(1)}, bf16[256,768]{1,0:T(8,128)(2,1)S(1)}) custom-call(bf16[3,256,384]{2,1,0:T(8,128)(2,1)S(1)} %bitcast.29, bf16[2,256,384]{2,1,0:T(8,128)(2,1)S(1)} %get-tuple-element.88.low_ref, bf16[2,256,384]{2,1,0:T(8,128)(2,1)S(1)} %get-tuple-element.87.high_ref, ...), custom_call_target="tpu_custom_call" | custom-call | flops 1073741824 | bytes 6291456 | tf_op jit(solution)/shard_map/fine_sides/pallas_call | solution.py:298
  146.2 0.1 collective-permute-start.18
  146.3 4.4 %collective-permute-start.19 = (bf16[256,768]{1,0:T(8,128)(2,1)S(1)}, bf16[256,768]{1,0:T(8,128)(2,1)S(1)}, u32[]{:S(2)}, u32[]{:S(2)}) collective-permute-start(bf16[256,768]{1,0:T(8,128)(2,1)S(1)} %get-tuple-element.80), channel_id=1, source_target_pairs={{1,2},{2,1},{3,4},{4,3},{5,6},{6,5},{7,8},{8,7},{9,10},{10,9},{11,... | collective-permute-start | bytes 1179656 | tf_op jit(solution)/shard_map/ppermute | solution.py:566
  150.7 4.3 %fine_middle.1 = (bf16[256,384]{1,0:T(8,128)(2,1)}, f32[128,768]{1,0:T(8,128)S(1)}, f32[256,768]{1,0:T(8,128)S(1)}, f32[128,768]{1,0:T(8,128)S(1)}) custom-call(bf16[3,256,384]{2,1,0:T(8,128)(2,1)S(1)} %bitcast.30, bf16[2,512,384]{2,1,0:T(8,128)(2,1)S(1)} %bitcast.25, bf16[256,384]{1,0:T(8,128)(2,1)S(1)} %spread.1.up_ref, ...), custom_call_target="tpu_custom_call" | custom-call | flops 1073741824 | bytes 6291456 | tf_op jit(solution)/shard_map/fine_middle/pallas_call | solution.py:298
  155.0 2.6 %collective-permute-done.19.outer_ref.side_out = bf16[256,768]{1,0:T(8,128)(2,1)S(1)} collective-permute-done((bf16[256,768]{1,0:T(8,128)(2,1)S(1)}, bf16[256,768]{1,0:T(8,128)(2,1)S(1)}, u32[]{:S(2)}, u32[]{:S(2)}) %collective-permute-start.19) | collective-permute-done | bytes 393248 | tf_op jit(solution)/shard_map/ppermute | solution.py:566
  157.6 0.1 add_strips.1
  157.7 2.4 %collective-permute-start.20 = (bf16[112,768]{1,0:T(8,128)(2,1)S(1)}, bf16[112,768]{1,0:T(8,128)(2,1)S(1)}, u32[]{:S(2)}, u32[]{:S(2)}) collective-permute-start(bf16[112,768]{1,0:T(8,128)(2,1)S(1)} %get-tuple-element.83), channel_id=1, source_target_pairs={{0,16},{16,0},{32,48},{48,32},{64,80},{80,64},{96,112},{112,96},{1... | collective-permute-start | bytes 516104 | tf_op jit(solution)/shard_map/ppermute | solution.py:560
  160.1 3.1 %collective-permute-start.21 = (bf16[112,768]{1,0:T(8,128)(2,1)S(1)}, bf16[112,768]{1,0:T(8,128)(2,1)S(1)}, u32[]{:S(2)}, u32[]{:S(2)}) collective-permute-start(bf16[112,768]{1,0:T(8,128)(2,1)S(1)} %get-tuple-element.84), channel_id=1, source_target_pairs={{16,32},{32,16},{48,64},{64,48},{80,96},{96,80},{17,33},{33,17},{4... | collective-permute-start | bytes 516104 | tf_op jit(solution)/shard_map/ppermute | solution.py:566
  163.2 1.5 collective-permute-done.20.row_in
  164.7 5.1 %collective-permute-done.21.row_out = bf16[112,768]{1,0:T(8,128)(2,1)S(1)} collective-permute-done((bf16[112,768]{1,0:T(8,128)(2,1)S(1)}, bf16[112,768]{1,0:T(8,128)(2,1)S(1)}, u32[]{:S(2)}, u32[]{:S(2)}) %collective-permute-start.21) | collective-permute-done | bytes 172064 | tf_op jit(solution)/shard_map/ppermute | solution.py:566
  169.8 0.9 add_all.1
  (16 shorter events, 0.0 us)
Async XLA Ops:
  0.6 13.0 %copy-start = (bf16[3,1536,192]{1,2,0:T(8,128)(2,1)S(1)}, bf16[3,1536,192]{1,2,0:T(8,128)(2,1)}, u32[]{:S(2)}) copy-start(bf16[3,1536,192]{1,2,0:T(8,128)(2,1)} %param.9) | copy-start | bytes 5308420
  0.6 1.3 copy-start.2
  1.9 0.9 copy-start.6
  4.0 1.9 %collective-permute-start = (bf16[3,512,128]{2,1,0:T(8,128)(2,1)}, bf16[3,512,128]{2,1,0:T(8,128)(2,1)S(1)}, u32[]{:S(2)}, u32[]{:S(2)}) collective-permute-start(bf16[3,512,128]{2,1,0:T(8,128)(2,1)} %get-tuple-element.45.refs_0_), channel_id=1, source_target_pairs={{0,1},{1,0},{2,3},{3,2},{4,5},{5,4},{6,7},{7,6},{8,9},{9,8},{10,11... | collective-permute-start | bytes 1179656 | tf_op jit(solution)/shard_map/ppermute | solution.py:560
  4.0 14.7 %collective-permute-start.1 = (bf16[3,512,128]{2,1,0:T(8,128)(2,1)}, bf16[3,512,128]{2,1,0:T(8,128)(2,1)}, u32[]{:S(2)}, u32[]{:S(2)}) collective-permute-start(bf16[3,512,128]{2,1,0:T(8,128)(2,1)} %get-tuple-element.45.refs_0_), channel_id=1, source_target_pairs={{0,8},{8,0},{1,9},{9,1},{2,10},{10,2},{3,11},{11,3},{4,12},{12,4},... | collective-permute-start | bytes 1179656 | tf_op jit(solution)/shard_map/ppermute | solution.py:560
  5.9 12.6 %copy-start.3 = (bf16[3,512,128]{2,1,0:T(8,128)(2,1)}, bf16[3,512,128]{2,1,0:T(8,128)(2,1)S(1)}, u32[]{:S(2)}) copy-start(bf16[3,512,128]{2,1,0:T(8,128)(2,1)S(1)} %collective-permute-done.refs_1_) | copy-start | bytes 1179652
  5.9 19.4 %collective-permute-start.6 = (bf16[3,512,128]{2,1,0:T(8,128)(2,1)}, bf16[3,512,128]{2,1,0:T(8,128)(2,1)}, u32[]{:S(2)}, u32[]{:S(2)}) collective-permute-start(bf16[3,512,128]{2,1,0:T(8,128)(2,1)} %get-tuple-element.53.refs_4_), channel_id=1, source_target_pairs={{0,6},{2,4},{4,2},{6,0},{1,7},{3,5},{5,3},{7,1},{8,14},{10,12},{12... | collective-permute-start | bytes 1179656 | tf_op jit(solution)/shard_map/ppermute | solution.py:560
  8.9 16.4 %collective-permute-start.5 = (bf16[3,512,128]{2,1,0:T(8,128)(2,1)}, bf16[3,512,128]{2,1,0:T(8,128)(2,1)}, u32[]{:S(2)}, u32[]{:S(2)}) collective-permute-start(bf16[3,512,128]{2,1,0:T(8,128)(2,1)} %get-tuple-element.53.refs_4_), channel_id=1, source_target_pairs={{0,2},{2,0},{4,6},{6,4},{1,3},{3,1},{5,7},{7,5},{8,10},{10,8},{12,... | collective-permute-start | bytes 1179656 | tf_op jit(solution)/shard_map/ppermute | solution.py:560
  10.1 11.0 %collective-permute-start.3 = (bf16[2,8,16,384]{3,2,1,0:T(8,128)(2,1)S(1)}, bf16[2,8,16,384]{3,2,1,0:T(8,128)(2,1)}, u32[]{:S(2)}, u32[]{:S(2)}) collective-permute-start(bf16[2,8,16,384]{3,2,1,0:T(8,128)(2,1)S(1)} %get-tuple-element.91), channel_id=1, source_target_pairs={{16,32},{32,16},{48,64},{64,48},{80,96},{96,80},{17,33},{33,17},{4... | collective-permute-start | bytes 589832 | tf_op jit(solution)/shard_map/ppermute | solution.py:566
  13.5 11.7 %collective-permute-start.2 = (bf16[2,8,16,384]{3,2,1,0:T(8,128)(2,1)S(1)}, bf16[2,8,16,384]{3,2,1,0:T(8,128)(2,1)}, u32[]{:S(2)}, u32[]{:S(2)}) collective-permute-start(bf16[2,8,16,384]{3,2,1,0:T(8,128)(2,1)S(1)} %get-tuple-element.92), channel_id=1, source_target_pairs={{0,16},{16,0},{32,48},{48,32},{64,80},{80,64},{96,112},{112,96},{1... | collective-permute-start | bytes 589832 | tf_op jit(solution)/shard_map/ppermute | solution.py:560
  25.3 2.1 %collective-permute-start.4 = (bf16[3,512,128]{2,1,0:T(8,128)(2,1)}, bf16[3,512,128]{2,1,0:T(8,128)(2,1)}, u32[]{:S(2)}, u32[]{:S(2)}) collective-permute-start(bf16[3,512,128]{2,1,0:T(8,128)(2,1)} %collective-permute-done.1.refs_2_), channel_id=1, source_target_pairs={{0,1},{1,0},{2,3},{3,2},{4,5},{5,4},{6,7},{7,6},{8,9},{9,8},{10,11... | collective-permute-start | bytes 1179656 | tf_op jit(solution)/shard_map/ppermute | solution.py:560
  25.3 18.2 %slice-start = ((bf16[3,16,16,384]{3,2,1,0:T(8,128)(2,1)}), bf16[2,16,16,384]{3,2,1,0:T(8,128)(2,1)S(1)}, s32[]{:S(2)}) async-start(bf16[3,16,16,384]{3,2,1,0:T(8,128)(2,1)} %param.5), calls=%async_computation.1 | async-start | bytes 786432 | tf_op jit(solution)/shard_map/slice | solution.py:599
  25.3 22.2 %collective-permute-start.7 = (bf16[3,512,128]{2,1,0:T(8,128)(2,1)}, bf16[3,512,128]{2,1,0:T(8,128)(2,1)S(1)}, u32[]{:S(2)}, u32[]{:S(2)}) collective-permute-start(bf16[3,512,128]{2,1,0:T(8,128)(2,1)} %get-tuple-element.53.refs_4_), channel_id=1, source_target_pairs={{0,4},{2,6},{4,0},{6,2},{1,5},{3,7},{5,1},{7,3},{8,12},{10,14},{12... | collective-permute-start | bytes 1179656 | tf_op jit(solution)/shard_map/ppermute | solution.py:560
  27.4 1.0 copy-start.4
  43.5 4.1 %copy-start.5 = (bf16[3,512,128]{2,1,0:T(8,128)(2,1)S(1)}, bf16[3,512,128]{2,1,0:T(8,128)(2,1)}, u32[]{:S(2)}) copy-start(bf16[3,512,128]{2,1,0:T(8,128)(2,1)} %copy-done.3) | copy-start | bytes 1179652
  43.7 11.2 %collective-permute-start.9 = (bf16[2,32,8,384]{3,2,1,0:T(8,128)(2,1)S(1)}, bf16[2,32,8,384]{3,2,1,0:T(8,128)(2,1)S(1)}, u32[]{:S(2)}, u32[]{:S(2)}) collective-permute-start(bf16[2,32,8,384]{3,2,1,0:T(8,128)(2,1)S(1)} %get-tuple-element.89), channel_id=1, source_target_pairs={{1,2},{2,1},{3,4},{4,3},{5,6},{6,5},{7,8},{8,7},{9,10},{10,9},{11,... | collective-permute-start | bytes 1179656 | tf_op jit(solution)/shard_map/ppermute | solution.py:566
  47.3 7.6 %collective-permute-start.8 = (bf16[2,32,8,384]{3,2,1,0:T(8,128)(2,1)S(1)}, bf16[2,32,8,384]{3,2,1,0:T(8,128)(2,1)S(1)}, u32[]{:S(2)}, u32[]{:S(2)}) collective-permute-start(bf16[2,32,8,384]{3,2,1,0:T(8,128)(2,1)S(1)} %get-tuple-element.90), channel_id=1, source_target_pairs={{0,1},{1,0},{2,3},{3,2},{4,5},{5,4},{6,7},{7,6},{8,9},{9,8},{10,11... | collective-permute-start | bytes 1179656 | tf_op jit(solution)/shard_map/ppermute | solution.py:560
  54.9 6.0 %collective-permute-start.12 = (f32[3,2,2048]{2,1,0:T(2,128)S(1)}, f32[3,2,2048]{2,1,0:T(2,128)S(1)}, u32[]{:S(2)}, u32[]{:S(2)}) collective-permute-start(f32[3,2,2048]{2,1,0:T(2,128)S(1)} %coarse_stats.3.refs_8_), channel_id=1, source_target_pairs={{0,4},{2,6},{4,0},{6,2},{1,5},{3,7},{5,1},{7,3},{8,12},{10,14},{12... | collective-permute-start | bytes 147464 | tf_op jit(solution)/shard_map/ppermute | solution.py:560
  55.1 5.8 %collective-permute-start.11 = (f32[3,2,2048]{2,1,0:T(2,128)S(1)}, f32[3,2,2048]{2,1,0:T(2,128)S(1)}, u32[]{:S(2)}, u32[]{:S(2)}) collective-permute-start(f32[3,2,2048]{2,1,0:T(2,128)S(1)} %coarse_stats.3.refs_8_), channel_id=1, source_target_pairs={{0,6},{2,4},{4,2},{6,0},{1,7},{3,5},{5,3},{7,1},{8,14},{10,12},{12... | collective-permute-start | bytes 147464 | tf_op jit(solution)/shard_map/ppermute | solution.py:560
  57.2 4.1 %collective-permute-start.10 = (f32[3,2,2048]{2,1,0:T(2,128)S(1)}, f32[3,2,2048]{2,1,0:T(2,128)S(1)}, u32[]{:S(2)}, u32[]{:S(2)}) collective-permute-start(f32[3,2,2048]{2,1,0:T(2,128)S(1)} %coarse_stats.3.refs_8_), channel_id=1, source_target_pairs={{0,2},{2,0},{4,6},{6,4},{1,3},{3,1},{5,7},{7,5},{8,10},{10,8},{12,... | collective-permute-start | bytes 147464 | tf_op jit(solution)/shard_map/ppermute | solution.py:560
  95.5 7.4 %copy-start.1 = (bf16[3,16,16,384]{3,2,1,0:T(8,128)(2,1)S(1)}, bf16[3,16,16,384]{3,2,1,0:T(8,128)(2,1)}, u32[]{:S(2)}) copy-start(bf16[3,16,16,384]{3,2,1,0:T(8,128)(2,1)} %param.5) | copy-start | bytes 1769476
  95.5 2.4 %collective-permute-start.16 = (bf16[2,3,512,128]{3,2,1,0:T(8,128)(2,1)S(1)}, bf16[2,3,512,128]{3,2,1,0:T(8,128)(2,1)S(1)}, u32[]{:S(2)}, u32[]{:S(2)}) collective-permute-start(bf16[2,3,512,128]{3,2,1,0:T(8,128)(2,1)S(1)} %get-tuple-element.67), channel_id=1, source_target_pairs={{0,1},{1,0},{2,3},{3,2},{4,5},{5,4},{6,7},{7,6},{8,9},{9,8},{10,11... | collective-permute-start | bytes 2359304 | tf_op jit(solution)/shard_map/ppermute | solution.py:560
  98.0 11.2 %collective-permute-start.17 = (bf16[3,512,128]{2,1,0:T(8,128)(2,1)S(1)}, bf16[3,512,128]{2,1,0:T(8,128)(2,1)S(1)}, u32[]{:S(2)}, u32[]{:S(2)}) collective-permute-start(bf16[3,512,128]{2,1,0:T(8,128)(2,1)S(1)} %fusion), channel_id=1, source_target_pairs={{0,8},{8,0},{1,9},{9,1},{2,10},{10,2},{3,11},{11,3},{4,12},{12,4},... | collective-permute-start | bytes 1179656 | tf_op jit(solution)/shard_map/ppermute | solution.py:560
  98.1 11.1 %collective-permute-start.13 = (bf16[192,512]{1,0:T(8,128)(2,1)S(1)}, bf16[192,512]{1,0:T(8,128)(2,1)S(1)}, u32[]{:S(2)}, u32[]{:S(2)}) collective-permute-start(bf16[192,512]{1,0:T(8,128)(2,1)S(1)} %get-tuple-element.63), channel_id=1, source_target_pairs={{0,2},{2,0},{4,6},{6,4},{1,3},{3,1},{5,7},{7,5},{8,10},{10,8},{12,... | collective-permute-start | bytes 589832 | tf_op jit(solution)/shard_map/ppermute | solution.py:560
  99.3 10.9 %collective-permute-start.14 = (bf16[192,512]{1,0:T(8,128)(2,1)S(1)}, bf16[192,512]{1,0:T(8,128)(2,1)S(1)}, u32[]{:S(2)}, u32[]{:S(2)}) collective-permute-start(bf16[192,512]{1,0:T(8,128)(2,1)S(1)} %get-tuple-element.64), channel_id=1, source_target_pairs={{0,4},{2,6},{4,0},{6,2},{1,5},{3,7},{5,1},{7,3},{8,12},{10,14},{12... | collective-permute-start | bytes 589832 | tf_op jit(solution)/shard_map/ppermute | solution.py:560
  101.2 11.5 %collective-permute-start.15 = (bf16[192,512]{1,0:T(8,128)(2,1)S(1)}, bf16[192,512]{1,0:T(8,128)(2,1)S(1)}, u32[]{:S(2)}, u32[]{:S(2)}) collective-permute-start(bf16[192,512]{1,0:T(8,128)(2,1)S(1)} %get-tuple-element.65), channel_id=1, source_target_pairs={{0,6},{2,4},{4,2},{6,0},{1,7},{3,5},{5,3},{7,1},{8,14},{10,12},{12... | collective-permute-start | bytes 589832 | tf_op jit(solution)/shard_map/ppermute | solution.py:560
  146.2 8.8 %collective-permute-start.18 = (bf16[256,768]{1,0:T(8,128)(2,1)S(1)}, bf16[256,768]{1,0:T(8,128)(2,1)S(1)}, u32[]{:S(2)}, u32[]{:S(2)}) collective-permute-start(bf16[256,768]{1,0:T(8,128)(2,1)S(1)} %get-tuple-element.79), channel_id=1, source_target_pairs={{0,1},{1,0},{2,3},{3,2},{4,5},{5,4},{6,7},{7,6},{8,9},{9,8},{10,11... | collective-permute-start | bytes 1179656 | tf_op jit(solution)/shard_map/ppermute | solution.py:560
  146.3 11.3 %collective-permute-start.19 = (bf16[256,768]{1,0:T(8,128)(2,1)S(1)}, bf16[256,768]{1,0:T(8,128)(2,1)S(1)}, u32[]{:S(2)}, u32[]{:S(2)}) collective-permute-start(bf16[256,768]{1,0:T(8,128)(2,1)S(1)} %get-tuple-element.80), channel_id=1, source_target_pairs={{1,2},{2,1},{3,4},{4,3},{5,6},{6,5},{7,8},{8,7},{9,10},{10,9},{11,... | collective-permute-start | bytes 1179656 | tf_op jit(solution)/shard_map/ppermute | solution.py:566
  157.7 7.0 %collective-permute-start.20 = (bf16[112,768]{1,0:T(8,128)(2,1)S(1)}, bf16[112,768]{1,0:T(8,128)(2,1)S(1)}, u32[]{:S(2)}, u32[]{:S(2)}) collective-permute-start(bf16[112,768]{1,0:T(8,128)(2,1)S(1)} %get-tuple-element.83), channel_id=1, source_target_pairs={{0,16},{16,0},{32,48},{48,32},{64,80},{80,64},{96,112},{112,96},{1... | collective-permute-start | bytes 516104 | tf_op jit(solution)/shard_map/ppermute | solution.py:560
  160.1 9.7 %collective-permute-start.21 = (bf16[112,768]{1,0:T(8,128)(2,1)S(1)}, bf16[112,768]{1,0:T(8,128)(2,1)S(1)}, u32[]{:S(2)}, u32[]{:S(2)}) collective-permute-start(bf16[112,768]{1,0:T(8,128)(2,1)S(1)} %get-tuple-element.84), channel_id=1, source_target_pairs={{16,32},{32,16},{48,64},{64,48},{80,96},{96,80},{17,33},{33,17},{4... | collective-permute-start | bytes 516104 | tf_op jit(solution)/shard_map/ppermute | solution.py:566

commit v10 on v9

--- a/solution.py
+++ b/solution.py
@@ -591,18 +591,12 @@
     )
     across = swapped(key_value, "zl")
     beside = swapped(key_value, "c")
-    beside, query_up, merge_weight, fine_qkv = lax.optimization_barrier(
-        (beside, query_up, merge_weight, fine_qkv)
-    )
+    beside, query_up, fine_qkv = lax.optimization_barrier((beside, query_up, fine_qkv))
     near = [query_up, swapped(query_up, "y", 1), swapped(query_up, "y", 3)]
     own_qkv = fine_qkv.reshape(3, own, width)
     edges = sent_rims(fine_qkv[1:], ROW, "zh", 1)
-    joint = lax.dot_general(
-        qkv_weight, merge_weight, (((1,), (1,)), ((), ())), preferred_element_type=F32
-    ).astype(BF16).reshape(3 * group, wide)
-    across, joint, *edges = lax.optimization_barrier((across, joint, *edges))
     corner = swapped(across, "c")
-    *near, joint = lax.optimization_barrier((*near, joint))
+    near = lax.optimization_barrier(near)
     far = swapped(near[0], "y", 2)
     keys = [key_value, beside, across, corner]
     queries = [near[0], near[1], far, near[2]]
@@ -613,15 +607,19 @@
     tall = jnp.concatenate([low, fine_qkv[1:], high], axis=1)
     edges = sent_rims(tall, COL, "c", 2)
     part = coarse_stats(keys, [far], [2], (part,), 256)
-    part, *edges = lax.optimization_barrier((part, *edges))
+    part, merge_weight, *edges = lax.optimization_barrier((part, merge_weight, *edges))
+    joint = lax.dot_general(
+        qkv_weight, merge_weight, (((1,), (1,)), ((), ())), preferred_element_type=F32
+    ).astype(BF16).reshape(3 * group, wide)
     stats = [part] + [swapped(part, "y", step) for step in (1, 3, 2)]
+    stats, joint = lax.optimization_barrier((stats, joint))
     kept, sent, *query_grads = coarse_grads(keys, queries, stats)
 
+    query_pieces = [query_grads[0], swapped(query_grads[2], "y", 2)]
     from_core = swapped(sent, "c")
     passed = (kept[1].astype(F32) + from_core[1].astype(F32)).astype(BF16)
     arrived = swapped(passed, "zl")
-    query_pieces = [query_grads[0]]
-    for step in (1, 2, 3):
+    for step in (1, 3):
         query_pieces.append(swapped(query_grads[step], "y", step))
     count = lax.axis_size(ROW)
     low, high = placed_rims(*edges, "c")

time: 171 us -> 164 us (0.959)
  blocking collectives: 27 us -> 29.5 us
  waiting for transfers between devices: 29.3 us -> 26.9 us
  other arithmetic: 2.71 us -> 0.67 us
  matrix products: 4.82 us -> 2.93 us
    ppermute x4, starting transfers between devices: 14.5 us -> 11.6 us  [exchanged(): return (swapped(inner, axis), lax.ppermute(outer, axis, beyond))]
    all_to_all x1, blocking collectives: 27 us -> 29.5 us  [shards(): pieces = lax.all_to_all(projected.reshape(count, -1, wide), ROW, 0, 0)]
    ppermute x18, waiting for transfers between devices: 17.1 us -> 15.2 us  [swapped(): lax.ppermute(array, axis, [(i, i ^ flip) for i in range(lax.axis_size(axi...]
    unnamed x1, matrix products: 4.82 us -> 2.93 us
  transfers between devices with their start and end apart: 22 -> 22, of which waited for: 14 -> 10; matrix products, arithmetic and copies ran while one was open for 4% -> 2% of each run, Pallas kernels for 17% -> 18%
where the time goes in v10:
time: 164 us
  Pallas kernels  71.3 us (43%)
  blocking collectives  29.5 us (18%)
  starting transfers between devices  29.2 us (18%)
  waiting for transfers between devices  26.9 us (16%)
  matrix products  2.93 us (2%)
  local copies, waits for them, and re-layouts  2.26 us (1%)
    pallas_call x1, Pallas kernels, coarse_grads(): pl.pallas_call(body, grid=(heads, blocks // 2), in_specs=[pl.BlockSpec((1...  34.1 us
    all_to_all x1, blocking collectives, shards(): pieces = lax.all_to_all(projected.reshape(count, -1, wide), ROW, 0, 0)  29.5 us
    pallas_call x2, Pallas kernels, coarse_stats(): pl.pallas_call(body, grid=(heads, number), in_specs=[pl.BlockSpec((1, tok...  19.6 us
    ppermute x18, starting transfers between devices, swapped(): lax.ppermute(array, axis, [(i, i ^ flip) for i in range(lax.axis_size(axi...  17.6 us
    ppermute x18, waiting for transfers between devices, swapped(): lax.ppermute(array, axis, [(i, i ^ flip) for i in range(lax.axis_size(axi...  15.2 us
    ppermute x4, waiting for transfers between devices, exchanged(): return (swapped(inner, axis), lax.ppermute(outer, axis, beyond))  11.7 us
    ppermute x4, starting transfers between devices, exchanged(): return (swapped(inner, axis), lax.ppermute(outer, axis, beyond))  11.6 us
    pallas_call x2, Pallas kernels, pair_call(): pl.pallas_call(body, grid=(pairs,), in_specs=[spec(array) for array in op...  7.98 us
  transfers between devices with their start and end apart: 22, of which 10 were waited for; matrix products, arithmetic and copies ran while one was open for 2% of the time, Pallas kernels for 18%

profile of v10, /device:TPU:96, one launch (start us, length us, event | category | flops | bytes accessed | tf_op | source)
XLA Modules:
  0.0 163.7 jit_solution(4202264532425055173)
XLA Ops:
  0.6 0.0 copy-start
  0.6 0.0 copy-start.1
  0.7 1.3 copy-done.2
  1.9 0.9 copy-done.3
  2.9 0.3 prepare.1
  3.2 0.1 collective-permute-start
  3.3 0.5 collective-permute-start.1
  3.7 1.2 collective-permute-done.refs_1_
  5.0 3.0 %collective-permute-start.4 = (bf16[3,512,128]{2,1,0:T(8,128)(2,1)S(1)}, bf16[3,512,128]{2,1,0:T(8,128)(2,1)}, u32[]{:S(2)}, u32[]{:S(2)}) collective-permute-start(bf16[3,512,128]{2,1,0:T(8,128)(2,1)S(1)} %get-tuple-element.50.refs_4_), channel_id=1, source_target_pairs={{0,6},{2,4},{4,2},{6,0},{1,7},{3,5},{5,3},{7,1},{8,14},{10,12},{12... | collective-permute-start | bytes 1179656 | tf_op jit(solution)/shard_map/ppermute | solution.py:560
  8.0 0.1 collective-permute-start.3
  8.1 6.8 %collective-permute-done.1.refs_2_ = bf16[3,512,128]{2,1,0:T(8,128)(2,1)} collective-permute-done((bf16[3,512,128]{2,1,0:T(8,128)(2,1)S(1)}, bf16[3,512,128]{2,1,0:T(8,128)(2,1)}, u32[]{:S(2)}, u32[]{:S(2)}) %collective-permute-start.1) | collective-permute-done | bytes 393248 | tf_op jit(solution)/shard_map/ppermute | solution.py:560
  14.9 0.0 collective-permute-start.2
  15.0 3.4 %collective-permute-start.6 = (bf16[2,8,16,384]{3,2,1,0:T(8,128)(2,1)S(1)}, bf16[2,8,16,384]{3,2,1,0:T(8,128)(2,1)S(1)}, u32[]{:S(2)}, u32[]{:S(2)}) collective-permute-start(bf16[2,8,16,384]{3,2,1,0:T(8,128)(2,1)S(1)} %get-tuple-element.91), channel_id=1, source_target_pairs={{16,32},{32,16},{48,64},{64,48},{80,96},{96,80},{17,33},{33,17},{4... | collective-permute-start | bytes 589832 | tf_op jit(solution)/shard_map/ppermute | solution.py:566
  18.3 0.0 slice-start
  18.4 0.1 collective-permute-start.5
  18.5 0.0 collective-permute-done.4.refs_6_.refs_7_
  18.5 0.5 collective-permute-done.3.refs_5_
  19.0 2.8 %collective-permute-start.7 = (bf16[3,512,128]{2,1,0:T(8,128)(2,1)S(1)}, bf16[3,512,128]{2,1,0:T(8,128)(2,1)S(1)}, u32[]{:S(2)}, u32[]{:S(2)}) collective-permute-start(bf16[3,512,128]{2,1,0:T(8,128)(2,1)S(1)} %get-tuple-element.50.refs_4_), channel_id=1, source_target_pairs={{0,4},{2,6},{4,0},{6,2},{1,5},{3,7},{5,1},{7,3},{8,12},{10,14},{12... | collective-permute-start | bytes 1179656 | tf_op jit(solution)/shard_map/ppermute | solution.py:560
  21.7 0.0 collective-permute-done.2.refs_3_
  21.8 14.0 %coarse_stats.2.refs_5_ = f32[3,2,2048]{2,1,0:T(2,128)S(1)} custom-call(bf16[3,512,128]{2,1,0:T(8,128)(2,1)S(1)} %get-tuple-element.45.refs_0_, bf16[3,512,128]{2,1,0:T(8,128)(2,1)S(1)} %collective-permute-done.refs_1_, bf16[3,512,128]{2,1,0:T(8,128)(2,1)} %collective-permute-done.1.refs_2_, bf16[3,512,128]{2,1,0:T(8,128)(2,1)} %collective-permute-done.2.refs_3_, ...), custom_call_target="tpu_custom_call" | custom-call | flops 9663676416 | bytes 2097152 | tf_op jit(solution)/shard_map/coarse_stats/pallas_call | solution.py:109
  35.8 0.0 collective-permute-done.6
  35.8 0.0 collective-permute-done.5
  35.9 0.1 pad_maximum_fusion
  36.0 0.1 broadcast_select_fusion
  36.1 1.9 %collective-permute-start.9 = (bf16[2,32,8,384]{3,2,1,0:T(8,128)(2,1)S(1)}, bf16[2,32,8,384]{3,2,1,0:T(8,128)(2,1)S(1)}, u32[]{:S(2)}, u32[]{:S(2)}) collective-permute-start(bf16[2,32,8,384]{3,2,1,0:T(8,128)(2,1)S(1)} %get-tuple-element.89), channel_id=1, source_target_pairs={{1,2},{2,1},{3,4},{4,3},{5,6},{6,5},{7,8},{8,7},{9,10},{10,9},{11,... | collective-permute-start | bytes 1179656 | tf_op jit(solution)/shard_map/ppermute | solution.py:566
  38.0 0.0 slice-start.1
  38.0 0.0 slice-start.2
  38.0 0.9 collective-permute-start.8
  38.9 5.6 %coarse_stats.3.refs_8_ = f32[3,2,2048]{2,1,0:T(2,128)S(1)} custom-call(bf16[3,512,128]{2,1,0:T(8,128)(2,1)S(1)} %get-tuple-element.45.refs_0_, bf16[3,512,128]{2,1,0:T(8,128)(2,1)S(1)} %collective-permute-done.refs_1_, bf16[3,512,128]{2,1,0:T(8,128)(2,1)} %collective-permute-done.1.refs_2_, bf16[3,512,128]{2,1,0:T(8,128)(2,1)} %collective-permute-done.2.refs_3_, ...), custom_call_target="tpu_custom_call" | custom-call | flops 3221225472 | bytes 2097152 | tf_op jit(solution)/shard_map/coarse_stats/pallas_call | solution.py:109
  44.5 2.8 %collective-permute-done.9 = bf16[2,32,8,384]{3,2,1,0:T(8,128)(2,1)S(1)} collective-permute-done((bf16[2,32,8,384]{3,2,1,0:T(8,128)(2,1)S(1)}, bf16[2,32,8,384]{3,2,1,0:T(8,128)(2,1)S(1)}, u32[]{:S(2)}, u32[]{:S(2)}) %collective-permute-start.9) | collective-permute-done | bytes 393248 | tf_op jit(solution)/shard_map/ppermute | solution.py:566
  47.3 0.0 collective-permute-done.8
  47.3 0.0 collective-permute-start.12
  47.3 1.2 collective-permute-start.11
  48.5 2.2 %collective-permute-start.10 = (f32[3,2,2048]{2,1,0:T(2,128)S(1)}, f32[3,2,2048]{2,1,0:T(2,128)S(1)}, u32[]{:S(2)}, u32[]{:S(2)}) collective-permute-start(f32[3,2,2048]{2,1,0:T(2,128)S(1)} %coarse_stats.3.refs_8_), channel_id=1, source_target_pairs={{0,2},{2,0},{4,6},{6,4},{1,3},{3,1},{5,7},{7,5},{8,10},{10,8},{12,... | collective-permute-start | bytes 147464 | tf_op jit(solution)/shard_map/ppermute | solution.py:560
  50.8 2.9 %fusion.1 = f32[1536,576]{0,1:S(1)} fusion(bf16[1536,1536]{1,0:T(8,128)(2,1)S(1)} %bitcast.35, bf16[1536,576]{0,1:T(8,128)(2,1)S(1)} %bitcast.23), kind=kOutput, calls=%fused_computation.11 | convolution fusion | flops 2717908992 | bytes 10027008
  53.7 0.2 convert_element_type.20
  53.9 0.0 collective-permute-done.12.refs_11_
  54.0 34.1 %coarse_grads.1 = (bf16[2,3,512,128]{3,2,1,0:T(8,128)(2,1)S(1)}, bf16[2,3,512,128]{3,2,1,0:T(8,128)(2,1)S(1)}, bf16[192,512]{1,0:T(8,128)(2,1)S(1)}, bf16[192,51...) custom-call(bf16[3,512,128]{2,1,0:T(8,128)(2,1)S(1)} %get-tuple-element.45.refs_0_, ...), custom_call_target="tpu_custom_call" | custom-call | flops 32212254720 | bytes 4194304 | tf_op jit(solution)/shard_map/coarse_grads/pallas_call | solution.py:184
  88.0 0.1 collective-permute-start.16
  88.1 2.3 %collective-permute-done.16.refs_5_ = bf16[2,3,512,128]{3,2,1,0:T(8,128)(2,1)S(1)} collective-permute-done((bf16[2,3,512,128]{3,2,1,0:T(8,128)(2,1)S(1)}, bf16[2,3,512,128]{3,2,1,0:T(8,128)(2,1)S(1)}, u32[]{:S(2)}, u32[]{:S(2)}) %collective-permute-start.16) | collective-permute-done | bytes 786464 | tf_op jit(solution)/shard_map/ppermute | solution.py:560
  90.4 0.1 fusion
  90.5 0.1 collective-permute-start.17
  90.6 1.3 collective-permute-start.13
  91.9 0.4 collective-permute-start.14
  92.3 2.5 %collective-permute-start.15 = (bf16[192,512]{1,0:T(8,128)(2,1)S(1)}, bf16[192,512]{1,0:T(8,128)(2,1)S(1)}, u32[]{:S(2)}, u32[]{:S(2)}) collective-permute-start(bf16[192,512]{1,0:T(8,128)(2,1)S(1)} %get-tuple-element.65), channel_id=1, source_target_pairs={{0,6},{2,4},{4,2},{6,0},{1,7},{3,5},{5,3},{7,1},{8,14},{10,12},{12... | collective-permute-start | bytes 589832 | tf_op jit(solution)/shard_map/ppermute | solution.py:560
  94.8 0.1 select_bitcast_fusion
  94.9 5.6 %fine_shares.1 = (bf16[6,512,256]{2,1,0:T(8,128)(2,1)S(1)}, bf16[6,512,256]{2,1,0:T(8,128)(2,1)S(1)}, f32[256,384]{1,0:T(8,128)S(1)}) custom-call(bf16[3,256,384]{2,1,0:T(8,128)(2,1)S(1)} %bitcast.28, bf16[2,512,384]{2,1,0:T(8,128)(2,1)S(1)} %bitcast.24, bf16[2,256,384]{2,1,0:T(8,128)(2,1)S(1)} %get-tuple-element.88.low_ref, ...), custom_call_target="tpu_custom_call" | custom-call | flops 1073741824 | bytes 6291456 | tf_op jit(solution)/shard_map/fine_shares/pallas_call | solution.py:203
  100.4 1.3 collective-permute-done.17.refs_6_
  101.8 0.0 collective-permute-done.14.refs_2_
  101.8 1.6 collective-permute-done.15.refs_3_
  103.4 2.4 %project.1 = bf16[512,1536]{1,0:T(8,128)(2,1)S(1)} custom-call(bf16[192,512]{1,0:T(8,128)(2,1)S(1)} %get-tuple-element.62.refs_0_, bf16[192,512]{1,0:T(8,128)(2,1)S(1)} %collective-permute-done.13.refs_1_, bf16[192,512]{1,0:T(8,128)(2,1)S(1)} %collective-permute-done.14.refs_2_, bf16[192,512]{1,0:T(8,128)(2,1)S(1)} %collective-permute-done.15.refs_3_, ...), custom_call_target="tpu_custom_call" | custom-call | flops 2147483648 | bytes 6291456 | tf_op jit(solution)/shard_map/project/pallas_call | solution.py:504
  105.8 29.5 %all_to_all.5.in_ref = bf16[8,64,1536]{2,1,0:T(8,128)(2,1)S(1)} all-to-all(bf16[8,64,1536]{2,1,0:T(8,128)(2,1)S(1)} %bitcast.27), channel_id=1, replica_groups=mesh['x'=4,'zh'=2,'zl'=2,'y'=4,'c'=2] {'x','zh'}, dimensions={0} | all-to-all | bytes 3145728 | tf_op jit(solution)/shard_map/all_to_all | solution.py:632
  135.3 0.4 spread.1.up_ref
  135.6 3.7 %fine_sides.1 = (f32[256,384]{1,0:T(8,128)S(1)}, bf16[256,768]{1,0:T(8,128)(2,1)S(1)}, bf16[256,768]{1,0:T(8,128)(2,1)S(1)}) custom-call(bf16[3,256,384]{2,1,0:T(8,128)(2,1)S(1)} %bitcast.29, bf16[2,256,384]{2,1,0:T(8,128)(2,1)S(1)} %get-tuple-element.88.low_ref, bf16[2,256,384]{2,1,0:T(8,128)(2,1)S(1)} %get-tuple-element.87.high_ref, ...), custom_call_target="tpu_custom_call" | custom-call | flops 1073741824 | bytes 6291456 | tf_op jit(solution)/shard_map/fine_sides/pallas_call | solution.py:298
  139.3 0.1 collective-permute-start.18
  139.4 3.0 %collective-permute-start.19 = (bf16[256,768]{1,0:T(8,128)(2,1)S(1)}, bf16[256,768]{1,0:T(8,128)(2,1)S(1)}, u32[]{:S(2)}, u32[]{:S(2)}) collective-permute-start(bf16[256,768]{1,0:T(8,128)(2,1)S(1)} %get-tuple-element.80), channel_id=1, source_target_pairs={{1,2},{2,1},{3,4},{4,3},{5,6},{6,5},{7,8},{8,7},{9,10},{10,9},{11,... | collective-permute-start | bytes 1179656 | tf_op jit(solution)/shard_map/ppermute | solution.py:566
  142.4 4.3 %fine_middle.1 = (bf16[256,384]{1,0:T(8,128)(2,1)}, f32[128,768]{1,0:T(8,128)S(1)}, f32[256,768]{1,0:T(8,128)S(1)}, f32[128,768]{1,0:T(8,128)S(1)}) custom-call(bf16[3,256,384]{2,1,0:T(8,128)(2,1)S(1)} %bitcast.30, bf16[2,512,384]{2,1,0:T(8,128)(2,1)S(1)} %bitcast.25, bf16[256,384]{1,0:T(8,128)(2,1)S(1)} %spread.1.up_ref, ...), custom_call_target="tpu_custom_call" | custom-call | flops 1073741824 | bytes 6291456 | tf_op jit(solution)/shard_map/fine_middle/pallas_call | solution.py:298
  146.7 4.0 %collective-permute-done.19.outer_ref.side_out = bf16[256,768]{1,0:T(8,128)(2,1)S(1)} collective-permute-done((bf16[256,768]{1,0:T(8,128)(2,1)S(1)}, bf16[256,768]{1,0:T(8,128)(2,1)S(1)}, u32[]{:S(2)}, u32[]{:S(2)}) %collective-permute-start.19) | collective-permute-done | bytes 393248 | tf_op jit(solution)/shard_map/ppermute | solution.py:566
  150.7 0.1 add_strips.1
  150.8 2.2 %collective-permute-start.20 = (bf16[112,768]{1,0:T(8,128)(2,1)S(1)}, bf16[112,768]{1,0:T(8,128)(2,1)S(1)}, u32[]{:S(2)}, u32[]{:S(2)}) collective-permute-start(bf16[112,768]{1,0:T(8,128)(2,1)S(1)} %get-tuple-element.83), channel_id=1, source_target_pairs={{0,16},{16,0},{32,48},{48,32},{64,80},{80,64},{96,112},{112,96},{1... | collective-permute-start | bytes 516104 | tf_op jit(solution)/shard_map/ppermute | solution.py:560
  153.1 3.3 %collective-permute-start.21 = (bf16[112,768]{1,0:T(8,128)(2,1)S(1)}, bf16[112,768]{1,0:T(8,128)(2,1)S(1)}, u32[]{:S(2)}, u32[]{:S(2)}) collective-permute-start(bf16[112,768]{1,0:T(8,128)(2,1)S(1)} %get-tuple-element.84), channel_id=1, source_target_pairs={{16,32},{32,16},{48,64},{64,48},{80,96},{96,80},{17,33},{33,17},{4... | collective-permute-start | bytes 516104 | tf_op jit(solution)/shard_map/ppermute | solution.py:566
  156.4 1.4 collective-permute-done.20.row_in
  157.8 4.9 %collective-permute-done.21.row_out = bf16[112,768]{1,0:T(8,128)(2,1)S(1)} collective-permute-done((bf16[112,768]{1,0:T(8,128)(2,1)S(1)}, bf16[112,768]{1,0:T(8,128)(2,1)S(1)}, u32[]{:S(2)}, u32[]{:S(2)}) %collective-permute-start.21) | collective-permute-done | bytes 172064 | tf_op jit(solution)/shard_map/ppermute | solution.py:566
  162.8 0.9 add_all.1
  (15 shorter events, 0.1 us)
Async XLA Ops:
  0.6 50.1 %copy-start = (bf16[3,1536,192]{1,2,0:T(8,128)(2,1)S(1)}, bf16[3,1536,192]{1,2,0:T(8,128)(2,1)}, u32[]{:S(2)}) copy-start(bf16[3,1536,192]{1,2,0:T(8,128)(2,1)} %param.9) | copy-start | bytes 5308420
  0.6 14.3 %copy-start.1 = (bf16[3,16,16,384]{3,2,1,0:T(8,128)(2,1)S(1)}, bf16[3,16,16,384]{3,2,1,0:T(8,128)(2,1)}, u32[]{:S(2)}) copy-start(bf16[3,16,16,384]{3,2,1,0:T(8,128)(2,1)} %param.5) | copy-start | bytes 1769476
  0.7 1.3 copy-start.2
  1.9 0.9 copy-start.3
  3.2 1.8 %collective-permute-start = (bf16[3,512,128]{2,1,0:T(8,128)(2,1)S(1)}, bf16[3,512,128]{2,1,0:T(8,128)(2,1)S(1)}, u32[]{:S(2)}, u32[]{:S(2)}) collective-permute-start(bf16[3,512,128]{2,1,0:T(8,128)(2,1)S(1)} %get-tuple-element.45.refs_0_), channel_id=1, source_target_pairs={{0,1},{1,0},{2,3},{3,2},{4,5},{5,4},{6,7},{7,6},{8,9},{9,8},{10,11... | collective-permute-start | bytes 1179656 | tf_op jit(solution)/shard_map/ppermute | solution.py:560
  3.3 11.6 %collective-permute-start.1 = (bf16[3,512,128]{2,1,0:T(8,128)(2,1)S(1)}, bf16[3,512,128]{2,1,0:T(8,128)(2,1)}, u32[]{:S(2)}, u32[]{:S(2)}) collective-permute-start(bf16[3,512,128]{2,1,0:T(8,128)(2,1)S(1)} %get-tuple-element.45.refs_0_), channel_id=1, source_target_pairs={{0,8},{8,0},{1,9},{9,1},{2,10},{10,2},{3,11},{11,3},{4,12},{12,4},... | collective-permute-start | bytes 1179656 | tf_op jit(solution)/shard_map/ppermute | solution.py:560
  5.0 13.5 %collective-permute-start.4 = (bf16[3,512,128]{2,1,0:T(8,128)(2,1)S(1)}, bf16[3,512,128]{2,1,0:T(8,128)(2,1)}, u32[]{:S(2)}, u32[]{:S(2)}) collective-permute-start(bf16[3,512,128]{2,1,0:T(8,128)(2,1)S(1)} %get-tuple-element.50.refs_4_), channel_id=1, source_target_pairs={{0,6},{2,4},{4,2},{6,0},{1,7},{3,5},{5,3},{7,1},{8,14},{10,12},{12... | collective-permute-start | bytes 1179656 | tf_op jit(solution)/shard_map/ppermute | solution.py:560
  8.0 11.0 %collective-permute-start.3 = (bf16[3,512,128]{2,1,0:T(8,128)(2,1)S(1)}, bf16[3,512,128]{2,1,0:T(8,128)(2,1)}, u32[]{:S(2)}, u32[]{:S(2)}) collective-permute-start(bf16[3,512,128]{2,1,0:T(8,128)(2,1)S(1)} %get-tuple-element.50.refs_4_), channel_id=1, source_target_pairs={{0,2},{2,0},{4,6},{6,4},{1,3},{3,1},{5,7},{7,5},{8,10},{10,8},{12,... | collective-permute-start | bytes 1179656 | tf_op jit(solution)/shard_map/ppermute | solution.py:560
  14.9 6.9 %collective-permute-start.2 = (bf16[3,512,128]{2,1,0:T(8,128)(2,1)}, bf16[3,512,128]{2,1,0:T(8,128)(2,1)}, u32[]{:S(2)}, u32[]{:S(2)}) collective-permute-start(bf16[3,512,128]{2,1,0:T(8,128)(2,1)} %collective-permute-done.1.refs_2_), channel_id=1, source_target_pairs={{0,1},{1,0},{2,3},{3,2},{4,5},{5,4},{6,7},{7,6},{8,9},{9,8},{10,11... | collective-permute-start | bytes 1179656 | tf_op jit(solution)/shard_map/ppermute | solution.py:560
  15.0 20.8 %collective-permute-start.6 = (bf16[2,8,16,384]{3,2,1,0:T(8,128)(2,1)S(1)}, bf16[2,8,16,384]{3,2,1,0:T(8,128)(2,1)S(1)}, u32[]{:S(2)}, u32[]{:S(2)}) collective-permute-start(bf16[2,8,16,384]{3,2,1,0:T(8,128)(2,1)S(1)} %get-tuple-element.91), channel_id=1, source_target_pairs={{16,32},{32,16},{48,64},{64,48},{80,96},{96,80},{17,33},{33,17},{4... | collective-permute-start | bytes 589832 | tf_op jit(solution)/shard_map/ppermute | solution.py:566
  18.3 17.5 %slice-start = ((bf16[3,16,16,384]{3,2,1,0:T(8,128)(2,1)}), bf16[2,16,16,384]{3,2,1,0:T(8,128)(2,1)S(1)}, s32[]{:S(2)}) async-start(bf16[3,16,16,384]{3,2,1,0:T(8,128)(2,1)} %param.5), calls=%async_computation.1 | async-start | bytes 786432 | tf_op jit(solution)/shard_map/slice | solution.py:597
  18.4 17.4 %collective-permute-start.5 = (bf16[2,8,16,384]{3,2,1,0:T(8,128)(2,1)S(1)}, bf16[2,8,16,384]{3,2,1,0:T(8,128)(2,1)S(1)}, u32[]{:S(2)}, u32[]{:S(2)}) collective-permute-start(bf16[2,8,16,384]{3,2,1,0:T(8,128)(2,1)S(1)} %get-tuple-element.92), channel_id=1, source_target_pairs={{0,16},{16,0},{32,48},{48,32},{64,80},{80,64},{96,112},{112,96},{1... | collective-permute-start | bytes 589832 | tf_op jit(solution)/shard_map/ppermute | solution.py:560
  19.0 19.9 %collective-permute-start.7 = (bf16[3,512,128]{2,1,0:T(8,128)(2,1)S(1)}, bf16[3,512,128]{2,1,0:T(8,128)(2,1)S(1)}, u32[]{:S(2)}, u32[]{:S(2)}) collective-permute-start(bf16[3,512,128]{2,1,0:T(8,128)(2,1)S(1)} %get-tuple-element.50.refs_4_), channel_id=1, source_target_pairs={{0,4},{2,6},{4,0},{6,2},{1,5},{3,7},{5,1},{7,3},{8,12},{10,14},{12... | collective-permute-start | bytes 1179656 | tf_op jit(solution)/shard_map/ppermute | solution.py:560
  36.1 11.2 %collective-permute-start.9 = (bf16[2,32,8,384]{3,2,1,0:T(8,128)(2,1)S(1)}, bf16[2,32,8,384]{3,2,1,0:T(8,128)(2,1)S(1)}, u32[]{:S(2)}, u32[]{:S(2)}) collective-permute-start(bf16[2,32,8,384]{3,2,1,0:T(8,128)(2,1)S(1)} %get-tuple-element.89), channel_id=1, source_target_pairs={{1,2},{2,1},{3,4},{4,3},{5,6},{6,5},{7,8},{8,7},{9,10},{10,9},{11,... | collective-permute-start | bytes 1179656 | tf_op jit(solution)/shard_map/ppermute | solution.py:566
  38.0 12.8 %slice-start.1 = ((s8[4718592]{0:T(1024)(128)(4,1)}), s8[4194304]{0:T(1024)(128)(4,1)S(1)}, s32[]{:S(2)}) async-start(s8[4718592]{0:T(1024)(128)(4,1)} %bitcast.34), calls=%async_computation.2 | async-start | bytes 8388608
  38.0 12.8 %slice-start.2 = ((s8[4718592]{0:T(1024)(128)(4,1)}), s8[524288]{0:T(1024)(128)(4,1)S(1)}, s32[]{:S(2)}) async-start(s8[4718592]{0:T(1024)(128)(4,1)} %bitcast.34), calls=%async_computation.3 | async-start | bytes 1048576
  38.0 9.3 %collective-permute-start.8 = (bf16[2,32,8,384]{3,2,1,0:T(8,128)(2,1)S(1)}, bf16[2,32,8,384]{3,2,1,0:T(8,128)(2,1)S(1)}, u32[]{:S(2)}, u32[]{:S(2)}) collective-permute-start(bf16[2,32,8,384]{3,2,1,0:T(8,128)(2,1)S(1)} %get-tuple-element.90), channel_id=1, source_target_pairs={{0,1},{1,0},{2,3},{3,2},{4,5},{5,4},{6,7},{7,6},{8,9},{9,8},{10,11... | collective-permute-start | bytes 1179656 | tf_op jit(solution)/shard_map/ppermute | solution.py:560
  47.3 6.7 %collective-permute-start.12 = (f32[3,2,2048]{2,1,0:T(2,128)S(1)}, f32[3,2,2048]{2,1,0:T(2,128)S(1)}, u32[]{:S(2)}, u32[]{:S(2)}) collective-permute-start(f32[3,2,2048]{2,1,0:T(2,128)S(1)} %coarse_stats.3.refs_8_), channel_id=1, source_target_pairs={{0,4},{2,6},{4,0},{6,2},{1,5},{3,7},{5,1},{7,3},{8,12},{10,14},{12... | collective-permute-start | bytes 147464 | tf_op jit(solution)/shard_map/ppermute | solution.py:560
  47.3 6.7 %collective-permute-start.11 = (f32[3,2,2048]{2,1,0:T(2,128)S(1)}, f32[3,2,2048]{2,1,0:T(2,128)S(1)}, u32[]{:S(2)}, u32[]{:S(2)}) collective-permute-start(f32[3,2,2048]{2,1,0:T(2,128)S(1)} %coarse_stats.3.refs_8_), channel_id=1, source_target_pairs={{0,6},{2,4},{4,2},{6,0},{1,7},{3,5},{5,3},{7,1},{8,14},{10,12},{12... | collective-permute-start | bytes 147464 | tf_op jit(solution)/shard_map/ppermute | solution.py:560
  48.5 5.4 %collective-permute-start.10 = (f32[3,2,2048]{2,1,0:T(2,128)S(1)}, f32[3,2,2048]{2,1,0:T(2,128)S(1)}, u32[]{:S(2)}, u32[]{:S(2)}) collective-permute-start(f32[3,2,2048]{2,1,0:T(2,128)S(1)} %coarse_stats.3.refs_8_), channel_id=1, source_target_pairs={{0,2},{2,0},{4,6},{6,4},{1,3},{3,1},{5,7},{7,5},{8,10},{10,8},{12,... | collective-permute-start | bytes 147464 | tf_op jit(solution)/shard_map/ppermute | solution.py:560
  88.0 2.4 %collective-permute-start.16 = (bf16[2,3,512,128]{3,2,1,0:T(8,128)(2,1)S(1)}, bf16[2,3,512,128]{3,2,1,0:T(8,128)(2,1)S(1)}, u32[]{:S(2)}, u32[]{:S(2)}) collective-permute-start(bf16[2,3,512,128]{3,2,1,0:T(8,128)(2,1)S(1)} %get-tuple-element.67), channel_id=1, source_target_pairs={{0,1},{1,0},{2,3},{3,2},{4,5},{5,4},{6,7},{7,6},{8,9},{9,8},{10,11... | collective-permute-start | bytes 2359304 | tf_op jit(solution)/shard_map/ppermute | solution.py:560
  90.5 11.2 %collective-permute-start.17 = (bf16[3,512,128]{2,1,0:T(8,128)(2,1)S(1)}, bf16[3,512,128]{2,1,0:T(8,128)(2,1)S(1)}, u32[]{:S(2)}, u32[]{:S(2)}) collective-permute-start(bf16[3,512,128]{2,1,0:T(8,128)(2,1)S(1)} %fusion), channel_id=1, source_target_pairs={{0,8},{8,0},{1,9},{9,1},{2,10},{10,2},{3,11},{11,3},{4,12},{12,4},... | collective-permute-start | bytes 1179656 | tf_op jit(solution)/shard_map/ppermute | solution.py:560
  90.6 11.1 %collective-permute-start.13 = (bf16[192,512]{1,0:T(8,128)(2,1)S(1)}, bf16[192,512]{1,0:T(8,128)(2,1)S(1)}, u32[]{:S(2)}, u32[]{:S(2)}) collective-permute-start(bf16[192,512]{1,0:T(8,128)(2,1)S(1)} %get-tuple-element.63), channel_id=1, source_target_pairs={{0,4},{2,6},{4,0},{6,2},{1,5},{3,7},{5,1},{7,3},{8,12},{10,14},{12... | collective-permute-start | bytes 589832 | tf_op jit(solution)/shard_map/ppermute | solution.py:560
  91.9 9.9 %collective-permute-start.14 = (bf16[192,512]{1,0:T(8,128)(2,1)S(1)}, bf16[192,512]{1,0:T(8,128)(2,1)S(1)}, u32[]{:S(2)}, u32[]{:S(2)}) collective-permute-start(bf16[192,512]{1,0:T(8,128)(2,1)S(1)} %get-tuple-element.64), channel_id=1, source_target_pairs={{0,2},{2,0},{4,6},{6,4},{1,3},{3,1},{5,7},{7,5},{8,10},{10,8},{12,... | collective-permute-start | bytes 589832 | tf_op jit(solution)/shard_map/ppermute | solution.py:560
  92.3 11.0 %collective-permute-start.15 = (bf16[192,512]{1,0:T(8,128)(2,1)S(1)}, bf16[192,512]{1,0:T(8,128)(2,1)S(1)}, u32[]{:S(2)}, u32[]{:S(2)}) collective-permute-start(bf16[192,512]{1,0:T(8,128)(2,1)S(1)} %get-tuple-element.65), channel_id=1, source_target_pairs={{0,6},{2,4},{4,2},{6,0},{1,7},{3,5},{5,3},{7,1},{8,14},{10,12},{12... | collective-permute-start | bytes 589832 | tf_op jit(solution)/shard_map/ppermute | solution.py:560
  139.3 7.4 %collective-permute-start.18 = (bf16[256,768]{1,0:T(8,128)(2,1)S(1)}, bf16[256,768]{1,0:T(8,128)(2,1)S(1)}, u32[]{:S(2)}, u32[]{:S(2)}) collective-permute-start(bf16[256,768]{1,0:T(8,128)(2,1)S(1)} %get-tuple-element.79), channel_id=1, source_target_pairs={{0,1},{1,0},{2,3},{3,2},{4,5},{5,4},{6,7},{7,6},{8,9},{9,8},{10,11... | collective-permute-start | bytes 1179656 | tf_op jit(solution)/shard_map/ppermute | solution.py:560
  139.4 11.3 %collective-permute-start.19 = (bf16[256,768]{1,0:T(8,128)(2,1)S(1)}, bf16[256,768]{1,0:T(8,128)(2,1)S(1)}, u32[]{:S(2)}, u32[]{:S(2)}) collective-permute-start(bf16[256,768]{1,0:T(8,128)(2,1)S(1)} %get-tuple-element.80), channel_id=1, source_target_pairs={{1,2},{2,1},{3,4},{4,3},{5,6},{6,5},{7,8},{8,7},{9,10},{10,9},{11,... | collective-permute-start | bytes 1179656 | tf_op jit(solution)/shard_map/ppermute | solution.py:566
  150.8 7.0 %collective-permute-start.20 = (bf16[112,768]{1,0:T(8,128)(2,1)S(1)}, bf16[112,768]{1,0:T(8,128)(2,1)S(1)}, u32[]{:S(2)}, u32[]{:S(2)}) collective-permute-start(bf16[112,768]{1,0:T(8,128)(2,1)S(1)} %get-tuple-element.83), channel_id=1, source_target_pairs={{0,16},{16,0},{32,48},{48,32},{64,80},{80,64},{96,112},{112,96},{1... | collective-permute-start | bytes 516104 | tf_op jit(solution)/shard_map/ppermute | solution.py:560
  153.1 9.7 %collective-permute-start.21 = (bf16[112,768]{1,0:T(8,128)(2,1)S(1)}, bf16[112,768]{1,0:T(8,128)(2,1)S(1)}, u32[]{:S(2)}, u32[]{:S(2)}) collective-permute-start(bf16[112,768]{1,0:T(8,128)(2,1)S(1)} %get-tuple-element.84), channel_id=1, source_target_pairs={{16,32},{32,16},{48,64},{64,48},{80,96},{96,80},{17,33},{33,17},{4... | collective-permute-start | bytes 516104 | tf_op jit(solution)/shard_map/ppermute | solution.py:566

commit v11 on v10

--- a/solution.py
+++ b/solution.py
@@ -567,11 +567,11 @@
 
 
 def sent_rims(block, axis, parity, at):
-    size = block.shape[at]
-    low = lax.slice_in_dim(block, 0, RIM, axis=at)
-    high = lax.slice_in_dim(block, size - RIM, None, axis=at)
+    far = block.shape[at] - RIM
     first = lax.axis_index(parity) == 0
-    return exchanged(jnp.where(first, high, low), jnp.where(first, low, high), axis)
+    inner = lax.dynamic_slice_in_dim(block, jnp.where(first, far, 0), RIM, axis=at)
+    outer = lax.dynamic_slice_in_dim(block, jnp.where(first, 0, far), RIM, axis=at)
+    return exchanged(inner, outer, axis)
 
 
 def placed_rims(inner, outer, parity):

time: 164 us -> 164 us (level)
  no operation moved by 1% of the time
where the time goes in v11:
time: 164 us
  Pallas kernels  71.3 us (43%)
  blocking collectives  29.5 us (18%)
  starting transfers between devices  29.2 us (18%)
  waiting for transfers between devices  26.9 us (16%)
  matrix products  2.93 us (2%)
  local copies, waits for them, and re-layouts  2.44 us (1%)
    pallas_call x1, Pallas kernels, coarse_grads(): pl.pallas_call(body, grid=(heads, blocks // 2), in_specs=[pl.BlockSpec((1...  34.1 us
    all_to_all x1, blocking collectives, shards(): pieces = lax.all_to_all(projected.reshape(count, -1, wide), ROW, 0, 0)  29.5 us
    pallas_call x2, Pallas kernels, coarse_stats(): pl.pallas_call(body, grid=(heads, number), in_specs=[pl.BlockSpec((1, tok...  19.6 us
    ppermute x18, starting transfers between devices, swapped(): lax.ppermute(array, axis, [(i, i ^ flip) for i in range(lax.axis_size(axi...  17.6 us
    ppermute x18, waiting for transfers between devices, swapped(): lax.ppermute(array, axis, [(i, i ^ flip) for i in range(lax.axis_size(axi...  15.1 us
    ppermute x4, waiting for transfers between devices, exchanged(): return (swapped(inner, axis), lax.ppermute(outer, axis, beyond))  11.8 us
    ppermute x4, starting transfers between devices, exchanged(): return (swapped(inner, axis), lax.ppermute(outer, axis, beyond))  11.6 us
    pallas_call x2, Pallas kernels, pair_call(): pl.pallas_call(body, grid=(pairs,), in_specs=[spec(array) for array in op...  7.98 us
  transfers between devices with their start and end apart: 22, of which 10 were waited for; matrix products, arithmetic and copies ran while one was open for 2% of the time, Pallas kernels for 18%

profile of v11, /device:TPU:96, one launch (start us, length us, event | category | flops | bytes accessed | tf_op | source)
XLA Modules:
  0.0 163.7 jit_solution(5795028001204058400)
XLA Ops:
  0.6 0.0 copy-start
  0.7 1.3 copy-done.2
  1.9 0.9 copy-done.3
  2.9 0.3 prepare.1
  3.2 0.1 collective-permute-start
  3.3 0.5 collective-permute-start.1
  3.7 1.2 collective-permute-done.refs_1_
  5.0 3.0 %collective-permute-start.4 = (bf16[3,512,128]{2,1,0:T(8,128)(2,1)S(1)}, bf16[3,512,128]{2,1,0:T(8,128)(2,1)}, u32[]{:S(2)}, u32[]{:S(2)}) collective-permute-start(bf16[3,512,128]{2,1,0:T(8,128)(2,1)S(1)} %get-tuple-element.50.refs_4_), channel_id=1, source_target_pairs={{0,6},{2,4},{4,2},{6,0},{1,7},{3,5},{5,3},{7,1},{8,14},{10,12},{12... | collective-permute-start | bytes 1179656 | tf_op jit(solution)/shard_map/ppermute | solution.py:560
  8.0 0.1 collective-permute-start.3
  8.1 6.8 %collective-permute-done.1.refs_2_ = bf16[3,512,128]{2,1,0:T(8,128)(2,1)} collective-permute-done((bf16[3,512,128]{2,1,0:T(8,128)(2,1)S(1)}, bf16[3,512,128]{2,1,0:T(8,128)(2,1)}, u32[]{:S(2)}, u32[]{:S(2)}) %collective-permute-start.1) | collective-permute-done | bytes 393248 | tf_op jit(solution)/shard_map/ppermute | solution.py:560
  14.9 0.0 collective-permute-start.2
  14.9 0.1 constant_dynamic-slice_fusion.2
  15.0 3.4 %collective-permute-start.6 = (bf16[2,8,16,384]{3,2,1,0:T(8,128)(2,1)S(1)}, bf16[2,8,16,384]{3,2,1,0:T(8,128)(2,1)S(1)}, u32[]{:S(2)}, u32[]{:S(2)}) collective-permute-start(bf16[2,8,16,384]{3,2,1,0:T(8,128)(2,1)S(1)} %get-tuple-element.93), channel_id=1, source_target_pairs={{16,32},{32,16},{48,64},{64,48},{80,96},{96,80},{17,33},{33,17},{4... | collective-permute-start | bytes 589832 | tf_op jit(solution)/shard_map/ppermute | solution.py:566
  18.4 0.1 collective-permute-start.5
  18.5 0.0 collective-permute-done.4.refs_6_.refs_7_
  18.5 0.5 collective-permute-done.3.refs_5_
  19.0 2.8 %collective-permute-start.7 = (bf16[3,512,128]{2,1,0:T(8,128)(2,1)S(1)}, bf16[3,512,128]{2,1,0:T(8,128)(2,1)S(1)}, u32[]{:S(2)}, u32[]{:S(2)}) collective-permute-start(bf16[3,512,128]{2,1,0:T(8,128)(2,1)S(1)} %get-tuple-element.50.refs_4_), channel_id=1, source_target_pairs={{0,4},{2,6},{4,0},{6,2},{1,5},{3,7},{5,1},{7,3},{8,12},{10,14},{12... | collective-permute-start | bytes 1179656 | tf_op jit(solution)/shard_map/ppermute | solution.py:560
  21.8 0.0 collective-permute-done.2.refs_3_
  21.8 14.0 %coarse_stats.2.refs_5_ = f32[3,2,2048]{2,1,0:T(2,128)S(1)} custom-call(bf16[3,512,128]{2,1,0:T(8,128)(2,1)S(1)} %get-tuple-element.45.refs_0_, bf16[3,512,128]{2,1,0:T(8,128)(2,1)S(1)} %collective-permute-done.refs_1_, bf16[3,512,128]{2,1,0:T(8,128)(2,1)} %collective-permute-done.1.refs_2_, bf16[3,512,128]{2,1,0:T(8,128)(2,1)} %collective-permute-done.2.refs_3_, ...), custom_call_target="tpu_custom_call" | custom-call | flops 9663676416 | bytes 2097152 | tf_op jit(solution)/shard_map/coarse_stats/pallas_call | solution.py:109
  35.8 0.0 collective-permute-done.6
  35.8 0.0 collective-permute-done.5
  35.9 0.1 pad_maximum_fusion
  36.0 0.1 constant_dynamic-slice_fusion
  36.1 1.9 %collective-permute-start.9 = (bf16[2,32,8,384]{3,2,1,0:T(8,128)(2,1)S(1)}, bf16[2,32,8,384]{3,2,1,0:T(8,128)(2,1)S(1)}, u32[]{:S(2)}, u32[]{:S(2)}) collective-permute-start(bf16[2,32,8,384]{3,2,1,0:T(8,128)(2,1)S(1)} %get-tuple-element.89), channel_id=1, source_target_pairs={{1,2},{2,1},{3,4},{4,3},{5,6},{6,5},{7,8},{8,7},{9,10},{10,9},{11,... | collective-permute-start | bytes 1179656 | tf_op jit(solution)/shard_map/ppermute | solution.py:566
  38.0 0.0 slice-start
  38.0 0.0 slice-start.1
  38.1 0.8 collective-permute-start.8
  38.9 5.6 %coarse_stats.3.refs_8_ = f32[3,2,2048]{2,1,0:T(2,128)S(1)} custom-call(bf16[3,512,128]{2,1,0:T(8,128)(2,1)S(1)} %get-tuple-element.45.refs_0_, bf16[3,512,128]{2,1,0:T(8,128)(2,1)S(1)} %collective-permute-done.refs_1_, bf16[3,512,128]{2,1,0:T(8,128)(2,1)} %collective-permute-done.1.refs_2_, bf16[3,512,128]{2,1,0:T(8,128)(2,1)} %collective-permute-done.2.refs_3_, ...), custom_call_target="tpu_custom_call" | custom-call | flops 3221225472 | bytes 2097152 | tf_op jit(solution)/shard_map/coarse_stats/pallas_call | solution.py:109
  44.5 2.8 %collective-permute-done.9 = bf16[2,32,8,384]{3,2,1,0:T(8,128)(2,1)S(1)} collective-permute-done((bf16[2,32,8,384]{3,2,1,0:T(8,128)(2,1)S(1)}, bf16[2,32,8,384]{3,2,1,0:T(8,128)(2,1)S(1)}, u32[]{:S(2)}, u32[]{:S(2)}) %collective-permute-start.9) | collective-permute-done | bytes 393248 | tf_op jit(solution)/shard_map/ppermute | solution.py:566
  47.3 0.0 collective-permute-done.8
  47.3 0.0 collective-permute-start.12
  47.3 1.2 collective-permute-start.11
  48.5 2.3 %collective-permute-start.10 = (f32[3,2,2048]{2,1,0:T(2,128)S(1)}, f32[3,2,2048]{2,1,0:T(2,128)S(1)}, u32[]{:S(2)}, u32[]{:S(2)}) collective-permute-start(f32[3,2,2048]{2,1,0:T(2,128)S(1)} %coarse_stats.3.refs_8_), channel_id=1, source_target_pairs={{0,2},{2,0},{4,6},{6,4},{1,3},{3,1},{5,7},{7,5},{8,10},{10,8},{12,... | collective-permute-start | bytes 147464 | tf_op jit(solution)/shard_map/ppermute | solution.py:560
  50.8 2.9 %fusion.1 = f32[1536,576]{0,1:S(1)} fusion(bf16[1536,1536]{1,0:T(8,128)(2,1)S(1)} %bitcast.35, bf16[1536,576]{0,1:T(8,128)(2,1)S(1)} %bitcast.23), kind=kOutput, calls=%fused_computation.11 | convolution fusion | flops 2717908992 | bytes 10027008
  53.8 0.2 convert_element_type.20
  54.0 0.0 collective-permute-done.11.refs_10_
  54.0 0.0 collective-permute-done.10.refs_9_
  54.0 34.1 %coarse_grads.1 = (bf16[2,3,512,128]{3,2,1,0:T(8,128)(2,1)S(1)}, bf16[2,3,512,128]{3,2,1,0:T(8,128)(2,1)S(1)}, bf16[192,512]{1,0:T(8,128)(2,1)S(1)}, bf16[192,51...) custom-call(bf16[3,512,128]{2,1,0:T(8,128)(2,1)S(1)} %get-tuple-element.45.refs_0_, ...), custom_call_target="tpu_custom_call" | custom-call | flops 32212254720 | bytes 4194304 | tf_op jit(solution)/shard_map/coarse_grads/pallas_call | solution.py:184
  88.1 0.1 collective-permute-start.16
  88.2 2.3 %collective-permute-done.16.refs_5_ = bf16[2,3,512,128]{3,2,1,0:T(8,128)(2,1)S(1)} collective-permute-done((bf16[2,3,512,128]{3,2,1,0:T(8,128)(2,1)S(1)}, bf16[2,3,512,128]{3,2,1,0:T(8,128)(2,1)S(1)}, u32[]{:S(2)}, u32[]{:S(2)}) %collective-permute-start.16) | collective-permute-done | bytes 786464 | tf_op jit(solution)/shard_map/ppermute | solution.py:560
  90.5 0.1 fusion
  90.6 0.1 collective-permute-start.17
  90.7 1.3 collective-permute-start.13
  91.9 0.4 collective-permute-start.14
  92.4 2.4 %collective-permute-start.15 = (bf16[192,512]{1,0:T(8,128)(2,1)S(1)}, bf16[192,512]{1,0:T(8,128)(2,1)S(1)}, u32[]{:S(2)}, u32[]{:S(2)}) collective-permute-start(bf16[192,512]{1,0:T(8,128)(2,1)S(1)} %get-tuple-element.65), channel_id=1, source_target_pairs={{0,6},{2,4},{4,2},{6,0},{1,7},{3,5},{5,3},{7,1},{8,14},{10,12},{12... | collective-permute-start | bytes 589832 | tf_op jit(solution)/shard_map/ppermute | solution.py:560
  94.8 0.1 select_bitcast_fusion
  94.9 5.6 %fine_shares.1 = (bf16[6,512,256]{2,1,0:T(8,128)(2,1)S(1)}, bf16[6,512,256]{2,1,0:T(8,128)(2,1)S(1)}, f32[256,384]{1,0:T(8,128)S(1)}) custom-call(bf16[3,256,384]{2,1,0:T(8,128)(2,1)S(1)} %bitcast.28, bf16[2,512,384]{2,1,0:T(8,128)(2,1)S(1)} %bitcast.24, bf16[2,256,384]{2,1,0:T(8,128)(2,1)S(1)} %get-tuple-element.88.low_ref, ...), custom_call_target="tpu_custom_call" | custom-call | flops 1073741824 | bytes 6291456 | tf_op jit(solution)/shard_map/fine_shares/pallas_call | solution.py:203
  100.5 1.3 collective-permute-done.17.refs_6_
  101.8 1.6 collective-permute-done.15.refs_3_
  103.4 2.4 %project.1 = bf16[512,1536]{1,0:T(8,128)(2,1)S(1)} custom-call(bf16[192,512]{1,0:T(8,128)(2,1)S(1)} %get-tuple-element.62.refs_0_, bf16[192,512]{1,0:T(8,128)(2,1)S(1)} %collective-permute-done.13.refs_1_, bf16[192,512]{1,0:T(8,128)(2,1)S(1)} %collective-permute-done.14.refs_2_, bf16[192,512]{1,0:T(8,128)(2,1)S(1)} %collective-permute-done.15.refs_3_, ...), custom_call_target="tpu_custom_call" | custom-call | flops 2147483648 | bytes 6291456 | tf_op jit(solution)/shard_map/project/pallas_call | solution.py:504
  105.8 29.5 %all_to_all.5.in_ref = bf16[8,64,1536]{2,1,0:T(8,128)(2,1)S(1)} all-to-all(bf16[8,64,1536]{2,1,0:T(8,128)(2,1)S(1)} %bitcast.27), channel_id=1, replica_groups=mesh['x'=4,'zh'=2,'zl'=2,'y'=4,'c'=2] {'x','zh'}, dimensions={0} | all-to-all | bytes 3145728 | tf_op jit(solution)/shard_map/all_to_all | solution.py:632
  135.3 0.4 spread.1.up_ref
  135.7 3.7 %fine_sides.1 = (f32[256,384]{1,0:T(8,128)S(1)}, bf16[256,768]{1,0:T(8,128)(2,1)S(1)}, bf16[256,768]{1,0:T(8,128)(2,1)S(1)}) custom-call(bf16[3,256,384]{2,1,0:T(8,128)(2,1)S(1)} %bitcast.29, bf16[2,256,384]{2,1,0:T(8,128)(2,1)S(1)} %get-tuple-element.88.low_ref, bf16[2,256,384]{2,1,0:T(8,128)(2,1)S(1)} %get-tuple-element.87.high_ref, ...), custom_call_target="tpu_custom_call" | custom-call | flops 1073741824 | bytes 6291456 | tf_op jit(solution)/shard_map/fine_sides/pallas_call | solution.py:298
  139.4 0.1 collective-permute-start.18
  139.5 3.0 %collective-permute-start.19 = (bf16[256,768]{1,0:T(8,128)(2,1)S(1)}, bf16[256,768]{1,0:T(8,128)(2,1)S(1)}, u32[]{:S(2)}, u32[]{:S(2)}) collective-permute-start(bf16[256,768]{1,0:T(8,128)(2,1)S(1)} %get-tuple-element.80), channel_id=1, source_target_pairs={{1,2},{2,1},{3,4},{4,3},{5,6},{6,5},{7,8},{8,7},{9,10},{10,9},{11,... | collective-permute-start | bytes 1179656 | tf_op jit(solution)/shard_map/ppermute | solution.py:566
  142.4 4.3 %fine_middle.1 = (bf16[256,384]{1,0:T(8,128)(2,1)}, f32[128,768]{1,0:T(8,128)S(1)}, f32[256,768]{1,0:T(8,128)S(1)}, f32[128,768]{1,0:T(8,128)S(1)}) custom-call(bf16[3,256,384]{2,1,0:T(8,128)(2,1)S(1)} %bitcast.30, bf16[2,512,384]{2,1,0:T(8,128)(2,1)S(1)} %bitcast.25, bf16[256,384]{1,0:T(8,128)(2,1)S(1)} %spread.1.up_ref, ...), custom_call_target="tpu_custom_call" | custom-call | flops 1073741824 | bytes 6291456 | tf_op jit(solution)/shard_map/fine_middle/pallas_call | solution.py:298
  146.7 0.0 collective-permute-done.18.inner_ref.side_in
  146.7 4.0 %collective-permute-done.19.outer_ref.side_out = bf16[256,768]{1,0:T(8,128)(2,1)S(1)} collective-permute-done((bf16[256,768]{1,0:T(8,128)(2,1)S(1)}, bf16[256,768]{1,0:T(8,128)(2,1)S(1)}, u32[]{:S(2)}, u32[]{:S(2)}) %collective-permute-start.19) | collective-permute-done | bytes 393248 | tf_op jit(solution)/shard_map/ppermute | solution.py:566
  150.7 0.1 add_strips.1
  150.9 2.2 %collective-permute-start.20 = (bf16[112,768]{1,0:T(8,128)(2,1)S(1)}, bf16[112,768]{1,0:T(8,128)(2,1)S(1)}, u32[]{:S(2)}, u32[]{:S(2)}) collective-permute-start(bf16[112,768]{1,0:T(8,128)(2,1)S(1)} %get-tuple-element.83), channel_id=1, source_target_pairs={{0,16},{16,0},{32,48},{48,32},{64,80},{80,64},{96,112},{112,96},{1... | collective-permute-start | bytes 516104 | tf_op jit(solution)/shard_map/ppermute | solution.py:560
  153.1 3.3 %collective-permute-start.21 = (bf16[112,768]{1,0:T(8,128)(2,1)S(1)}, bf16[112,768]{1,0:T(8,128)(2,1)S(1)}, u32[]{:S(2)}, u32[]{:S(2)}) collective-permute-start(bf16[112,768]{1,0:T(8,128)(2,1)S(1)} %get-tuple-element.84), channel_id=1, source_target_pairs={{16,32},{32,16},{48,64},{64,48},{80,96},{96,80},{17,33},{33,17},{4... | collective-permute-start | bytes 516104 | tf_op jit(solution)/shard_map/ppermute | solution.py:566
  156.4 1.4 collective-permute-done.20.row_in
  157.9 4.9 %collective-permute-done.21.row_out = bf16[112,768]{1,0:T(8,128)(2,1)S(1)} collective-permute-done((bf16[112,768]{1,0:T(8,128)(2,1)S(1)}, bf16[112,768]{1,0:T(8,128)(2,1)S(1)}, u32[]{:S(2)}, u32[]{:S(2)}) %collective-permute-start.21) | collective-permute-done | bytes 172064 | tf_op jit(solution)/shard_map/ppermute | solution.py:566
  162.8 0.9 add_all.1
  (14 shorter events, 0.1 us)
Async XLA Ops:
  0.6 50.2 %copy-start = (bf16[3,1536,192]{1,2,0:T(8,128)(2,1)S(1)}, bf16[3,1536,192]{1,2,0:T(8,128)(2,1)}, u32[]{:S(2)}) copy-start(bf16[3,1536,192]{1,2,0:T(8,128)(2,1)} %param.9) | copy-start | bytes 5308420
  0.6 14.3 %copy-start.1 = (bf16[3,16,16,384]{3,2,1,0:T(8,128)(2,1)S(1)}, bf16[3,16,16,384]{3,2,1,0:T(8,128)(2,1)}, u32[]{:S(2)}) copy-start(bf16[3,16,16,384]{3,2,1,0:T(8,128)(2,1)} %param.5) | copy-start | bytes 1769476
  0.7 1.3 copy-start.2
  1.9 0.9 copy-start.3
  3.2 1.8 %collective-permute-start = (bf16[3,512,128]{2,1,0:T(8,128)(2,1)S(1)}, bf16[3,512,128]{2,1,0:T(8,128)(2,1)S(1)}, u32[]{:S(2)}, u32[]{:S(2)}) collective-permute-start(bf16[3,512,128]{2,1,0:T(8,128)(2,1)S(1)} %get-tuple-element.45.refs_0_), channel_id=1, source_target_pairs={{0,1},{1,0},{2,3},{3,2},{4,5},{5,4},{6,7},{7,6},{8,9},{9,8},{10,11... | collective-permute-start | bytes 1179656 | tf_op jit(solution)/shard_map/ppermute | solution.py:560
  3.3 11.6 %collective-permute-start.1 = (bf16[3,512,128]{2,1,0:T(8,128)(2,1)S(1)}, bf16[3,512,128]{2,1,0:T(8,128)(2,1)}, u32[]{:S(2)}, u32[]{:S(2)}) collective-permute-start(bf16[3,512,128]{2,1,0:T(8,128)(2,1)S(1)} %get-tuple-element.45.refs_0_), channel_id=1, source_target_pairs={{0,8},{8,0},{1,9},{9,1},{2,10},{10,2},{3,11},{11,3},{4,12},{12,4},... | collective-permute-start | bytes 1179656 | tf_op jit(solution)/shard_map/ppermute | solution.py:560
  5.0 13.5 %collective-permute-start.4 = (bf16[3,512,128]{2,1,0:T(8,128)(2,1)S(1)}, bf16[3,512,128]{2,1,0:T(8,128)(2,1)}, u32[]{:S(2)}, u32[]{:S(2)}) collective-permute-start(bf16[3,512,128]{2,1,0:T(8,128)(2,1)S(1)} %get-tuple-element.50.refs_4_), channel_id=1, source_target_pairs={{0,6},{2,4},{4,2},{6,0},{1,7},{3,5},{5,3},{7,1},{8,14},{10,12},{12... | collective-permute-start | bytes 1179656 | tf_op jit(solution)/shard_map/ppermute | solution.py:560
  8.0 11.0 %collective-permute-start.3 = (bf16[3,512,128]{2,1,0:T(8,128)(2,1)S(1)}, bf16[3,512,128]{2,1,0:T(8,128)(2,1)}, u32[]{:S(2)}, u32[]{:S(2)}) collective-permute-start(bf16[3,512,128]{2,1,0:T(8,128)(2,1)S(1)} %get-tuple-element.50.refs_4_), channel_id=1, source_target_pairs={{0,2},{2,0},{4,6},{6,4},{1,3},{3,1},{5,7},{7,5},{8,10},{10,8},{12,... | collective-permute-start | bytes 1179656 | tf_op jit(solution)/shard_map/ppermute | solution.py:560
  14.9 6.9 %collective-permute-start.2 = (bf16[3,512,128]{2,1,0:T(8,128)(2,1)}, bf16[3,512,128]{2,1,0:T(8,128)(2,1)}, u32[]{:S(2)}, u32[]{:S(2)}) collective-permute-start(bf16[3,512,128]{2,1,0:T(8,128)(2,1)} %collective-permute-done.1.refs_2_), channel_id=1, source_target_pairs={{0,1},{1,0},{2,3},{3,2},{4,5},{5,4},{6,7},{7,6},{8,9},{9,8},{10,11... | collective-permute-start | bytes 1179656 | tf_op jit(solution)/shard_map/ppermute | solution.py:560
  15.0 20.8 %collective-permute-start.6 = (bf16[2,8,16,384]{3,2,1,0:T(8,128)(2,1)S(1)}, bf16[2,8,16,384]{3,2,1,0:T(8,128)(2,1)S(1)}, u32[]{:S(2)}, u32[]{:S(2)}) collective-permute-start(bf16[2,8,16,384]{3,2,1,0:T(8,128)(2,1)S(1)} %get-tuple-element.93), channel_id=1, source_target_pairs={{16,32},{32,16},{48,64},{64,48},{80,96},{96,80},{17,33},{33,17},{4... | collective-permute-start | bytes 589832 | tf_op jit(solution)/shard_map/ppermute | solution.py:566
  18.4 17.4 %collective-permute-start.5 = (bf16[2,8,16,384]{3,2,1,0:T(8,128)(2,1)S(1)}, bf16[2,8,16,384]{3,2,1,0:T(8,128)(2,1)S(1)}, u32[]{:S(2)}, u32[]{:S(2)}) collective-permute-start(bf16[2,8,16,384]{3,2,1,0:T(8,128)(2,1)S(1)} %get-tuple-element.94), channel_id=1, source_target_pairs={{0,16},{16,0},{32,48},{48,32},{64,80},{80,64},{96,112},{112,96},{1... | collective-permute-start | bytes 589832 | tf_op jit(solution)/shard_map/ppermute | solution.py:560
  19.0 19.9 %collective-permute-start.7 = (bf16[3,512,128]{2,1,0:T(8,128)(2,1)S(1)}, bf16[3,512,128]{2,1,0:T(8,128)(2,1)S(1)}, u32[]{:S(2)}, u32[]{:S(2)}) collective-permute-start(bf16[3,512,128]{2,1,0:T(8,128)(2,1)S(1)} %get-tuple-element.50.refs_4_), channel_id=1, source_target_pairs={{0,4},{2,6},{4,0},{6,2},{1,5},{3,7},{5,1},{7,3},{8,12},{10,14},{12... | collective-permute-start | bytes 1179656 | tf_op jit(solution)/shard_map/ppermute | solution.py:560
  36.1 11.2 %collective-permute-start.9 = (bf16[2,32,8,384]{3,2,1,0:T(8,128)(2,1)S(1)}, bf16[2,32,8,384]{3,2,1,0:T(8,128)(2,1)S(1)}, u32[]{:S(2)}, u32[]{:S(2)}) collective-permute-start(bf16[2,32,8,384]{3,2,1,0:T(8,128)(2,1)S(1)} %get-tuple-element.89), channel_id=1, source_target_pairs={{1,2},{2,1},{3,4},{4,3},{5,6},{6,5},{7,8},{8,7},{9,10},{10,9},{11,... | collective-permute-start | bytes 1179656 | tf_op jit(solution)/shard_map/ppermute | solution.py:566
  38.0 12.8 %slice-start = ((s8[4718592]{0:T(1024)(128)(4,1)}), s8[4194304]{0:T(1024)(128)(4,1)S(1)}, s32[]{:S(2)}) async-start(s8[4718592]{0:T(1024)(128)(4,1)} %bitcast.34), calls=%async_computation.1 | async-start | bytes 8388608
  38.0 12.8 %slice-start.1 = ((s8[4718592]{0:T(1024)(128)(4,1)}), s8[524288]{0:T(1024)(128)(4,1)S(1)}, s32[]{:S(2)}) async-start(s8[4718592]{0:T(1024)(128)(4,1)} %bitcast.34), calls=%async_computation.2 | async-start | bytes 1048576
  38.1 9.3 %collective-permute-start.8 = (bf16[2,32,8,384]{3,2,1,0:T(8,128)(2,1)S(1)}, bf16[2,32,8,384]{3,2,1,0:T(8,128)(2,1)S(1)}, u32[]{:S(2)}, u32[]{:S(2)}) collective-permute-start(bf16[2,32,8,384]{3,2,1,0:T(8,128)(2,1)S(1)} %get-tuple-element.90), channel_id=1, source_target_pairs={{0,1},{1,0},{2,3},{3,2},{4,5},{5,4},{6,7},{7,6},{8,9},{9,8},{10,11... | collective-permute-start | bytes 1179656 | tf_op jit(solution)/shard_map/ppermute | solution.py:560
  47.3 6.7 %collective-permute-start.12 = (f32[3,2,2048]{2,1,0:T(2,128)S(1)}, f32[3,2,2048]{2,1,0:T(2,128)S(1)}, u32[]{:S(2)}, u32[]{:S(2)}) collective-permute-start(f32[3,2,2048]{2,1,0:T(2,128)S(1)} %coarse_stats.3.refs_8_), channel_id=1, source_target_pairs={{0,4},{2,6},{4,0},{6,2},{1,5},{3,7},{5,1},{7,3},{8,12},{10,14},{12... | collective-permute-start | bytes 147464 | tf_op jit(solution)/shard_map/ppermute | solution.py:560
  47.3 6.7 %collective-permute-start.11 = (f32[3,2,2048]{2,1,0:T(2,128)S(1)}, f32[3,2,2048]{2,1,0:T(2,128)S(1)}, u32[]{:S(2)}, u32[]{:S(2)}) collective-permute-start(f32[3,2,2048]{2,1,0:T(2,128)S(1)} %coarse_stats.3.refs_8_), channel_id=1, source_target_pairs={{0,6},{2,4},{4,2},{6,0},{1,7},{3,5},{5,3},{7,1},{8,14},{10,12},{12... | collective-permute-start | bytes 147464 | tf_op jit(solution)/shard_map/ppermute | solution.py:560
  48.5 5.4 %collective-permute-start.10 = (f32[3,2,2048]{2,1,0:T(2,128)S(1)}, f32[3,2,2048]{2,1,0:T(2,128)S(1)}, u32[]{:S(2)}, u32[]{:S(2)}) collective-permute-start(f32[3,2,2048]{2,1,0:T(2,128)S(1)} %coarse_stats.3.refs_8_), channel_id=1, source_target_pairs={{0,2},{2,0},{4,6},{6,4},{1,3},{3,1},{5,7},{7,5},{8,10},{10,8},{12,... | collective-permute-start | bytes 147464 | tf_op jit(solution)/shard_map/ppermute | solution.py:560
  88.1 2.4 %collective-permute-start.16 = (bf16[2,3,512,128]{3,2,1,0:T(8,128)(2,1)S(1)}, bf16[2,3,512,128]{3,2,1,0:T(8,128)(2,1)S(1)}, u32[]{:S(2)}, u32[]{:S(2)}) collective-permute-start(bf16[2,3,512,128]{3,2,1,0:T(8,128)(2,1)S(1)} %get-tuple-element.67), channel_id=1, source_target_pairs={{0,1},{1,0},{2,3},{3,2},{4,5},{5,4},{6,7},{7,6},{8,9},{9,8},{10,11... | collective-permute-start | bytes 2359304 | tf_op jit(solution)/shard_map/ppermute | solution.py:560
  90.6 11.2 %collective-permute-start.17 = (bf16[3,512,128]{2,1,0:T(8,128)(2,1)S(1)}, bf16[3,512,128]{2,1,0:T(8,128)(2,1)S(1)}, u32[]{:S(2)}, u32[]{:S(2)}) collective-permute-start(bf16[3,512,128]{2,1,0:T(8,128)(2,1)S(1)} %fusion), channel_id=1, source_target_pairs={{0,8},{8,0},{1,9},{9,1},{2,10},{10,2},{3,11},{11,3},{4,12},{12,4},... | collective-permute-start | bytes 1179656 | tf_op jit(solution)/shard_map/ppermute | solution.py:560
  90.7 11.1 %collective-permute-start.13 = (bf16[192,512]{1,0:T(8,128)(2,1)S(1)}, bf16[192,512]{1,0:T(8,128)(2,1)S(1)}, u32[]{:S(2)}, u32[]{:S(2)}) collective-permute-start(bf16[192,512]{1,0:T(8,128)(2,1)S(1)} %get-tuple-element.63), channel_id=1, source_target_pairs={{0,4},{2,6},{4,0},{6,2},{1,5},{3,7},{5,1},{7,3},{8,12},{10,14},{12... | collective-permute-start | bytes 589832 | tf_op jit(solution)/shard_map/ppermute | solution.py:560
  91.9 9.9 %collective-permute-start.14 = (bf16[192,512]{1,0:T(8,128)(2,1)S(1)}, bf16[192,512]{1,0:T(8,128)(2,1)S(1)}, u32[]{:S(2)}, u32[]{:S(2)}) collective-permute-start(bf16[192,512]{1,0:T(8,128)(2,1)S(1)} %get-tuple-element.64), channel_id=1, source_target_pairs={{0,2},{2,0},{4,6},{6,4},{1,3},{3,1},{5,7},{7,5},{8,10},{10,8},{12,... | collective-permute-start | bytes 589832 | tf_op jit(solution)/shard_map/ppermute | solution.py:560
  92.4 11.0 %collective-permute-start.15 = (bf16[192,512]{1,0:T(8,128)(2,1)S(1)}, bf16[192,512]{1,0:T(8,128)(2,1)S(1)}, u32[]{:S(2)}, u32[]{:S(2)}) collective-permute-start(bf16[192,512]{1,0:T(8,128)(2,1)S(1)} %get-tuple-element.65), channel_id=1, source_target_pairs={{0,6},{2,4},{4,2},{6,0},{1,7},{3,5},{5,3},{7,1},{8,14},{10,12},{12... | collective-permute-start | bytes 589832 | tf_op jit(solution)/shard_map/ppermute | solution.py:560
  139.4 7.4 %collective-permute-start.18 = (bf16[256,768]{1,0:T(8,128)(2,1)S(1)}, bf16[256,768]{1,0:T(8,128)(2,1)S(1)}, u32[]{:S(2)}, u32[]{:S(2)}) collective-permute-start(bf16[256,768]{1,0:T(8,128)(2,1)S(1)} %get-tuple-element.79), channel_id=1, source_target_pairs={{0,1},{1,0},{2,3},{3,2},{4,5},{5,4},{6,7},{7,6},{8,9},{9,8},{10,11... | collective-permute-start | bytes 1179656 | tf_op jit(solution)/shard_map/ppermute | solution.py:560
  139.5 11.3 %collective-permute-start.19 = (bf16[256,768]{1,0:T(8,128)(2,1)S(1)}, bf16[256,768]{1,0:T(8,128)(2,1)S(1)}, u32[]{:S(2)}, u32[]{:S(2)}) collective-permute-start(bf16[256,768]{1,0:T(8,128)(2,1)S(1)} %get-tuple-element.80), channel_id=1, source_target_pairs={{1,2},{2,1},{3,4},{4,3},{5,6},{6,5},{7,8},{8,7},{9,10},{10,9},{11,... | collective-permute-start | bytes 1179656 | tf_op jit(solution)/shard_map/ppermute | solution.py:566
  150.9 7.0 %collective-permute-start.20 = (bf16[112,768]{1,0:T(8,128)(2,1)S(1)}, bf16[112,768]{1,0:T(8,128)(2,1)S(1)}, u32[]{:S(2)}, u32[]{:S(2)}) collective-permute-start(bf16[112,768]{1,0:T(8,128)(2,1)S(1)} %get-tuple-element.83), channel_id=1, source_target_pairs={{0,16},{16,0},{32,48},{48,32},{64,80},{80,64},{96,112},{112,96},{1... | collective-permute-start | bytes 516104 | tf_op jit(solution)/shard_map/ppermute | solution.py:560
  153.1 9.7 %collective-permute-start.21 = (bf16[112,768]{1,0:T(8,128)(2,1)S(1)}, bf16[112,768]{1,0:T(8,128)(2,1)S(1)}, u32[]{:S(2)}, u32[]{:S(2)}) collective-permute-start(bf16[112,768]{1,0:T(8,128)(2,1)S(1)} %get-tuple-element.84), channel_id=1, source_target_pairs={{16,32},{32,16},{48,64},{64,48},{80,96},{96,80},{17,33},{33,17},{4... | collective-permute-start | bytes 516104 | tf_op jit(solution)/shard_map/ppermute | solution.py:566
